TPU v7x, 32 devices: a whole 2x2x4 slice. The times are simulated.
32 devices in a mesh: xg: 4 (over x, core), yd: 8 (over z, y).
Axes of the slice: x: 2, y: 2, z: 4, core: 2. Of those that a mesh axis runs over, the one named last changes fastest.
Arguments:
- mobile: float32 [512, 1, 1024], P('yd', None, 'xg'), may hold values from 0 to 2
- dispersion_x: float32 [512, 1, 1024], P('yd', None, 'xg'), may hold values from 0.5 to 200000
- dispersion_y: float32 [512, 1, 1024], P('yd', None, 'xg'), may hold values from 0.5 to 200000
- capacity: float32 [512, 1, 1024], P('yd', None, 'xg'), may hold values from 0.5 to 8
- immobile: float32 [4, 512, 1, 1024], P(None, 'yd', None, 'xg'), may hold values from 0 to 2
- exchange_rates: float32 [4], replicated, may hold values from 0.02 to 50
- rate_shares: float32 [4], replicated, may hold values from 0.1 to 1
Outputs:
- updated: float32 [512, 1, 1024], P('yd', None, 'xg')
All inputs are finite; a program needn't handle non-finite values.
Results may differ from a plain program's by a relative error of at most 0.0003.
Values sent between devices are 32-bit elements; how exact they have to be, the bound alone decides.
No kernel may reach another device: no remote copies, remote signals or barrier semaphores. Data moves between devices by JAX's collectives and lax.ppermute only.
A program may use at most 64 MiB of HBM per device.

v0:
```python
import jax
import jax.numpy as jnp
from jax import lax
from jax.sharding import PartitionSpec as P


def shifted_2(value, axis, steps):
    count = lax.axis_size(axis)
    pairs = [(source, (source + steps) % count) for source in range(count)]
    return lax.ppermute(value, axis, pairs)


def shifted(values, stride, axis, filling):
    length = values.shape[axis]
    if stride > 0:
        kept_part = lax.slice_in_dim(values, 0, length - stride, axis=axis)
        filler = jnp.full_like(lax.slice_in_dim(values, 0, stride, axis=axis), filling)
        return jnp.concatenate([filler, kept_part], axis=axis)
    backward = -stride
    kept_part = lax.slice_in_dim(values, backward, length, axis=axis)
    filler = jnp.full_like(lax.slice_in_dim(values, 0, backward, axis=axis), filling)
    return jnp.concatenate([kept_part, filler], axis=axis)


def pick_at(values, position, axis):
    return lax.index_in_dim(values, position, axis, keepdims=False)


def periodic_solve(face_coef, storage, right_side, axis):
    length = right_side.shape[axis]
    sub_coef = -face_coef
    super_coef = -jnp.roll(face_coef, -1, axis)
    main_coef = storage + face_coef - super_coef
    stride = 1
    while stride < length // 2:
        sub_left = jnp.roll(sub_coef, stride, axis)
        main_left = jnp.roll(main_coef, stride, axis)
        super_left = jnp.roll(super_coef, stride, axis)
        side_left = jnp.roll(right_side, stride, axis)
        sub_right = jnp.roll(sub_coef, -stride, axis)
        main_right = jnp.roll(main_coef, -stride, axis)
        super_right = jnp.roll(super_coef, -stride, axis)
        side_right = jnp.roll(right_side, -stride, axis)
        left_ratio = sub_coef / main_left
        right_ratio = super_coef / main_right
        main_coef = main_coef - left_ratio * super_left - right_ratio * sub_right
        right_side = right_side - left_ratio * side_left - right_ratio * side_right
        sub_coef = -left_ratio * sub_left
        super_coef = -right_ratio * super_right
        stride = stride * 2
    coupling = sub_coef + super_coef
    main_other = jnp.roll(main_coef, stride, axis)
    coupling_other = jnp.roll(coupling, stride, axis)
    side_other = jnp.roll(right_side, stride, axis)
    return (right_side * main_other - coupling * side_other) / (
        main_coef * main_other - coupling * coupling_other
    )


def block_solve(face_coef, storage, source, axis):
    length = source.shape[axis]
    position = lax.broadcasted_iota(jnp.int32, source.shape, axis)
    at_first = position == 0
    at_last = position == length - 1
    following = shifted(face_coef, -1, axis, 0.0)
    nothing = jnp.zeros_like(source)
    sub_coef = jnp.where(at_first | at_last, nothing, -face_coef)
    super_coef = jnp.where(at_last, nothing, -following)
    main_coef = jnp.where(at_last, 1.0, storage + face_coef + following)
    right_side = jnp.stack(
        [
            jnp.where(at_last, nothing, source),
            jnp.where(at_first, face_coef, nothing),
            jnp.where(at_last, 1.0, nothing),
        ]
    )
    stride = 1
    while stride < length:
        sub_left = shifted(sub_coef, stride, axis, 0.0)
        main_left = shifted(main_coef, stride, axis, 1.0)
        super_left = shifted(super_coef, stride, axis, 0.0)
        side_left = shifted(right_side, stride, axis + 1, 0.0)
        sub_right = shifted(sub_coef, -stride, axis, 0.0)
        main_right = shifted(main_coef, -stride, axis, 1.0)
        super_right = shifted(super_coef, -stride, axis, 0.0)
        side_right = shifted(right_side, -stride, axis + 1, 0.0)
        left_ratio = sub_coef / main_left
        right_ratio = super_coef / main_right
        right_side = right_side - left_ratio[None] * side_left - right_ratio[None] * side_right
        main_coef = main_coef - left_ratio * super_left - right_ratio * sub_right
        sub_coef = -left_ratio * sub_left
        super_coef = -right_ratio * super_right
        stride = stride * 2
    return right_side / main_coef[None]


def reduced_rows(solved, face_coef, storage, source, upcoming, axis):
    from_next, face_next = upcoming
    length = source.shape[axis]
    face_last = pick_at(face_coef, length - 1, axis)
    sub_last = -face_last
    super_last = -face_next
    main_last = pick_at(storage, length - 1, axis) + face_last + face_next
    coef_prev = sub_last * pick_at(solved[1], length - 2, axis)
    coef_self = (
        main_last + sub_last * pick_at(solved[2], length - 2, axis) + super_last * from_next[1]
    )
    coef_next = super_last * from_next[2]
    target = (
        pick_at(source, length - 1, axis)
        - sub_last * pick_at(solved[0], length - 2, axis)
        - super_last * from_next[0]
    )
    return (coef_prev, coef_self, coef_next, target)


def dense_cyclic(all_rows, group_size):
    matrix_rows = []
    targets = []
    for row_index in range(group_size):
        entries = [jnp.zeros_like(all_rows[row_index, 1]) for column in range(group_size)]
        entries[(row_index - 1) % group_size] = all_rows[row_index, 0]
        entries[row_index] = all_rows[row_index, 1]
        entries[(row_index + 1) % group_size] = all_rows[row_index, 2]
        matrix_rows.append(entries)
        targets.append(all_rows[row_index, 3])
    for pivot in range(group_size):
        for row_index in range(pivot + 1, group_size):
            factor = matrix_rows[row_index][pivot] / matrix_rows[pivot][pivot]
            matrix_rows[row_index] = [
                matrix_rows[row_index][column] - factor * matrix_rows[pivot][column]
                for column in range(group_size)
            ]
            targets[row_index] = targets[row_index] - factor * targets[pivot]
    solutions = [None] * group_size
    for row_index in reversed(range(group_size)):
        total = targets[row_index]
        for column in range(row_index + 1, group_size):
            total = total - matrix_rows[row_index][column] * solutions[column]
        solutions[row_index] = total / matrix_rows[row_index][row_index]
    return jnp.stack(solutions)


def local(mobile, dispersion_x, dispersion_y, capacity, immobile, exchange_rates, rate_shares):
    weights = rate_shares * exchange_rates / (1.0 + exchange_rates)
    gain_terms = capacity[None] * weights[:, None, None, None]
    storage = 1.0 + jnp.sum(gain_terms, axis=0)
    source = mobile + jnp.sum(gain_terms * immobile, axis=0)
    solved = block_solve(dispersion_x, storage, source, 2)
    head_values = pick_at(solved, 0, 3)
    upcoming = shifted_2((head_values, pick_at(dispersion_x, 0, 2)), "xg", -1)
    rows = reduced_rows(solved, dispersion_x, storage, source, upcoming, 2)
    group_size = lax.axis_size("xg")
    all_rows = lax.all_gather(jnp.stack(rows)[None], "xg", axis=0, tiled=True)
    solutions = dense_cyclic(all_rows, group_size)
    own_index = lax.axis_index("xg")
    own_value = lax.dynamic_index_in_dim(solutions, own_index, 0, keepdims=False)
    prev_value = lax.dynamic_index_in_dim(
        solutions, (own_index + group_size - 1) % group_size, 0, keepdims=False
    )
    after_x = solved[0] + solved[1] * prev_value[..., None] + solved[2] * own_value[..., None]
    group_count = lax.axis_size("yd")

    def regroup(values):
        return values.reshape(values.shape[0], group_count, -1)

    line_values = lax.all_to_all(regroup(after_x), "yd", split_axis=1, concat_axis=0, tiled=True)
    line_faces = lax.all_to_all(
        regroup(dispersion_y), "yd", split_axis=1, concat_axis=0, tiled=True
    )
    line_storage = lax.all_to_all(regroup(storage), "yd", split_axis=1, concat_axis=0, tiled=True)
    solved_lines = periodic_solve(line_faces, line_storage, line_storage * line_values, 0)
    updated = lax.all_to_all(solved_lines, "yd", split_axis=0, concat_axis=1, tiled=True)
    updated = updated.reshape(after_x.shape)
    return updated


def solution(mesh):
    return jax.shard_map(
        local,
        mesh=mesh,
        in_specs=(
            P("yd", None, "xg"),
            P("yd", None, "xg"),
            P("yd", None, "xg"),
            P("yd", None, "xg"),
            P(None, "yd", None, "xg"),
            P(),
            P(),
        ),
        out_specs=P("yd", None, "xg"),
        check_vma=False,
    )
```

profile of v0, /device:TPU:0, one launch (start us, length us, event | category | flops | bytes accessed | tf_op | source)
XLA Modules:
  0.0 72.0 jit_solution(7970653988725002045)
XLA Ops:
  0.0 0.9 %copy.95 = f32[64,1,256]{2,0,1:T(8,128)S(1)} copy(f32[64,1,256]{2,1,0:T(1,128)} %param.10) | data formatting | bytes 131072
  0.9 1.6 %fusion = (f32[64,256]{1,0:T(8,128)S(1)}, f32[64,256]{1,0:T(8,128)S(1)}) fusion(f32[4,64,1,256]{3,2,1,0:T(1,128)} %param.11, f32[64,256]{1,0:T(8,128)S(1)} %bitcast.400, f32[4]{0:T(128)S(1)} %add_divide_fusion), kind=kLoop, calls=%fused_computation.2 | loop fusion | flops 229376 | bytes 458768 | tf_op jit(solution)/shard_map/reduce_sum | solution.py:148
  2.7 0.8 %reshape.12653 = f32[8,1,2048]{2,1,0:T(1,128)} reshape(f32[8,32,64]{2,1,0:T(8,128)S(1)} %bitcast.394) | data formatting | bytes 131072
  3.4 7.4 %all-to-all-start = ((f32[8,1,2048]{2,1,0:T(1,128)}), f32[8,1,2048]{2,1,0:T(1,128)S(1)}, u32[]{:S(2)}, u32[]{:S(2)}) async-start(f32[8,1,2048]{2,1,0:T(1,128)} %reshape.12653), calls=%async_computation | async-start | bytes 131072 | tf_op jit(solution)/shard_map/all_to_all | solution.py:171
  11.2 0.7 %copy-done.3 = f32[64,1,256]{2,1,0:T(1,128)S(1)} copy-done((f32[64,1,256]{2,1,0:T(1,128)S(1)}, f32[64,1,256]{2,1,0:T(1,128)}, u32[]{:S(2)}) %copy-start.3) | copy-done | bytes 65560
  12.0 0.1 fusion.99
  12.1 0.1 multiply_subtract_fusion.6
  12.3 0.1 fusion.98
  12.5 0.1 multiply_subtract_fusion.13
  12.7 0.1 fusion.79
  12.9 0.1 multiply_subtract_fusion.5
  13.0 0.1 fusion.97
  13.3 0.1 multiply_subtract_fusion.12
  13.5 0.1 fusion.81
  13.7 0.1 multiply_subtract_fusion.4
  13.8 0.1 fusion.96
  14.1 0.1 multiply_subtract_fusion.11
  14.3 0.1 fusion.83
  14.4 0.1 multiply_subtract_fusion.3
  14.8 0.1 multiply_subtract_fusion.10
  15.1 0.1 fusion.85
  15.2 0.1 multiply_subtract_fusion.2
  15.3 0.1 fusion.94
  15.6 0.1 multiply_subtract_fusion.9
  15.9 0.1 fusion.87
  16.0 0.1 multiply_subtract_fusion.1
  16.1 0.1 fusion.93
  16.4 0.1 multiply_subtract_fusion.8
  16.7 0.1 fusion.89
  16.8 0.1 multiply_subtract_fusion
  17.1 0.1 multiply_subtract_fusion.7
  17.6 0.7 collective-permute-start.1
  18.3 0.6 slice_reduce_fusion.1
  18.9 1.0 %collective-permute-start = (f32[64,1]{0,1:T(1,128)S(1)}, f32[64,1]{0,1:T(1,128)S(1)}, u32[]{:S(2)}, u32[]{:S(2)}) collective-permute-start(f32[64,1]{0,1:T(1,128)S(1)} %bitcast.403), channel_id=1, source_target_pairs={{0,24},{8,0},{16,8},{24,16},{1,25},{9,1},{17,9},{25,17},{2,26},{10... | collective-permute-start | bytes 776 | tf_op jit(solution)/shard_map/ppermute | solution.py:10
  19.9 0.2 fusion.41
  20.1 0.6 copy-done.4
  20.8 0.8 %reshape.12651 = f32[8,1,2048]{2,1,0:T(1,128)} reshape(f32[8,32,64]{2,1,0:T(8,128)S(1)} %bitcast.395) | data formatting | bytes 131072
  21.9 5.2 %all-gather = f32[16,64,1]{1,2,0:T(1,128)S(1)} all-gather(f32[4,64,1]{1,2,0:T(1,128)S(1)} %pad_maximum_fusion.2), channel_id=2, replica_groups=mesh['xg'=4,'yd'=8] {'xg'}, dimensions={0}, use_global_device_ids=true | all-gather | bytes 5120 | tf_op jit(solution)/shard_map/all_gather | solution.py:154
  27.2 0.7 %reshape.12655 = f32[8,1,2048]{2,1,0:T(1,128)} reshape(f32[8,32,64]{2,1,0:T(8,128)S(1)} %fusion.189) | data formatting | bytes 131072
  28.0 6.0 %all-to-all-start.2 = ((f32[8,1,2048]{2,1,0:T(1,128)}), f32[8,1,2048]{2,1,0:T(1,128)S(1)}, u32[]{:S(2)}, u32[]{:S(2)}) async-start(f32[8,1,2048]{2,1,0:T(1,128)} %reshape.12651), calls=%async_computation.2 | async-start | bytes 131072 | tf_op jit(solution)/shard_map/all_to_all | solution.py:168
  34.0 0.6 broadcast.430
  34.5 0.8 %reduce.14 = f32[8,2048]{1,0:T(8,128)S(1)} reduce(f32[8,1,2048]{2,1,0:T(1,128)S(1)} %all-to-all-done, f32[]{:T(128)} %broadcast.430), dimensions={1}, to_apply=%all_to_all.50.reduce_sub_computation | reduce | bytes 131076 | tf_op jit(solution)/shard_map/all_to_all | solution.py:171
  35.5 5.4 %all-to-all-done.2 = f32[8,1,2048]{2,1,0:T(1,128)S(1)} async-done(((f32[8,1,2048]{2,1,0:T(1,128)}), f32[8,1,2048]{2,1,0:T(1,128)S(1)}, u32[]{:S(2)}, u32[]{:S(2)}) %all-to-all-start.2) | async-done | bytes 65568 | tf_op jit(solution)/shard_map/all_to_all | solution.py:168
  40.9 3.3 %all-to-all-start.1 = ((f32[8,1,2048]{2,1,0:T(1,128)}), f32[8,1,2048]{2,1,0:T(1,128)S(1)}, u32[]{:S(2)}, u32[]{:S(2)}) async-start(f32[8,1,2048]{2,1,0:T(1,128)} %reshape.12655), calls=%async_computation.1 | async-start | bytes 131072 | tf_op jit(solution)/shard_map/all_to_all | solution.py:167
  44.2 0.8 %reduce.15 = f32[8,2048]{1,0:T(8,128)S(1)} reduce(f32[8,1,2048]{2,1,0:T(1,128)S(1)} %all-to-all-done.2, f32[]{:T(128)} %broadcast.430), dimensions={1}, to_apply=%all_to_all.58.reduce_sub_computation | reduce | bytes 131076 | tf_op jit(solution)/shard_map/all_to_all | solution.py:168
  45.4 0.5 copy-done
  46.1 4.9 %all-to-all-done.1 = f32[8,1,2048]{2,1,0:T(1,128)S(1)} async-done(((f32[8,1,2048]{2,1,0:T(1,128)}), f32[8,1,2048]{2,1,0:T(1,128)S(1)}, u32[]{:S(2)}, u32[]{:S(2)}) %all-to-all-start.1) | async-done | bytes 65568 | tf_op jit(solution)/shard_map/all_to_all | solution.py:167
  51.1 0.8 %reduce.16 = f32[8,2048]{1,0:T(8,128)S(1)} reduce(f32[8,1,2048]{2,1,0:T(1,128)S(1)} %all-to-all-done.1, f32[]{:T(128)} %broadcast.430), dimensions={1}, to_apply=%all_to_all.54.reduce_sub_computation | reduce | bytes 131076 | tf_op jit(solution)/shard_map/all_to_all | solution.py:167
  52.2 0.7 %copy-done.1 = f32[512,1,32]{0,2,1:T(8,128)S(1)} copy-done((f32[512,1,32]{0,2,1:T(8,128)S(1)}, f32[512,1,32]{0,2,1:T(8,128)}, u32[]{:S(2)}) %copy-start.1) | copy-done | bytes 65560
  53.5 0.1 fusion.2
  54.2 0.1 fusion.6
  55.1 0.1 fusion.10
  55.9 0.1 fusion.14
  56.8 0.1 fusion.18
  57.7 0.1 fusion.22
  58.6 0.1 fusion.26
  59.5 0.7 reduce.17
  60.2 0.1 copy.96
  60.3 0.2 reshape.12657
  60.5 9.3 %all_to_all.69 = f32[8,1,2048]{2,1,0:T(1,128)S(1)} all-to-all(f32[8,1,2048]{2,1,0:T(1,128)S(1)} %reshape.12657), channel_id=1, replica_groups=mesh['xg'=4,'yd'=8] {'yd'}, dimensions={0} | all-to-all | bytes 131072 | tf_op jit(solution)/shard_map/all_to_all | solution.py:173
  69.8 0.8 %reduce.18 = f32[8,2048]{1,0:T(8,128)S(1)} reduce(f32[8,1,2048]{2,1,0:T(1,128)S(1)} %all_to_all.69, f32[]{:T(128)} %broadcast.430), dimensions={1}, to_apply=%all_to_all.62.reduce_sub_computation | reduce | bytes 131076 | tf_op jit(solution)/shard_map/all_to_all | solution.py:173
  70.6 0.4 reshape.12658
  71.1 0.1 copy.86
  71.2 0.7 copy.85
  (169 shorter events, 9.5 us)
Async XLA Ops:
  0.0 0.9 %copy-start.5 = (f32[4]{0:T(128)S(1)}, f32[4]{0:T(128)}, u32[]{:S(2)}) copy-start(f32[4]{0:T(128)} %param.12) | copy-start | bytes 52
  0.0 0.9 %copy-start.6 = (f32[4]{0:T(128)S(1)}, f32[4]{0:T(128)}, u32[]{:S(2)}) copy-start(f32[4]{0:T(128)} %param.13) | copy-start | bytes 52
  3.4 7.5 %copy-start.2 = (f32[64,1,256]{2,1,0:T(1,128)S(1)}, f32[64,1,256]{2,1,0:T(1,128)}, u32[]{:S(2)}) copy-start(f32[64,1,256]{2,1,0:T(1,128)} %param.8) | copy-start | bytes 196612
  3.4 24.5 %all-to-all-start = ((f32[8,1,2048]{2,1,0:T(1,128)}), f32[8,1,2048]{2,1,0:T(1,128)S(1)}, u32[]{:S(2)}, u32[]{:S(2)}) async-start(f32[8,1,2048]{2,1,0:T(1,128)} %reshape.12653), calls=%async_computation | async-start | bytes 131072 | tf_op jit(solution)/shard_map/all_to_all | solution.py:171
  11.1 0.8 %copy-start.3 = (f32[64,1,256]{2,1,0:T(1,128)S(1)}, f32[64,1,256]{2,1,0:T(1,128)}, u32[]{:S(2)}) copy-start(f32[64,1,256]{2,1,0:T(1,128)} %param.7) | copy-start | bytes 196612
  17.6 4.3 %collective-permute-start.1 = (f32[3,64,1]{1,2,0:T(1,128)S(1)}, f32[3,64,1]{1,2,0:T(1,128)S(1)}, u32[]{:S(2)}, u32[]{:S(2)}) collective-permute-start(f32[3,64,1]{1,2,0:T(1,128)S(1)} %squeeze.95), channel_id=1, source_target_pairs={{0,24},{8,0},{16,8},{24,16},{1,25},{9,1},{17,9},{25,17},{2,26},{10... | collective-permute-start | bytes 2312 | tf_op jit(solution)/shard_map/ppermute | solution.py:10
  18.9 3.0 %collective-permute-start = (f32[64,1]{0,1:T(1,128)S(1)}, f32[64,1]{0,1:T(1,128)S(1)}, u32[]{:S(2)}, u32[]{:S(2)}) collective-permute-start(f32[64,1]{0,1:T(1,128)S(1)} %bitcast.403), channel_id=1, source_target_pairs={{0,24},{8,0},{16,8},{24,16},{1,25},{9,1},{17,9},{25,17},{2,26},{10... | collective-permute-start | bytes 776 | tf_op jit(solution)/shard_map/ppermute | solution.py:10
  19.9 0.8 %copy-start.4 = (f32[64,1,256]{2,1,0:T(1,128)S(1)}, f32[64,1,256]{2,1,0:T(1,128)}, u32[]{:S(2)}) copy-start(f32[64,1,256]{2,1,0:T(1,128)} %param.9) | copy-start | bytes 196612
  28.0 12.9 %all-to-all-start.2 = ((f32[8,1,2048]{2,1,0:T(1,128)}), f32[8,1,2048]{2,1,0:T(1,128)S(1)}, u32[]{:S(2)}, u32[]{:S(2)}) async-start(f32[8,1,2048]{2,1,0:T(1,128)} %reshape.12651), calls=%async_computation.2 | async-start | bytes 131072 | tf_op jit(solution)/shard_map/all_to_all | solution.py:168
  40.9 10.2 %all-to-all-start.1 = ((f32[8,1,2048]{2,1,0:T(1,128)}), f32[8,1,2048]{2,1,0:T(1,128)S(1)}, u32[]{:S(2)}, u32[]{:S(2)}) async-start(f32[8,1,2048]{2,1,0:T(1,128)} %reshape.12655), calls=%async_computation.1 | async-start | bytes 131072 | tf_op jit(solution)/shard_map/all_to_all | solution.py:167
  45.3 0.6 copy-start
  52.1 0.8 %copy-start.1 = (f32[512,1,32]{0,2,1:T(8,128)S(1)}, f32[512,1,32]{0,2,1:T(8,128)}, u32[]{:S(2)}) copy-start(f32[512,1,32]{0,2,1:T(8,128)} %copy-done) | copy-start | bytes 196612
  52.1 0.8 %slice-start = ((f32[512,1,32]{0,2,1:T(8,128)}), f32[1,1,32]{0,2,1:T(8,128)S(1)}, s32[]{:S(2)}) async-start(f32[512,1,32]{0,2,1:T(8,128)} %copy-done), calls=%async_computation.4 | async-start | bytes 32768 | tf_op jit(solution)/shard_map/jit(_roll_static)/slice | solution.py:32
where the time goes:
time: 72.6 us; the launch traced here: 72 us
  starting transfers between devices  18.4 us (25%)
  local copies, waits for them, and re-layouts  17 us (23%)
  blocking collectives  14.5 us (20%)
  other arithmetic  10.9 us (15%)
  waiting for transfers between devices  10.3 us (14%)
  between operations  0.86 us (1%)
    all_to_all x1, blocking collectives, local(): lax.all_to_all(solved_lines, 'yd', split_axis=0, concat_axis=1, tiled=True)  9.29 us
    all_to_all x1, starting transfers between devices, local(): lax.all_to_all(regroup(storage), 'yd', split_axis=1, concat_axis=0, tiled...  7.41 us
    unnamed x26, local copies, waits for them, and re-layouts  6.84 us
    all_to_all x1, starting transfers between devices, local(): lax.all_to_all(regroup(dispersion_y), 'yd', split_axis=1, concat_axis=0,...  5.99 us
    all_to_all x1, waiting for transfers between devices, local(): lax.all_to_all(regroup(dispersion_y), 'yd', split_axis=1, concat_axis=0,...  5.39 us
    all_gather x1, blocking collectives, local(): all_rows = lax.all_gather(jnp.stack(rows)[None], 'xg', axis=0, tiled=True)  5.17 us
    all_to_all x1, waiting for transfers between devices, local(): lax.all_to_all(regroup(after_x), 'yd', split_axis=1, concat_axis=0, tiled...  4.92 us
    all_to_all x1, starting transfers between devices, local(): lax.all_to_all(regroup(after_x), 'yd', split_axis=1, concat_axis=0, tiled...  3.35 us
  transfers between devices with their start and end apart: 5, of which 2 were waited for; matrix products, arithmetic and copies ran while one was open for 15% of the time, Pallas kernels for 0%

commit v1 on v0

v1 whole, which is shorter than its diff:
```python
import functools

import jax
import jax.numpy as jnp
from jax import lax
from jax.experimental import pallas as pl
from jax.experimental.pallas import tpu as pltpu
from jax.sharding import PartitionSpec as P

LANES = 128
SUBLANES = 8
QUANTITIES = 5
VMEM = pltpu.VMEM


def inverse(value):
    return 1.0 / value


def plus(first, second):
    if first is None:
        return second
    return first + second


def join_coefs(left, right):
    coupling_1, head_1, tail_1 = left
    coupling_2, head_2, tail_2 = right
    middle = plus(head_2, tail_1)
    inv = inverse(coupling_1 + coupling_2 + middle)
    weight_1 = coupling_1 * inv
    weight_2 = coupling_2 * inv
    joined = (coupling_1 * weight_2, plus(head_1, weight_1 * middle), tail_2 + weight_2 * middle)
    return joined, (weight_1, weight_2, inv)


def join_sides(left, right, node):
    head_1, tail_1 = left
    head_2, tail_2 = right
    weight_1, weight_2, inv = node
    side = plus(head_2, tail_1)
    joined = (plus(head_1, weight_1 * side), tail_2 + weight_2 * side)
    return joined, side * inv


def middle_value(node, given, before, after):
    return given + node[0] * before + node[1] * after


def ahead(value, step, axis):
    return pltpu.roll(value, value.shape[axis] - step, axis)


def behind(value, step, axis):
    return pltpu.roll(value, step, axis)


def doubling(count):
    steps = []
    step = 1
    while step < count:
        steps.append(step)
        step *= 2
    return steps


def tree_coefs(leaves, rolls):
    nodes = []
    level = leaves
    while len(level) > 1:
        following = []
        for index in range(0, len(level), 2):
            joined, node = join_coefs(level[index], level[index + 1])
            following.append(joined)
            nodes.append(node)
        level = following
    piece = level[0]
    for step, axis in rolls:
        piece, node = join_coefs(piece, tuple(ahead(part, step, axis) for part in piece))
        nodes.append(node)
    return piece, nodes


def tree_sides(leaves, rolls, nodes):
    givens = []
    level = leaves
    while len(level) > 1:
        following = []
        for index in range(0, len(level), 2):
            joined, given = join_sides(level[index], level[index + 1], nodes[len(givens)])
            following.append(joined)
            givens.append(given)
        level = following
    piece = level[0]
    for step, axis in rolls:
        other = tuple(ahead(part, step, axis) for part in piece)
        piece, given = join_sides(piece, other, nodes[len(givens)])
        givens.append(given)
    return piece, givens


def tree_values(before, after, rolls, count, nodes, givens):
    place = len(nodes)
    for step, axis in reversed(rolls):
        place -= 1
        middle = middle_value(nodes[place], givens[place], before, after)
        upper = (lax.broadcasted_iota(jnp.int32, middle.shape, axis) & step) != 0
        before = jnp.where(upper, behind(middle, step, axis), before)
        after = jnp.where(upper, behind(after, step, axis), middle)
    bounds = [before, after]
    while len(bounds) - 1 < count:
        width = len(bounds) - 1
        place -= width
        following = [bounds[0]]
        for index in range(width):
            following.append(
                middle_value(
                    nodes[place + index], givens[place + index], bounds[index], bounds[index + 1]
                )
            )
            following.append(bounds[index + 1])
        bounds = following
    return bounds[1:]


def ring_ends(slots, index):
    level = slots
    path = []
    bit = 0
    while len(level) > 1:
        upper = ((index >> bit) & 1) == 1
        following = []
        for place in range(0, len(level), 2):
            own, other = level[place], level[place + 1]
            left = [jnp.where(upper, b, a) for a, b in zip(own, other)]
            right = [jnp.where(upper, a, b) for a, b in zip(own, other)]
            coefs, node = join_coefs(left[:3], right[:3])
            sides, given = join_sides(left[3:], right[3:], node)
            if place == 0:
                path.append((node, given, upper))
            following.append(coefs + sides)
        level = following
        bit += 1
    _, head, tail, side_head, side_tail = level[0]
    before = after = (side_head + side_tail) * inverse(head + tail)
    for node, given, upper in reversed(path):
        middle = middle_value(node, given, before, after)
        before = jnp.where(upper, middle, before)
        after = jnp.where(upper, after, middle)
    return before, after


def capacity_weights(rates_ref, shares_ref, zones):
    weights = []
    for zone in range(zones):
        rate = jnp.full((1, LANES), rates_ref[zone], jnp.float32)
        share = jnp.full((1, LANES), shares_ref[zone], jnp.float32)
        weights.append(share * rate / (1.0 + rate))
    return weights


def strided(ref, start, size, stride):
    return ref[pl.ds(start, size, stride=stride), :]


def x_rolls(halves):
    return [(step, 0) for step in doubling(SUBLANES)] + [(step, 1) for step in doubling(halves)]


def y_rolls():
    return [(step, 0) for step in doubling(SUBLANES)]


def x_forward_kernel(
    halves, zones, mobile_ref, faces_ref, capacity_ref, immobile_ref, rates_ref, shares_ref,
    message_ref, state_ref, faces_t, storage_t, source_t,
):
    rows = mobile_ref.shape[0]
    stride = LANES // SUBLANES
    weights = capacity_weights(rates_ref, shares_ref, zones)
    capacity = capacity_ref[...]
    faces_t[...] = faces_ref[...].T
    storage_t[...] = (1.0 + capacity * sum(weights[1:], weights[0])).T
    total = weights[0] * immobile_ref[0:rows, :]
    for zone in range(1, zones):
        total = total + weights[zone] * immobile_ref[zone * rows : (zone + 1) * rows, :]
    source_t[...] = (mobile_ref[...] + capacity * total).T
    coefs, sides = [], []
    for index in range(stride):
        coefs.append((strided(faces_t, index, SUBLANES, stride), None, strided(storage_t, index, SUBLANES, stride)))
        sides.append((None, strided(source_t, index, SUBLANES, stride)))
    rolls = x_rolls(halves)
    piece, nodes = tree_coefs(coefs, rolls)
    side, givens = tree_sides(sides, rolls, nodes)
    for place, (node, given) in enumerate(zip(nodes, givens)):
        state_ref[3 * place] = node[0]
        state_ref[3 * place + 1] = node[1]
        state_ref[3 * place + 2] = given
    for row, value in enumerate(piece + side):
        message_ref[row : row + 1, :] = value[0:1, :]


def y_coefs_kernel(
    halves, zones, faces_ref, capacity_ref, rates_ref, shares_ref, rows_ref, state_ref, storage_ref
):
    rows = faces_ref.shape[0]
    stride = rows // SUBLANES
    weights = capacity_weights(rates_ref, shares_ref, zones)
    storage_ref[...] = 1.0 + capacity_ref[...] * sum(weights[1:], weights[0])
    place = 0
    for half in range(halves):
        coefs = []
        for index in range(half, stride, halves):
            coefs.append((strided(faces_ref, index, SUBLANES, stride), None, strided(storage_ref, index, SUBLANES, stride)))
        piece, nodes = tree_coefs(coefs, y_rolls())
        for node in nodes:
            for part in node:
                state_ref[place] = part
                place += 1
        for number, value in enumerate(piece):
            row = number * halves + half
            rows_ref[row : row + 1, :] = value[0:1, :]


def slot_rows(refs, number, height, quantity_rows):
    slots = []
    for ref in refs:
        for slot in range(ref.shape[0] // height):
            slots.append(
                tuple(
                    ref[slot * height + quantity * quantity_rows : slot * height + (quantity + 1) * quantity_rows, :]
                    for quantity in range(QUANTITIES)
                )
            )
    assert len(slots) == number
    return slots


def x_back_kernel(halves, axis, pieces, *refs):
    message_refs = refs[:pieces]
    x_state, y_state, rows_ref, storage_ref = refs[pieces : pieces + 4]
    message_ref, given_ref = refs[pieces + 4 : pieces + 6]
    values_t, sides_ref = refs[pieces + 6 :]
    rows = storage_ref.shape[0]
    count = lax.axis_size(axis)
    slots = slot_rows(message_refs, count, message_refs[0].shape[0], 1)
    before, after = ring_ends(slots, lax.axis_index(axis))
    before = jnp.broadcast_to(before, (SUBLANES, rows))
    after = jnp.broadcast_to(after, (SUBLANES, rows))
    rolls = x_rolls(halves)
    stride = LANES // SUBLANES
    total = stride - 1 + len(rolls)
    nodes = [(x_state[3 * place], x_state[3 * place + 1]) for place in range(total)]
    givens = [x_state[3 * place + 2] for place in range(total)]
    values = tree_values(before, after, rolls, stride, nodes, givens)
    for index, value in enumerate(values):
        values_t[pl.ds(index, SUBLANES, stride=stride), :] = value
    sides_ref[...] = storage_ref[...] * values_t[...].T
    stride = rows // SUBLANES
    place = 0
    height = 3 * halves
    message_ref[0:height, :] = rows_ref[0:height, :]
    total = stride // halves - 1 + len(y_rolls())
    for half in range(halves):
        sides = [(None, strided(sides_ref, index, SUBLANES, stride)) for index in range(half, stride, halves)]
        nodes = [tuple(y_state[3 * (half * total + node) + part] for part in range(3)) for node in range(total)]
        piece, givens = tree_sides(sides, y_rolls(), nodes)
        for given in givens:
            given_ref[place] = given
            place += 1
        for number, value in enumerate(piece):
            row = height + number * halves + half
            message_ref[row : row + 1, :] = value[0:1, :]


def y_back_kernel(halves, axis, pieces, *refs):
    message_refs = refs[:pieces]
    y_state, given_ref, out_ref = refs[pieces:]
    rows = out_ref.shape[0]
    stride = rows // SUBLANES
    count = lax.axis_size(axis)
    slots = slot_rows(message_refs, count, message_refs[0].shape[0], halves)
    before, after = ring_ends(slots, lax.axis_index(axis))
    total = stride // halves - 1 + len(y_rolls())
    for half in range(halves):
        first = jnp.broadcast_to(before[half : half + 1, :], (SUBLANES, LANES))
        last = jnp.broadcast_to(after[half : half + 1, :], (SUBLANES, LANES))
        nodes = [tuple(y_state[3 * (half * total + node) + part] for part in range(2)) for node in range(total)]
        givens = [given_ref[half * total + node] for node in range(total)]
        values = tree_values(first, last, y_rolls(), stride // halves, nodes, givens)
        for index, value in enumerate(values):
            out_ref[pl.ds(index * halves + half, SUBLANES, stride=stride), :] = value


def exchange(message, axis):
    count = lax.axis_size(axis)
    pieces = [message]
    held = message
    step = 1
    while step < count:
        received = lax.ppermute(held, axis, [(index, index ^ step) for index in range(count)])
        pieces.append(received)
        step *= 2
        if step < count:
            held = jnp.concatenate([held, received], axis=0)
    return pieces


def f32(*shape):
    return jax.ShapeDtypeStruct(shape, jnp.float32)


def held_f32(*shape):
    return VMEM(shape, jnp.float32)


def kernel_call(body, operands, scalars, outputs, scratch):
    spec = pl.BlockSpec(memory_space=VMEM)
    small = pl.BlockSpec(memory_space=pltpu.SMEM)
    return pl.pallas_call(
        body,
        out_shape=outputs,
        in_specs=[spec] * len(operands) + [small] * len(scalars),
        out_specs=[spec] * len(outputs),
        scratch_shapes=scratch,
        compiler_params=pltpu.CompilerParams(vmem_limit_bytes=16 * 1024 * 1024),
    )(*operands, *scalars)


def local(mobile, dispersion_x, dispersion_y, capacity, immobile, exchange_rates, rate_shares):
    shape = mobile.shape
    lines, width = shape[0] * shape[1], shape[2]
    zones = immobile.shape[0]
    halves = width // LANES
    rows = lines * halves
    assert rows == LANES

    def flat(values):
        return values.reshape(-1, LANES)

    mobile, dispersion_x, dispersion_y = flat(mobile), flat(dispersion_x), flat(dispersion_y)
    capacity, immobile = flat(capacity), flat(immobile)
    square = VMEM((rows, LANES), jnp.float32)
    x_nodes = LANES // SUBLANES - 1 + len(x_rolls(halves))
    y_nodes = halves * (rows // SUBLANES // halves - 1 + len(y_rolls()))
    y_height = -(-QUANTITIES * halves // SUBLANES) * SUBLANES
    message, x_state = kernel_call(
        functools.partial(x_forward_kernel, halves, zones),
        (mobile, dispersion_x, capacity, immobile),
        (exchange_rates, rate_shares),
        [f32(SUBLANES, rows), held_f32(3 * x_nodes, SUBLANES, rows)],
        [square] * 3,
    )
    y_rows, y_state, storage = kernel_call(
        functools.partial(y_coefs_kernel, halves, zones),
        (dispersion_y, capacity),
        (exchange_rates, rate_shares),
        [held_f32(SUBLANES, LANES), held_f32(3 * y_nodes, SUBLANES, LANES), held_f32(rows, LANES)],
        [],
    )
    pieces = exchange(message, "xg")
    message, givens = kernel_call(
        functools.partial(x_back_kernel, halves, "xg", len(pieces)),
        (*pieces, x_state, y_state, y_rows, storage),
        (),
        [f32(y_height, LANES), held_f32(y_nodes, SUBLANES, LANES)],
        [square] * 2,
    )
    pieces = exchange(message, "yd")
    (updated,) = kernel_call(
        functools.partial(y_back_kernel, halves, "yd", len(pieces)),
        (*pieces, y_state, givens),
        (),
        [f32(rows, LANES)],
        [],
    )
    return updated.reshape(shape)


def solution(mesh):
    field = P("yd", None, "xg")
    return jax.shard_map(
        local,
        mesh=mesh,
        in_specs=(field, field, field, field, P(None, "yd", None, "xg"), P(), P()),
        out_specs=field,
        check_vma=False,
    )
```

time: 72.6 us -> 24.6 us (0.34)
  blocking collectives: 14.5 us -> 0 us
  local copies, waits for them, and re-layouts: 17 us -> 4.14 us
  other arithmetic: 10.9 us -> 0.01 us
  starting transfers between devices: 18.4 us -> 10.6 us
  waiting for transfers between devices: 10.3 us -> 7.02 us
  Pallas kernels: 0 us -> 2.51 us
  between operations: 0.86 us -> 0.04 us
    all_to_all x3 -> x0, starting transfers between devices: 16.8 us -> none  [the longest x1 7.41 us: local(): lax.all_to_all(regroup(storage), 'yd', split_axis=1, concat_axis=0, tiled...]
    all_to_all x3 -> x0, waiting for transfers between devices: 10.3 us -> none  [the longest x1 5.39 us: local(): lax.all_to_all(regroup(dispersion_y), 'yd', split_axis=1, concat_axis=0,...]
    all_to_all x1 -> x0, blocking collectives: 9.29 us -> none  [local(): lax.all_to_all(solved_lines, 'yd', split_axis=0, concat_axis=1, tiled=True)]
    ppermute x2 -> x5, starting transfers between devices: 1.68 us -> 10.6 us  [exchange(): lax.ppermute(held, axis, [(index, index ^ step) for index in range(count)])]
    slice x108 -> x0, local copies, waits for them, and re-layouts: 8.02 us -> none  [the longest x23 1.88 us: shifted(): kept_part = lax.slice_in_dim(values, 0, length - stride, axis=axis)]
    ppermute x2 -> x5, waiting for transfers between devices: 0.01 us -> 7.02 us  [exchange(): lax.ppermute(held, axis, [(index, index ^ step) for index in range(count)])]
    all_gather x1 -> x0, blocking collectives: 5.17 us -> none  [local(): all_rows = lax.all_gather(jnp.stack(rows)[None], 'xg', axis=0, tiled=True)]
    sub x31 -> x0, other arithmetic: 3.54 us -> none  [the longest x8 1.08 us: periodic_solve(): right_side = right_side - left_ratio * side_left - right_ratio * side_right]
  transfers between devices with their start and end apart: 5 -> 5, of which waited for: 2 -> 5; matrix products, arithmetic and copies ran while one was open for 15% -> 0% of each run, Pallas kernels for 0% -> 3%
where the time goes in v1:
time: 24.6 us; the launch traced here: 24.3 us
  starting transfers between devices  10.6 us (43%)
  waiting for transfers between devices  7.02 us (29%)
  local copies, waits for them, and re-layouts  4.14 us (17%)
  Pallas kernels  2.51 us (10%)
    ppermute x5, starting transfers between devices, exchange(): lax.ppermute(held, axis, [(index, index ^ step) for index in range(count)])  10.6 us
    ppermute x5, waiting for transfers between devices, exchange(): lax.ppermute(held, axis, [(index, index ^ step) for index in range(count)])  7.02 us
    unnamed x16, local copies, waits for them, and re-layouts  4.14 us
    pallas_call x4, Pallas kernels, kernel_call(): pl.pallas_call(body, out_shape=outputs, in_specs=[spec] * len(operands) +...  2.51 us
  transfers between devices with their start and end apart: 5, of which 5 were waited for; matrix products, arithmetic and copies ran while one was open for 0% of the time, Pallas kernels for 3%

profile of v1, /device:TPU:0, one launch (start us, length us, event | category | flops | bytes accessed | tf_op | source)
XLA Modules:
  0.0 24.3 jit_solution(4584340557054737902)
XLA Ops:
  0.0 0.0 copy-start.6
  0.0 0.0 copy-start.7
  0.0 0.7 %copy-done.6 = f32[4]{0:T(128)S(1)} copy-done((f32[4]{0:T(128)S(1)}, f32[4]{0:T(128)}, u32[]{:S(2)}) %copy-start.6) | copy-done | bytes 40
  0.7 0.0 copy-done.7
  0.7 0.0 copy-start
  0.7 0.9 %copy-done = f32[4,64,1,256]{3,2,1,0:T(1,128)S(1)} copy-done((f32[4,64,1,256]{3,2,1,0:T(1,128)S(1)}, f32[4,64,1,256]{3,2,1,0:T(1,128)}, u32[]{:S(2)}) %copy-start) | copy-done | bytes 262168
  1.6 0.0 copy-start.1
  1.6 0.8 %copy-done.1 = f32[64,1,256]{2,1,0:T(1,128)S(1)} copy-done((f32[64,1,256]{2,1,0:T(1,128)S(1)}, f32[64,1,256]{2,1,0:T(1,128)}, u32[]{:S(2)}) %copy-start.1) | copy-done | bytes 65560
  2.5 0.0 copy-start.3
  2.5 0.8 %copy-done.3 = f32[64,1,256]{2,1,0:T(1,128)S(1)} copy-done((f32[64,1,256]{2,1,0:T(1,128)S(1)}, f32[64,1,256]{2,1,0:T(1,128)}, u32[]{:S(2)}) %copy-start.3) | copy-done | bytes 65560
  3.3 0.0 copy-start.4
  3.3 0.8 %copy-done.4 = f32[64,1,256]{2,1,0:T(1,128)S(1)} copy-done((f32[64,1,256]{2,1,0:T(1,128)S(1)}, f32[64,1,256]{2,1,0:T(1,128)}, u32[]{:S(2)}) %copy-start.4) | copy-done | bytes 65560
  4.1 0.0 copy-start.2
  4.1 0.0 copy-start.5
  4.1 0.8 %shard_map.73 = (f32[8,128]{1,0:T(8,128)S(1)}, f32[57,8,128]{2,1,0:T(8,128)S(1)}) custom-call(f32[128,128]{1,0:T(8,128)S(1)} %bitcast.9, f32[128,128]{1,0:T(8,128)S(1)} %bitcast.10, f32[128,128]{1,0:T(8,128)S(1)} %bitcast.7, f32[512,128]{1,0:T(8,128)S(1)} %bitcast.6, f32[4]{0:T(128)S(1)} %copy-done.6, f32[4]{0:T(128)S(1)} %copy-done.7), custom_call_target="tpu_custom_call" | custom-call | tf_op jit(solution)/shard_map/pallas_call | solution.py:320
  5.0 0.5 %collective-permute-start = (f32[8,128]{1,0:T(8,128)S(1)}, f32[8,128]{1,0:T(8,128)S(1)}, u32[]{:S(2)}, u32[]{:S(2)}) collective-permute-start(f32[8,128]{1,0:T(8,128)S(1)} %get-tuple-element.12.refs_0_), channel_id=1, source_target_pairs={{0,8},{8,0},{16,24},{24,16},{1,9},{9,1},{17,25},{25,17},{2,10},{10... | collective-permute-start | bytes 12296 | tf_op jit(solution)/shard_map/ppermute | solution.py:301
  5.5 0.8 %collective-permute-done.refs_1_ = f32[8,128]{1,0:T(8,128)S(1)} collective-permute-done((f32[8,128]{1,0:T(8,128)S(1)}, f32[8,128]{1,0:T(8,128)S(1)}, u32[]{:S(2)}, u32[]{:S(2)}) %collective-permute-start) | collective-permute-done | bytes 4128 | tf_op jit(solution)/shard_map/ppermute | solution.py:301
  6.3 2.8 %collective-permute-start.1 = (f32[16,128]{1,0:T(8,128)S(1)}, f32[16,128]{1,0:T(8,128)S(1)}, u32[]{:S(2)}, u32[]{:S(2)}) collective-permute-start(f32[16,128]{1,0:T(8,128)S(1)} %pad_maximum_fusion.2), channel_id=1, source_target_pairs={{0,16},{8,24},{16,0},{24,8},{1,17},{9,25},{17,1},{25,9},{2,18},{10... | collective-permute-start | bytes 24584 | tf_op jit(solution)/shard_map/ppermute | solution.py:301
  9.2 0.0 copy-done.2
  9.2 0.0 copy-done.5
  9.2 0.7 %shard_map.74 = (f32[8,128]{1,0:T(8,128)S(1)}, f32[60,8,128]{2,1,0:T(8,128)S(1)}, f32[128,128]{1,0:T(8,128)S(1)}) custom-call(f32[128,128]{1,0:T(8,128)S(1)} %bitcast.11, f32[128,128]{1,0:T(8,128)S(1)} %bitcast.8, f32[4]{0:T(128)S(1)} %copy-done.6, f32[4]{0:T(128)S(1)} %copy-done.7), custom_call_target="tpu_custom_call" | custom-call | tf_op jit(solution)/shard_map/pallas_call | solution.py:320
  9.8 1.0 %collective-permute-done.1.refs_2_ = f32[16,128]{1,0:T(8,128)S(1)} collective-permute-done((f32[16,128]{1,0:T(8,128)S(1)}, f32[16,128]{1,0:T(8,128)S(1)}, u32[]{:S(2)}, u32[]{:S(2)}) %collective-permute-start.1) | collective-permute-done | bytes 8224 | tf_op jit(solution)/shard_map/ppermute | solution.py:301
  10.8 0.3 %shard_map.75 = (f32[16,128]{1,0:T(8,128)S(1)}, f32[20,8,128]{2,1,0:T(8,128)S(1)}) custom-call(f32[8,128]{1,0:T(8,128)S(1)} %get-tuple-element.12.refs_0_, f32[8,128]{1,0:T(8,128)S(1)} %collective-permute-done.refs_1_, f32[16,128]{1,0:T(8,128)S(1)} %collective-permute-done.1.refs_2_, f32[57,8,128]{2,1,0:T(8,128)S(1)} %get-tuple-element.13.refs_3_, ...), custom_call_target="tpu_custom_call" | custom-call | tf_op jit(solution)/shard_map/pallas_call | solution.py:320
  11.1 2.1 %collective-permute-start.2 = (f32[16,128]{1,0:T(8,128)S(1)}, f32[16,128]{1,0:T(8,128)S(1)}, u32[]{:S(2)}, u32[]{:S(2)}) collective-permute-start(f32[16,128]{1,0:T(8,128)S(1)} %get-tuple-element.17.refs_0_), channel_id=1, source_target_pairs={{0,1},{1,0},{2,3},{3,2},{4,5},{5,4},{6,7},{7,6},{8,9},{9,8},{10,11... | collective-permute-start | bytes 24584 | tf_op jit(solution)/shard_map/ppermute | solution.py:301
  13.2 1.6 %collective-permute-done.2.refs_1_ = f32[16,128]{1,0:T(8,128)S(1)} collective-permute-done((f32[16,128]{1,0:T(8,128)S(1)}, f32[16,128]{1,0:T(8,128)S(1)}, u32[]{:S(2)}, u32[]{:S(2)}) %collective-permute-start.2) | collective-permute-done | bytes 8224 | tf_op jit(solution)/shard_map/ppermute | solution.py:301
  14.8 2.1 %collective-permute-start.3 = (f32[32,128]{1,0:T(8,128)S(1)}, f32[32,128]{1,0:T(8,128)S(1)}, u32[]{:S(2)}, u32[]{:S(2)}) collective-permute-start(f32[32,128]{1,0:T(8,128)S(1)} %pad_maximum_fusion.1), channel_id=1, source_target_pairs={{0,2},{1,3},{2,0},{3,1},{4,6},{5,7},{6,4},{7,5},{8,10},{9,11},{10,... | collective-permute-start | bytes 49160 | tf_op jit(solution)/shard_map/ppermute | solution.py:301
  16.9 1.7 %collective-permute-done.3.refs_2_ = f32[32,128]{1,0:T(8,128)S(1)} collective-permute-done((f32[32,128]{1,0:T(8,128)S(1)}, f32[32,128]{1,0:T(8,128)S(1)}, u32[]{:S(2)}, u32[]{:S(2)}) %collective-permute-start.3) | collective-permute-done | bytes 16416 | tf_op jit(solution)/shard_map/ppermute | solution.py:301
  18.6 3.0 %collective-permute-start.4 = (f32[64,128]{1,0:T(8,128)S(1)}, f32[64,128]{1,0:T(8,128)S(1)}, u32[]{:S(2)}, u32[]{:S(2)}) collective-permute-start(f32[64,128]{1,0:T(8,128)S(1)} %pad_maximum_fusion), channel_id=1, source_target_pairs={{0,4},{1,5},{2,6},{3,7},{4,0},{5,1},{6,2},{7,3},{8,12},{9,13},{10,... | collective-permute-start | bytes 98312 | tf_op jit(solution)/shard_map/ppermute | solution.py:301
  21.7 1.9 %collective-permute-done.4.refs_3_ = f32[64,128]{1,0:T(8,128)S(1)} collective-permute-done((f32[64,128]{1,0:T(8,128)S(1)}, f32[64,128]{1,0:T(8,128)S(1)}, u32[]{:S(2)}, u32[]{:S(2)}) %collective-permute-start.4) | collective-permute-done | bytes 32800 | tf_op jit(solution)/shard_map/ppermute | solution.py:301
  23.6 0.7 %shard_map.76 = f32[128,128]{1,0:T(8,128)} custom-call(f32[16,128]{1,0:T(8,128)S(1)} %get-tuple-element.17.refs_0_, f32[16,128]{1,0:T(8,128)S(1)} %collective-permute-done.2.refs_1_, f32[32,128]{1,0:T(8,128)S(1)} %collective-permute-done.3.refs_2_, f32[64,128]{1,0:T(8,128)S(1)} %collective-permute-done.4.refs_3_, ...), custom_call_target="tpu_custom_call" | custom-call | tf_op jit(solution)/shard_map/pallas_call | solution.py:320
  (3 shorter events, 0.0 us)
Async XLA Ops:
  0.0 0.7 %copy-start.6 = (f32[4]{0:T(128)S(1)}, f32[4]{0:T(128)}, u32[]{:S(2)}) copy-start(f32[4]{0:T(128)} %rates_ref.3) | copy-start | bytes 52
  0.0 0.7 %copy-start.7 = (f32[4]{0:T(128)S(1)}, f32[4]{0:T(128)}, u32[]{:S(2)}) copy-start(f32[4]{0:T(128)} %shares_ref.3) | copy-start | bytes 52
  0.7 0.9 %copy-start = (f32[4,64,1,256]{3,2,1,0:T(1,128)S(1)}, f32[4,64,1,256]{3,2,1,0:T(1,128)}, u32[]{:S(2)}) copy-start(f32[4,64,1,256]{3,2,1,0:T(1,128)} %param.11) | copy-start | bytes 786436
  1.6 0.8 %copy-start.1 = (f32[64,1,256]{2,1,0:T(1,128)S(1)}, f32[64,1,256]{2,1,0:T(1,128)}, u32[]{:S(2)}) copy-start(f32[64,1,256]{2,1,0:T(1,128)} %param.10) | copy-start | bytes 196612
  2.5 0.8 %copy-start.3 = (f32[64,1,256]{2,1,0:T(1,128)S(1)}, f32[64,1,256]{2,1,0:T(1,128)}, u32[]{:S(2)}) copy-start(f32[64,1,256]{2,1,0:T(1,128)} %param.7) | copy-start | bytes 196612
  3.3 0.8 %copy-start.4 = (f32[64,1,256]{2,1,0:T(1,128)S(1)}, f32[64,1,256]{2,1,0:T(1,128)}, u32[]{:S(2)}) copy-start(f32[64,1,256]{2,1,0:T(1,128)} %param.8) | copy-start | bytes 196612
  4.1 5.0 %copy-start.2 = (f32[64,1,256]{2,1,0:T(1,128)S(1)}, f32[64,1,256]{2,1,0:T(1,128)}, u32[]{:S(2)}) copy-start(f32[64,1,256]{2,1,0:T(1,128)} %param.10) | copy-start | bytes 196612
  4.1 5.0 %copy-start.5 = (f32[64,1,256]{2,1,0:T(1,128)S(1)}, f32[64,1,256]{2,1,0:T(1,128)}, u32[]{:S(2)}) copy-start(f32[64,1,256]{2,1,0:T(1,128)} %param.9) | copy-start | bytes 196612
  5.0 1.3 %collective-permute-start = (f32[8,128]{1,0:T(8,128)S(1)}, f32[8,128]{1,0:T(8,128)S(1)}, u32[]{:S(2)}, u32[]{:S(2)}) collective-permute-start(f32[8,128]{1,0:T(8,128)S(1)} %get-tuple-element.12.refs_0_), channel_id=1, source_target_pairs={{0,8},{8,0},{16,24},{24,16},{1,9},{9,1},{17,25},{25,17},{2,10},{10... | collective-permute-start | bytes 12296 | tf_op jit(solution)/shard_map/ppermute | solution.py:301
  6.3 4.5 %collective-permute-start.1 = (f32[16,128]{1,0:T(8,128)S(1)}, f32[16,128]{1,0:T(8,128)S(1)}, u32[]{:S(2)}, u32[]{:S(2)}) collective-permute-start(f32[16,128]{1,0:T(8,128)S(1)} %pad_maximum_fusion.2), channel_id=1, source_target_pairs={{0,16},{8,24},{16,0},{24,8},{1,17},{9,25},{17,1},{25,9},{2,18},{10... | collective-permute-start | bytes 24584 | tf_op jit(solution)/shard_map/ppermute | solution.py:301
  11.1 3.7 %collective-permute-start.2 = (f32[16,128]{1,0:T(8,128)S(1)}, f32[16,128]{1,0:T(8,128)S(1)}, u32[]{:S(2)}, u32[]{:S(2)}) collective-permute-start(f32[16,128]{1,0:T(8,128)S(1)} %get-tuple-element.17.refs_0_), channel_id=1, source_target_pairs={{0,1},{1,0},{2,3},{3,2},{4,5},{5,4},{6,7},{7,6},{8,9},{9,8},{10,11... | collective-permute-start | bytes 24584 | tf_op jit(solution)/shard_map/ppermute | solution.py:301
  14.8 3.8 %collective-permute-start.3 = (f32[32,128]{1,0:T(8,128)S(1)}, f32[32,128]{1,0:T(8,128)S(1)}, u32[]{:S(2)}, u32[]{:S(2)}) collective-permute-start(f32[32,128]{1,0:T(8,128)S(1)} %pad_maximum_fusion.1), channel_id=1, source_target_pairs={{0,2},{1,3},{2,0},{3,1},{4,6},{5,7},{6,4},{7,5},{8,10},{9,11},{10,... | collective-permute-start | bytes 49160 | tf_op jit(solution)/shard_map/ppermute | solution.py:301
  18.6 4.9 %collective-permute-start.4 = (f32[64,128]{1,0:T(8,128)S(1)}, f32[64,128]{1,0:T(8,128)S(1)}, u32[]{:S(2)}, u32[]{:S(2)}) collective-permute-start(f32[64,128]{1,0:T(8,128)S(1)} %pad_maximum_fusion), channel_id=1, source_target_pairs={{0,4},{1,5},{2,6},{3,7},{4,0},{5,1},{6,2},{7,3},{8,12},{9,13},{10,... | collective-permute-start | bytes 98312 | tf_op jit(solution)/shard_map/ppermute | solution.py:301

commit v2 on v1

--- a/solution.py
+++ b/solution.py
@@ -150,13 +150,9 @@
     return before, after
 
 
-def capacity_weights(rates_ref, shares_ref, zones):
-    weights = []
-    for zone in range(zones):
-        rate = jnp.full((1, LANES), rates_ref[zone], jnp.float32)
-        share = jnp.full((1, LANES), shares_ref[zone], jnp.float32)
-        weights.append(share * rate / (1.0 + rate))
-    return weights
+def capacity_weights(rates, shares):
+    weights = shares * rates / (1.0 + rates)
+    return [weights[:, zone : zone + 1] for zone in range(weights.shape[1])]
 
 
 def strided(ref, start, size, stride):
@@ -172,18 +168,34 @@
 
 
 def x_forward_kernel(
-    halves, zones, mobile_ref, faces_ref, capacity_ref, immobile_ref, rates_ref, shares_ref,
-    message_ref, state_ref, faces_t, storage_t, source_t,
+    halves, mobile_hbm, faces_hbm, capacity_hbm, immobile_hbm, rates_hbm, shares_hbm,
+    message_ref, state_ref, storage_ref,
+    mobile_ref, faces_ref, capacity_ref, immobile_ref, rates_ref, shares_ref, arrived,
+    faces_t, storage_t, source_t,
 ):
+    pairs = (
+        (rates_hbm, rates_ref), (shares_hbm, shares_ref), (capacity_hbm, capacity_ref),
+        (faces_hbm, faces_ref), (immobile_hbm, immobile_ref), (mobile_hbm, mobile_ref),
+    )
+    copies = [pltpu.make_async_copy(pair[0], pair[1], arrived.at[place]) for place, pair in enumerate(pairs)]
+    for copy in copies:
+        copy.start()
     rows = mobile_ref.shape[0]
     stride = LANES // SUBLANES
-    weights = capacity_weights(rates_ref, shares_ref, zones)
+    for copy in copies[:3]:
+        copy.wait()
+    weights = capacity_weights(rates_ref[...], shares_ref[...])
     capacity = capacity_ref[...]
+    storage = 1.0 + capacity * sum(weights[1:], weights[0])
+    storage_ref[...] = storage
+    storage_t[...] = storage.T
+    copies[3].wait()
     faces_t[...] = faces_ref[...].T
-    storage_t[...] = (1.0 + capacity * sum(weights[1:], weights[0])).T
+    copies[4].wait()
     total = weights[0] * immobile_ref[0:rows, :]
-    for zone in range(1, zones):
+    for zone in range(1, len(weights)):
         total = total + weights[zone] * immobile_ref[zone * rows : (zone + 1) * rows, :]
+    copies[5].wait()
     source_t[...] = (mobile_ref[...] + capacity * total).T
     coefs, sides = [], []
     for index in range(stride):
@@ -200,13 +212,9 @@
         message_ref[row : row + 1, :] = value[0:1, :]
 
 
-def y_coefs_kernel(
-    halves, zones, faces_ref, capacity_ref, rates_ref, shares_ref, rows_ref, state_ref, storage_ref
-):
+def y_coefs_kernel(halves, faces_ref, storage_ref, rows_ref, state_ref):
     rows = faces_ref.shape[0]
     stride = rows // SUBLANES
-    weights = capacity_weights(rates_ref, shares_ref, zones)
-    storage_ref[...] = 1.0 + capacity_ref[...] * sum(weights[1:], weights[0])
     place = 0
     for half in range(halves):
         coefs = []
@@ -233,6 +241,21 @@
                 )
             )
     assert len(slots) == number
+    return slots
+
+
+def gathered_rows(ref, number, own, quantity_rows):
+    height = ref.shape[0] // number
+    slots = []
+    for slot in range(number):
+        start = pl.multiple_of((own ^ slot) * height, height)
+        block = ref[pl.ds(start, height), :]
+        slots.append(
+            tuple(
+                block[quantity * quantity_rows : (quantity + 1) * quantity_rows, :]
+                for quantity in range(QUANTITIES)
+            )
+        )
     return slots
 
 
@@ -279,8 +302,9 @@
     rows = out_ref.shape[0]
     stride = rows // SUBLANES
     count = lax.axis_size(axis)
-    slots = slot_rows(message_refs, count, message_refs[0].shape[0], halves)
-    before, after = ring_ends(slots, lax.axis_index(axis))
+    own = lax.axis_index(axis)
+    slots = gathered_rows(message_refs[0], count, own, halves)
+    before, after = ring_ends(slots, own)
     total = stride // halves - 1 + len(y_rolls())
     for half in range(halves):
         first = jnp.broadcast_to(before[half : half + 1, :], (SUBLANES, LANES))
@@ -314,17 +338,15 @@
     return VMEM(shape, jnp.float32)
 
 
-def kernel_call(body, operands, scalars, outputs, scratch):
-    spec = pl.BlockSpec(memory_space=VMEM)
-    small = pl.BlockSpec(memory_space=pltpu.SMEM)
+def kernel_call(body, operands, outputs, scratch, space=VMEM):
     return pl.pallas_call(
         body,
         out_shape=outputs,
-        in_specs=[spec] * len(operands) + [small] * len(scalars),
-        out_specs=[spec] * len(outputs),
+        in_specs=[pl.BlockSpec(memory_space=space)] * len(operands),
+        out_specs=[pl.BlockSpec(memory_space=VMEM)] * len(outputs),
         scratch_shapes=scratch,
         compiler_params=pltpu.CompilerParams(vmem_limit_bytes=16 * 1024 * 1024),
-    )(*operands, *scalars)
+    )(*operands)
 
 
 def local(mobile, dispersion_x, dispersion_y, capacity, immobile, exchange_rates, rate_shares):
@@ -344,33 +366,37 @@
     x_nodes = LANES // SUBLANES - 1 + len(x_rolls(halves))
     y_nodes = halves * (rows // SUBLANES // halves - 1 + len(y_rolls()))
     y_height = -(-QUANTITIES * halves // SUBLANES) * SUBLANES
-    message, x_state = kernel_call(
-        functools.partial(x_forward_kernel, halves, zones),
-        (mobile, dispersion_x, capacity, immobile),
-        (exchange_rates, rate_shares),
-        [f32(SUBLANES, rows), held_f32(3 * x_nodes, SUBLANES, rows)],
-        [square] * 3,
-    )
-    y_rows, y_state, storage = kernel_call(
-        functools.partial(y_coefs_kernel, halves, zones),
-        (dispersion_y, capacity),
-        (exchange_rates, rate_shares),
-        [held_f32(SUBLANES, LANES), held_f32(3 * y_nodes, SUBLANES, LANES), held_f32(rows, LANES)],
+    message, x_state, storage = kernel_call(
+        functools.partial(x_forward_kernel, halves),
+        tuple(
+            pltpu.with_memory_space_constraint(value, pltpu.HBM)
+            for value in (mobile, dispersion_x, capacity, immobile, exchange_rates[None], rate_shares[None])
+        ),
+        [f32(SUBLANES, rows), held_f32(3 * x_nodes, SUBLANES, rows), held_f32(rows, LANES)],
+        [square] * 3
+        + [VMEM((zones * rows, LANES), jnp.float32)]
+        + [VMEM((1, zones), jnp.float32)] * 2
+        + [pltpu.SemaphoreType.DMA((6,))]
+        + [square] * 3,
+        pltpu.HBM,
+    )
+    y_rows, y_state = kernel_call(
+        functools.partial(y_coefs_kernel, halves),
+        (dispersion_y, storage),
+        [held_f32(SUBLANES, LANES), held_f32(3 * y_nodes, SUBLANES, LANES)],
         [],
     )
     pieces = exchange(message, "xg")
     message, givens = kernel_call(
         functools.partial(x_back_kernel, halves, "xg", len(pieces)),
         (*pieces, x_state, y_state, y_rows, storage),
-        (),
         [f32(y_height, LANES), held_f32(y_nodes, SUBLANES, LANES)],
         [square] * 2,
     )
-    pieces = exchange(message, "yd")
+    pieces = [lax.all_gather(message, "yd", axis=0, tiled=True)]
     (updated,) = kernel_call(
         functools.partial(y_back_kernel, halves, "yd", len(pieces)),
         (*pieces, y_state, givens),
-        (),
         [f32(rows, LANES)],
         [],
     )

time: 24.6 us -> 40 us (1.63)
  blocking collectives: 0 us -> 31.4 us
  starting transfers between devices: 10.6 us -> 3.35 us
  waiting for transfers between devices: 7.02 us -> 2.35 us
  local copies, waits for them, and re-layouts: 4.14 us -> 0.01 us
    all_gather x0 -> x1, blocking collectives: none -> 31.4 us  [local(): pieces = [lax.all_gather(message, 'yd', axis=0, tiled=True)]]
    ppermute x5 -> x2, starting transfers between devices: 10.6 us -> 3.35 us  [exchange(): lax.ppermute(held, axis, [(index, index ^ step) for index in range(count)])]
    ppermute x5 -> x2, waiting for transfers between devices: 7.02 us -> 2.35 us  [exchange(): lax.ppermute(held, axis, [(index, index ^ step) for index in range(count)])]
    unnamed x16 -> x2, local copies, waits for them, and re-layouts: 4.14 us -> 0.01 us
  transfers between devices with their start and end apart: 5 -> 2, of which waited for: 5 -> 2; matrix products, arithmetic and copies ran while one was open for 0% -> 0% of each run, Pallas kernels for 3% -> 0%
where the time goes in v2:
time: 40 us; the launch traced here: 39.8 us
  blocking collectives  31.4 us (78%)
  starting transfers between devices  3.35 us (8%)
  Pallas kernels  2.74 us (7%)
  waiting for transfers between devices  2.35 us (6%)
    all_gather x1, blocking collectives, local(): pieces = [lax.all_gather(message, 'yd', axis=0, tiled=True)]  31.4 us
    ppermute x2, starting transfers between devices, exchange(): lax.ppermute(held, axis, [(index, index ^ step) for index in range(count)])  3.35 us
    pallas_call x4, Pallas kernels, kernel_call(): pl.pallas_call(body, out_shape=outputs, in_specs=[pl.BlockSpec(memory_spa...  2.74 us
    ppermute x2, waiting for transfers between devices, exchange(): lax.ppermute(held, axis, [(index, index ^ step) for index in range(count)])  2.35 us
  transfers between devices with their start and end apart: 2, of which 2 were waited for; matrix products, arithmetic and copies ran while one was open for 0% of the time, Pallas kernels for 0%

profile of v2, /device:TPU:0, one launch (start us, length us, event | category | flops | bytes accessed | tf_op | source)
XLA Modules:
  0.0 39.8 jit_solution(7387177084692135989)
XLA Ops:
  0.0 0.0 copy-start
  0.0 1.6 %shard_map.73 = (f32[8,128]{1,0:T(8,128)S(1)}, f32[57,8,128]{2,1,0:T(8,128)S(1)}, f32[128,128]{1,0:T(8,128)S(1)}) custom-call(f32[128,128]{1,0:T(8,128)} %bitcast.10, f32[128,128]{1,0:T(8,128)} %bitcast.11, f32[128,128]{1,0:T(8,128)} %bitcast.12, f32[512,128]{1,0:T(8,128)} %bitcast.9, f32[1,4]{1,0:T(1,128)} %bitcast.13, f32[1,4]{1,0:T(1,128)} %bitcast.14), custom_call_target="tpu_custom_call" | custom-call | tf_op jit(solution)/shard_map/pallas_call | solution.py:342
  1.6 0.5 %collective-permute-start = (f32[8,128]{1,0:T(8,128)S(1)}, f32[8,128]{1,0:T(8,128)S(1)}, u32[]{:S(2)}, u32[]{:S(2)}) collective-permute-start(f32[8,128]{1,0:T(8,128)S(1)} %get-tuple-element.12.refs_0_), channel_id=1, source_target_pairs={{0,8},{8,0},{16,24},{24,16},{1,9},{9,1},{17,25},{25,17},{2,10},{10... | collective-permute-start | bytes 12296 | tf_op jit(solution)/shard_map/ppermute | solution.py:325
  2.1 0.8 %collective-permute-done.refs_1_ = f32[8,128]{1,0:T(8,128)S(1)} collective-permute-done((f32[8,128]{1,0:T(8,128)S(1)}, f32[8,128]{1,0:T(8,128)S(1)}, u32[]{:S(2)}, u32[]{:S(2)}) %collective-permute-start) | collective-permute-done | bytes 4128 | tf_op jit(solution)/shard_map/ppermute | solution.py:325
  3.0 2.8 %collective-permute-start.1 = (f32[16,128]{1,0:T(8,128)S(1)}, f32[16,128]{1,0:T(8,128)S(1)}, u32[]{:S(2)}, u32[]{:S(2)}) collective-permute-start(f32[16,128]{1,0:T(8,128)S(1)} %pad_maximum_fusion), channel_id=1, source_target_pairs={{0,16},{8,24},{16,0},{24,8},{1,17},{9,25},{17,1},{25,9},{2,18},{10... | collective-permute-start | bytes 24584 | tf_op jit(solution)/shard_map/ppermute | solution.py:325
  5.8 0.0 copy-done
  5.8 0.1 shard_map.74
  5.9 1.5 %collective-permute-done.1.refs_2_ = f32[16,128]{1,0:T(8,128)S(1)} collective-permute-done((f32[16,128]{1,0:T(8,128)S(1)}, f32[16,128]{1,0:T(8,128)S(1)}, u32[]{:S(2)}, u32[]{:S(2)}) %collective-permute-start.1) | collective-permute-done | bytes 8224 | tf_op jit(solution)/shard_map/ppermute | solution.py:325
  7.4 0.3 shard_map.75
  7.7 31.4 %all_gather.3.refs_0_ = f32[128,128]{1,0:T(8,128)S(1)} all-gather(f32[16,128]{1,0:T(8,128)S(1)} %get-tuple-element.17), channel_id=1, replica_groups=mesh['xg'=4,'yd'=8] {'yd'}, dimensions={0}, use_global_device_ids=true | all-gather | bytes 73728 | tf_op jit(solution)/shard_map/all_gather | solution.py:396
  39.1 0.7 %shard_map.76 = f32[128,128]{1,0:T(8,128)} custom-call(f32[128,128]{1,0:T(8,128)S(1)} %all_gather.3.refs_0_, f32[60,8,128]{2,1,0:T(8,128)S(1)} %get-tuple-element.15.refs_4_.refs_1_, f32[20,8,128]{2,1,0:T(8,128)S(1)} %get-tuple-element.18.refs_2_), custom_call_target="tpu_custom_call" | custom-call | tf_op jit(solution)/shard_map/pallas_call | solution.py:342
  (1 shorter events, 0.0 us)
Async XLA Ops:
  0.0 5.8 %copy-start = (f32[64,1,256]{2,1,0:T(1,128)S(1)}, f32[64,1,256]{2,1,0:T(1,128)}, u32[]{:S(2)}) copy-start(f32[64,1,256]{2,1,0:T(1,128)} %param.9) | copy-start | bytes 196612
  1.6 1.3 %collective-permute-start = (f32[8,128]{1,0:T(8,128)S(1)}, f32[8,128]{1,0:T(8,128)S(1)}, u32[]{:S(2)}, u32[]{:S(2)}) collective-permute-start(f32[8,128]{1,0:T(8,128)S(1)} %get-tuple-element.12.refs_0_), channel_id=1, source_target_pairs={{0,8},{8,0},{16,24},{24,16},{1,9},{9,1},{17,25},{25,17},{2,10},{10... | collective-permute-start | bytes 12296 | tf_op jit(solution)/shard_map/ppermute | solution.py:325
  3.0 4.5 %collective-permute-start.1 = (f32[16,128]{1,0:T(8,128)S(1)}, f32[16,128]{1,0:T(8,128)S(1)}, u32[]{:S(2)}, u32[]{:S(2)}) collective-permute-start(f32[16,128]{1,0:T(8,128)S(1)} %pad_maximum_fusion), channel_id=1, source_target_pairs={{0,16},{8,24},{16,0},{24,8},{1,17},{9,25},{17,1},{25,9},{2,18},{10... | collective-permute-start | bytes 24584 | tf_op jit(solution)/shard_map/ppermute | solution.py:325

commit v3 on v2

--- a/solution.py
+++ b/solution.py
@@ -241,21 +241,6 @@
                 )
             )
     assert len(slots) == number
-    return slots
-
-
-def gathered_rows(ref, number, own, quantity_rows):
-    height = ref.shape[0] // number
-    slots = []
-    for slot in range(number):
-        start = pl.multiple_of((own ^ slot) * height, height)
-        block = ref[pl.ds(start, height), :]
-        slots.append(
-            tuple(
-                block[quantity * quantity_rows : (quantity + 1) * quantity_rows, :]
-                for quantity in range(QUANTITIES)
-            )
-        )
     return slots
 
 
@@ -303,7 +288,7 @@
     stride = rows // SUBLANES
     count = lax.axis_size(axis)
     own = lax.axis_index(axis)
-    slots = gathered_rows(message_refs[0], count, own, halves)
+    slots = slot_rows(message_refs, count, message_refs[0].shape[0], halves)
     before, after = ring_ends(slots, own)
     total = stride // halves - 1 + len(y_rolls())
     for half in range(halves):
@@ -393,7 +378,7 @@
         [f32(y_height, LANES), held_f32(y_nodes, SUBLANES, LANES)],
         [square] * 2,
     )
-    pieces = [lax.all_gather(message, "yd", axis=0, tiled=True)]
+    pieces = exchange(message, "yd")
     (updated,) = kernel_call(
         functools.partial(y_back_kernel, halves, "yd", len(pieces)),
         (*pieces, y_state, givens),

time: 40 us -> 21.1 us (0.53)
  blocking collectives: 31.4 us -> 0 us
  starting transfers between devices: 3.35 us -> 10.6 us
  waiting for transfers between devices: 2.35 us -> 7.59 us
    all_gather x1 -> x0, blocking collectives: 31.4 us -> none  [local(): pieces = [lax.all_gather(message, 'yd', axis=0, tiled=True)]]
    ppermute x2 -> x5, starting transfers between devices: 3.35 us -> 10.6 us  [exchange(): lax.ppermute(held, axis, [(index, index ^ step) for index in range(count)])]
    ppermute x2 -> x5, waiting for transfers between devices: 2.35 us -> 7.59 us  [exchange(): lax.ppermute(held, axis, [(index, index ^ step) for index in range(count)])]
  transfers between devices with their start and end apart: 2 -> 5, of which waited for: 2 -> 5; matrix products, arithmetic and copies ran while one was open for 0% -> 0% of each run, Pallas kernels for 0% -> 0%
where the time goes in v3:
time: 21.1 us; the launch traced here: 20.9 us
  starting transfers between devices  10.6 us (50%)
  waiting for transfers between devices  7.59 us (36%)
  Pallas kernels  2.72 us (13%)
    ppermute x5, starting transfers between devices, exchange(): lax.ppermute(held, axis, [(index, index ^ step) for index in range(count)])  10.6 us
    ppermute x5, waiting for transfers between devices, exchange(): lax.ppermute(held, axis, [(index, index ^ step) for index in range(count)])  7.59 us
    pallas_call x4, Pallas kernels, kernel_call(): pl.pallas_call(body, out_shape=outputs, in_specs=[pl.BlockSpec(memory_spa...  2.72 us
  transfers between devices with their start and end apart: 5, of which 5 were waited for; matrix products, arithmetic and copies ran while one was open for 0% of the time, Pallas kernels for 0%

profile of v3, /device:TPU:0, one launch (start us, length us, event | category | flops | bytes accessed | tf_op | source)
XLA Modules:
  0.0 20.9 jit_solution(13296055253935866393)
XLA Ops:
  0.0 0.0 copy-start
  0.0 1.6 %shard_map.73 = (f32[8,128]{1,0:T(8,128)S(1)}, f32[57,8,128]{2,1,0:T(8,128)S(1)}, f32[128,128]{1,0:T(8,128)S(1)}) custom-call(f32[128,128]{1,0:T(8,128)} %bitcast.10, f32[128,128]{1,0:T(8,128)} %bitcast.11, f32[128,128]{1,0:T(8,128)} %bitcast.12, f32[512,128]{1,0:T(8,128)} %bitcast.9, f32[1,4]{1,0:T(1,128)} %bitcast.13, f32[1,4]{1,0:T(1,128)} %bitcast.14), custom_call_target="tpu_custom_call" | custom-call | tf_op jit(solution)/shard_map/pallas_call | solution.py:327
  1.6 0.5 %collective-permute-start = (f32[8,128]{1,0:T(8,128)S(1)}, f32[8,128]{1,0:T(8,128)S(1)}, u32[]{:S(2)}, u32[]{:S(2)}) collective-permute-start(f32[8,128]{1,0:T(8,128)S(1)} %get-tuple-element.12.refs_0_), channel_id=1, source_target_pairs={{0,8},{8,0},{16,24},{24,16},{1,9},{9,1},{17,25},{25,17},{2,10},{10... | collective-permute-start | bytes 12296 | tf_op jit(solution)/shard_map/ppermute | solution.py:310
  2.1 0.8 %collective-permute-done.refs_1_ = f32[8,128]{1,0:T(8,128)S(1)} collective-permute-done((f32[8,128]{1,0:T(8,128)S(1)}, f32[8,128]{1,0:T(8,128)S(1)}, u32[]{:S(2)}, u32[]{:S(2)}) %collective-permute-start) | collective-permute-done | bytes 4128 | tf_op jit(solution)/shard_map/ppermute | solution.py:310
  3.0 2.8 %collective-permute-start.1 = (f32[16,128]{1,0:T(8,128)S(1)}, f32[16,128]{1,0:T(8,128)S(1)}, u32[]{:S(2)}, u32[]{:S(2)}) collective-permute-start(f32[16,128]{1,0:T(8,128)S(1)} %pad_maximum_fusion.2), channel_id=1, source_target_pairs={{0,16},{8,24},{16,0},{24,8},{1,17},{9,25},{17,1},{25,9},{2,18},{10... | collective-permute-start | bytes 24584 | tf_op jit(solution)/shard_map/ppermute | solution.py:310
  5.8 0.0 copy-done
  5.8 0.1 shard_map.74
  5.9 1.5 %collective-permute-done.1.refs_2_ = f32[16,128]{1,0:T(8,128)S(1)} collective-permute-done((f32[16,128]{1,0:T(8,128)S(1)}, f32[16,128]{1,0:T(8,128)S(1)}, u32[]{:S(2)}, u32[]{:S(2)}) %collective-permute-start.1) | collective-permute-done | bytes 8224 | tf_op jit(solution)/shard_map/ppermute | solution.py:310
  7.4 0.3 %shard_map.75 = (f32[16,128]{1,0:T(8,128)S(1)}, f32[20,8,128]{2,1,0:T(8,128)S(1)}) custom-call(f32[8,128]{1,0:T(8,128)S(1)} %get-tuple-element.12.refs_0_, f32[8,128]{1,0:T(8,128)S(1)} %collective-permute-done.refs_1_, f32[16,128]{1,0:T(8,128)S(1)} %collective-permute-done.1.refs_2_, f32[57,8,128]{2,1,0:T(8,128)S(1)} %get-tuple-element.13.refs_3_, ...), custom_call_target="tpu_custom_call" | custom-call | tf_op jit(solution)/shard_map/pallas_call | solution.py:327
  7.7 2.1 %collective-permute-start.2 = (f32[16,128]{1,0:T(8,128)S(1)}, f32[16,128]{1,0:T(8,128)S(1)}, u32[]{:S(2)}, u32[]{:S(2)}) collective-permute-start(f32[16,128]{1,0:T(8,128)S(1)} %get-tuple-element.17.refs_0_), channel_id=1, source_target_pairs={{0,1},{1,0},{2,3},{3,2},{4,5},{5,4},{6,7},{7,6},{8,9},{9,8},{10,11... | collective-permute-start | bytes 24584 | tf_op jit(solution)/shard_map/ppermute | solution.py:310
  9.8 1.6 %collective-permute-done.2.refs_1_ = f32[16,128]{1,0:T(8,128)S(1)} collective-permute-done((f32[16,128]{1,0:T(8,128)S(1)}, f32[16,128]{1,0:T(8,128)S(1)}, u32[]{:S(2)}, u32[]{:S(2)}) %collective-permute-start.2) | collective-permute-done | bytes 8224 | tf_op jit(solution)/shard_map/ppermute | solution.py:310
  11.5 2.1 %collective-permute-start.3 = (f32[32,128]{1,0:T(8,128)S(1)}, f32[32,128]{1,0:T(8,128)S(1)}, u32[]{:S(2)}, u32[]{:S(2)}) collective-permute-start(f32[32,128]{1,0:T(8,128)S(1)} %pad_maximum_fusion.1), channel_id=1, source_target_pairs={{0,2},{1,3},{2,0},{3,1},{4,6},{5,7},{6,4},{7,5},{8,10},{9,11},{10,... | collective-permute-start | bytes 49160 | tf_op jit(solution)/shard_map/ppermute | solution.py:310
  13.5 1.7 %collective-permute-done.3.refs_2_ = f32[32,128]{1,0:T(8,128)S(1)} collective-permute-done((f32[32,128]{1,0:T(8,128)S(1)}, f32[32,128]{1,0:T(8,128)S(1)}, u32[]{:S(2)}, u32[]{:S(2)}) %collective-permute-start.3) | collective-permute-done | bytes 16416 | tf_op jit(solution)/shard_map/ppermute | solution.py:310
  15.3 3.0 %collective-permute-start.4 = (f32[64,128]{1,0:T(8,128)S(1)}, f32[64,128]{1,0:T(8,128)S(1)}, u32[]{:S(2)}, u32[]{:S(2)}) collective-permute-start(f32[64,128]{1,0:T(8,128)S(1)} %pad_maximum_fusion), channel_id=1, source_target_pairs={{0,4},{1,5},{2,6},{3,7},{4,0},{5,1},{6,2},{7,3},{8,12},{9,13},{10,... | collective-permute-start | bytes 98312 | tf_op jit(solution)/shard_map/ppermute | solution.py:310
  18.3 1.9 %collective-permute-done.4.refs_3_ = f32[64,128]{1,0:T(8,128)S(1)} collective-permute-done((f32[64,128]{1,0:T(8,128)S(1)}, f32[64,128]{1,0:T(8,128)S(1)}, u32[]{:S(2)}, u32[]{:S(2)}) %collective-permute-start.4) | collective-permute-done | bytes 32800 | tf_op jit(solution)/shard_map/ppermute | solution.py:310
  20.2 0.7 %shard_map.76 = f32[128,128]{1,0:T(8,128)} custom-call(f32[16,128]{1,0:T(8,128)S(1)} %get-tuple-element.17.refs_0_, f32[16,128]{1,0:T(8,128)S(1)} %collective-permute-done.2.refs_1_, f32[32,128]{1,0:T(8,128)S(1)} %collective-permute-done.3.refs_2_, f32[64,128]{1,0:T(8,128)S(1)} %collective-permute-done.4.refs_3_, ...), custom_call_target="tpu_custom_call" | custom-call | tf_op jit(solution)/shard_map/pallas_call | solution.py:327
  (3 shorter events, 0.0 us)
Async XLA Ops:
  0.0 5.8 %copy-start = (f32[64,1,256]{2,1,0:T(1,128)S(1)}, f32[64,1,256]{2,1,0:T(1,128)}, u32[]{:S(2)}) copy-start(f32[64,1,256]{2,1,0:T(1,128)} %param.9) | copy-start | bytes 196612
  1.6 1.3 %collective-permute-start = (f32[8,128]{1,0:T(8,128)S(1)}, f32[8,128]{1,0:T(8,128)S(1)}, u32[]{:S(2)}, u32[]{:S(2)}) collective-permute-start(f32[8,128]{1,0:T(8,128)S(1)} %get-tuple-element.12.refs_0_), channel_id=1, source_target_pairs={{0,8},{8,0},{16,24},{24,16},{1,9},{9,1},{17,25},{25,17},{2,10},{10... | collective-permute-start | bytes 12296 | tf_op jit(solution)/shard_map/ppermute | solution.py:310
  3.0 4.5 %collective-permute-start.1 = (f32[16,128]{1,0:T(8,128)S(1)}, f32[16,128]{1,0:T(8,128)S(1)}, u32[]{:S(2)}, u32[]{:S(2)}) collective-permute-start(f32[16,128]{1,0:T(8,128)S(1)} %pad_maximum_fusion.2), channel_id=1, source_target_pairs={{0,16},{8,24},{16,0},{24,8},{1,17},{9,25},{17,1},{25,9},{2,18},{10... | collective-permute-start | bytes 24584 | tf_op jit(solution)/shard_map/ppermute | solution.py:310
  7.7 3.7 %collective-permute-start.2 = (f32[16,128]{1,0:T(8,128)S(1)}, f32[16,128]{1,0:T(8,128)S(1)}, u32[]{:S(2)}, u32[]{:S(2)}) collective-permute-start(f32[16,128]{1,0:T(8,128)S(1)} %get-tuple-element.17.refs_0_), channel_id=1, source_target_pairs={{0,1},{1,0},{2,3},{3,2},{4,5},{5,4},{6,7},{7,6},{8,9},{9,8},{10,11... | collective-permute-start | bytes 24584 | tf_op jit(solution)/shard_map/ppermute | solution.py:310
  11.5 3.8 %collective-permute-start.3 = (f32[32,128]{1,0:T(8,128)S(1)}, f32[32,128]{1,0:T(8,128)S(1)}, u32[]{:S(2)}, u32[]{:S(2)}) collective-permute-start(f32[32,128]{1,0:T(8,128)S(1)} %pad_maximum_fusion.1), channel_id=1, source_target_pairs={{0,2},{1,3},{2,0},{3,1},{4,6},{5,7},{6,4},{7,5},{8,10},{9,11},{10,... | collective-permute-start | bytes 49160 | tf_op jit(solution)/shard_map/ppermute | solution.py:310
  15.3 4.9 %collective-permute-start.4 = (f32[64,128]{1,0:T(8,128)S(1)}, f32[64,128]{1,0:T(8,128)S(1)}, u32[]{:S(2)}, u32[]{:S(2)}) collective-permute-start(f32[64,128]{1,0:T(8,128)S(1)} %pad_maximum_fusion), channel_id=1, source_target_pairs={{0,4},{1,5},{2,6},{3,7},{4,0},{5,1},{6,2},{7,3},{8,12},{9,13},{10,... | collective-permute-start | bytes 98312 | tf_op jit(solution)/shard_map/ppermute | solution.py:310

commit v4 on v3

--- a/solution.py
+++ b/solution.py
@@ -123,31 +123,35 @@
     return bounds[1:]
 
 
-def ring_ends(slots, index):
+def ring_bounds(slots, index):
     level = slots
-    path = []
+    rounds = []
     bit = 0
     while len(level) > 1:
         upper = ((index >> bit) & 1) == 1
-        following = []
+        following, nodes = [], []
         for place in range(0, len(level), 2):
             own, other = level[place], level[place + 1]
             left = [jnp.where(upper, b, a) for a, b in zip(own, other)]
             right = [jnp.where(upper, a, b) for a, b in zip(own, other)]
             coefs, node = join_coefs(left[:3], right[:3])
             sides, given = join_sides(left[3:], right[3:], node)
-            if place == 0:
-                path.append((node, given, upper))
+            nodes.append((node, given))
             following.append(coefs + sides)
+        rounds.append((nodes, upper))
         level = following
         bit += 1
     _, head, tail, side_head, side_tail = level[0]
-    before = after = (side_head + side_tail) * inverse(head + tail)
-    for node, given, upper in reversed(path):
-        middle = middle_value(node, given, before, after)
-        before = jnp.where(upper, middle, before)
-        after = jnp.where(upper, after, middle)
-    return before, after
+    last = (side_head + side_tail) * inverse(head + tail)
+    bounds = [(last, last)]
+    for nodes, upper in reversed(rounds):
+        following = []
+        for (node, given), (before, after) in zip(nodes, bounds):
+            middle = middle_value(node, given, before, after)
+            following.append((jnp.where(upper, middle, before), jnp.where(upper, after, middle)))
+            following.append((jnp.where(upper, before, middle), jnp.where(upper, middle, after)))
+        bounds = following
+    return bounds
 
 
 def capacity_weights(rates, shares):
@@ -168,14 +172,15 @@
 
 
 def x_forward_kernel(
-    halves, mobile_hbm, faces_hbm, capacity_hbm, immobile_hbm, rates_hbm, shares_hbm,
-    message_ref, state_ref, storage_ref,
+    halves, mobile_hbm, faces_hbm, across_hbm, capacity_hbm, immobile_hbm, rates_hbm, shares_hbm,
+    message_ref, block_ref,
     mobile_ref, faces_ref, capacity_ref, immobile_ref, rates_ref, shares_ref, arrived,
     faces_t, storage_t, source_t,
 ):
     pairs = (
         (rates_hbm, rates_ref), (shares_hbm, shares_ref), (capacity_hbm, capacity_ref),
         (faces_hbm, faces_ref), (immobile_hbm, immobile_ref), (mobile_hbm, mobile_ref),
+        (across_hbm, block_ref.at[mobile_ref.shape[0] : 2 * mobile_ref.shape[0], :]),
     )
     copies = [pltpu.make_async_copy(pair[0], pair[1], arrived.at[place]) for place, pair in enumerate(pairs)]
     for copy in copies:
@@ -187,7 +192,7 @@
     weights = capacity_weights(rates_ref[...], shares_ref[...])
     capacity = capacity_ref[...]
     storage = 1.0 + capacity * sum(weights[1:], weights[0])
-    storage_ref[...] = storage
+    block_ref[0:rows, :] = storage
     storage_t[...] = storage.T
     copies[3].wait()
     faces_t[...] = faces_ref[...].T
@@ -204,115 +209,196 @@
     rolls = x_rolls(halves)
     piece, nodes = tree_coefs(coefs, rolls)
     side, givens = tree_sides(sides, rolls, nodes)
-    for place, (node, given) in enumerate(zip(nodes, givens)):
-        state_ref[3 * place] = node[0]
-        state_ref[3 * place + 1] = node[1]
-        state_ref[3 * place + 2] = given
+    start = 2 * rows
+    for node, given in zip(nodes, givens):
+        for part in (node[0], node[1], given):
+            block_ref[start : start + SUBLANES, :] = part
+            start += SUBLANES
     for row, value in enumerate(piece + side):
         message_ref[row : row + 1, :] = value[0:1, :]
-
-
-def y_coefs_kernel(halves, faces_ref, storage_ref, rows_ref, state_ref):
-    rows = faces_ref.shape[0]
+    copies[6].wait()
+
+
+def y_coefs_kernel(halves, block_ref, rows_ref, state_ref):
+    rows = rows_ref.shape[1]
     stride = rows // SUBLANES
-    place = 0
+    start = 0
     for half in range(halves):
         coefs = []
         for index in range(half, stride, halves):
-            coefs.append((strided(faces_ref, index, SUBLANES, stride), None, strided(storage_ref, index, SUBLANES, stride)))
+            storage = strided(block_ref, index, SUBLANES, stride)
+            coefs.append((strided(block_ref, rows + index, SUBLANES, stride), None, storage))
         piece, nodes = tree_coefs(coefs, y_rolls())
         for node in nodes:
             for part in node:
-                state_ref[place] = part
-                place += 1
+                state_ref[start : start + SUBLANES, :] = part
+                start += SUBLANES
         for number, value in enumerate(piece):
             row = number * halves + half
             rows_ref[row : row + 1, :] = value[0:1, :]
 
 
-def slot_rows(refs, number, height, quantity_rows):
+def state_parts(ref, first, total, parts):
+    return [
+        tuple(
+            ref[(3 * place + part) * SUBLANES : (3 * place + part + 1) * SUBLANES, :]
+            for part in range(parts)
+        )
+        for place in range(first, first + total)
+    ]
+
+
+def message_slots(refs, height, quantity_rows):
     slots = []
     for ref in refs:
-        for slot in range(ref.shape[0] // height):
+        for start in range(0, ref.shape[0], height):
             slots.append(
                 tuple(
-                    ref[slot * height + quantity * quantity_rows : slot * height + (quantity + 1) * quantity_rows, :]
+                    ref[start + quantity * quantity_rows : start + (quantity + 1) * quantity_rows, :]
                     for quantity in range(QUANTITIES)
                 )
             )
-    assert len(slots) == number
     return slots
 
 
-def x_back_kernel(halves, axis, pieces, *refs):
-    message_refs = refs[:pieces]
-    x_state, y_state, rows_ref, storage_ref = refs[pieces : pieces + 4]
-    message_ref, given_ref = refs[pieces + 4 : pieces + 6]
-    values_t, sides_ref = refs[pieces + 6 :]
-    rows = storage_ref.shape[0]
-    count = lax.axis_size(axis)
-    slots = slot_rows(message_refs, count, message_refs[0].shape[0], 1)
-    before, after = ring_ends(slots, lax.axis_index(axis))
-    before = jnp.broadcast_to(before, (SUBLANES, rows))
-    after = jnp.broadcast_to(after, (SUBLANES, rows))
+def x_back(halves, bounds, block_ref, values_t, sides_ref):
+    rows = values_t.shape[1]
+    before, after = (jnp.broadcast_to(bound, (SUBLANES, rows)) for bound in bounds)
     rolls = x_rolls(halves)
     stride = LANES // SUBLANES
     total = stride - 1 + len(rolls)
-    nodes = [(x_state[3 * place], x_state[3 * place + 1]) for place in range(total)]
-    givens = [x_state[3 * place + 2] for place in range(total)]
-    values = tree_values(before, after, rolls, stride, nodes, givens)
+    parts = state_parts(block_ref.at[2 * rows :, :], 0, total, 3)
+    values = tree_values(before, after, rolls, stride, parts, [part[2] for part in parts])
     for index, value in enumerate(values):
         values_t[pl.ds(index, SUBLANES, stride=stride), :] = value
-    sides_ref[...] = storage_ref[...] * values_t[...].T
+    sides_ref[...] = block_ref[0:rows, :] * values_t[...].T
+
+
+def x_back_kernel(halves, axis, pieces, *refs):
+    slots = message_slots(refs[:pieces], SUBLANES, 1)
+    block_refs, rows_refs, state_refs = (refs[pieces + 2 * pair : pieces + 2 * pair + 2] for pair in range(3))
+    message_ref, *given_refs = refs[pieces + 6 : pieces + 9]
+    scratch = refs[pieces + 9 :]
+    bounds = ring_bounds(slots, lax.axis_index(axis))
+    rows = scratch[0].shape[1]
     stride = rows // SUBLANES
-    place = 0
-    height = 3 * halves
-    message_ref[0:height, :] = rows_ref[0:height, :]
     total = stride // halves - 1 + len(y_rolls())
-    for half in range(halves):
-        sides = [(None, strided(sides_ref, index, SUBLANES, stride)) for index in range(half, stride, halves)]
-        nodes = [tuple(y_state[3 * (half * total + node) + part] for part in range(3)) for node in range(total)]
-        piece, givens = tree_sides(sides, y_rolls(), nodes)
-        for given in givens:
-            given_ref[place] = given
-            place += 1
-        for number, value in enumerate(piece):
-            row = height + number * halves + half
-            message_ref[row : row + 1, :] = value[0:1, :]
-
-
-def y_back_kernel(halves, axis, pieces, *refs):
-    message_refs = refs[:pieces]
-    y_state, given_ref, out_ref = refs[pieces:]
+    both = 2 * halves
+    for block in range(2):
+        values_t, sides_ref = scratch[2 * block : 2 * block + 2]
+        x_back(halves, bounds[1 - block], block_refs[block], values_t, sides_ref)
+        start = 0
+        for half in range(halves):
+            place = block * halves + half
+            sides = [(None, strided(sides_ref, index, SUBLANES, stride)) for index in range(half, stride, halves)]
+            nodes = state_parts(state_refs[block], half * total, total, 3)
+            piece, givens = tree_sides(sides, y_rolls(), nodes)
+            for given in givens:
+                given_refs[block][start : start + SUBLANES, :] = given
+                start += SUBLANES
+            for number in range(3):
+                row = number * halves + half
+                message_ref[number * both + place : number * both + place + 1, :] = rows_refs[block][row : row + 1, :]
+            for number, value in enumerate(piece):
+                row = (3 + number) * both + place
+                message_ref[row : row + 1, :] = value[0:1, :]
+
+
+def y_ring_kernel(halves, axis, height, pieces, *refs):
+    slots = message_slots(refs[:pieces], height, 2 * halves)
+    bounds = ring_bounds(slots, lax.axis_index(axis))
+    for ref, (before, after) in zip(refs[pieces:], bounds):
+        ref[0 : 2 * halves, :] = before
+        ref[2 * halves : 4 * halves, :] = after
+
+
+def y_back_kernel(halves, axes, hubs, sent, *refs):
+    own_ref, *sent_refs = refs[: 1 + sent]
+    state_ref, own_given, sent_given, out_ref = refs[1 + sent :]
     rows = out_ref.shape[0]
     stride = rows // SUBLANES
-    count = lax.axis_size(axis)
-    own = lax.axis_index(axis)
-    slots = slot_rows(message_refs, count, message_refs[0].shape[0], halves)
-    before, after = ring_ends(slots, own)
+    other = lax.axis_index(axes[0]) % 2 == 0
+    place = lax.axis_index(axes[1])
+    solved = place == hubs[0]
+    for hub in hubs[1:]:
+        solved = solved | (place == hub)
+    ends = jnp.where(solved & jnp.logical_not(other), own_ref[...], 0.0)
+    for ref in sent_refs:
+        ends = ends + ref[...]
     total = stride // halves - 1 + len(y_rolls())
+    both = 2 * halves
     for half in range(halves):
-        first = jnp.broadcast_to(before[half : half + 1, :], (SUBLANES, LANES))
-        last = jnp.broadcast_to(after[half : half + 1, :], (SUBLANES, LANES))
-        nodes = [tuple(y_state[3 * (half * total + node) + part] for part in range(2)) for node in range(total)]
-        givens = [given_ref[half * total + node] for node in range(total)]
-        values = tree_values(first, last, y_rolls(), stride // halves, nodes, givens)
+        bounds = []
+        for end in range(2):
+            row = end * both + half
+            bound = jnp.where(other, ends[row : row + 1, :], ends[row + halves : row + halves + 1, :])
+            bounds.append(jnp.broadcast_to(bound, (SUBLANES, LANES)))
+        nodes = state_parts(state_ref, half * total, total, 2)
+        givens = []
+        for node in range(half * total, (half + 1) * total):
+            part = slice(node * SUBLANES, (node + 1) * SUBLANES)
+            givens.append(jnp.where(other, sent_given[part, :], own_given[part, :]))
+        values = tree_values(*bounds, y_rolls(), stride // halves, nodes, givens)
         for index, value in enumerate(values):
             out_ref[pl.ds(index * halves + half, SUBLANES, stride=stride), :] = value
 
 
-def exchange(message, axis):
-    count = lax.axis_size(axis)
+def send(value, pairs):
+    width = lax.axis_size("yd")
+    flat = [(source[0] * width + source[1], target[0] * width + target[1]) for source, target in pairs]
+    return lax.ppermute(value, ("xg", "yd"), flat)
+
+
+def x_exchange(message, block):
+    count, lines = lax.axis_size("xg"), range(lax.axis_size("yd"))
+    odd = range(1, count, 2)
+    pieces = [message]
+    for chip in range(0, count, 2):
+        if chip:
+            pieces.append(send(message, [((index ^ chip, line), (index, line)) for index in odd for line in lines]))
+        pieces.append(send(message, [((index ^ chip ^ 1, line), (index, line)) for index in odd for line in lines]))
+    to_odd = [((index - 1, line), (index, line)) for index in odd for line in lines]
+    return pieces, send(block, to_odd)
+
+
+def to_even(value):
+    odd = range(1, lax.axis_size("xg"), 2)
+    return send(value, [((index, line), (index - 1, line)) for index in odd for line in range(lax.axis_size("yd"))])
+
+
+def y_hubs(count):
+    return [count // 4, count // 2] if 4 <= count <= 8 else list(range(count))
+
+
+def y_gather(message):
+    count = lax.axis_size("yd")
+    hubs = y_hubs(count)
+    odd = range(1, lax.axis_size("xg"), 2)
+    if len(hubs) < count:
+        return [message] + [
+            send(message, [((index, hub ^ slot), (index, hub)) for index in odd for hub in hubs])
+            for slot in range(1, count)
+        ]
     pieces = [message]
     held = message
-    step = 1
-    while step < count:
-        received = lax.ppermute(held, axis, [(index, index ^ step) for index in range(count)])
+    for step in doubling(count):
+        received = send(held, [((index, line ^ step), (index, line)) for index in odd for line in range(count)])
         pieces.append(received)
-        step *= 2
-        if step < count:
-            held = jnp.concatenate([held, received], axis=0)
+        held = jnp.concatenate([held, received], axis=0)
     return pieces
+
+
+def y_spread(bounds):
+    hubs = y_hubs(lax.axis_size("yd"))
+    odd = range(1, lax.axis_size("xg"), 2)
+    sent = []
+    for slot, value in enumerate(bounds):
+        for step in (1, 0):
+            if slot or step:
+                sent.append(
+                    send(value, [((index, hub), (index - step, hub ^ slot)) for index in odd for hub in hubs])
+                )
+    return sent
 
 
 def f32(*shape):
@@ -350,38 +436,55 @@
     square = VMEM((rows, LANES), jnp.float32)
     x_nodes = LANES // SUBLANES - 1 + len(x_rolls(halves))
     y_nodes = halves * (rows // SUBLANES // halves - 1 + len(y_rolls()))
-    y_height = -(-QUANTITIES * halves // SUBLANES) * SUBLANES
-    message, x_state, storage = kernel_call(
+    message, block = kernel_call(
         functools.partial(x_forward_kernel, halves),
         tuple(
             pltpu.with_memory_space_constraint(value, pltpu.HBM)
-            for value in (mobile, dispersion_x, capacity, immobile, exchange_rates[None], rate_shares[None])
+            for value in (
+                mobile, dispersion_x, dispersion_y, capacity, immobile, exchange_rates[None], rate_shares[None],
+            )
         ),
-        [f32(SUBLANES, rows), held_f32(3 * x_nodes, SUBLANES, rows), held_f32(rows, LANES)],
+        [f32(SUBLANES, rows), held_f32(2 * rows + 3 * x_nodes * SUBLANES, LANES)],
         [square] * 3
         + [VMEM((zones * rows, LANES), jnp.float32)]
         + [VMEM((1, zones), jnp.float32)] * 2
-        + [pltpu.SemaphoreType.DMA((6,))]
+        + [pltpu.SemaphoreType.DMA((7,))]
         + [square] * 3,
         pltpu.HBM,
     )
-    y_rows, y_state = kernel_call(
-        functools.partial(y_coefs_kernel, halves),
-        (dispersion_y, storage),
-        [held_f32(SUBLANES, LANES), held_f32(3 * y_nodes, SUBLANES, LANES)],
+    pieces, other_block = x_exchange(message, block)
+    y_rows, y_state = zip(
+        *(
+            kernel_call(
+                functools.partial(y_coefs_kernel, halves),
+                (part,),
+                [held_f32(SUBLANES, LANES), held_f32(3 * y_nodes * SUBLANES, LANES)],
+                [],
+            )
+            for part in (other_block, block)
+        )
+    )
+    height = -(-QUANTITIES * 2 * halves // SUBLANES) * SUBLANES
+    message, other_givens, givens = kernel_call(
+        functools.partial(x_back_kernel, halves, "xg", len(pieces)),
+        (*pieces, other_block, block, *y_rows, *y_state),
+        [f32(height, LANES), f32(y_nodes * SUBLANES, LANES), held_f32(y_nodes * SUBLANES, LANES)],
+        [square] * 4,
+    )
+    pieces = y_gather(message)
+    sent_givens = to_even(other_givens)
+    count = lax.axis_size("yd")
+    hubs = y_hubs(count)
+    bounds = kernel_call(
+        functools.partial(y_ring_kernel, halves, "yd", height, len(pieces)),
+        tuple(pieces),
+        [f32(4 * halves, LANES)] * (count // len(hubs)),
         [],
     )
-    pieces = exchange(message, "xg")
-    message, givens = kernel_call(
-        functools.partial(x_back_kernel, halves, "xg", len(pieces)),
-        (*pieces, x_state, y_state, y_rows, storage),
-        [f32(y_height, LANES), held_f32(y_nodes, SUBLANES, LANES)],
-        [square] * 2,
-    )
-    pieces = exchange(message, "yd")
+    sent = y_spread(bounds)
     (updated,) = kernel_call(
-        functools.partial(y_back_kernel, halves, "yd", len(pieces)),
-        (*pieces, y_state, givens),
+        functools.partial(y_back_kernel, halves, ("xg", "yd"), hubs, len(sent)),
+        (bounds[0], *sent, y_state[1], givens, sent_givens),
         [f32(rows, LANES)],
         [],
     )

time: 21.1 us -> 40.5 us (1.92)
  the two profiles are of different devices: /device:TPU:0 before, /device:TPU:4 now
where the time goes in v4:
time: 40.5 us; the launch traced here: 40.1 us
  starting transfers between devices  18.6 us (46%)
  waiting for transfers between devices  18.3 us (45%)
  Pallas kernels  2.87 us (7%)
    ppermute x19, starting transfers between devices, send(): return lax.ppermute(value, ('xg', 'yd'), flat)  18.6 us
    ppermute x19, waiting for transfers between devices, send(): return lax.ppermute(value, ('xg', 'yd'), flat)  18.3 us
    pallas_call x6, Pallas kernels, kernel_call(): pl.pallas_call(body, out_shape=outputs, in_specs=[pl.BlockSpec(memory_spa...  2.87 us
  transfers between devices with their start and end apart: 19, of which 2 were waited for; matrix products, arithmetic and copies ran while one was open for 0% of the time, Pallas kernels for 1%

profile of v4, /device:TPU:4, one launch (start us, length us, event | category | flops | bytes accessed | tf_op | source)
XLA Modules:
  0.0 40.1 jit_solution(13939953114219210812)
XLA Ops:
  0.0 1.6 %shard_map.73 = (f32[8,128]{1,0:T(8,128)S(1)}, f32[712,128]{1,0:T(8,128)S(1)}) custom-call(f32[128,128]{1,0:T(8,128)} %bitcast.9, f32[128,128]{1,0:T(8,128)} %bitcast.10, f32[128,128]{1,0:T(8,128)} %bitcast.11, f32[128,128]{1,0:T(8,128)} %bitcast.12, f32[512,128]{1,0:T(8,128)} %bitcast.8, f32[1,4]{1,0:T(1,128)} %bitcast.13, f32[1,4]{1,0:T(1,128)} %bitcast.14), custom_call_target="tpu_custom_call" | custom-call | tf_op jit(solution)/shard_map/pallas_call | solution.py:413
  1.6 1.8 %collective-permute-start.3 = (f32[712,128]{1,0:T(8,128)S(1)}, f32[712,128]{1,0:T(8,128)S(1)}, u32[]{:S(2)}, u32[]{:S(2)}) collective-permute-start(f32[712,128]{1,0:T(8,128)S(1)} %get-tuple-element.19.block_ref.refs_5_), channel_id=1, source_target_pairs={{0,8},{1,9},{2,10},{3,11},{4,12},{5,13},{6,14},{7,15},{16,24},{17,... | collective-permute-start | bytes 1093640 | tf_op jit(solution)/shard_map/ppermute | solution.py:349
  3.4 2.4 %collective-permute-start.2 = (f32[8,128]{1,0:T(8,128)S(1)}, f32[8,128]{1,0:T(8,128)S(1)}, u32[]{:S(2)}, u32[]{:S(2)}) collective-permute-start(f32[8,128]{1,0:T(8,128)S(1)} %get-tuple-element.18.refs_0_), channel_id=1, source_target_pairs={{16,8},{17,9},{18,10},{19,11},{20,12},{21,13},{22,14},{23,15},{0,2... | collective-permute-start | bytes 12296 | tf_op jit(solution)/shard_map/ppermute | solution.py:349
  5.7 0.7 %collective-permute-start.1 = (f32[8,128]{1,0:T(8,128)S(1)}, f32[8,128]{1,0:T(8,128)S(1)}, u32[]{:S(2)}, u32[]{:S(2)}) collective-permute-start(f32[8,128]{1,0:T(8,128)S(1)} %get-tuple-element.18.refs_0_), channel_id=1, source_target_pairs={{24,8},{25,9},{26,10},{27,11},{28,12},{29,13},{30,14},{31,15},{8,2... | collective-permute-start | bytes 12296 | tf_op jit(solution)/shard_map/ppermute | solution.py:349
  6.4 2.7 %collective-permute-start = (f32[8,128]{1,0:T(8,128)S(1)}, f32[8,128]{1,0:T(8,128)S(1)}, u32[]{:S(2)}, u32[]{:S(2)}) collective-permute-start(f32[8,128]{1,0:T(8,128)S(1)} %get-tuple-element.18.refs_0_), channel_id=1, source_target_pairs={{0,8},{1,9},{2,10},{3,11},{4,12},{5,13},{6,14},{7,15},{16,24},{17,... | collective-permute-start | bytes 12296 | tf_op jit(solution)/shard_map/ppermute | solution.py:349
  9.1 0.1 shard_map.75
  9.2 0.0 collective-permute-done.3.block_ref.refs_4_
  9.2 0.1 shard_map.74
  9.3 0.0 collective-permute-done.2.refs_3_
  9.3 0.0 collective-permute-done.1.refs_2_
  9.3 0.6 %collective-permute-done.refs_1_ = f32[8,128]{1,0:T(8,128)S(1)} collective-permute-done((f32[8,128]{1,0:T(8,128)S(1)}, f32[8,128]{1,0:T(8,128)S(1)}, u32[]{:S(2)}, u32[]{:S(2)}) %collective-permute-start) | collective-permute-done | bytes 4128 | tf_op jit(solution)/shard_map/ppermute | solution.py:349
  9.9 0.3 shard_map.76
  10.2 1.3 %collective-permute-start.18 = (f32[160,128]{1,0:T(8,128)S(1)}, f32[160,128]{1,0:T(8,128)S(1)}, u32[]{:S(2)}, u32[]{:S(2)}) collective-permute-start(f32[160,128]{1,0:T(8,128)S(1)} %get-tuple-element.30), channel_id=1, source_target_pairs={{8,0},{9,1},{10,2},{11,3},{12,4},{13,5},{14,6},{15,7},{24,16},{25,... | collective-permute-start | bytes 245768 | tf_op jit(solution)/shard_map/ppermute | solution.py:349
  11.5 0.7 %collective-permute-start.10 = (f32[24,128]{1,0:T(8,128)S(1)}, f32[24,128]{1,0:T(8,128)S(1)}, u32[]{:S(2)}, u32[]{:S(2)}) collective-permute-start(f32[24,128]{1,0:T(8,128)S(1)} %get-tuple-element.24.refs_0_), channel_id=1, source_target_pairs={{13,10},{11,12},{29,26},{27,28}} | collective-permute-start | bytes 36872 | tf_op jit(solution)/shard_map/ppermute | solution.py:349
  12.2 0.7 %collective-permute-start.9 = (f32[24,128]{1,0:T(8,128)S(1)}, f32[24,128]{1,0:T(8,128)S(1)}, u32[]{:S(2)}, u32[]{:S(2)}) collective-permute-start(f32[24,128]{1,0:T(8,128)S(1)} %get-tuple-element.24.refs_0_), channel_id=1, source_target_pairs={{12,10},{10,12},{28,26},{26,28}} | collective-permute-start | bytes 36872 | tf_op jit(solution)/shard_map/ppermute | solution.py:349
  12.9 0.7 %collective-permute-start.8 = (f32[24,128]{1,0:T(8,128)S(1)}, f32[24,128]{1,0:T(8,128)S(1)}, u32[]{:S(2)}, u32[]{:S(2)}) collective-permute-start(f32[24,128]{1,0:T(8,128)S(1)} %get-tuple-element.24.refs_0_), channel_id=1, source_target_pairs={{15,10},{9,12},{31,26},{25,28}} | collective-permute-start | bytes 36872 | tf_op jit(solution)/shard_map/ppermute | solution.py:349
  13.5 0.7 %collective-permute-start.7 = (f32[24,128]{1,0:T(8,128)S(1)}, f32[24,128]{1,0:T(8,128)S(1)}, u32[]{:S(2)}, u32[]{:S(2)}) collective-permute-start(f32[24,128]{1,0:T(8,128)S(1)} %get-tuple-element.24.refs_0_), channel_id=1, source_target_pairs={{14,10},{8,12},{30,26},{24,28}} | collective-permute-start | bytes 36872 | tf_op jit(solution)/shard_map/ppermute | solution.py:349
  14.2 0.0 collective-permute-done.10.refs_7_
  14.2 0.7 %collective-permute-start.6 = (f32[24,128]{1,0:T(8,128)S(1)}, f32[24,128]{1,0:T(8,128)S(1)}, u32[]{:S(2)}, u32[]{:S(2)}) collective-permute-start(f32[24,128]{1,0:T(8,128)S(1)} %get-tuple-element.24.refs_0_), channel_id=1, source_target_pairs={{9,10},{15,12},{25,26},{31,28}} | collective-permute-start | bytes 36872 | tf_op jit(solution)/shard_map/ppermute | solution.py:349
  14.9 0.0 collective-permute-done.9.refs_6_
  14.9 0.7 %collective-permute-start.5 = (f32[24,128]{1,0:T(8,128)S(1)}, f32[24,128]{1,0:T(8,128)S(1)}, u32[]{:S(2)}, u32[]{:S(2)}) collective-permute-start(f32[24,128]{1,0:T(8,128)S(1)} %get-tuple-element.24.refs_0_), channel_id=1, source_target_pairs={{8,10},{14,12},{24,26},{30,28}} | collective-permute-start | bytes 36872 | tf_op jit(solution)/shard_map/ppermute | solution.py:349
  15.6 0.0 collective-permute-done.8.refs_5_
  15.6 0.7 %collective-permute-start.4 = (f32[24,128]{1,0:T(8,128)S(1)}, f32[24,128]{1,0:T(8,128)S(1)}, u32[]{:S(2)}, u32[]{:S(2)}) collective-permute-start(f32[24,128]{1,0:T(8,128)S(1)} %get-tuple-element.24.refs_0_), channel_id=1, source_target_pairs={{11,10},{13,12},{27,26},{29,28}} | collective-permute-start | bytes 36872 | tf_op jit(solution)/shard_map/ppermute | solution.py:349
  16.2 0.0 collective-permute-done.7.refs_4_
  16.3 0.0 collective-permute-done.6.refs_3_
  16.3 0.0 collective-permute-done.5.refs_2_
  16.3 0.0 collective-permute-done.4.refs_1_
  16.3 0.1 shard_map.77
  16.3 0.7 %collective-permute-start.11 = (f32[8,128]{1,0:T(8,128)S(1)}, f32[8,128]{1,0:T(8,128)S(1)}, u32[]{:S(2)}, u32[]{:S(2)}) collective-permute-start(f32[8,128]{1,0:T(8,128)S(1)} %get-tuple-element.25.refs_0_), channel_id=1, source_target_pairs={{10,2},{12,4},{26,18},{28,20}} | collective-permute-start | bytes 12296 | tf_op jit(solution)/shard_map/ppermute | solution.py:349
  17.0 0.7 %collective-permute-start.13 = (f32[8,128]{1,0:T(8,128)S(1)}, f32[8,128]{1,0:T(8,128)S(1)}, u32[]{:S(2)}, u32[]{:S(2)}) collective-permute-start(f32[8,128]{1,0:T(8,128)S(1)} %get-tuple-element.26), channel_id=1, source_target_pairs={{10,11},{12,13},{26,27},{28,29}} | collective-permute-start | bytes 12296 | tf_op jit(solution)/shard_map/ppermute | solution.py:349
  17.7 0.7 %collective-permute-start.12 = (f32[8,128]{1,0:T(8,128)S(1)}, f32[8,128]{1,0:T(8,128)S(1)}, u32[]{:S(2)}, u32[]{:S(2)}) collective-permute-start(f32[8,128]{1,0:T(8,128)S(1)} %get-tuple-element.26), channel_id=1, source_target_pairs={{10,3},{12,5},{26,19},{28,21}} | collective-permute-start | bytes 12296 | tf_op jit(solution)/shard_map/ppermute | solution.py:349
  18.4 0.7 %collective-permute-start.15 = (f32[8,128]{1,0:T(8,128)S(1)}, f32[8,128]{1,0:T(8,128)S(1)}, u32[]{:S(2)}, u32[]{:S(2)}) collective-permute-start(f32[8,128]{1,0:T(8,128)S(1)} %get-tuple-element.27), channel_id=1, source_target_pairs={{10,8},{12,14},{26,24},{28,30}} | collective-permute-start | bytes 12296 | tf_op jit(solution)/shard_map/ppermute | solution.py:349
  19.0 0.0 collective-permute-done.11.refs_1_
  19.0 0.7 %collective-permute-start.14 = (f32[8,128]{1,0:T(8,128)S(1)}, f32[8,128]{1,0:T(8,128)S(1)}, u32[]{:S(2)}, u32[]{:S(2)}) collective-permute-start(f32[8,128]{1,0:T(8,128)S(1)} %get-tuple-element.27), channel_id=1, source_target_pairs={{10,0},{12,6},{26,16},{28,22}} | collective-permute-start | bytes 12296 | tf_op jit(solution)/shard_map/ppermute | solution.py:349
  19.7 0.0 collective-permute-done.13.refs_3_
  19.7 0.7 %collective-permute-start.17 = (f32[8,128]{1,0:T(8,128)S(1)}, f32[8,128]{1,0:T(8,128)S(1)}, u32[]{:S(2)}, u32[]{:S(2)}) collective-permute-start(f32[8,128]{1,0:T(8,128)S(1)} %get-tuple-element.28), channel_id=1, source_target_pairs={{10,9},{12,15},{26,25},{28,31}} | collective-permute-start | bytes 12296 | tf_op jit(solution)/shard_map/ppermute | solution.py:349
  20.4 0.0 collective-permute-done.12.refs_2_
  20.4 1.3 %collective-permute-start.16 = (f32[8,128]{1,0:T(8,128)S(1)}, f32[8,128]{1,0:T(8,128)S(1)}, u32[]{:S(2)}, u32[]{:S(2)}) collective-permute-start(f32[8,128]{1,0:T(8,128)S(1)} %get-tuple-element.28), channel_id=1, source_target_pairs={{10,1},{12,7},{26,17},{28,23}} | collective-permute-start | bytes 12296 | tf_op jit(solution)/shard_map/ppermute | solution.py:349
  21.7 0.0 collective-permute-done.15.refs_5_
  21.7 0.0 collective-permute-done.14.refs_4_
  21.7 0.0 collective-permute-done.17.refs_7_
  21.7 17.7 %collective-permute-done.16.refs_6_ = f32[8,128]{1,0:T(8,128)S(1)} collective-permute-done((f32[8,128]{1,0:T(8,128)S(1)}, f32[8,128]{1,0:T(8,128)S(1)}, u32[]{:S(2)}, u32[]{:S(2)}) %collective-permute-start.16) | collective-permute-done | bytes 4128 | tf_op jit(solution)/shard_map/ppermute | solution.py:349
  39.4 0.0 collective-permute-done.18.refs_10_
  39.4 0.7 %shard_map.78 = f32[128,128]{1,0:T(8,128)} custom-call(f32[8,128]{1,0:T(8,128)S(1)} %get-tuple-element.25.refs_0_, f32[8,128]{1,0:T(8,128)S(1)} %collective-permute-done.11.refs_1_, f32[8,128]{1,0:T(8,128)S(1)} %collective-permute-done.12.refs_2_, f32[8,128]{1,0:T(8,128)S(1)} %collective-permute-done.13.refs_3_, ...), custom_call_target="tpu_custom_call" | custom-call | tf_op jit(solution)/shard_map/pallas_call | solution.py:413
Async XLA Ops:
  1.6 7.6 %collective-permute-start.3 = (f32[712,128]{1,0:T(8,128)S(1)}, f32[712,128]{1,0:T(8,128)S(1)}, u32[]{:S(2)}, u32[]{:S(2)}) collective-permute-start(f32[712,128]{1,0:T(8,128)S(1)} %get-tuple-element.19.block_ref.refs_5_), channel_id=1, source_target_pairs={{0,8},{1,9},{2,10},{3,11},{4,12},{5,13},{6,14},{7,15},{16,24},{17,... | collective-permute-start | bytes 1093640 | tf_op jit(solution)/shard_map/ppermute | solution.py:349
  3.4 5.9 %collective-permute-start.2 = (f32[8,128]{1,0:T(8,128)S(1)}, f32[8,128]{1,0:T(8,128)S(1)}, u32[]{:S(2)}, u32[]{:S(2)}) collective-permute-start(f32[8,128]{1,0:T(8,128)S(1)} %get-tuple-element.18.refs_0_), channel_id=1, source_target_pairs={{16,8},{17,9},{18,10},{19,11},{20,12},{21,13},{22,14},{23,15},{0,2... | collective-permute-start | bytes 12296 | tf_op jit(solution)/shard_map/ppermute | solution.py:349
  5.7 3.6 %collective-permute-start.1 = (f32[8,128]{1,0:T(8,128)S(1)}, f32[8,128]{1,0:T(8,128)S(1)}, u32[]{:S(2)}, u32[]{:S(2)}) collective-permute-start(f32[8,128]{1,0:T(8,128)S(1)} %get-tuple-element.18.refs_0_), channel_id=1, source_target_pairs={{24,8},{25,9},{26,10},{27,11},{28,12},{29,13},{30,14},{31,15},{8,2... | collective-permute-start | bytes 12296 | tf_op jit(solution)/shard_map/ppermute | solution.py:349
  6.4 3.5 %collective-permute-start = (f32[8,128]{1,0:T(8,128)S(1)}, f32[8,128]{1,0:T(8,128)S(1)}, u32[]{:S(2)}, u32[]{:S(2)}) collective-permute-start(f32[8,128]{1,0:T(8,128)S(1)} %get-tuple-element.18.refs_0_), channel_id=1, source_target_pairs={{0,8},{1,9},{2,10},{3,11},{4,12},{5,13},{6,14},{7,15},{16,24},{17,... | collective-permute-start | bytes 12296 | tf_op jit(solution)/shard_map/ppermute | solution.py:349
  10.2 29.2 %collective-permute-start.18 = (f32[160,128]{1,0:T(8,128)S(1)}, f32[160,128]{1,0:T(8,128)S(1)}, u32[]{:S(2)}, u32[]{:S(2)}) collective-permute-start(f32[160,128]{1,0:T(8,128)S(1)} %get-tuple-element.30), channel_id=1, source_target_pairs={{8,0},{9,1},{10,2},{11,3},{12,4},{13,5},{14,6},{15,7},{24,16},{25,... | collective-permute-start | bytes 245768 | tf_op jit(solution)/shard_map/ppermute | solution.py:349
  11.5 2.7 %collective-permute-start.10 = (f32[24,128]{1,0:T(8,128)S(1)}, f32[24,128]{1,0:T(8,128)S(1)}, u32[]{:S(2)}, u32[]{:S(2)}) collective-permute-start(f32[24,128]{1,0:T(8,128)S(1)} %get-tuple-element.24.refs_0_), channel_id=1, source_target_pairs={{13,10},{11,12},{29,26},{27,28}} | collective-permute-start | bytes 36872 | tf_op jit(solution)/shard_map/ppermute | solution.py:349
  12.2 2.7 %collective-permute-start.9 = (f32[24,128]{1,0:T(8,128)S(1)}, f32[24,128]{1,0:T(8,128)S(1)}, u32[]{:S(2)}, u32[]{:S(2)}) collective-permute-start(f32[24,128]{1,0:T(8,128)S(1)} %get-tuple-element.24.refs_0_), channel_id=1, source_target_pairs={{12,10},{10,12},{28,26},{26,28}} | collective-permute-start | bytes 36872 | tf_op jit(solution)/shard_map/ppermute | solution.py:349
  12.9 2.7 %collective-permute-start.8 = (f32[24,128]{1,0:T(8,128)S(1)}, f32[24,128]{1,0:T(8,128)S(1)}, u32[]{:S(2)}, u32[]{:S(2)}) collective-permute-start(f32[24,128]{1,0:T(8,128)S(1)} %get-tuple-element.24.refs_0_), channel_id=1, source_target_pairs={{15,10},{9,12},{31,26},{25,28}} | collective-permute-start | bytes 36872 | tf_op jit(solution)/shard_map/ppermute | solution.py:349
  13.5 2.7 %collective-permute-start.7 = (f32[24,128]{1,0:T(8,128)S(1)}, f32[24,128]{1,0:T(8,128)S(1)}, u32[]{:S(2)}, u32[]{:S(2)}) collective-permute-start(f32[24,128]{1,0:T(8,128)S(1)} %get-tuple-element.24.refs_0_), channel_id=1, source_target_pairs={{14,10},{8,12},{30,26},{24,28}} | collective-permute-start | bytes 36872 | tf_op jit(solution)/shard_map/ppermute | solution.py:349
  14.2 2.0 %collective-permute-start.6 = (f32[24,128]{1,0:T(8,128)S(1)}, f32[24,128]{1,0:T(8,128)S(1)}, u32[]{:S(2)}, u32[]{:S(2)}) collective-permute-start(f32[24,128]{1,0:T(8,128)S(1)} %get-tuple-element.24.refs_0_), channel_id=1, source_target_pairs={{9,10},{15,12},{25,26},{31,28}} | collective-permute-start | bytes 36872 | tf_op jit(solution)/shard_map/ppermute | solution.py:349
  14.9 1.4 %collective-permute-start.5 = (f32[24,128]{1,0:T(8,128)S(1)}, f32[24,128]{1,0:T(8,128)S(1)}, u32[]{:S(2)}, u32[]{:S(2)}) collective-permute-start(f32[24,128]{1,0:T(8,128)S(1)} %get-tuple-element.24.refs_0_), channel_id=1, source_target_pairs={{8,10},{14,12},{24,26},{30,28}} | collective-permute-start | bytes 36872 | tf_op jit(solution)/shard_map/ppermute | solution.py:349
  15.6 0.7 %collective-permute-start.4 = (f32[24,128]{1,0:T(8,128)S(1)}, f32[24,128]{1,0:T(8,128)S(1)}, u32[]{:S(2)}, u32[]{:S(2)}) collective-permute-start(f32[24,128]{1,0:T(8,128)S(1)} %get-tuple-element.24.refs_0_), channel_id=1, source_target_pairs={{11,10},{13,12},{27,26},{29,28}} | collective-permute-start | bytes 36872 | tf_op jit(solution)/shard_map/ppermute | solution.py:349
  16.3 2.7 %collective-permute-start.11 = (f32[8,128]{1,0:T(8,128)S(1)}, f32[8,128]{1,0:T(8,128)S(1)}, u32[]{:S(2)}, u32[]{:S(2)}) collective-permute-start(f32[8,128]{1,0:T(8,128)S(1)} %get-tuple-element.25.refs_0_), channel_id=1, source_target_pairs={{10,2},{12,4},{26,18},{28,20}} | collective-permute-start | bytes 12296 | tf_op jit(solution)/shard_map/ppermute | solution.py:349
  17.0 2.7 %collective-permute-start.13 = (f32[8,128]{1,0:T(8,128)S(1)}, f32[8,128]{1,0:T(8,128)S(1)}, u32[]{:S(2)}, u32[]{:S(2)}) collective-permute-start(f32[8,128]{1,0:T(8,128)S(1)} %get-tuple-element.26), channel_id=1, source_target_pairs={{10,11},{12,13},{26,27},{28,29}} | collective-permute-start | bytes 12296 | tf_op jit(solution)/shard_map/ppermute | solution.py:349
  17.7 2.7 %collective-permute-start.12 = (f32[8,128]{1,0:T(8,128)S(1)}, f32[8,128]{1,0:T(8,128)S(1)}, u32[]{:S(2)}, u32[]{:S(2)}) collective-permute-start(f32[8,128]{1,0:T(8,128)S(1)} %get-tuple-element.26), channel_id=1, source_target_pairs={{10,3},{12,5},{26,19},{28,21}} | collective-permute-start | bytes 12296 | tf_op jit(solution)/shard_map/ppermute | solution.py:349
  18.4 3.3 %collective-permute-start.15 = (f32[8,128]{1,0:T(8,128)S(1)}, f32[8,128]{1,0:T(8,128)S(1)}, u32[]{:S(2)}, u32[]{:S(2)}) collective-permute-start(f32[8,128]{1,0:T(8,128)S(1)} %get-tuple-element.27), channel_id=1, source_target_pairs={{10,8},{12,14},{26,24},{28,30}} | collective-permute-start | bytes 12296 | tf_op jit(solution)/shard_map/ppermute | solution.py:349
  19.0 2.7 %collective-permute-start.14 = (f32[8,128]{1,0:T(8,128)S(1)}, f32[8,128]{1,0:T(8,128)S(1)}, u32[]{:S(2)}, u32[]{:S(2)}) collective-permute-start(f32[8,128]{1,0:T(8,128)S(1)} %get-tuple-element.27), channel_id=1, source_target_pairs={{10,0},{12,6},{26,16},{28,22}} | collective-permute-start | bytes 12296 | tf_op jit(solution)/shard_map/ppermute | solution.py:349
  19.7 2.0 %collective-permute-start.17 = (f32[8,128]{1,0:T(8,128)S(1)}, f32[8,128]{1,0:T(8,128)S(1)}, u32[]{:S(2)}, u32[]{:S(2)}) collective-permute-start(f32[8,128]{1,0:T(8,128)S(1)} %get-tuple-element.28), channel_id=1, source_target_pairs={{10,9},{12,15},{26,25},{28,31}} | collective-permute-start | bytes 12296 | tf_op jit(solution)/shard_map/ppermute | solution.py:349
  20.4 19.0 %collective-permute-start.16 = (f32[8,128]{1,0:T(8,128)S(1)}, f32[8,128]{1,0:T(8,128)S(1)}, u32[]{:S(2)}, u32[]{:S(2)}) collective-permute-start(f32[8,128]{1,0:T(8,128)S(1)} %get-tuple-element.28), channel_id=1, source_target_pairs={{10,1},{12,7},{26,17},{28,23}} | collective-permute-start | bytes 12296 | tf_op jit(solution)/shard_map/ppermute | solution.py:349

commit v5 on v4

--- a/solution.py
+++ b/solution.py
@@ -312,19 +312,11 @@
         ref[2 * halves : 4 * halves, :] = after
 
 
-def y_back_kernel(halves, axes, hubs, sent, *refs):
-    own_ref, *sent_refs = refs[: 1 + sent]
-    state_ref, own_given, sent_given, out_ref = refs[1 + sent :]
+def y_back_kernel(halves, axis, own_ref, sent_ref, state_ref, own_given, sent_given, out_ref):
     rows = out_ref.shape[0]
     stride = rows // SUBLANES
-    other = lax.axis_index(axes[0]) % 2 == 0
-    place = lax.axis_index(axes[1])
-    solved = place == hubs[0]
-    for hub in hubs[1:]:
-        solved = solved | (place == hub)
-    ends = jnp.where(solved & jnp.logical_not(other), own_ref[...], 0.0)
-    for ref in sent_refs:
-        ends = ends + ref[...]
+    other = lax.axis_index(axis) % 2 == 0
+    ends = jnp.where(other, sent_ref[...], own_ref[...])
     total = stride // halves - 1 + len(y_rolls())
     both = 2 * halves
     for half in range(halves):
@@ -343,62 +335,44 @@
             out_ref[pl.ds(index * halves + half, SUBLANES, stride=stride), :] = value
 
 
-def send(value, pairs):
+def swap(value, steps):
     width = lax.axis_size("yd")
-    flat = [(source[0] * width + source[1], target[0] * width + target[1]) for source, target in pairs]
-    return lax.ppermute(value, ("xg", "yd"), flat)
+    pairs = []
+    for index in range(lax.axis_size("xg")):
+        step = steps(index)
+        for line in range(width):
+            pairs.append((index * width + line, (index ^ step[0]) * width + (line ^ step[1])))
+    return lax.ppermute(value, ("xg", "yd"), pairs)
+
+
+def swap_cores(value):
+    return swap(value, lambda index: (1, 0))
+
+
+def swap_odd(value, step):
+    return swap(value, lambda index: step if index % 2 else (0, 0))
+
+
+def gather_odd(pieces, held, steps):
+    for place, step in enumerate(steps):
+        received = swap_odd(held, step)
+        pieces.append(received)
+        if place < len(steps) - 1:
+            held = jnp.concatenate([held, received], axis=0)
+    return pieces
 
 
 def x_exchange(message, block):
-    count, lines = lax.axis_size("xg"), range(lax.axis_size("yd"))
-    odd = range(1, count, 2)
-    pieces = [message]
-    for chip in range(0, count, 2):
-        if chip:
-            pieces.append(send(message, [((index ^ chip, line), (index, line)) for index in odd for line in lines]))
-        pieces.append(send(message, [((index ^ chip ^ 1, line), (index, line)) for index in odd for line in lines]))
-    to_odd = [((index - 1, line), (index, line)) for index in odd for line in lines]
-    return pieces, send(block, to_odd)
-
-
-def to_even(value):
-    odd = range(1, lax.axis_size("xg"), 2)
-    return send(value, [((index, line), (index - 1, line)) for index in odd for line in range(lax.axis_size("yd"))])
-
-
-def y_hubs(count):
-    return [count // 4, count // 2] if 4 <= count <= 8 else list(range(count))
-
-
-def y_gather(message):
-    count = lax.axis_size("yd")
-    hubs = y_hubs(count)
-    odd = range(1, lax.axis_size("xg"), 2)
-    if len(hubs) < count:
-        return [message] + [
-            send(message, [((index, hub ^ slot), (index, hub)) for index in odd for hub in hubs])
-            for slot in range(1, count)
-        ]
-    pieces = [message]
-    held = message
-    for step in doubling(count):
-        received = send(held, [((index, line ^ step), (index, line)) for index in odd for line in range(count)])
-        pieces.append(received)
-        held = jnp.concatenate([held, received], axis=0)
-    return pieces
-
-
-def y_spread(bounds):
-    hubs = y_hubs(lax.axis_size("yd"))
-    odd = range(1, lax.axis_size("xg"), 2)
-    sent = []
-    for slot, value in enumerate(bounds):
-        for step in (1, 0):
-            if slot or step:
-                sent.append(
-                    send(value, [((index, hub), (index - step, hub ^ slot)) for index in odd for hub in hubs])
-                )
-    return sent
+    other = swap_cores(message)
+    block, other = lax.optimization_barrier((block, other))
+    other_block = swap_cores(block)
+    steps = [(2 * step, 0) for step in doubling(lax.axis_size("xg") // 2)]
+    held = jnp.concatenate([message, other], axis=0)
+    return gather_odd([message, other], held, steps), other_block
+
+
+def y_exchange(message):
+    return gather_odd([message], message, [(0, step) for step in doubling(lax.axis_size("yd"))])
 
 
 def f32(*shape):
@@ -471,20 +445,17 @@
         [f32(height, LANES), f32(y_nodes * SUBLANES, LANES), held_f32(y_nodes * SUBLANES, LANES)],
         [square] * 4,
     )
-    pieces = y_gather(message)
-    sent_givens = to_even(other_givens)
-    count = lax.axis_size("yd")
-    hubs = y_hubs(count)
-    bounds = kernel_call(
+    pieces = y_exchange(message)
+    sent_givens = swap_cores(other_givens)
+    (bounds,) = kernel_call(
         functools.partial(y_ring_kernel, halves, "yd", height, len(pieces)),
         tuple(pieces),
-        [f32(4 * halves, LANES)] * (count // len(hubs)),
+        [f32(4 * halves, LANES)],
         [],
     )
-    sent = y_spread(bounds)
     (updated,) = kernel_call(
-        functools.partial(y_back_kernel, halves, ("xg", "yd"), hubs, len(sent)),
-        (bounds[0], *sent, y_state[1], givens, sent_givens),
+        functools.partial(y_back_kernel, halves, "xg"),
+        (bounds, swap_cores(bounds), y_state[1], givens, sent_givens),
         [f32(rows, LANES)],
         [],
     )

time: 40.5 us -> 26 us (0.64)
  the two profiles are of different devices: /device:TPU:4 before, /device:TPU:0 now
where the time goes in v5:
time: 26 us; the launch traced here: 25.8 us
  starting transfers between devices  20.6 us (79%)
  Pallas kernels  2.86 us (11%)
  waiting for transfers between devices  2.24 us (9%)
    ppermute x8, starting transfers between devices, swap(): return lax.ppermute(value, ('xg', 'yd'), pairs)  20.6 us
    pallas_call x6, Pallas kernels, kernel_call(): pl.pallas_call(body, out_shape=outputs, in_specs=[pl.BlockSpec(memory_spa...  2.86 us
    ppermute x8, waiting for transfers between devices, swap(): return lax.ppermute(value, ('xg', 'yd'), pairs)  2.24 us
  transfers between devices with their start and end apart: 8, of which 3 were waited for; matrix products, arithmetic and copies ran while one was open for 0% of the time, Pallas kernels for 1%

profile of v5, /device:TPU:0, one launch (start us, length us, event | category | flops | bytes accessed | tf_op | source)
XLA Modules:
  0.0 25.8 jit_solution(10745941801691806424)
XLA Ops:
  0.0 1.6 %shard_map.73 = (f32[8,128]{1,0:T(8,128)S(1)}, f32[712,128]{1,0:T(8,128)S(1)}) custom-call(f32[128,128]{1,0:T(8,128)} %bitcast.9, f32[128,128]{1,0:T(8,128)} %bitcast.10, f32[128,128]{1,0:T(8,128)} %bitcast.11, f32[128,128]{1,0:T(8,128)} %bitcast.12, f32[512,128]{1,0:T(8,128)} %bitcast.8, f32[1,4]{1,0:T(1,128)} %bitcast.13, f32[1,4]{1,0:T(1,128)} %bitcast.14), custom_call_target="tpu_custom_call" | custom-call | tf_op jit(solution)/shard_map/pallas_call | solution.py:387
  1.6 0.5 %collective-permute-start = (f32[8,128]{1,0:T(8,128)S(1)}, f32[8,128]{1,0:T(8,128)S(1)}, u32[]{:S(2)}, u32[]{:S(2)}) collective-permute-start(f32[8,128]{1,0:T(8,128)S(1)} %get-tuple-element.16.refs_0_), channel_id=1, source_target_pairs={{0,8},{1,9},{2,10},{3,11},{4,12},{5,13},{6,14},{7,15},{8,0},{9,1},... | collective-permute-start | bytes 12296 | tf_op jit(solution)/shard_map/ppermute | solution.py:345
  2.1 0.8 %collective-permute-done.refs_1_ = f32[8,128]{1,0:T(8,128)S(1)} collective-permute-done((f32[8,128]{1,0:T(8,128)S(1)}, f32[8,128]{1,0:T(8,128)S(1)}, u32[]{:S(2)}, u32[]{:S(2)}) %collective-permute-start) | collective-permute-done | bytes 4128 | tf_op jit(solution)/shard_map/ppermute | solution.py:345
  2.9 0.3 %collective-permute-start.2 = (f32[712,128]{1,0:T(8,128)S(1)}, f32[712,128]{1,0:T(8,128)S(1)}, u32[]{:S(2)}, u32[]{:S(2)}) collective-permute-start(f32[712,128]{1,0:T(8,128)S(1)} %get-tuple-element.19.block_ref.refs_4_), channel_id=1, source_target_pairs={{0,8},{1,9},{2,10},{3,11},{4,12},{5,13},{6,14},{7,15},{8,0},{9,1},... | collective-permute-start | bytes 1093640 | tf_op jit(solution)/shard_map/ppermute | solution.py:345
  3.3 0.6 %collective-permute-start.1 = (f32[16,128]{1,0:T(8,128)S(1)}, f32[16,128]{1,0:T(8,128)S(1)}, u32[]{:S(2)}, u32[]{:S(2)}) collective-permute-start(f32[16,128]{1,0:T(8,128)S(1)} %pad_maximum_fusion.2), channel_id=1, source_target_pairs={{0,0},{1,1},{2,2},{3,3},{4,4},{5,5},{6,6},{7,7},{8,24},{9,25},{10,... | collective-permute-start | bytes 24584 | tf_op jit(solution)/shard_map/ppermute | solution.py:345
  3.9 0.1 shard_map.75
  4.0 0.6 %collective-permute-done.2.block_ref.refs_3_ = f32[712,128]{1,0:T(8,128)S(1)} collective-permute-done((f32[712,128]{1,0:T(8,128)S(1)}, f32[712,128]{1,0:T(8,128)S(1)}, u32[]{:S(2)}, u32[]{:S(2)}) %collective-permute-start.2) | collective-permute-done | bytes 364576 | tf_op jit(solution)/shard_map/ppermute | solution.py:345
  4.6 0.1 shard_map.74
  4.7 0.0 collective-permute-done.1.refs_2_
  4.7 0.4 %shard_map.76 = (f32[24,128]{1,0:T(8,128)S(1)}, f32[160,128]{1,0:T(8,128)S(1)}, f32[160,128]{1,0:T(8,128)S(1)}) custom-call(f32[8,128]{1,0:T(8,128)S(1)} %get-tuple-element.16.refs_0_, f32[8,128]{1,0:T(8,128)S(1)} %collective-permute-done.refs_1_, f32[16,128]{1,0:T(8,128)S(1)} %collective-permute-done.1.refs_2_, ...), custom_call_target="tpu_custom_call" | custom-call | tf_op jit(solution)/shard_map/pallas_call | solution.py:387
  5.1 0.7 %collective-permute-start.3 = (f32[24,128]{1,0:T(8,128)S(1)}, f32[24,128]{1,0:T(8,128)S(1)}, u32[]{:S(2)}, u32[]{:S(2)}) collective-permute-start(f32[24,128]{1,0:T(8,128)S(1)} %get-tuple-element.24.refs_0_), channel_id=1, source_target_pairs={{0,0},{1,1},{2,2},{3,3},{4,4},{5,5},{6,6},{7,7},{8,9},{9,8},{10,11... | collective-permute-start | bytes 36872 | tf_op jit(solution)/shard_map/ppermute | solution.py:345
  5.8 0.0 collective-permute-done.3.refs_1_
  5.8 0.7 %collective-permute-start.4 = (f32[48,128]{1,0:T(8,128)S(1)}, f32[48,128]{1,0:T(8,128)S(1)}, u32[]{:S(2)}, u32[]{:S(2)}) collective-permute-start(f32[48,128]{1,0:T(8,128)S(1)} %pad_maximum_fusion.1), channel_id=1, source_target_pairs={{0,0},{1,1},{2,2},{3,3},{4,4},{5,5},{6,6},{7,7},{8,10},{9,11},{10,... | collective-permute-start | bytes 73736 | tf_op jit(solution)/shard_map/ppermute | solution.py:345
  6.4 10.8 %collective-permute-start.7 = (f32[160,128]{1,0:T(8,128)S(1)}, f32[160,128]{1,0:T(8,128)S(1)}, u32[]{:S(2)}, u32[]{:S(2)}) collective-permute-start(f32[160,128]{1,0:T(8,128)S(1)} %get-tuple-element.26), channel_id=1, source_target_pairs={{0,8},{1,9},{2,10},{3,11},{4,12},{5,13},{6,14},{7,15},{8,0},{9,1},... | collective-permute-start | bytes 245768 | tf_op jit(solution)/shard_map/ppermute | solution.py:345
  17.2 0.0 collective-permute-done.4.refs_2_
  17.2 0.7 %collective-permute-start.5 = (f32[96,128]{1,0:T(8,128)S(1)}, f32[96,128]{1,0:T(8,128)S(1)}, u32[]{:S(2)}, u32[]{:S(2)}) collective-permute-start(f32[96,128]{1,0:T(8,128)S(1)} %pad_maximum_fusion), channel_id=1, source_target_pairs={{0,0},{1,1},{2,2},{3,3},{4,4},{5,5},{6,6},{7,7},{8,12},{9,13},{10,... | collective-permute-start | bytes 147464 | tf_op jit(solution)/shard_map/ppermute | solution.py:345
  17.9 0.0 collective-permute-done.5.refs_3_
  17.9 0.1 shard_map.77.own_ref
  18.0 6.4 %collective-permute-start.6 = (f32[8,128]{1,0:T(8,128)S(1)}, f32[8,128]{1,0:T(8,128)S(1)}, u32[]{:S(2)}, u32[]{:S(2)}) collective-permute-start(f32[8,128]{1,0:T(8,128)S(1)} %shard_map.77.own_ref), channel_id=1, source_target_pairs={{0,8},{1,9},{2,10},{3,11},{4,12},{5,13},{6,14},{7,15},{8,0},{9,1},... | collective-permute-start | bytes 12296 | tf_op jit(solution)/shard_map/ppermute | solution.py:345
  24.3 0.0 collective-permute-done.7.sent_given
  24.3 0.8 %collective-permute-done.6.sent_ref = f32[8,128]{1,0:T(8,128)S(1)} collective-permute-done((f32[8,128]{1,0:T(8,128)S(1)}, f32[8,128]{1,0:T(8,128)S(1)}, u32[]{:S(2)}, u32[]{:S(2)}) %collective-permute-start.6) | collective-permute-done | bytes 4128 | tf_op jit(solution)/shard_map/ppermute | solution.py:345
  25.1 0.7 %shard_map.78 = f32[128,128]{1,0:T(8,128)} custom-call(f32[8,128]{1,0:T(8,128)S(1)} %shard_map.77.own_ref, f32[8,128]{1,0:T(8,128)S(1)} %collective-permute-done.6.sent_ref, f32[480,128]{1,0:T(8,128)S(1)} %get-tuple-element.23.refs_8_.state_ref, f32[160,128]{1,0:T(8,128)S(1)} %get-tuple-element.25.own_given, f32[160,128]{1,0:T(8,128)S(1)} %collective-permute-done.7.sent_given), custom_call_target="tpu_custom_call" | custom-call | tf_op jit(solution)/shard_map/pallas_call | solution.py:387
  (3 shorter events, 0.0 us)
Async XLA Ops:
  1.6 1.3 %collective-permute-start = (f32[8,128]{1,0:T(8,128)S(1)}, f32[8,128]{1,0:T(8,128)S(1)}, u32[]{:S(2)}, u32[]{:S(2)}) collective-permute-start(f32[8,128]{1,0:T(8,128)S(1)} %get-tuple-element.16.refs_0_), channel_id=1, source_target_pairs={{0,8},{1,9},{2,10},{3,11},{4,12},{5,13},{6,14},{7,15},{8,0},{9,1},... | collective-permute-start | bytes 12296 | tf_op jit(solution)/shard_map/ppermute | solution.py:345
  2.9 1.7 %collective-permute-start.2 = (f32[712,128]{1,0:T(8,128)S(1)}, f32[712,128]{1,0:T(8,128)S(1)}, u32[]{:S(2)}, u32[]{:S(2)}) collective-permute-start(f32[712,128]{1,0:T(8,128)S(1)} %get-tuple-element.19.block_ref.refs_4_), channel_id=1, source_target_pairs={{0,8},{1,9},{2,10},{3,11},{4,12},{5,13},{6,14},{7,15},{8,0},{9,1},... | collective-permute-start | bytes 1093640 | tf_op jit(solution)/shard_map/ppermute | solution.py:345
  3.3 1.4 %collective-permute-start.1 = (f32[16,128]{1,0:T(8,128)S(1)}, f32[16,128]{1,0:T(8,128)S(1)}, u32[]{:S(2)}, u32[]{:S(2)}) collective-permute-start(f32[16,128]{1,0:T(8,128)S(1)} %pad_maximum_fusion.2), channel_id=1, source_target_pairs={{0,0},{1,1},{2,2},{3,3},{4,4},{5,5},{6,6},{7,7},{8,24},{9,25},{10,... | collective-permute-start | bytes 24584 | tf_op jit(solution)/shard_map/ppermute | solution.py:345
  5.1 0.7 %collective-permute-start.3 = (f32[24,128]{1,0:T(8,128)S(1)}, f32[24,128]{1,0:T(8,128)S(1)}, u32[]{:S(2)}, u32[]{:S(2)}) collective-permute-start(f32[24,128]{1,0:T(8,128)S(1)} %get-tuple-element.24.refs_0_), channel_id=1, source_target_pairs={{0,0},{1,1},{2,2},{3,3},{4,4},{5,5},{6,6},{7,7},{8,9},{9,8},{10,11... | collective-permute-start | bytes 36872 | tf_op jit(solution)/shard_map/ppermute | solution.py:345
  5.8 11.5 %collective-permute-start.4 = (f32[48,128]{1,0:T(8,128)S(1)}, f32[48,128]{1,0:T(8,128)S(1)}, u32[]{:S(2)}, u32[]{:S(2)}) collective-permute-start(f32[48,128]{1,0:T(8,128)S(1)} %pad_maximum_fusion.1), channel_id=1, source_target_pairs={{0,0},{1,1},{2,2},{3,3},{4,4},{5,5},{6,6},{7,7},{8,10},{9,11},{10,... | collective-permute-start | bytes 73736 | tf_op jit(solution)/shard_map/ppermute | solution.py:345
  6.4 17.9 %collective-permute-start.7 = (f32[160,128]{1,0:T(8,128)S(1)}, f32[160,128]{1,0:T(8,128)S(1)}, u32[]{:S(2)}, u32[]{:S(2)}) collective-permute-start(f32[160,128]{1,0:T(8,128)S(1)} %get-tuple-element.26), channel_id=1, source_target_pairs={{0,8},{1,9},{2,10},{3,11},{4,12},{5,13},{6,14},{7,15},{8,0},{9,1},... | collective-permute-start | bytes 245768 | tf_op jit(solution)/shard_map/ppermute | solution.py:345
  17.2 0.7 %collective-permute-start.5 = (f32[96,128]{1,0:T(8,128)S(1)}, f32[96,128]{1,0:T(8,128)S(1)}, u32[]{:S(2)}, u32[]{:S(2)}) collective-permute-start(f32[96,128]{1,0:T(8,128)S(1)} %pad_maximum_fusion), channel_id=1, source_target_pairs={{0,0},{1,1},{2,2},{3,3},{4,4},{5,5},{6,6},{7,7},{8,12},{9,13},{10,... | collective-permute-start | bytes 147464 | tf_op jit(solution)/shard_map/ppermute | solution.py:345
  18.0 7.2 %collective-permute-start.6 = (f32[8,128]{1,0:T(8,128)S(1)}, f32[8,128]{1,0:T(8,128)S(1)}, u32[]{:S(2)}, u32[]{:S(2)}) collective-permute-start(f32[8,128]{1,0:T(8,128)S(1)} %shard_map.77.own_ref), channel_id=1, source_target_pairs={{0,8},{1,9},{2,10},{3,11},{4,12},{5,13},{6,14},{7,15},{8,0},{9,1},... | collective-permute-start | bytes 12296 | tf_op jit(solution)/shard_map/ppermute | solution.py:345

commit v6 on v5

--- a/solution.py
+++ b/solution.py
@@ -238,26 +238,22 @@
             rows_ref[row : row + 1, :] = value[0:1, :]
 
 
-def state_parts(ref, first, total, parts):
+def state_parts(ref, first, total, parts, pitch=3):
     return [
         tuple(
-            ref[(3 * place + part) * SUBLANES : (3 * place + part + 1) * SUBLANES, :]
+            ref[(pitch * place + part) * SUBLANES : (pitch * place + part + 1) * SUBLANES, :]
             for part in range(parts)
         )
         for place in range(first, first + total)
     ]
 
 
-def message_slots(refs, height, quantity_rows):
+def message_slots(refs, height, pitch, quantity_rows, skips):
+    blocks = [(ref, start) for ref in refs for start in range(0, ref.shape[0], height)]
     slots = []
-    for ref in refs:
-        for start in range(0, ref.shape[0], height):
-            slots.append(
-                tuple(
-                    ref[start + quantity * quantity_rows : start + (quantity + 1) * quantity_rows, :]
-                    for quantity in range(QUANTITIES)
-                )
-            )
+    for (ref, start), skip in zip(blocks, skips):
+        rows = [start + quantity * pitch + skip for quantity in range(QUANTITIES)]
+        slots.append(tuple(ref[row : row + quantity_rows, :] for row in rows))
     return slots
 
 
@@ -274,11 +270,12 @@
     sides_ref[...] = block_ref[0:rows, :] * values_t[...].T
 
 
-def x_back_kernel(halves, axis, pieces, *refs):
-    slots = message_slots(refs[:pieces], SUBLANES, 1)
+def x_back_kernel(halves, axis, order, pieces, *refs):
+    slots = message_slots(refs[:pieces], SUBLANES, 1, 1, [0] * len(order))
+    slots = [slots[order.index(place)] for place in range(len(order))]
     block_refs, rows_refs, state_refs = (refs[pieces + 2 * pair : pieces + 2 * pair + 2] for pair in range(3))
-    message_ref, *given_refs = refs[pieces + 6 : pieces + 9]
-    scratch = refs[pieces + 9 :]
+    message_ref, given_ref = refs[pieces + 6 : pieces + 8]
+    scratch = refs[pieces + 8 :]
     bounds = ring_bounds(slots, lax.axis_index(axis))
     rows = scratch[0].shape[1]
     stride = rows // SUBLANES
@@ -286,16 +283,17 @@
     both = 2 * halves
     for block in range(2):
         values_t, sides_ref = scratch[2 * block : 2 * block + 2]
-        x_back(halves, bounds[1 - block], block_refs[block], values_t, sides_ref)
+        x_back(halves, bounds[block], block_refs[block], values_t, sides_ref)
         start = 0
         for half in range(halves):
             place = block * halves + half
             sides = [(None, strided(sides_ref, index, SUBLANES, stride)) for index in range(half, stride, halves)]
             nodes = state_parts(state_refs[block], half * total, total, 3)
             piece, givens = tree_sides(sides, y_rolls(), nodes)
-            for given in givens:
-                given_refs[block][start : start + SUBLANES, :] = given
-                start += SUBLANES
+            if block == 0:
+                for given in givens:
+                    given_ref[start : start + SUBLANES, :] = given
+                    start += SUBLANES
             for number in range(3):
                 row = number * halves + half
                 message_ref[number * both + place : number * both + place + 1, :] = rows_refs[block][row : row + 1, :]
@@ -304,75 +302,60 @@
                 message_ref[row : row + 1, :] = value[0:1, :]
 
 
-def y_ring_kernel(halves, axis, height, pieces, *refs):
-    slots = message_slots(refs[:pieces], height, 2 * halves)
-    bounds = ring_bounds(slots, lax.axis_index(axis))
-    for ref, (before, after) in zip(refs[pieces:], bounds):
-        ref[0 : 2 * halves, :] = before
-        ref[2 * halves : 4 * halves, :] = after
-
-
-def y_back_kernel(halves, axis, own_ref, sent_ref, state_ref, own_given, sent_given, out_ref):
+def y_back_kernel(halves, axis, height, traded, pieces, *refs):
+    state_ref, given_ref, out_ref = refs[pieces:]
     rows = out_ref.shape[0]
     stride = rows // SUBLANES
-    other = lax.axis_index(axis) % 2 == 0
-    ends = jnp.where(other, sent_ref[...], own_ref[...])
+    slots = message_slots(refs[:pieces], height, 2 * halves, halves, [halves if odd else 0 for odd in traded])
+    ends = ring_bounds(slots, lax.axis_index(axis))[0]
     total = stride // halves - 1 + len(y_rolls())
-    both = 2 * halves
     for half in range(halves):
-        bounds = []
-        for end in range(2):
-            row = end * both + half
-            bound = jnp.where(other, ends[row : row + 1, :], ends[row + halves : row + halves + 1, :])
-            bounds.append(jnp.broadcast_to(bound, (SUBLANES, LANES)))
+        bounds = [jnp.broadcast_to(end[half : half + 1, :], (SUBLANES, LANES)) for end in ends]
         nodes = state_parts(state_ref, half * total, total, 2)
-        givens = []
-        for node in range(half * total, (half + 1) * total):
-            part = slice(node * SUBLANES, (node + 1) * SUBLANES)
-            givens.append(jnp.where(other, sent_given[part, :], own_given[part, :]))
+        givens = [part[0] for part in state_parts(given_ref, half * total, total, 1, 1)]
         values = tree_values(*bounds, y_rolls(), stride // halves, nodes, givens)
         for index, value in enumerate(values):
             out_ref[pl.ds(index * halves + half, SUBLANES, stride=stride), :] = value
 
 
-def swap(value, steps):
+def trade(value, x_step, y_step):
     width = lax.axis_size("yd")
     pairs = []
     for index in range(lax.axis_size("xg")):
-        step = steps(index)
         for line in range(width):
-            pairs.append((index * width + line, (index ^ step[0]) * width + (line ^ step[1])))
+            pairs.append((index * width + line, (index ^ x_step) * width + (line ^ y_step)))
     return lax.ppermute(value, ("xg", "yd"), pairs)
 
 
-def swap_cores(value):
-    return swap(value, lambda index: (1, 0))
-
-
-def swap_odd(value, step):
-    return swap(value, lambda index: step if index % 2 else (0, 0))
-
-
-def gather_odd(pieces, held, steps):
-    for place, step in enumerate(steps):
-        received = swap_odd(held, step)
+def x_exchange(message, block):
+    other = trade(message, 1, 0)
+    block, other = lax.optimization_barrier((block, other))
+    other_block = trade(block, 1, 0)
+    pieces = [message, other]
+    order = [0, 1]
+    held = jnp.concatenate(pieces, axis=0)
+    for step in doubling(lax.axis_size("xg") // 2):
+        received = trade(held, 2 * step + 1, 0)
         pieces.append(received)
-        if place < len(steps) - 1:
+        order += [place ^ (2 * step + 1) for place in order]
+        if 4 * step < lax.axis_size("xg"):
             held = jnp.concatenate([held, received], axis=0)
-    return pieces
-
-
-def x_exchange(message, block):
-    other = swap_cores(message)
-    block, other = lax.optimization_barrier((block, other))
-    other_block = swap_cores(block)
-    steps = [(2 * step, 0) for step in doubling(lax.axis_size("xg") // 2)]
-    held = jnp.concatenate([message, other], axis=0)
-    return gather_odd([message, other], held, steps), other_block
+    return pieces, order, other_block
 
 
 def y_exchange(message):
-    return gather_odd([message], message, [(0, step) for step in doubling(lax.axis_size("yd"))])
+    count = lax.axis_size("yd")
+    stages = [[1], [2, 4, 6]] if count == 8 else [[step] for step in doubling(count)]
+    pieces = [message]
+    traded = [False]
+    held = message
+    for stage in stages:
+        received = [trade(held, 1, step) for step in stage]
+        pieces += received
+        traded += [not odd for odd in traded] * len(stage)
+        if len(traded) < count:
+            held = jnp.concatenate([held] + received, axis=0)
+    return pieces, traded
 
 
 def f32(*shape):
@@ -426,7 +409,7 @@
         + [square] * 3,
         pltpu.HBM,
     )
-    pieces, other_block = x_exchange(message, block)
+    pieces, order, other_block = x_exchange(message, block)
     y_rows, y_state = zip(
         *(
             kernel_call(
@@ -435,27 +418,20 @@
                 [held_f32(SUBLANES, LANES), held_f32(3 * y_nodes * SUBLANES, LANES)],
                 [],
             )
-            for part in (other_block, block)
+            for part in (block, other_block)
         )
     )
     height = -(-QUANTITIES * 2 * halves // SUBLANES) * SUBLANES
-    message, other_givens, givens = kernel_call(
-        functools.partial(x_back_kernel, halves, "xg", len(pieces)),
-        (*pieces, other_block, block, *y_rows, *y_state),
-        [f32(height, LANES), f32(y_nodes * SUBLANES, LANES), held_f32(y_nodes * SUBLANES, LANES)],
+    message, givens = kernel_call(
+        functools.partial(x_back_kernel, halves, "xg", order, len(pieces)),
+        (*pieces, block, other_block, *y_rows, *y_state),
+        [f32(height, LANES), held_f32(y_nodes * SUBLANES, LANES)],
         [square] * 4,
     )
-    pieces = y_exchange(message)
-    sent_givens = swap_cores(other_givens)
-    (bounds,) = kernel_call(
-        functools.partial(y_ring_kernel, halves, "yd", height, len(pieces)),
-        tuple(pieces),
-        [f32(4 * halves, LANES)],
-        [],
-    )
+    pieces, traded = y_exchange(message)
     (updated,) = kernel_call(
-        functools.partial(y_back_kernel, halves, "xg"),
-        (bounds, swap_cores(bounds), y_state[1], givens, sent_givens),
+        functools.partial(y_back_kernel, halves, "yd", height, traded, len(pieces)),
+        (*pieces, y_state[0], givens),
         [f32(rows, LANES)],
         [],
     )

time: 26 us -> 19.6 us (0.75)
  starting transfers between devices: 20.6 us -> 9.4 us
  waiting for transfers between devices: 2.24 us -> 7.2 us
    ppermute x8 -> x7, starting transfers between devices: 20.6 us -> 9.4 us  [trade(): return lax.ppermute(value, ('xg', 'yd'), pairs)]
    ppermute x8 -> x7, waiting for transfers between devices: 2.24 us -> 7.2 us  [trade(): return lax.ppermute(value, ('xg', 'yd'), pairs)]
    pallas_call x6 -> x5, Pallas kernels: 2.86 us -> 2.86 us  [kernel_call(): pl.pallas_call(body, out_shape=outputs, in_specs=[pl.BlockSpec(memory_spa...]
  transfers between devices with their start and end apart: 8 -> 7, of which waited for: 3 -> 5; matrix products, arithmetic and copies ran while one was open for 0% -> 0% of each run, Pallas kernels for 1% -> 1%
where the time goes in v6:
time: 19.6 us; the launch traced here: 19.5 us
  starting transfers between devices  9.4 us (48%)
  waiting for transfers between devices  7.2 us (37%)
  Pallas kernels  2.86 us (15%)
    ppermute x7, starting transfers between devices, trade(): return lax.ppermute(value, ('xg', 'yd'), pairs)  9.4 us
    ppermute x7, waiting for transfers between devices, trade(): return lax.ppermute(value, ('xg', 'yd'), pairs)  7.2 us
    pallas_call x5, Pallas kernels, kernel_call(): pl.pallas_call(body, out_shape=outputs, in_specs=[pl.BlockSpec(memory_spa...  2.86 us
  transfers between devices with their start and end apart: 7, of which 5 were waited for; matrix products, arithmetic and copies ran while one was open for 0% of the time, Pallas kernels for 1%

profile of v6, /device:TPU:0, one launch (start us, length us, event | category | flops | bytes accessed | tf_op | source)
XLA Modules:
  0.0 19.5 jit_solution(7445889531003055250)
XLA Ops:
  0.0 1.6 %shard_map.73 = (f32[8,128]{1,0:T(8,128)S(1)}, f32[712,128]{1,0:T(8,128)S(1)}) custom-call(f32[128,128]{1,0:T(8,128)} %bitcast.9, f32[128,128]{1,0:T(8,128)} %bitcast.10, f32[128,128]{1,0:T(8,128)} %bitcast.11, f32[128,128]{1,0:T(8,128)} %bitcast.12, f32[512,128]{1,0:T(8,128)} %bitcast.8, f32[1,4]{1,0:T(1,128)} %bitcast.13, f32[1,4]{1,0:T(1,128)} %bitcast.14), custom_call_target="tpu_custom_call" | custom-call | tf_op jit(solution)/shard_map/pallas_call | solution.py:370
  1.6 0.5 %collective-permute-start = (f32[8,128]{1,0:T(8,128)S(1)}, f32[8,128]{1,0:T(8,128)S(1)}, u32[]{:S(2)}, u32[]{:S(2)}) collective-permute-start(f32[8,128]{1,0:T(8,128)S(1)} %get-tuple-element.15.refs_0_), channel_id=1, source_target_pairs={{0,8},{1,9},{2,10},{3,11},{4,12},{5,13},{6,14},{7,15},{8,0},{9,1},... | collective-permute-start | bytes 12296 | tf_op jit(solution)/shard_map/ppermute | solution.py:327
  2.1 0.8 %collective-permute-done.refs_1_ = f32[8,128]{1,0:T(8,128)S(1)} collective-permute-done((f32[8,128]{1,0:T(8,128)S(1)}, f32[8,128]{1,0:T(8,128)S(1)}, u32[]{:S(2)}, u32[]{:S(2)}) %collective-permute-start) | collective-permute-done | bytes 4128 | tf_op jit(solution)/shard_map/ppermute | solution.py:327
  2.9 0.3 %collective-permute-start.2 = (f32[712,128]{1,0:T(8,128)S(1)}, f32[712,128]{1,0:T(8,128)S(1)}, u32[]{:S(2)}, u32[]{:S(2)}) collective-permute-start(f32[712,128]{1,0:T(8,128)S(1)} %get-tuple-element.18.block_ref.refs_3_), channel_id=1, source_target_pairs={{0,8},{1,9},{2,10},{3,11},{4,12},{5,13},{6,14},{7,15},{8,0},{9,1},... | collective-permute-start | bytes 1093640 | tf_op jit(solution)/shard_map/ppermute | solution.py:327
  3.3 2.6 %collective-permute-start.1 = (f32[16,128]{1,0:T(8,128)S(1)}, f32[16,128]{1,0:T(8,128)S(1)}, u32[]{:S(2)}, u32[]{:S(2)}) collective-permute-start(f32[16,128]{1,0:T(8,128)S(1)} %pad_maximum_fusion), channel_id=1, source_target_pairs={{0,24},{1,25},{2,26},{3,27},{4,28},{5,29},{6,30},{7,31},{8,16},{9,... | collective-permute-start | bytes 24584 | tf_op jit(solution)/shard_map/ppermute | solution.py:327
  5.9 0.1 shard_map.74
  6.0 0.0 collective-permute-done.2.block_ref.refs_4_
  6.0 0.1 shard_map.75
  6.1 1.2 %collective-permute-done.1.refs_2_ = f32[16,128]{1,0:T(8,128)S(1)} collective-permute-done((f32[16,128]{1,0:T(8,128)S(1)}, f32[16,128]{1,0:T(8,128)S(1)}, u32[]{:S(2)}, u32[]{:S(2)}) %collective-permute-start.1) | collective-permute-done | bytes 8224 | tf_op jit(solution)/shard_map/ppermute | solution.py:327
  7.2 0.3 %shard_map.76 = (f32[24,128]{1,0:T(8,128)S(1)}, f32[160,128]{1,0:T(8,128)S(1)}) custom-call(f32[8,128]{1,0:T(8,128)S(1)} %get-tuple-element.15.refs_0_, f32[8,128]{1,0:T(8,128)S(1)} %collective-permute-done.refs_1_, f32[16,128]{1,0:T(8,128)S(1)} %collective-permute-done.1.refs_2_, f32[712,128]{1,0:T(8,128)S(1)} %get-tuple-element.18.block_ref.refs_3_, ...), custom_call_target="tpu_custom_call" | custom-call | tf_op jit(solution)/shard_map/pallas_call | solution.py:370
  7.6 1.8 %collective-permute-start.3 = (f32[24,128]{1,0:T(8,128)S(1)}, f32[24,128]{1,0:T(8,128)S(1)}, u32[]{:S(2)}, u32[]{:S(2)}) collective-permute-start(f32[24,128]{1,0:T(8,128)S(1)} %get-tuple-element.23.refs_0_), channel_id=1, source_target_pairs={{0,9},{1,8},{2,11},{3,10},{4,13},{5,12},{6,15},{7,14},{8,1},{9,0},... | collective-permute-start | bytes 36872 | tf_op jit(solution)/shard_map/ppermute | solution.py:327
  9.4 1.4 %collective-permute-done.3.refs_1_ = f32[24,128]{1,0:T(8,128)S(1)} collective-permute-done((f32[24,128]{1,0:T(8,128)S(1)}, f32[24,128]{1,0:T(8,128)S(1)}, u32[]{:S(2)}, u32[]{:S(2)}) %collective-permute-start.3) | collective-permute-done | bytes 12320 | tf_op jit(solution)/shard_map/ppermute | solution.py:327
  10.8 3.8 %collective-permute-start.6 = (f32[48,128]{1,0:T(8,128)S(1)}, f32[48,128]{1,0:T(8,128)S(1)}, u32[]{:S(2)}, u32[]{:S(2)}) collective-permute-start(f32[48,128]{1,0:T(8,128)S(1)} %constant_dynamic-update-slice_fusion), channel_id=1, source_target_pairs={{0,14},{1,15},{2,12},{3,13},{4,10},{5,11},{6,8},{7,9},{8,6},{9,7},... | collective-permute-start | bytes 73736 | tf_op jit(solution)/shard_map/ppermute | solution.py:327
  14.6 0.0 collective-permute-start.5
  14.6 0.3 %collective-permute-start.4 = (f32[48,128]{1,0:T(8,128)S(1)}, f32[48,128]{1,0:T(8,128)S(1)}, u32[]{:S(2)}, u32[]{:S(2)}) collective-permute-start(f32[48,128]{1,0:T(8,128)S(1)} %constant_dynamic-update-slice_fusion), channel_id=1, source_target_pairs={{0,10},{1,11},{2,8},{3,9},{4,14},{5,15},{6,12},{7,13},{8,2},{9,3},... | collective-permute-start | bytes 73736 | tf_op jit(solution)/shard_map/ppermute | solution.py:327
  15.0 1.2 %collective-permute-done.6.refs_4_ = f32[48,128]{1,0:T(8,128)S(1)} collective-permute-done((f32[48,128]{1,0:T(8,128)S(1)}, f32[48,128]{1,0:T(8,128)S(1)}, u32[]{:S(2)}, u32[]{:S(2)}) %collective-permute-start.6) | collective-permute-done | bytes 24608 | tf_op jit(solution)/shard_map/ppermute | solution.py:327
  16.1 2.6 %collective-permute-done.5.refs_3_ = f32[48,128]{1,0:T(8,128)S(1)} collective-permute-done((f32[48,128]{1,0:T(8,128)S(1)}, f32[48,128]{1,0:T(8,128)S(1)}, u32[]{:S(2)}, u32[]{:S(2)}) %collective-permute-start.5) | collective-permute-done | bytes 24608 | tf_op jit(solution)/shard_map/ppermute | solution.py:327
  18.8 0.0 collective-permute-done.4.refs_2_
  18.8 0.7 %shard_map.77 = f32[128,128]{1,0:T(8,128)} custom-call(f32[24,128]{1,0:T(8,128)S(1)} %get-tuple-element.23.refs_0_, f32[24,128]{1,0:T(8,128)S(1)} %collective-permute-done.3.refs_1_, f32[48,128]{1,0:T(8,128)S(1)} %collective-permute-done.4.refs_2_, f32[48,128]{1,0:T(8,128)S(1)} %collective-permute-done.5.refs_3_, ...), custom_call_target="tpu_custom_call" | custom-call | tf_op jit(solution)/shard_map/pallas_call | solution.py:370
  (3 shorter events, 0.0 us)
Async XLA Ops:
  1.6 1.3 %collective-permute-start = (f32[8,128]{1,0:T(8,128)S(1)}, f32[8,128]{1,0:T(8,128)S(1)}, u32[]{:S(2)}, u32[]{:S(2)}) collective-permute-start(f32[8,128]{1,0:T(8,128)S(1)} %get-tuple-element.15.refs_0_), channel_id=1, source_target_pairs={{0,8},{1,9},{2,10},{3,11},{4,12},{5,13},{6,14},{7,15},{8,0},{9,1},... | collective-permute-start | bytes 12296 | tf_op jit(solution)/shard_map/ppermute | solution.py:327
  2.9 3.0 %collective-permute-start.2 = (f32[712,128]{1,0:T(8,128)S(1)}, f32[712,128]{1,0:T(8,128)S(1)}, u32[]{:S(2)}, u32[]{:S(2)}) collective-permute-start(f32[712,128]{1,0:T(8,128)S(1)} %get-tuple-element.18.block_ref.refs_3_), channel_id=1, source_target_pairs={{0,8},{1,9},{2,10},{3,11},{4,12},{5,13},{6,14},{7,15},{8,0},{9,1},... | collective-permute-start | bytes 1093640 | tf_op jit(solution)/shard_map/ppermute | solution.py:327
  3.3 4.0 %collective-permute-start.1 = (f32[16,128]{1,0:T(8,128)S(1)}, f32[16,128]{1,0:T(8,128)S(1)}, u32[]{:S(2)}, u32[]{:S(2)}) collective-permute-start(f32[16,128]{1,0:T(8,128)S(1)} %pad_maximum_fusion), channel_id=1, source_target_pairs={{0,24},{1,25},{2,26},{3,27},{4,28},{5,29},{6,30},{7,31},{8,16},{9,... | collective-permute-start | bytes 24584 | tf_op jit(solution)/shard_map/ppermute | solution.py:327
  7.6 3.2 %collective-permute-start.3 = (f32[24,128]{1,0:T(8,128)S(1)}, f32[24,128]{1,0:T(8,128)S(1)}, u32[]{:S(2)}, u32[]{:S(2)}) collective-permute-start(f32[24,128]{1,0:T(8,128)S(1)} %get-tuple-element.23.refs_0_), channel_id=1, source_target_pairs={{0,9},{1,8},{2,11},{3,10},{4,13},{5,12},{6,15},{7,14},{8,1},{9,0},... | collective-permute-start | bytes 36872 | tf_op jit(solution)/shard_map/ppermute | solution.py:327
  10.8 5.3 %collective-permute-start.6 = (f32[48,128]{1,0:T(8,128)S(1)}, f32[48,128]{1,0:T(8,128)S(1)}, u32[]{:S(2)}, u32[]{:S(2)}) collective-permute-start(f32[48,128]{1,0:T(8,128)S(1)} %constant_dynamic-update-slice_fusion), channel_id=1, source_target_pairs={{0,14},{1,15},{2,12},{3,13},{4,10},{5,11},{6,8},{7,9},{8,6},{9,7},... | collective-permute-start | bytes 73736 | tf_op jit(solution)/shard_map/ppermute | solution.py:327
  14.6 4.2 %collective-permute-start.5 = (f32[48,128]{1,0:T(8,128)S(1)}, f32[48,128]{1,0:T(8,128)S(1)}, u32[]{:S(2)}, u32[]{:S(2)}) collective-permute-start(f32[48,128]{1,0:T(8,128)S(1)} %constant_dynamic-update-slice_fusion), channel_id=1, source_target_pairs={{0,12},{1,13},{2,14},{3,15},{4,8},{5,9},{6,10},{7,11},{8,4},{9,5},... | collective-permute-start | bytes 73736 | tf_op jit(solution)/shard_map/ppermute | solution.py:327
  14.6 4.2 %collective-permute-start.4 = (f32[48,128]{1,0:T(8,128)S(1)}, f32[48,128]{1,0:T(8,128)S(1)}, u32[]{:S(2)}, u32[]{:S(2)}) collective-permute-start(f32[48,128]{1,0:T(8,128)S(1)} %constant_dynamic-update-slice_fusion), channel_id=1, source_target_pairs={{0,10},{1,11},{2,8},{3,9},{4,14},{5,15},{6,12},{7,13},{8,2},{9,3},... | collective-permute-start | bytes 73736 | tf_op jit(solution)/shard_map/ppermute | solution.py:327

commit v7 on v6

--- a/solution.py
+++ b/solution.py
@@ -123,6 +123,12 @@
     return bounds[1:]
 
 
+def choose(condition, first, second):
+    if isinstance(condition, bool):
+        return first if condition else second
+    return jnp.where(condition, first, second)
+
+
 def ring_bounds(slots, index):
     level = slots
     rounds = []
@@ -132,8 +138,8 @@
         following, nodes = [], []
         for place in range(0, len(level), 2):
             own, other = level[place], level[place + 1]
-            left = [jnp.where(upper, b, a) for a, b in zip(own, other)]
-            right = [jnp.where(upper, a, b) for a, b in zip(own, other)]
+            left = [choose(upper, b, a) for a, b in zip(own, other)]
+            right = [choose(upper, a, b) for a, b in zip(own, other)]
             coefs, node = join_coefs(left[:3], right[:3])
             sides, given = join_sides(left[3:], right[3:], node)
             nodes.append((node, given))
@@ -148,8 +154,8 @@
         following = []
         for (node, given), (before, after) in zip(nodes, bounds):
             middle = middle_value(node, given, before, after)
-            following.append((jnp.where(upper, middle, before), jnp.where(upper, after, middle)))
-            following.append((jnp.where(upper, before, middle), jnp.where(upper, middle, after)))
+            following.append((choose(upper, middle, before), choose(upper, after, middle)))
+            following.append((choose(upper, before, middle), choose(upper, middle, after)))
         bounds = following
     return bounds
 
@@ -270,44 +276,44 @@
     sides_ref[...] = block_ref[0:rows, :] * values_t[...].T
 
 
-def x_back_kernel(halves, axis, order, pieces, *refs):
+def x_back_kernel(halves, axis, copies, order, pieces, *refs):
     slots = message_slots(refs[:pieces], SUBLANES, 1, 1, [0] * len(order))
     slots = [slots[order.index(place)] for place in range(len(order))]
-    block_refs, rows_refs, state_refs = (refs[pieces + 2 * pair : pieces + 2 * pair + 2] for pair in range(3))
-    message_ref, given_ref = refs[pieces + 6 : pieces + 8]
-    scratch = refs[pieces + 8 :]
-    bounds = ring_bounds(slots, lax.axis_index(axis))
-    rows = scratch[0].shape[1]
+    block_ref, rows_ref, state_ref, message_ref, given_ref, values_t, sides_ref = refs[pieces:]
+    rows = values_t.shape[1]
     stride = rows // SUBLANES
     total = stride // halves - 1 + len(y_rolls())
-    both = 2 * halves
-    for block in range(2):
-        values_t, sides_ref = scratch[2 * block : 2 * block + 2]
-        x_back(halves, bounds[block], block_refs[block], values_t, sides_ref)
-        start = 0
-        for half in range(halves):
-            place = block * halves + half
-            sides = [(None, strided(sides_ref, index, SUBLANES, stride)) for index in range(half, stride, halves)]
-            nodes = state_parts(state_refs[block], half * total, total, 3)
-            piece, givens = tree_sides(sides, y_rolls(), nodes)
-            if block == 0:
-                for given in givens:
-                    given_ref[start : start + SUBLANES, :] = given
-                    start += SUBLANES
-            for number in range(3):
-                row = number * halves + half
-                message_ref[number * both + place : number * both + place + 1, :] = rows_refs[block][row : row + 1, :]
-            for number, value in enumerate(piece):
-                row = (3 + number) * both + place
-                message_ref[row : row + 1, :] = value[0:1, :]
-
-
-def y_back_kernel(halves, axis, height, traded, pieces, *refs):
-    state_ref, given_ref, out_ref = refs[pieces:]
+    height = QUANTITIES * halves
+
+    def put(row, value):
+        for copy in range(copies):
+            message_ref[copy * height + row : copy * height + row + 1, :] = value
+
+    for row in range(3 * halves):
+        put(row, rows_ref[row : row + 1, :])
+    x_back(halves, ring_bounds(slots, lax.axis_index(axis))[0], block_ref, values_t, sides_ref)
+    start = 0
+    for half in range(halves):
+        sides = [(None, strided(sides_ref, index, SUBLANES, stride)) for index in range(half, stride, halves)]
+        nodes = state_parts(state_ref, half * total, total, 3)
+        piece, givens = tree_sides(sides, y_rolls(), nodes)
+        for given in givens:
+            given_ref[start : start + SUBLANES, :] = given
+            start += SUBLANES
+        for number, value in enumerate(piece):
+            put((3 + number) * halves + half, value[0:1, :])
+
+
+def y_back_kernel(halves, axis, gathered_ref, state_ref, given_ref, out_ref):
     rows = out_ref.shape[0]
     stride = rows // SUBLANES
-    slots = message_slots(refs[:pieces], height, 2 * halves, halves, [halves if odd else 0 for odd in traded])
-    ends = ring_bounds(slots, lax.axis_index(axis))[0]
+    height = QUANTITIES * halves
+    count = gathered_ref.shape[0] // height
+    slots = message_slots([gathered_ref], height, halves, halves, [0] * count)
+    own = lax.axis_index(axis)
+    ends = [jnp.zeros((halves, LANES), jnp.float32)] * 2
+    for place, bounds in enumerate(ring_bounds(slots, 0)):
+        ends = [jnp.where(own == place, bound, end) for bound, end in zip(bounds, ends)]
     total = stride // halves - 1 + len(y_rolls())
     for half in range(halves):
         bounds = [jnp.broadcast_to(end[half : half + 1, :], (SUBLANES, LANES)) for end in ends]
@@ -327,11 +333,8 @@
     return lax.ppermute(value, ("xg", "yd"), pairs)
 
 
-def x_exchange(message, block):
-    other = trade(message, 1, 0)
-    block, other = lax.optimization_barrier((block, other))
-    other_block = trade(block, 1, 0)
-    pieces = [message, other]
+def x_exchange(message):
+    pieces = [message, trade(message, 1, 0)]
     order = [0, 1]
     held = jnp.concatenate(pieces, axis=0)
     for step in doubling(lax.axis_size("xg") // 2):
@@ -340,22 +343,13 @@
         order += [place ^ (2 * step + 1) for place in order]
         if 4 * step < lax.axis_size("xg"):
             held = jnp.concatenate([held, received], axis=0)
-    return pieces, order, other_block
-
-
-def y_exchange(message):
+    return pieces, order
+
+
+def y_exchange(copies):
     count = lax.axis_size("yd")
-    stages = [[1], [2, 4, 6]] if count == 8 else [[step] for step in doubling(count)]
-    pieces = [message]
-    traded = [False]
-    held = message
-    for stage in stages:
-        received = [trade(held, 1, step) for step in stage]
-        pieces += received
-        traded += [not odd for odd in traded] * len(stage)
-        if len(traded) < count:
-            held = jnp.concatenate([held] + received, axis=0)
-    return pieces, traded
+    flat = copies.reshape(count, 1, -1)
+    return lax.all_to_all(flat, "yd", split_axis=0, concat_axis=0, tiled=True).reshape(copies.shape)
 
 
 def f32(*shape):
@@ -409,29 +403,23 @@
         + [square] * 3,
         pltpu.HBM,
     )
-    pieces, order, other_block = x_exchange(message, block)
-    y_rows, y_state = zip(
-        *(
-            kernel_call(
-                functools.partial(y_coefs_kernel, halves),
-                (part,),
-                [held_f32(SUBLANES, LANES), held_f32(3 * y_nodes * SUBLANES, LANES)],
-                [],
-            )
-            for part in (block, other_block)
-        )
-    )
-    height = -(-QUANTITIES * 2 * halves // SUBLANES) * SUBLANES
-    message, givens = kernel_call(
-        functools.partial(x_back_kernel, halves, "xg", order, len(pieces)),
-        (*pieces, block, other_block, *y_rows, *y_state),
-        [f32(height, LANES), held_f32(y_nodes * SUBLANES, LANES)],
-        [square] * 4,
-    )
-    pieces, traded = y_exchange(message)
+    pieces, order = x_exchange(message)
+    y_rows, y_state = kernel_call(
+        functools.partial(y_coefs_kernel, halves),
+        (block,),
+        [held_f32(SUBLANES, LANES), held_f32(3 * y_nodes * SUBLANES, LANES)],
+        [],
+    )
+    count = lax.axis_size("yd")
+    copies, givens = kernel_call(
+        functools.partial(x_back_kernel, halves, "xg", count, order, len(pieces)),
+        (*pieces, block, y_rows, y_state),
+        [f32(count * QUANTITIES * halves, LANES), held_f32(y_nodes * SUBLANES, LANES)],
+        [square] * 2,
+    )
     (updated,) = kernel_call(
-        functools.partial(y_back_kernel, halves, "yd", height, traded, len(pieces)),
-        (*pieces, y_state[0], givens),
+        functools.partial(y_back_kernel, halves, "yd"),
+        (y_exchange(copies), y_state, givens),
         [f32(rows, LANES)],
         [],
     )

time: 19.6 us -> 20.9 us (1.066)
  blocking collectives: 0 us -> 12.8 us
  starting transfers between devices: 9.4 us -> 3.12 us
  waiting for transfers between devices: 7.2 us -> 2.09 us
    all_to_all x0 -> x1, blocking collectives: none -> 12.8 us  [y_exchange(): lax.all_to_all(flat, 'yd', split_axis=0, concat_axis=0, tiled=True)]
    ppermute x7 -> x2, starting transfers between devices: 9.4 us -> 3.12 us  [trade(): return lax.ppermute(value, ('xg', 'yd'), pairs)]
    ppermute x7 -> x2, waiting for transfers between devices: 7.2 us -> 2.09 us  [trade(): return lax.ppermute(value, ('xg', 'yd'), pairs)]
    pallas_call x5 -> x4, Pallas kernels: 2.86 us -> 2.7 us  [kernel_call(): pl.pallas_call(body, out_shape=outputs, in_specs=[pl.BlockSpec(memory_spa...]
  transfers between devices with their start and end apart: 7 -> 2, of which waited for: 5 -> 2; matrix products, arithmetic and copies ran while one was open for 0% -> 0% of each run, Pallas kernels for 1% -> 0%
where the time goes in v7:
time: 20.9 us; the launch traced here: 20.8 us
  blocking collectives  12.8 us (61%)
  starting transfers between devices  3.12 us (15%)
  Pallas kernels  2.7 us (13%)
  waiting for transfers between devices  2.09 us (10%)
    all_to_all x1, blocking collectives, y_exchange(): lax.all_to_all(flat, 'yd', split_axis=0, concat_axis=0, tiled=True)  12.8 us
    ppermute x2, starting transfers between devices, trade(): return lax.ppermute(value, ('xg', 'yd'), pairs)  3.12 us
    pallas_call x4, Pallas kernels, kernel_call(): pl.pallas_call(body, out_shape=outputs, in_specs=[pl.BlockSpec(memory_spa...  2.7 us
    ppermute x2, waiting for transfers between devices, trade(): return lax.ppermute(value, ('xg', 'yd'), pairs)  2.09 us
  transfers between devices with their start and end apart: 2, of which 2 were waited for; matrix products, arithmetic and copies ran while one was open for 0% of the time, Pallas kernels for 0%

profile of v7, /device:TPU:0, one launch (start us, length us, event | category | flops | bytes accessed | tf_op | source)
XLA Modules:
  0.0 20.8 jit_solution(5936672234949244965)
XLA Ops:
  0.0 1.6 %shard_map.73 = (f32[8,128]{1,0:T(8,128)S(1)}, f32[712,128]{1,0:T(8,128)S(1)}) custom-call(f32[128,128]{1,0:T(8,128)} %bitcast.13, f32[128,128]{1,0:T(8,128)} %bitcast.14, f32[128,128]{1,0:T(8,128)} %bitcast.15, f32[128,128]{1,0:T(8,128)} %bitcast.16, f32[512,128]{1,0:T(8,128)} %bitcast.12, f32[1,4]{1,0:T(1,128)} %bitcast.17, f32[1,4]{1,0:T(1,128)} %bitcast.18), custom_call_target="tpu_custom_call" | custom-call | tf_op jit(solution)/shard_map/pallas_call | solution.py:364
  1.6 0.5 %collective-permute-start = (f32[8,128]{1,0:T(8,128)S(1)}, f32[8,128]{1,0:T(8,128)S(1)}, u32[]{:S(2)}, u32[]{:S(2)}) collective-permute-start(f32[8,128]{1,0:T(8,128)S(1)} %get-tuple-element.11.refs_0_), channel_id=1, source_target_pairs={{0,8},{1,9},{2,10},{3,11},{4,12},{5,13},{6,14},{7,15},{8,0},{9,1},... | collective-permute-start | bytes 12296 | tf_op jit(solution)/shard_map/ppermute | solution.py:333
  2.1 0.8 %collective-permute-done.refs_1_ = f32[8,128]{1,0:T(8,128)S(1)} collective-permute-done((f32[8,128]{1,0:T(8,128)S(1)}, f32[8,128]{1,0:T(8,128)S(1)}, u32[]{:S(2)}, u32[]{:S(2)}) %collective-permute-start) | collective-permute-done | bytes 4128 | tf_op jit(solution)/shard_map/ppermute | solution.py:333
  2.9 2.6 %collective-permute-start.1 = (f32[16,128]{1,0:T(8,128)S(1)}, f32[16,128]{1,0:T(8,128)S(1)}, u32[]{:S(2)}, u32[]{:S(2)}) collective-permute-start(f32[16,128]{1,0:T(8,128)S(1)} %pad_maximum_fusion), channel_id=1, source_target_pairs={{0,24},{1,25},{2,26},{3,27},{4,28},{5,29},{6,30},{7,31},{8,16},{9,... | collective-permute-start | bytes 24584 | tf_op jit(solution)/shard_map/ppermute | solution.py:333
  5.5 0.1 shard_map.74
  5.6 1.3 %collective-permute-done.1.refs_2_ = f32[16,128]{1,0:T(8,128)S(1)} collective-permute-done((f32[16,128]{1,0:T(8,128)S(1)}, f32[16,128]{1,0:T(8,128)S(1)}, u32[]{:S(2)}, u32[]{:S(2)}) %collective-permute-start.1) | collective-permute-done | bytes 8224 | tf_op jit(solution)/shard_map/ppermute | solution.py:333
  6.9 0.3 %shard_map.75 = (f32[80,128]{1,0:T(8,128)S(1)}, f32[160,128]{1,0:T(8,128)S(1)}) custom-call(f32[8,128]{1,0:T(8,128)S(1)} %get-tuple-element.11.refs_0_, f32[8,128]{1,0:T(8,128)S(1)} %collective-permute-done.refs_1_, f32[16,128]{1,0:T(8,128)S(1)} %collective-permute-done.1.refs_2_, f32[712,128]{1,0:T(8,128)S(1)} %get-tuple-element.12.block_ref.refs_3_, ...), custom_call_target="tpu_custom_call" | custom-call | tf_op jit(solution)/shard_map/pallas_call | solution.py:364
  7.2 12.8 %all_to_all.5 = f32[8,1,1280]{2,1,0:T(1,128)S(1)} all-to-all(f32[8,1,1280]{2,1,0:T(1,128)S(1)} %bitcast.11), channel_id=1, replica_groups=mesh['xg'=4,'yd'=8] {'yd'}, dimensions={0} | all-to-all | bytes 81920 | tf_op jit(solution)/shard_map/all_to_all | solution.py:352
  20.0 0.7 %shard_map.76 = f32[128,128]{1,0:T(8,128)} custom-call(f32[80,128]{1,0:T(8,128)S(1)} %bitcast.10, f32[480,128]{1,0:T(8,128)S(1)} %get-tuple-element.14.refs_5_.state_ref, f32[160,128]{1,0:T(8,128)S(1)} %get-tuple-element.16.given_ref), custom_call_target="tpu_custom_call" | custom-call | tf_op jit(solution)/shard_map/pallas_call | solution.py:364
  (1 shorter events, 0.0 us)
Async XLA Ops:
  1.6 1.3 %collective-permute-start = (f32[8,128]{1,0:T(8,128)S(1)}, f32[8,128]{1,0:T(8,128)S(1)}, u32[]{:S(2)}, u32[]{:S(2)}) collective-permute-start(f32[8,128]{1,0:T(8,128)S(1)} %get-tuple-element.11.refs_0_), channel_id=1, source_target_pairs={{0,8},{1,9},{2,10},{3,11},{4,12},{5,13},{6,14},{7,15},{8,0},{9,1},... | collective-permute-start | bytes 12296 | tf_op jit(solution)/shard_map/ppermute | solution.py:333
  2.9 4.0 %collective-permute-start.1 = (f32[16,128]{1,0:T(8,128)S(1)}, f32[16,128]{1,0:T(8,128)S(1)}, u32[]{:S(2)}, u32[]{:S(2)}) collective-permute-start(f32[16,128]{1,0:T(8,128)S(1)} %pad_maximum_fusion), channel_id=1, source_target_pairs={{0,24},{1,25},{2,26},{3,27},{4,28},{5,29},{6,30},{7,31},{8,16},{9,... | collective-permute-start | bytes 24584 | tf_op jit(solution)/shard_map/ppermute | solution.py:333

commit v8 on v6

--- a/solution.py
+++ b/solution.py
@@ -121,6 +121,12 @@
             following.append(bounds[index + 1])
         bounds = following
     return bounds[1:]
+
+
+def choose(condition, first, second):
+    if isinstance(condition, bool):
+        return first if condition else second
+    return jnp.where(condition, first, second)
 
 
 def ring_bounds(slots, index):
@@ -270,17 +276,29 @@
     sides_ref[...] = block_ref[0:rows, :] * values_t[...].T
 
 
+def quantity(number):
+    return slice(number * LANES, (number + 1) * LANES)
+
+
+def put_traded(ref, row, rows, number, value):
+    ref[(row + rows // 2) % rows : (row + rows // 2) % rows + value.shape[0], quantity(number)] = value
+
+
 def x_back_kernel(halves, axis, order, pieces, *refs):
     slots = message_slots(refs[:pieces], SUBLANES, 1, 1, [0] * len(order))
     slots = [slots[order.index(place)] for place in range(len(order))]
     block_refs, rows_refs, state_refs = (refs[pieces + 2 * pair : pieces + 2 * pair + 2] for pair in range(3))
-    message_ref, given_ref = refs[pieces + 6 : pieces + 8]
-    scratch = refs[pieces + 8 :]
+    kept_ref, sent_ref, given_ref = refs[pieces + 6 : pieces + 9]
+    scratch = refs[pieces + 9 :]
     bounds = ring_bounds(slots, lax.axis_index(axis))
     rows = scratch[0].shape[1]
     stride = rows // SUBLANES
     total = stride // halves - 1 + len(y_rolls())
-    both = 2 * halves
+
+    def put(row, number, value):
+        kept_ref[row : row + 1, quantity(number)] = value
+        put_traded(sent_ref, row, 2 * halves, number, value)
+
     for block in range(2):
         values_t, sides_ref = scratch[2 * block : 2 * block + 2]
         x_back(halves, bounds[block], block_refs[block], values_t, sides_ref)
@@ -296,21 +314,56 @@
                     start += SUBLANES
             for number in range(3):
                 row = number * halves + half
-                message_ref[number * both + place : number * both + place + 1, :] = rows_refs[block][row : row + 1, :]
+                put(place, number, rows_refs[block][row : row + 1, :])
             for number, value in enumerate(piece):
-                row = (3 + number) * both + place
-                message_ref[row : row + 1, :] = value[0:1, :]
-
-
-def y_back_kernel(halves, axis, height, traded, pieces, *refs):
-    state_ref, given_ref, out_ref = refs[pieces:]
+                put(place, 3 + number, value[0:1, :])
+
+
+def read_message(ref):
+    return [ref[:, quantity(number)] for number in range(QUANTITIES)]
+
+
+def join_by_bit(own, other, upper):
+    left = [choose(upper, b, a) for a, b in zip(own, other)]
+    right = [choose(upper, a, b) for a, b in zip(own, other)]
+    coefs, node = join_coefs(left[:3], right[:3])
+    sides, given = join_sides(left[3:], right[3:], node)
+    return coefs + sides, (node[0], node[1], given)
+
+
+def own_bit(axis, bit):
+    return ((lax.axis_index(axis) >> bit) & 1) == 1
+
+
+def y_join_kernel(axis, bit, own_ref, other_ref, kept_ref, sent_ref, path_ref):
+    joined, path = join_by_bit(read_message(own_ref), read_message(other_ref), own_bit(axis, bit))
+    rows = own_ref.shape[0]
+    for number, value in enumerate(joined):
+        kept_ref[:, quantity(number)] = value
+        for row in (0, rows // 2):
+            put_traded(sent_ref, row, rows, number, value[row : row + rows // 2, :])
+    for number, value in enumerate(path):
+        path_ref[:, quantity(number)] = value
+
+
+def y_back_kernel(halves, axis, rounds, own_ref, other_ref, *refs):
+    path_refs = refs[: rounds - 1]
+    state_ref, given_ref, out_ref = refs[rounds - 1 :]
     rows = out_ref.shape[0]
     stride = rows // SUBLANES
-    slots = message_slots(refs[:pieces], height, 2 * halves, halves, [halves if odd else 0 for odd in traded])
-    ends = ring_bounds(slots, lax.axis_index(axis))[0]
+    joined, path = join_by_bit(read_message(own_ref), read_message(other_ref), own_bit(axis, rounds - 1))
+    _, head, tail, side_head, side_tail = joined
+    before = after = (side_head + side_tail) * inverse(head + tail)
+    paths = [[ref[:, quantity(number)] for number in range(3)] for ref in path_refs] + [path]
+    for bit in reversed(range(rounds)):
+        node = paths[bit]
+        middle = middle_value(node, node[2], before, after)
+        upper = own_bit(axis, bit)
+        before = jnp.where(upper, middle, before)
+        after = jnp.where(upper, after, middle)
     total = stride // halves - 1 + len(y_rolls())
     for half in range(halves):
-        bounds = [jnp.broadcast_to(end[half : half + 1, :], (SUBLANES, LANES)) for end in ends]
+        bounds = [jnp.broadcast_to(end[half : half + 1, :], (SUBLANES, LANES)) for end in (before, after)]
         nodes = state_parts(state_ref, half * total, total, 2)
         givens = [part[0] for part in state_parts(given_ref, half * total, total, 1, 1)]
         values = tree_values(*bounds, y_rolls(), stride // halves, nodes, givens)
@@ -343,19 +396,21 @@
     return pieces, order, other_block
 
 
-def y_exchange(message):
-    count = lax.axis_size("yd")
-    stages = [[1], [2, 4, 6]] if count == 8 else [[step] for step in doubling(count)]
-    pieces = [message]
-    traded = [False]
-    held = message
-    for stage in stages:
-        received = [trade(held, 1, step) for step in stage]
-        pieces += received
-        traded += [not odd for odd in traded] * len(stage)
-        if len(traded) < count:
-            held = jnp.concatenate([held] + received, axis=0)
-    return pieces, traded
+def y_exchange(kept, sent):
+    rows = kept.shape[0]
+    paths = []
+    steps = doubling(lax.axis_size("yd"))
+    for bit, step in enumerate(steps):
+        received = trade(sent, 1, step)
+        if bit < len(steps) - 1:
+            kept, sent, path = kernel_call(
+                functools.partial(y_join_kernel, "yd", bit),
+                (kept, received),
+                [held_f32(*kept.shape), f32(*kept.shape), held_f32(rows, 3 * LANES)],
+                [],
+            )
+            paths.append(path)
+    return [kept, received] + paths, len(steps)
 
 
 def f32(*shape):
@@ -421,16 +476,19 @@
             for part in (block, other_block)
         )
     )
-    height = -(-QUANTITIES * 2 * halves // SUBLANES) * SUBLANES
-    message, givens = kernel_call(
+    kept, sent, givens = kernel_call(
         functools.partial(x_back_kernel, halves, "xg", order, len(pieces)),
         (*pieces, block, other_block, *y_rows, *y_state),
-        [f32(height, LANES), held_f32(y_nodes * SUBLANES, LANES)],
+        [
+            held_f32(2 * halves, QUANTITIES * LANES),
+            f32(2 * halves, QUANTITIES * LANES),
+            held_f32(y_nodes * SUBLANES, LANES),
+        ],
         [square] * 4,
     )
-    pieces, traded = y_exchange(message)
+    pieces, rounds = y_exchange(kept, sent)
     (updated,) = kernel_call(
-        functools.partial(y_back_kernel, halves, "yd", height, traded, len(pieces)),
+        functools.partial(y_back_kernel, halves, "yd", rounds),
         (*pieces, y_state[0], givens),
         [f32(rows, LANES)],
         [],

time: 19.6 us -> 19.1 us (0.974)
  waiting for transfers between devices: 7.2 us -> 6.15 us
  starting transfers between devices: 9.4 us -> 9.89 us
    ppermute x7 -> x6, waiting for transfers between devices: 7.2 us -> 6.15 us  [trade(): return lax.ppermute(value, ('xg', 'yd'), pairs)]
    ppermute x7 -> x6, starting transfers between devices: 9.4 us -> 9.89 us  [trade(): return lax.ppermute(value, ('xg', 'yd'), pairs)]
    pallas_call x5 -> x7, Pallas kernels: 2.86 us -> 2.85 us  [kernel_call(): pl.pallas_call(body, out_shape=outputs, in_specs=[pl.BlockSpec(memory_spa...]
  transfers between devices with their start and end apart: 7 -> 6, of which waited for: 5 -> 5; matrix products, arithmetic and copies ran while one was open for 0% -> 0% of each run, Pallas kernels for 1% -> 1%
where the time goes in v8:
time: 19.1 us; the launch traced here: 18.9 us
  starting transfers between devices  9.89 us (52%)
  waiting for transfers between devices  6.15 us (32%)
  Pallas kernels  2.85 us (15%)
    ppermute x6, starting transfers between devices, trade(): return lax.ppermute(value, ('xg', 'yd'), pairs)  9.89 us
    ppermute x6, waiting for transfers between devices, trade(): return lax.ppermute(value, ('xg', 'yd'), pairs)  6.15 us
    pallas_call x7, Pallas kernels, kernel_call(): pl.pallas_call(body, out_shape=outputs, in_specs=[pl.BlockSpec(memory_spa...  2.85 us
  transfers between devices with their start and end apart: 6, of which 5 were waited for; matrix products, arithmetic and copies ran while one was open for 0% of the time, Pallas kernels for 1%

profile of v8, /device:TPU:0, one launch (start us, length us, event | category | flops | bytes accessed | tf_op | source)
XLA Modules:
  0.0 18.9 jit_solution(18379994047877490724)
XLA Ops:
  0.0 1.6 %shard_map.73 = (f32[8,128]{1,0:T(8,128)S(1)}, f32[712,128]{1,0:T(8,128)S(1)}) custom-call(f32[128,128]{1,0:T(8,128)} %bitcast.9, f32[128,128]{1,0:T(8,128)} %bitcast.10, f32[128,128]{1,0:T(8,128)} %bitcast.11, f32[128,128]{1,0:T(8,128)} %bitcast.12, f32[512,128]{1,0:T(8,128)} %bitcast.8, f32[1,4]{1,0:T(1,128)} %bitcast.13, f32[1,4]{1,0:T(1,128)} %bitcast.14), custom_call_target="tpu_custom_call" | custom-call | tf_op jit(solution)/shard_map/pallas_call | solution.py:425
  1.6 0.5 %collective-permute-start = (f32[8,128]{1,0:T(8,128)S(1)}, f32[8,128]{1,0:T(8,128)S(1)}, u32[]{:S(2)}, u32[]{:S(2)}) collective-permute-start(f32[8,128]{1,0:T(8,128)S(1)} %get-tuple-element.22.refs_0_), channel_id=1, source_target_pairs={{0,8},{1,9},{2,10},{3,11},{4,12},{5,13},{6,14},{7,15},{8,0},{9,1},... | collective-permute-start | bytes 12296 | tf_op jit(solution)/shard_map/ppermute | solution.py:380
  2.1 0.8 %collective-permute-done.refs_1_ = f32[8,128]{1,0:T(8,128)S(1)} collective-permute-done((f32[8,128]{1,0:T(8,128)S(1)}, f32[8,128]{1,0:T(8,128)S(1)}, u32[]{:S(2)}, u32[]{:S(2)}) %collective-permute-start) | collective-permute-done | bytes 4128 | tf_op jit(solution)/shard_map/ppermute | solution.py:380
  2.9 0.3 %collective-permute-start.2 = (f32[712,128]{1,0:T(8,128)S(1)}, f32[712,128]{1,0:T(8,128)S(1)}, u32[]{:S(2)}, u32[]{:S(2)}) collective-permute-start(f32[712,128]{1,0:T(8,128)S(1)} %get-tuple-element.25.block_ref.refs_3_), channel_id=1, source_target_pairs={{0,8},{1,9},{2,10},{3,11},{4,12},{5,13},{6,14},{7,15},{8,0},{9,1},... | collective-permute-start | bytes 1093640 | tf_op jit(solution)/shard_map/ppermute | solution.py:380
  3.3 2.6 %collective-permute-start.1 = (f32[16,128]{1,0:T(8,128)S(1)}, f32[16,128]{1,0:T(8,128)S(1)}, u32[]{:S(2)}, u32[]{:S(2)}) collective-permute-start(f32[16,128]{1,0:T(8,128)S(1)} %pad_maximum_fusion), channel_id=1, source_target_pairs={{0,24},{1,25},{2,26},{3,27},{4,28},{5,29},{6,30},{7,31},{8,16},{9,... | collective-permute-start | bytes 24584 | tf_op jit(solution)/shard_map/ppermute | solution.py:380
  5.9 0.1 shard_map.74
  6.0 0.0 collective-permute-done.2.block_ref.refs_4_
  6.0 0.1 shard_map.75
  6.1 1.2 %collective-permute-done.1.refs_2_ = f32[16,128]{1,0:T(8,128)S(1)} collective-permute-done((f32[16,128]{1,0:T(8,128)S(1)}, f32[16,128]{1,0:T(8,128)S(1)}, u32[]{:S(2)}, u32[]{:S(2)}) %collective-permute-start.1) | collective-permute-done | bytes 8224 | tf_op jit(solution)/shard_map/ppermute | solution.py:380
  7.2 0.4 %shard_map.76 = (f32[4,640]{1,0:T(4,128)S(1)}, f32[4,640]{1,0:T(4,128)S(1)}, f32[160,128]{1,0:T(8,128)S(1)}) custom-call(f32[8,128]{1,0:T(8,128)S(1)} %get-tuple-element.22.refs_0_, f32[8,128]{1,0:T(8,128)S(1)} %collective-permute-done.refs_1_, f32[16,128]{1,0:T(8,128)S(1)} %collective-permute-done.1.refs_2_, ...), custom_call_target="tpu_custom_call" | custom-call | tf_op jit(solution)/shard_map/pallas_call | solution.py:425
  7.6 1.8 %collective-permute-start.3 = (f32[4,640]{1,0:T(4,128)S(1)}, f32[4,640]{1,0:T(4,128)S(1)}, u32[]{:S(2)}, u32[]{:S(2)}) collective-permute-start(f32[4,640]{1,0:T(4,128)S(1)} %get-tuple-element.31), channel_id=1, source_target_pairs={{0,9},{1,8},{2,11},{3,10},{4,13},{5,12},{6,15},{7,14},{8,1},{9,0},... | collective-permute-start | bytes 30728 | tf_op jit(solution)/shard_map/ppermute | solution.py:380
  9.4 1.4 %collective-permute-done.3.other_ref = f32[4,640]{1,0:T(4,128)S(1)} collective-permute-done((f32[4,640]{1,0:T(4,128)S(1)}, f32[4,640]{1,0:T(4,128)S(1)}, u32[]{:S(2)}, u32[]{:S(2)}) %collective-permute-start.3) | collective-permute-done | bytes 10272 | tf_op jit(solution)/shard_map/ppermute | solution.py:380
  10.8 1.8 %collective-permute-start.4 = (f32[4,640]{1,0:T(4,128)S(1)}, f32[4,640]{1,0:T(4,128)S(1)}, u32[]{:S(2)}, u32[]{:S(2)}) collective-permute-start(f32[4,640]{1,0:T(4,128)S(1)} %get-tuple-element.33), channel_id=1, source_target_pairs={{0,10},{1,11},{2,8},{3,9},{4,14},{5,15},{6,12},{7,13},{8,2},{9,3},... | collective-permute-start | bytes 30728 | tf_op jit(solution)/shard_map/ppermute | solution.py:380
  12.6 1.4 %collective-permute-done.4.other_ref = f32[4,640]{1,0:T(4,128)S(1)} collective-permute-done((f32[4,640]{1,0:T(4,128)S(1)}, f32[4,640]{1,0:T(4,128)S(1)}, u32[]{:S(2)}, u32[]{:S(2)}) %collective-permute-start.4) | collective-permute-done | bytes 10272 | tf_op jit(solution)/shard_map/ppermute | solution.py:380
  14.0 2.8 %collective-permute-start.5 = (f32[4,640]{1,0:T(4,128)S(1)}, f32[4,640]{1,0:T(4,128)S(1)}, u32[]{:S(2)}, u32[]{:S(2)}) collective-permute-start(f32[4,640]{1,0:T(4,128)S(1)} %get-tuple-element.35), channel_id=1, source_target_pairs={{0,12},{1,13},{2,14},{3,15},{4,8},{5,9},{6,10},{7,11},{8,4},{9,5},... | collective-permute-start | bytes 30728 | tf_op jit(solution)/shard_map/ppermute | solution.py:380
  16.8 1.4 %collective-permute-done.5.other_ref = f32[4,640]{1,0:T(4,128)S(1)} collective-permute-done((f32[4,640]{1,0:T(4,128)S(1)}, f32[4,640]{1,0:T(4,128)S(1)}, u32[]{:S(2)}, u32[]{:S(2)}) %collective-permute-start.5) | collective-permute-done | bytes 10272 | tf_op jit(solution)/shard_map/ppermute | solution.py:380
  18.2 0.7 %shard_map.79 = f32[128,128]{1,0:T(8,128)} custom-call(f32[4,640]{1,0:T(4,128)S(1)} %get-tuple-element.34.own_ref, f32[4,640]{1,0:T(4,128)S(1)} %collective-permute-done.5.other_ref, f32[4,384]{1,0:T(4,128)S(1)} %get-tuple-element.36.refs_0_, f32[4,384]{1,0:T(4,128)S(1)} %get-tuple-element.37.refs_1_, f32[480,128]{1,0:T(8,128)S(1)} %get-tuple-element.28.refs_7_.refs_2_, ...), custom_call_target="tpu_custom_call" | custom-call | tf_op jit(solution)/shard_map/pallas_call | solution.py:425
  (3 shorter events, 0.0 us)
Async XLA Ops:
  1.6 1.3 %collective-permute-start = (f32[8,128]{1,0:T(8,128)S(1)}, f32[8,128]{1,0:T(8,128)S(1)}, u32[]{:S(2)}, u32[]{:S(2)}) collective-permute-start(f32[8,128]{1,0:T(8,128)S(1)} %get-tuple-element.22.refs_0_), channel_id=1, source_target_pairs={{0,8},{1,9},{2,10},{3,11},{4,12},{5,13},{6,14},{7,15},{8,0},{9,1},... | collective-permute-start | bytes 12296 | tf_op jit(solution)/shard_map/ppermute | solution.py:380
  2.9 3.0 %collective-permute-start.2 = (f32[712,128]{1,0:T(8,128)S(1)}, f32[712,128]{1,0:T(8,128)S(1)}, u32[]{:S(2)}, u32[]{:S(2)}) collective-permute-start(f32[712,128]{1,0:T(8,128)S(1)} %get-tuple-element.25.block_ref.refs_3_), channel_id=1, source_target_pairs={{0,8},{1,9},{2,10},{3,11},{4,12},{5,13},{6,14},{7,15},{8,0},{9,1},... | collective-permute-start | bytes 1093640 | tf_op jit(solution)/shard_map/ppermute | solution.py:380
  3.3 4.0 %collective-permute-start.1 = (f32[16,128]{1,0:T(8,128)S(1)}, f32[16,128]{1,0:T(8,128)S(1)}, u32[]{:S(2)}, u32[]{:S(2)}) collective-permute-start(f32[16,128]{1,0:T(8,128)S(1)} %pad_maximum_fusion), channel_id=1, source_target_pairs={{0,24},{1,25},{2,26},{3,27},{4,28},{5,29},{6,30},{7,31},{8,16},{9,... | collective-permute-start | bytes 24584 | tf_op jit(solution)/shard_map/ppermute | solution.py:380
  7.6 3.2 %collective-permute-start.3 = (f32[4,640]{1,0:T(4,128)S(1)}, f32[4,640]{1,0:T(4,128)S(1)}, u32[]{:S(2)}, u32[]{:S(2)}) collective-permute-start(f32[4,640]{1,0:T(4,128)S(1)} %get-tuple-element.31), channel_id=1, source_target_pairs={{0,9},{1,8},{2,11},{3,10},{4,13},{5,12},{6,15},{7,14},{8,1},{9,0},... | collective-permute-start | bytes 30728 | tf_op jit(solution)/shard_map/ppermute | solution.py:380
  10.8 3.2 %collective-permute-start.4 = (f32[4,640]{1,0:T(4,128)S(1)}, f32[4,640]{1,0:T(4,128)S(1)}, u32[]{:S(2)}, u32[]{:S(2)}) collective-permute-start(f32[4,640]{1,0:T(4,128)S(1)} %get-tuple-element.33), channel_id=1, source_target_pairs={{0,10},{1,11},{2,8},{3,9},{4,14},{5,15},{6,12},{7,13},{8,2},{9,3},... | collective-permute-start | bytes 30728 | tf_op jit(solution)/shard_map/ppermute | solution.py:380
  14.0 4.2 %collective-permute-start.5 = (f32[4,640]{1,0:T(4,128)S(1)}, f32[4,640]{1,0:T(4,128)S(1)}, u32[]{:S(2)}, u32[]{:S(2)}) collective-permute-start(f32[4,640]{1,0:T(4,128)S(1)} %get-tuple-element.35), channel_id=1, source_target_pairs={{0,12},{1,13},{2,14},{3,15},{4,8},{5,9},{6,10},{7,11},{8,4},{9,5},... | collective-permute-start | bytes 30728 | tf_op jit(solution)/shard_map/ppermute | solution.py:380

commit v9 on v8

--- a/solution.py
+++ b/solution.py
@@ -380,20 +380,18 @@
     return lax.ppermute(value, ("xg", "yd"), pairs)
 
 
-def x_exchange(message, block):
-    other = trade(message, 1, 0)
-    block, other = lax.optimization_barrier((block, other))
-    other_block = trade(block, 1, 0)
-    pieces = [message, other]
-    order = [0, 1]
-    held = jnp.concatenate(pieces, axis=0)
+def x_exchange(message):
+    held = message
+    pieces = [message]
+    order = [0]
     for step in doubling(lax.axis_size("xg") // 2):
         received = trade(held, 2 * step + 1, 0)
         pieces.append(received)
         order += [place ^ (2 * step + 1) for place in order]
-        if 4 * step < lax.axis_size("xg"):
-            held = jnp.concatenate([held, received], axis=0)
-    return pieces, order, other_block
+        held = jnp.concatenate([held, received], axis=0)
+    pieces.append(trade(held, 1, 0))
+    order += [place ^ 1 for place in order]
+    return pieces, order
 
 
 def y_exchange(kept, sent):
@@ -464,21 +462,21 @@
         + [square] * 3,
         pltpu.HBM,
     )
-    pieces, order, other_block = x_exchange(message, block)
-    y_rows, y_state = zip(
-        *(
-            kernel_call(
-                functools.partial(y_coefs_kernel, halves),
-                (part,),
-                [held_f32(SUBLANES, LANES), held_f32(3 * y_nodes * SUBLANES, LANES)],
-                [],
-            )
-            for part in (block, other_block)
+    def y_coefs(part):
+        return kernel_call(
+            functools.partial(y_coefs_kernel, halves),
+            (part,),
+            [held_f32(SUBLANES, LANES), held_f32(3 * y_nodes * SUBLANES, LANES)],
+            [],
         )
-    )
+
+    pieces, order = x_exchange(message)
+    y_rows, y_state = y_coefs(block)
+    other_block = trade(block, 1, 0)
+    other_rows, other_state = y_coefs(other_block)
     kept, sent, givens = kernel_call(
         functools.partial(x_back_kernel, halves, "xg", order, len(pieces)),
-        (*pieces, block, other_block, *y_rows, *y_state),
+        (*pieces, block, other_block, y_rows, other_rows, y_state, other_state),
         [
             held_f32(2 * halves, QUANTITIES * LANES),
             f32(2 * halves, QUANTITIES * LANES),
@@ -489,7 +487,7 @@
     pieces, rounds = y_exchange(kept, sent)
     (updated,) = kernel_call(
         functools.partial(y_back_kernel, halves, "yd", rounds),
-        (*pieces, y_state[0], givens),
+        (*pieces, y_state, givens),
         [f32(rows, LANES)],
         [],
     )

time: 19.1 us -> 19 us (level)
  starting transfers between devices: 9.89 us -> 9.62 us
  waiting for transfers between devices: 6.15 us -> 6.39 us
    ppermute x6, starting transfers between devices: 9.89 us -> 9.62 us  [trade(): return lax.ppermute(value, ('xg', 'yd'), pairs)]
    ppermute x6, waiting for transfers between devices: 6.15 us -> 6.39 us  [trade(): return lax.ppermute(value, ('xg', 'yd'), pairs)]
where the time goes in v9:
time: 19 us; the launch traced here: 18.9 us
  starting transfers between devices  9.62 us (51%)
  waiting for transfers between devices  6.39 us (34%)
  Pallas kernels  2.85 us (15%)
    ppermute x6, starting transfers between devices, trade(): return lax.ppermute(value, ('xg', 'yd'), pairs)  9.62 us
    ppermute x6, waiting for transfers between devices, trade(): return lax.ppermute(value, ('xg', 'yd'), pairs)  6.39 us
    pallas_call x7, Pallas kernels, kernel_call(): pl.pallas_call(body, out_shape=outputs, in_specs=[pl.BlockSpec(memory_spa...  2.85 us
  transfers between devices with their start and end apart: 6, of which 5 were waited for; matrix products, arithmetic and copies ran while one was open for 0% of the time, Pallas kernels for 1%

profile of v9, /device:TPU:0, one launch (start us, length us, event | category | flops | bytes accessed | tf_op | source)
XLA Modules:
  0.0 18.9 jit_solution(9818253937413652410)
XLA Ops:
  0.0 1.6 %shard_map.73 = (f32[8,128]{1,0:T(8,128)S(1)}, f32[712,128]{1,0:T(8,128)S(1)}) custom-call(f32[128,128]{1,0:T(8,128)} %bitcast.9, f32[128,128]{1,0:T(8,128)} %bitcast.10, f32[128,128]{1,0:T(8,128)} %bitcast.11, f32[128,128]{1,0:T(8,128)} %bitcast.12, f32[512,128]{1,0:T(8,128)} %bitcast.8, f32[1,4]{1,0:T(1,128)} %bitcast.13, f32[1,4]{1,0:T(1,128)} %bitcast.14), custom_call_target="tpu_custom_call" | custom-call | tf_op jit(solution)/shard_map/pallas_call | solution.py:423
  1.6 0.5 %collective-permute-start.2 = (f32[712,128]{1,0:T(8,128)S(1)}, f32[712,128]{1,0:T(8,128)S(1)}, u32[]{:S(2)}, u32[]{:S(2)}) collective-permute-start(f32[712,128]{1,0:T(8,128)S(1)} %get-tuple-element.21.block_ref.refs_3_), channel_id=1, source_target_pairs={{0,8},{1,9},{2,10},{3,11},{4,12},{5,13},{6,14},{7,15},{8,0},{9,1},... | collective-permute-start | bytes 1093640 | tf_op jit(solution)/shard_map/ppermute | solution.py:380
  2.1 2.6 %collective-permute-start = (f32[8,128]{1,0:T(8,128)S(1)}, f32[8,128]{1,0:T(8,128)S(1)}, u32[]{:S(2)}, u32[]{:S(2)}) collective-permute-start(f32[8,128]{1,0:T(8,128)S(1)} %get-tuple-element.20.refs_0_), channel_id=1, source_target_pairs={{0,24},{1,25},{2,26},{3,27},{4,28},{5,29},{6,30},{7,31},{8,16},{9,... | collective-permute-start | bytes 12296 | tf_op jit(solution)/shard_map/ppermute | solution.py:380
  4.7 1.3 %collective-permute-done.refs_1_ = f32[8,128]{1,0:T(8,128)S(1)} collective-permute-done((f32[8,128]{1,0:T(8,128)S(1)}, f32[8,128]{1,0:T(8,128)S(1)}, u32[]{:S(2)}, u32[]{:S(2)}) %collective-permute-start) | collective-permute-done | bytes 4128 | tf_op jit(solution)/shard_map/ppermute | solution.py:380
  6.1 0.1 collective-permute-start.1
  6.1 0.1 shard_map.74
  6.2 0.0 collective-permute-done.2.block_ref.refs_4_
  6.2 0.1 shard_map.75
  6.3 0.9 %collective-permute-done.1.refs_2_ = f32[16,128]{1,0:T(8,128)S(1)} collective-permute-done((f32[16,128]{1,0:T(8,128)S(1)}, f32[16,128]{1,0:T(8,128)S(1)}, u32[]{:S(2)}, u32[]{:S(2)}) %collective-permute-start.1) | collective-permute-done | bytes 8224 | tf_op jit(solution)/shard_map/ppermute | solution.py:380
  7.2 0.4 %shard_map.76 = (f32[4,640]{1,0:T(4,128)S(1)}, f32[4,640]{1,0:T(4,128)S(1)}, f32[160,128]{1,0:T(8,128)S(1)}) custom-call(f32[8,128]{1,0:T(8,128)S(1)} %get-tuple-element.20.refs_0_, f32[8,128]{1,0:T(8,128)S(1)} %collective-permute-done.refs_1_, f32[16,128]{1,0:T(8,128)S(1)} %collective-permute-done.1.refs_2_, ...), custom_call_target="tpu_custom_call" | custom-call | tf_op jit(solution)/shard_map/pallas_call | solution.py:423
  7.6 1.8 %collective-permute-start.3 = (f32[4,640]{1,0:T(4,128)S(1)}, f32[4,640]{1,0:T(4,128)S(1)}, u32[]{:S(2)}, u32[]{:S(2)}) collective-permute-start(f32[4,640]{1,0:T(4,128)S(1)} %get-tuple-element.27), channel_id=1, source_target_pairs={{0,9},{1,8},{2,11},{3,10},{4,13},{5,12},{6,15},{7,14},{8,1},{9,0},... | collective-permute-start | bytes 30728 | tf_op jit(solution)/shard_map/ppermute | solution.py:380
  9.4 1.4 %collective-permute-done.3.other_ref = f32[4,640]{1,0:T(4,128)S(1)} collective-permute-done((f32[4,640]{1,0:T(4,128)S(1)}, f32[4,640]{1,0:T(4,128)S(1)}, u32[]{:S(2)}, u32[]{:S(2)}) %collective-permute-start.3) | collective-permute-done | bytes 10272 | tf_op jit(solution)/shard_map/ppermute | solution.py:380
  10.8 1.8 %collective-permute-start.4 = (f32[4,640]{1,0:T(4,128)S(1)}, f32[4,640]{1,0:T(4,128)S(1)}, u32[]{:S(2)}, u32[]{:S(2)}) collective-permute-start(f32[4,640]{1,0:T(4,128)S(1)} %get-tuple-element.29), channel_id=1, source_target_pairs={{0,10},{1,11},{2,8},{3,9},{4,14},{5,15},{6,12},{7,13},{8,2},{9,3},... | collective-permute-start | bytes 30728 | tf_op jit(solution)/shard_map/ppermute | solution.py:380
  12.6 1.4 %collective-permute-done.4.other_ref = f32[4,640]{1,0:T(4,128)S(1)} collective-permute-done((f32[4,640]{1,0:T(4,128)S(1)}, f32[4,640]{1,0:T(4,128)S(1)}, u32[]{:S(2)}, u32[]{:S(2)}) %collective-permute-start.4) | collective-permute-done | bytes 10272 | tf_op jit(solution)/shard_map/ppermute | solution.py:380
  14.0 2.8 %collective-permute-start.5 = (f32[4,640]{1,0:T(4,128)S(1)}, f32[4,640]{1,0:T(4,128)S(1)}, u32[]{:S(2)}, u32[]{:S(2)}) collective-permute-start(f32[4,640]{1,0:T(4,128)S(1)} %get-tuple-element.31), channel_id=1, source_target_pairs={{0,12},{1,13},{2,14},{3,15},{4,8},{5,9},{6,10},{7,11},{8,4},{9,5},... | collective-permute-start | bytes 30728 | tf_op jit(solution)/shard_map/ppermute | solution.py:380
  16.8 1.4 %collective-permute-done.5.other_ref = f32[4,640]{1,0:T(4,128)S(1)} collective-permute-done((f32[4,640]{1,0:T(4,128)S(1)}, f32[4,640]{1,0:T(4,128)S(1)}, u32[]{:S(2)}, u32[]{:S(2)}) %collective-permute-start.5) | collective-permute-done | bytes 10272 | tf_op jit(solution)/shard_map/ppermute | solution.py:380
  18.2 0.7 %shard_map.79 = f32[128,128]{1,0:T(8,128)} custom-call(f32[4,640]{1,0:T(4,128)S(1)} %get-tuple-element.30.own_ref, f32[4,640]{1,0:T(4,128)S(1)} %collective-permute-done.5.other_ref, f32[4,384]{1,0:T(4,128)S(1)} %get-tuple-element.32.refs_0_, f32[4,384]{1,0:T(4,128)S(1)} %get-tuple-element.33.refs_1_, f32[480,128]{1,0:T(8,128)S(1)} %get-tuple-element.24.refs_7_.refs_2_, ...), custom_call_target="tpu_custom_call" | custom-call | tf_op jit(solution)/shard_map/pallas_call | solution.py:423
  (3 shorter events, 0.0 us)
Async XLA Ops:
  1.6 4.6 %collective-permute-start.2 = (f32[712,128]{1,0:T(8,128)S(1)}, f32[712,128]{1,0:T(8,128)S(1)}, u32[]{:S(2)}, u32[]{:S(2)}) collective-permute-start(f32[712,128]{1,0:T(8,128)S(1)} %get-tuple-element.21.block_ref.refs_3_), channel_id=1, source_target_pairs={{0,8},{1,9},{2,10},{3,11},{4,12},{5,13},{6,14},{7,15},{8,0},{9,1},... | collective-permute-start | bytes 1093640 | tf_op jit(solution)/shard_map/ppermute | solution.py:380
  2.1 3.9 %collective-permute-start = (f32[8,128]{1,0:T(8,128)S(1)}, f32[8,128]{1,0:T(8,128)S(1)}, u32[]{:S(2)}, u32[]{:S(2)}) collective-permute-start(f32[8,128]{1,0:T(8,128)S(1)} %get-tuple-element.20.refs_0_), channel_id=1, source_target_pairs={{0,24},{1,25},{2,26},{3,27},{4,28},{5,29},{6,30},{7,31},{8,16},{9,... | collective-permute-start | bytes 12296 | tf_op jit(solution)/shard_map/ppermute | solution.py:380
  6.1 1.2 %collective-permute-start.1 = (f32[16,128]{1,0:T(8,128)S(1)}, f32[16,128]{1,0:T(8,128)S(1)}, u32[]{:S(2)}, u32[]{:S(2)}) collective-permute-start(f32[16,128]{1,0:T(8,128)S(1)} %pad_maximum_fusion), channel_id=1, source_target_pairs={{0,8},{1,9},{2,10},{3,11},{4,12},{5,13},{6,14},{7,15},{8,0},{9,1},... | collective-permute-start | bytes 24584 | tf_op jit(solution)/shard_map/ppermute | solution.py:380
  7.6 3.2 %collective-permute-start.3 = (f32[4,640]{1,0:T(4,128)S(1)}, f32[4,640]{1,0:T(4,128)S(1)}, u32[]{:S(2)}, u32[]{:S(2)}) collective-permute-start(f32[4,640]{1,0:T(4,128)S(1)} %get-tuple-element.27), channel_id=1, source_target_pairs={{0,9},{1,8},{2,11},{3,10},{4,13},{5,12},{6,15},{7,14},{8,1},{9,0},... | collective-permute-start | bytes 30728 | tf_op jit(solution)/shard_map/ppermute | solution.py:380
  10.8 3.2 %collective-permute-start.4 = (f32[4,640]{1,0:T(4,128)S(1)}, f32[4,640]{1,0:T(4,128)S(1)}, u32[]{:S(2)}, u32[]{:S(2)}) collective-permute-start(f32[4,640]{1,0:T(4,128)S(1)} %get-tuple-element.29), channel_id=1, source_target_pairs={{0,10},{1,11},{2,8},{3,9},{4,14},{5,15},{6,12},{7,13},{8,2},{9,3},... | collective-permute-start | bytes 30728 | tf_op jit(solution)/shard_map/ppermute | solution.py:380
  14.0 4.2 %collective-permute-start.5 = (f32[4,640]{1,0:T(4,128)S(1)}, f32[4,640]{1,0:T(4,128)S(1)}, u32[]{:S(2)}, u32[]{:S(2)}) collective-permute-start(f32[4,640]{1,0:T(4,128)S(1)} %get-tuple-element.31), channel_id=1, source_target_pairs={{0,12},{1,13},{2,14},{3,15},{4,8},{5,9},{6,10},{7,11},{8,4},{9,5},... | collective-permute-start | bytes 30728 | tf_op jit(solution)/shard_map/ppermute | solution.py:380

commit v10 on v9

--- a/solution.py
+++ b/solution.py
@@ -183,15 +183,16 @@
     mobile_ref, faces_ref, capacity_ref, immobile_ref, rates_ref, shares_ref, arrived,
     faces_t, storage_t, source_t,
 ):
-    pairs = (
-        (rates_hbm, rates_ref), (shares_hbm, shares_ref), (capacity_hbm, capacity_ref),
-        (faces_hbm, faces_ref), (immobile_hbm, immobile_ref), (mobile_hbm, mobile_ref),
-        (across_hbm, block_ref.at[mobile_ref.shape[0] : 2 * mobile_ref.shape[0], :]),
-    )
+    rows = mobile_ref.shape[0]
+    zones = [slice(start, start + rows) for start in range(0, immobile_ref.shape[0], rows)]
+    pairs = [
+        (rates_hbm, rates_ref), (shares_hbm, shares_ref), (capacity_hbm, capacity_ref), (faces_hbm, faces_ref),
+        *((immobile_hbm.at[zone, :], immobile_ref.at[zone, :]) for zone in zones),
+        (mobile_hbm, mobile_ref), (across_hbm, block_ref.at[rows : 2 * rows, :]),
+    ]
     copies = [pltpu.make_async_copy(pair[0], pair[1], arrived.at[place]) for place, pair in enumerate(pairs)]
     for copy in copies:
         copy.start()
-    rows = mobile_ref.shape[0]
     stride = LANES // SUBLANES
     for copy in copies[:3]:
         copy.wait()
@@ -202,11 +203,11 @@
     storage_t[...] = storage.T
     copies[3].wait()
     faces_t[...] = faces_ref[...].T
-    copies[4].wait()
-    total = weights[0] * immobile_ref[0:rows, :]
-    for zone in range(1, len(weights)):
-        total = total + weights[zone] * immobile_ref[zone * rows : (zone + 1) * rows, :]
-    copies[5].wait()
+    total = None
+    for copy, weight, zone in zip(copies[4:], weights, zones):
+        copy.wait()
+        total = plus(total, weight * immobile_ref[zone, :])
+    copies[-2].wait()
     source_t[...] = (mobile_ref[...] + capacity * total).T
     coefs, sides = [], []
     for index in range(stride):
@@ -222,7 +223,7 @@
             start += SUBLANES
     for row, value in enumerate(piece + side):
         message_ref[row : row + 1, :] = value[0:1, :]
-    copies[6].wait()
+    copies[-1].wait()
 
 
 def y_coefs_kernel(halves, block_ref, rows_ref, state_ref):
@@ -380,6 +381,19 @@
     return lax.ppermute(value, ("xg", "yd"), pairs)
 
 
+def pack_kernel(first_ref, second_ref, out_ref):
+    height = first_ref.shape[0]
+    out_ref[0:height, :] = first_ref[...]
+    out_ref[height:, :] = second_ref[...]
+
+
+def pack(first, second):
+    (packed,) = kernel_call(
+        pack_kernel, (first, second), [f32(first.shape[0] + second.shape[0], first.shape[1])], [], cost=10000000000
+    )
+    return packed
+
+
 def x_exchange(message):
     held = message
     pieces = [message]
@@ -388,7 +402,7 @@
         received = trade(held, 2 * step + 1, 0)
         pieces.append(received)
         order += [place ^ (2 * step + 1) for place in order]
-        held = jnp.concatenate([held, received], axis=0)
+        held = pack(held, received)
     pieces.append(trade(held, 1, 0))
     order += [place ^ 1 for place in order]
     return pieces, order
@@ -419,13 +433,14 @@
     return VMEM(shape, jnp.float32)
 
 
-def kernel_call(body, operands, outputs, scratch, space=VMEM):
+def kernel_call(body, operands, outputs, scratch, space=VMEM, cost=500000):
     return pl.pallas_call(
         body,
         out_shape=outputs,
         in_specs=[pl.BlockSpec(memory_space=space)] * len(operands),
         out_specs=[pl.BlockSpec(memory_space=VMEM)] * len(outputs),
         scratch_shapes=scratch,
+        cost_estimate=pl.CostEstimate(flops=cost, bytes_accessed=cost, transcendentals=0),
         compiler_params=pltpu.CompilerParams(vmem_limit_bytes=16 * 1024 * 1024),
     )(*operands)
 
@@ -458,7 +473,7 @@
         [square] * 3
         + [VMEM((zones * rows, LANES), jnp.float32)]
         + [VMEM((1, zones), jnp.float32)] * 2
-        + [pltpu.SemaphoreType.DMA((7,))]
+        + [pltpu.SemaphoreType.DMA((6 + zones,))]
         + [square] * 3,
         pltpu.HBM,
     )

time: 19 us -> 18.9 us (level)
  waiting for transfers between devices: 6.39 us -> 5.44 us
  starting transfers between devices: 9.62 us -> 10.2 us
  Pallas kernels: 2.85 us -> 3.08 us
    ppermute x6, waiting for transfers between devices: 6.39 us -> 5.44 us  [trade(): return lax.ppermute(value, ('xg', 'yd'), pairs)]
    ppermute x6, starting transfers between devices: 9.62 us -> 10.2 us  [trade(): return lax.ppermute(value, ('xg', 'yd'), pairs)]
    pallas_call x7 -> x8, Pallas kernels: 2.85 us -> 3.08 us  [kernel_call(): pl.pallas_call(body, out_shape=outputs, in_specs=[pl.BlockSpec(memory_spa...]
where the time goes in v10:
time: 18.9 us; the launch traced here: 18.8 us
  starting transfers between devices  10.2 us (54%)
  waiting for transfers between devices  5.44 us (29%)
  Pallas kernels  3.08 us (16%)
    ppermute x6, starting transfers between devices, trade(): return lax.ppermute(value, ('xg', 'yd'), pairs)  10.2 us
    ppermute x6, waiting for transfers between devices, trade(): return lax.ppermute(value, ('xg', 'yd'), pairs)  5.44 us
    pallas_call x8, Pallas kernels, kernel_call(): pl.pallas_call(body, out_shape=outputs, in_specs=[pl.BlockSpec(memory_spa...  3.08 us
  transfers between devices with their start and end apart: 6, of which 5 were waited for; matrix products, arithmetic and copies ran while one was open for 0% of the time, Pallas kernels for 1%

profile of v10, /device:TPU:0, one launch (start us, length us, event | category | flops | bytes accessed | tf_op | source)
XLA Modules:
  0.0 18.8 jit_solution(13700039677688932633)
XLA Ops:
  0.0 1.8 %shard_map.73 = (f32[8,128]{1,0:T(8,128)S(1)}, f32[712,128]{1,0:T(8,128)S(1)}) custom-call(f32[128,128]{1,0:T(8,128)} %bitcast.9, f32[128,128]{1,0:T(8,128)} %bitcast.10, f32[128,128]{1,0:T(8,128)} %bitcast.11, f32[128,128]{1,0:T(8,128)} %bitcast.12, f32[512,128]{1,0:T(8,128)} %bitcast.8, f32[1,4]{1,0:T(1,128)} %bitcast.13, f32[1,4]{1,0:T(1,128)} %bitcast.14), custom_call_target="tpu_custom_call" | custom-call | flops 500000 | bytes 500000 | tf_op jit(solution)/shard_map/pallas_call | solution.py:437
  1.8 2.4 %collective-permute-start = (f32[8,128]{1,0:T(8,128)S(1)}, f32[8,128]{1,0:T(8,128)S(1)}, u32[]{:S(2)}, u32[]{:S(2)}) collective-permute-start(f32[8,128]{1,0:T(8,128)S(1)} %get-tuple-element.20.first_ref.refs_0_), channel_id=1, source_target_pairs={{0,24},{1,25},{2,26},{3,27},{4,28},{5,29},{6,30},{7,31},{8,16},{9,... | collective-permute-start | bytes 12296 | tf_op jit(solution)/shard_map/ppermute | solution.py:381
  4.3 0.7 %collective-permute-start.2 = (f32[712,128]{1,0:T(8,128)S(1)}, f32[712,128]{1,0:T(8,128)S(1)}, u32[]{:S(2)}, u32[]{:S(2)}) collective-permute-start(f32[712,128]{1,0:T(8,128)S(1)} %get-tuple-element.21.block_ref.refs_3_), channel_id=1, source_target_pairs={{0,8},{1,9},{2,10},{3,11},{4,12},{5,13},{6,14},{7,15},{8,0},{9,1},... | collective-permute-start | bytes 1093640 | tf_op jit(solution)/shard_map/ppermute | solution.py:381
  4.9 0.7 %collective-permute-done.second_ref.refs_1_ = f32[8,128]{1,0:T(8,128)S(1)} collective-permute-done((f32[8,128]{1,0:T(8,128)S(1)}, f32[8,128]{1,0:T(8,128)S(1)}, u32[]{:S(2)}, u32[]{:S(2)}) %collective-permute-start) | collective-permute-done | bytes 4128 | tf_op jit(solution)/shard_map/ppermute | solution.py:381
  5.6 0.6 %collective-permute-start.1 = (f32[16,128]{1,0:T(8,128)S(1)}, f32[16,128]{1,0:T(8,128)S(1)}, u32[]{:S(2)}, u32[]{:S(2)}) collective-permute-start(f32[16,128]{1,0:T(8,128)S(1)} %shard_map.74), channel_id=1, source_target_pairs={{0,8},{1,9},{2,10},{3,11},{4,12},{5,13},{6,14},{7,15},{8,0},{9,1},... | collective-permute-start | bytes 24584 | tf_op jit(solution)/shard_map/ppermute | solution.py:381
  6.2 0.1 shard_map.75
  6.3 0.0 collective-permute-done.2.block_ref.refs_4_
  6.3 0.1 shard_map.76
  6.4 0.6 %collective-permute-done.1.refs_2_ = f32[16,128]{1,0:T(8,128)S(1)} collective-permute-done((f32[16,128]{1,0:T(8,128)S(1)}, f32[16,128]{1,0:T(8,128)S(1)}, u32[]{:S(2)}, u32[]{:S(2)}) %collective-permute-start.1) | collective-permute-done | bytes 8224 | tf_op jit(solution)/shard_map/ppermute | solution.py:381
  7.1 0.3 %shard_map.77 = (f32[4,640]{1,0:T(4,128)S(1)}, f32[4,640]{1,0:T(4,128)S(1)}, f32[160,128]{1,0:T(8,128)S(1)}) custom-call(f32[8,128]{1,0:T(8,128)S(1)} %get-tuple-element.20.first_ref.refs_0_, f32[8,128]{1,0:T(8,128)S(1)} %collective-permute-done.second_ref.refs_1_, f32[16,128]{1,0:T(8,128)S(1)} %collective-permute-done.1.refs_2_, ...), custom_call_target="tpu_custom_call" | custom-call | flops 500000 | bytes 500000 | tf_op jit(solution)/shard_map/pallas_call | solution.py:437
  7.4 1.8 %collective-permute-start.3 = (f32[4,640]{1,0:T(4,128)S(1)}, f32[4,640]{1,0:T(4,128)S(1)}, u32[]{:S(2)}, u32[]{:S(2)}) collective-permute-start(f32[4,640]{1,0:T(4,128)S(1)} %get-tuple-element.27), channel_id=1, source_target_pairs={{0,9},{1,8},{2,11},{3,10},{4,13},{5,12},{6,15},{7,14},{8,1},{9,0},... | collective-permute-start | bytes 30728 | tf_op jit(solution)/shard_map/ppermute | solution.py:381
  9.3 1.4 %collective-permute-done.3.other_ref = f32[4,640]{1,0:T(4,128)S(1)} collective-permute-done((f32[4,640]{1,0:T(4,128)S(1)}, f32[4,640]{1,0:T(4,128)S(1)}, u32[]{:S(2)}, u32[]{:S(2)}) %collective-permute-start.3) | collective-permute-done | bytes 10272 | tf_op jit(solution)/shard_map/ppermute | solution.py:381
  10.7 1.8 %collective-permute-start.4 = (f32[4,640]{1,0:T(4,128)S(1)}, f32[4,640]{1,0:T(4,128)S(1)}, u32[]{:S(2)}, u32[]{:S(2)}) collective-permute-start(f32[4,640]{1,0:T(4,128)S(1)} %get-tuple-element.29), channel_id=1, source_target_pairs={{0,10},{1,11},{2,8},{3,9},{4,14},{5,15},{6,12},{7,13},{8,2},{9,3},... | collective-permute-start | bytes 30728 | tf_op jit(solution)/shard_map/ppermute | solution.py:381
  12.5 1.4 %collective-permute-done.4.other_ref = f32[4,640]{1,0:T(4,128)S(1)} collective-permute-done((f32[4,640]{1,0:T(4,128)S(1)}, f32[4,640]{1,0:T(4,128)S(1)}, u32[]{:S(2)}, u32[]{:S(2)}) %collective-permute-start.4) | collective-permute-done | bytes 10272 | tf_op jit(solution)/shard_map/ppermute | solution.py:381
  13.9 2.8 %collective-permute-start.5 = (f32[4,640]{1,0:T(4,128)S(1)}, f32[4,640]{1,0:T(4,128)S(1)}, u32[]{:S(2)}, u32[]{:S(2)}) collective-permute-start(f32[4,640]{1,0:T(4,128)S(1)} %get-tuple-element.31), channel_id=1, source_target_pairs={{0,12},{1,13},{2,14},{3,15},{4,8},{5,9},{6,10},{7,11},{8,4},{9,5},... | collective-permute-start | bytes 30728 | tf_op jit(solution)/shard_map/ppermute | solution.py:381
  16.7 1.4 %collective-permute-done.5.other_ref = f32[4,640]{1,0:T(4,128)S(1)} collective-permute-done((f32[4,640]{1,0:T(4,128)S(1)}, f32[4,640]{1,0:T(4,128)S(1)}, u32[]{:S(2)}, u32[]{:S(2)}) %collective-permute-start.5) | collective-permute-done | bytes 10272 | tf_op jit(solution)/shard_map/ppermute | solution.py:381
  18.1 0.7 %shard_map.80 = f32[128,128]{1,0:T(8,128)} custom-call(f32[4,640]{1,0:T(4,128)S(1)} %get-tuple-element.30.own_ref, f32[4,640]{1,0:T(4,128)S(1)} %collective-permute-done.5.other_ref, f32[4,384]{1,0:T(4,128)S(1)} %get-tuple-element.32.refs_0_, f32[4,384]{1,0:T(4,128)S(1)} %get-tuple-element.33.refs_1_, f32[480,128]{1,0:T(8,128)S(1)} %get-tuple-element.24.refs_7_.refs_2_, ...), custom_call_target="tpu_custom_call" | custom-call | flops 500000 | bytes 500000 | tf_op jit(solution)/shard_map/pallas_call | solution.py:437
  (3 shorter events, 0.0 us)
Async XLA Ops:
  1.8 3.8 %collective-permute-start = (f32[8,128]{1,0:T(8,128)S(1)}, f32[8,128]{1,0:T(8,128)S(1)}, u32[]{:S(2)}, u32[]{:S(2)}) collective-permute-start(f32[8,128]{1,0:T(8,128)S(1)} %get-tuple-element.20.first_ref.refs_0_), channel_id=1, source_target_pairs={{0,24},{1,25},{2,26},{3,27},{4,28},{5,29},{6,30},{7,31},{8,16},{9,... | collective-permute-start | bytes 12296 | tf_op jit(solution)/shard_map/ppermute | solution.py:381
  4.3 2.1 %collective-permute-start.2 = (f32[712,128]{1,0:T(8,128)S(1)}, f32[712,128]{1,0:T(8,128)S(1)}, u32[]{:S(2)}, u32[]{:S(2)}) collective-permute-start(f32[712,128]{1,0:T(8,128)S(1)} %get-tuple-element.21.block_ref.refs_3_), channel_id=1, source_target_pairs={{0,8},{1,9},{2,10},{3,11},{4,12},{5,13},{6,14},{7,15},{8,0},{9,1},... | collective-permute-start | bytes 1093640 | tf_op jit(solution)/shard_map/ppermute | solution.py:381
  5.6 1.5 %collective-permute-start.1 = (f32[16,128]{1,0:T(8,128)S(1)}, f32[16,128]{1,0:T(8,128)S(1)}, u32[]{:S(2)}, u32[]{:S(2)}) collective-permute-start(f32[16,128]{1,0:T(8,128)S(1)} %shard_map.74), channel_id=1, source_target_pairs={{0,8},{1,9},{2,10},{3,11},{4,12},{5,13},{6,14},{7,15},{8,0},{9,1},... | collective-permute-start | bytes 24584 | tf_op jit(solution)/shard_map/ppermute | solution.py:381
  7.4 3.2 %collective-permute-start.3 = (f32[4,640]{1,0:T(4,128)S(1)}, f32[4,640]{1,0:T(4,128)S(1)}, u32[]{:S(2)}, u32[]{:S(2)}) collective-permute-start(f32[4,640]{1,0:T(4,128)S(1)} %get-tuple-element.27), channel_id=1, source_target_pairs={{0,9},{1,8},{2,11},{3,10},{4,13},{5,12},{6,15},{7,14},{8,1},{9,0},... | collective-permute-start | bytes 30728 | tf_op jit(solution)/shard_map/ppermute | solution.py:381
  10.7 3.2 %collective-permute-start.4 = (f32[4,640]{1,0:T(4,128)S(1)}, f32[4,640]{1,0:T(4,128)S(1)}, u32[]{:S(2)}, u32[]{:S(2)}) collective-permute-start(f32[4,640]{1,0:T(4,128)S(1)} %get-tuple-element.29), channel_id=1, source_target_pairs={{0,10},{1,11},{2,8},{3,9},{4,14},{5,15},{6,12},{7,13},{8,2},{9,3},... | collective-permute-start | bytes 30728 | tf_op jit(solution)/shard_map/ppermute | solution.py:381
  13.9 4.2 %collective-permute-start.5 = (f32[4,640]{1,0:T(4,128)S(1)}, f32[4,640]{1,0:T(4,128)S(1)}, u32[]{:S(2)}, u32[]{:S(2)}) collective-permute-start(f32[4,640]{1,0:T(4,128)S(1)} %get-tuple-element.31), channel_id=1, source_target_pairs={{0,12},{1,13},{2,14},{3,15},{4,8},{5,9},{6,10},{7,11},{8,4},{9,5},... | collective-permute-start | bytes 30728 | tf_op jit(solution)/shard_map/ppermute | solution.py:381

commit v11 on v10

--- a/solution.py
+++ b/solution.py
@@ -184,30 +184,30 @@
     faces_t, storage_t, source_t,
 ):
     rows = mobile_ref.shape[0]
-    zones = [slice(start, start + rows) for start in range(0, immobile_ref.shape[0], rows)]
-    pairs = [
-        (rates_hbm, rates_ref), (shares_hbm, shares_ref), (capacity_hbm, capacity_ref), (faces_hbm, faces_ref),
-        *((immobile_hbm.at[zone, :], immobile_ref.at[zone, :]) for zone in zones),
-        (mobile_hbm, mobile_ref), (across_hbm, block_ref.at[rows : 2 * rows, :]),
-    ]
+    pairs = (
+        (immobile_hbm, immobile_ref), (capacity_hbm, capacity_ref), (mobile_hbm, mobile_ref), (faces_hbm, faces_ref),
+        (rates_hbm, rates_ref), (shares_hbm, shares_ref), (across_hbm, block_ref.at[rows : 2 * rows, :]),
+    )
     copies = [pltpu.make_async_copy(pair[0], pair[1], arrived.at[place]) for place, pair in enumerate(pairs)]
     for copy in copies:
         copy.start()
+    immobile_copy, capacity_copy, mobile_copy, faces_copy, rates_copy, shares_copy, across_copy = copies
     stride = LANES // SUBLANES
-    for copy in copies[:3]:
-        copy.wait()
+    faces_copy.wait()
+    faces_t[...] = faces_ref[...].T
+    rates_copy.wait()
+    shares_copy.wait()
+    capacity_copy.wait()
     weights = capacity_weights(rates_ref[...], shares_ref[...])
     capacity = capacity_ref[...]
     storage = 1.0 + capacity * sum(weights[1:], weights[0])
     block_ref[0:rows, :] = storage
     storage_t[...] = storage.T
-    copies[3].wait()
-    faces_t[...] = faces_ref[...].T
+    immobile_copy.wait()
     total = None
-    for copy, weight, zone in zip(copies[4:], weights, zones):
-        copy.wait()
-        total = plus(total, weight * immobile_ref[zone, :])
-    copies[-2].wait()
+    for zone, weight in enumerate(weights):
+        total = plus(total, weight * immobile_ref[zone * rows : (zone + 1) * rows, :])
+    mobile_copy.wait()
     source_t[...] = (mobile_ref[...] + capacity * total).T
     coefs, sides = [], []
     for index in range(stride):
@@ -223,19 +223,32 @@
             start += SUBLANES
     for row, value in enumerate(piece + side):
         message_ref[row : row + 1, :] = value[0:1, :]
-    copies[-1].wait()
-
-
-def y_coefs_kernel(halves, block_ref, rows_ref, state_ref):
+    across_copy.wait()
+
+
+def ends_responses(shape):
+    one, nothing = jnp.ones(shape, jnp.float32), jnp.zeros(shape, jnp.float32)
+    return ((one, nothing), (nothing, one))
+
+
+def prepare_kernel(halves, block_ref, rows_ref, lines_ref, sums_ref, state_ref, spread_ref):
     rows = rows_ref.shape[1]
+    stride = LANES // SUBLANES
+    rolls = x_rolls(halves)
+    total = stride - 1 + len(rolls)
+    nodes = state_parts(block_ref.at[2 * rows :, :], 0, total, 3)
+    nothing = jnp.zeros((SUBLANES, rows), jnp.float32)
+    cases = [((nothing, nothing), [node[2] for node in nodes])]
+    cases += [(ends, [0.0] * total) for ends in ends_responses((SUBLANES, rows))]
+    for case, (ends, givens) in enumerate(cases):
+        for index, value in enumerate(tree_values(*ends, rolls, stride, nodes, givens)):
+            lines_ref[pl.ds(case * LANES + index, SUBLANES, stride=stride), :] = value
     stride = rows // SUBLANES
     start = 0
     for half in range(halves):
-        coefs = []
-        for index in range(half, stride, halves):
-            storage = strided(block_ref, index, SUBLANES, stride)
-            coefs.append((strided(block_ref, rows + index, SUBLANES, stride), None, storage))
-        piece, nodes = tree_coefs(coefs, y_rolls())
+        storage = [strided(block_ref, index, SUBLANES, stride) for index in range(half, stride, halves)]
+        faces = [strided(block_ref, rows + index, SUBLANES, stride) for index in range(half, stride, halves)]
+        piece, nodes = tree_coefs([(face, None, held) for face, held in zip(faces, storage)], y_rolls())
         for node in nodes:
             for part in node:
                 state_ref[start : start + SUBLANES, :] = part
@@ -243,6 +256,12 @@
         for number, value in enumerate(piece):
             row = number * halves + half
             rows_ref[row : row + 1, :] = value[0:1, :]
+        for case, ends in enumerate(ends_responses((SUBLANES, LANES))):
+            values = tree_values(*ends, y_rolls(), len(storage), nodes, [0.0] * len(nodes))
+            for index, (value, held) in enumerate(zip(values, storage)):
+                place = pl.ds(case * rows + index * halves + half, SUBLANES, stride=stride)
+                spread_ref[place, :] = value
+                sums_ref[place, :] = value * held
 
 
 def state_parts(ref, first, total, parts, pitch=3):
@@ -264,60 +283,67 @@
     return slots
 
 
-def x_back(halves, bounds, block_ref, values_t, sides_ref):
-    rows = values_t.shape[1]
-    before, after = (jnp.broadcast_to(bound, (SUBLANES, rows)) for bound in bounds)
-    rolls = x_rolls(halves)
-    stride = LANES // SUBLANES
-    total = stride - 1 + len(rolls)
-    parts = state_parts(block_ref.at[2 * rows :, :], 0, total, 3)
-    values = tree_values(before, after, rolls, stride, parts, [part[2] for part in parts])
-    for index, value in enumerate(values):
-        values_t[pl.ds(index, SUBLANES, stride=stride), :] = value
-    sides_ref[...] = block_ref[0:rows, :] * values_t[...].T
-
-
 def quantity(number):
     return slice(number * LANES, (number + 1) * LANES)
 
 
 def put_traded(ref, row, rows, number, value):
     ref[(row + rows // 2) % rows : (row + rows // 2) % rows + value.shape[0], quantity(number)] = value
+
+
+def along_line(bound, halves, rows):
+    value = jnp.broadcast_to(bound, (SUBLANES, rows))
+    lane = lax.broadcasted_iota(jnp.int32, value.shape, 1)
+    for step in doubling(halves):
+        value = jnp.where((lane & step) != 0, behind(value, step, 1), value)
+    return value[0:1, :]
 
 
 def x_back_kernel(halves, axis, order, pieces, *refs):
     slots = message_slots(refs[:pieces], SUBLANES, 1, 1, [0] * len(order))
     slots = [slots[order.index(place)] for place in range(len(order))]
-    block_refs, rows_refs, state_refs = (refs[pieces + 2 * pair : pieces + 2 * pair + 2] for pair in range(3))
-    kept_ref, sent_ref, given_ref = refs[pieces + 6 : pieces + 9]
-    scratch = refs[pieces + 9 :]
+    lines_refs, sums_refs, rows_refs = (refs[pieces + 2 * pair : pieces + 2 * pair + 2] for pair in range(3))
+    kept_ref, sent_ref, values_ref = refs[pieces + 6 :]
     bounds = ring_bounds(slots, lax.axis_index(axis))
-    rows = scratch[0].shape[1]
-    stride = rows // SUBLANES
-    total = stride // halves - 1 + len(y_rolls())
+    rows = values_ref.shape[0]
 
     def put(row, number, value):
         kept_ref[row : row + 1, quantity(number)] = value
         put_traded(sent_ref, row, 2 * halves, number, value)
 
     for block in range(2):
-        values_t, sides_ref = scratch[2 * block : 2 * block + 2]
-        x_back(halves, bounds[block], block_refs[block], values_t, sides_ref)
-        start = 0
         for half in range(halves):
-            place = block * halves + half
-            sides = [(None, strided(sides_ref, index, SUBLANES, stride)) for index in range(half, stride, halves)]
-            nodes = state_parts(state_refs[block], half * total, total, 3)
-            piece, givens = tree_sides(sides, y_rolls(), nodes)
-            if block == 0:
-                for given in givens:
-                    given_ref[start : start + SUBLANES, :] = given
-                    start += SUBLANES
             for number in range(3):
                 row = number * halves + half
-                put(place, number, rows_refs[block][row : row + 1, :])
-            for number, value in enumerate(piece):
-                put(place, 3 + number, value[0:1, :])
+                put(block * halves + half, number, rows_refs[block][row : row + 1, :])
+    for block in range(2):
+        lines_ref, sums_ref = lines_refs[block], sums_refs[block]
+        before, after = (along_line(bound, halves, rows) for bound in bounds[block])
+        values = lines_ref[0:LANES, :] + lines_ref[LANES : 2 * LANES, :] * before + lines_ref[2 * LANES :, :] * after
+        values = values.T
+        if block == 0:
+            values_ref[...] = values
+        for end in range(2):
+            parts = (values * sums_ref[end * rows : (end + 1) * rows, :]).reshape(-1, SUBLANES, LANES)
+            side = jnp.sum(parts, axis=0)
+            for step in doubling(SUBLANES // halves):
+                side = side + behind(side, step * halves, 0)
+            for half in range(halves):
+                put(block * halves + half, 3 + end, side[half : half + 1, :])
+
+
+def y_given_kernel(halves, block_ref, values_ref, state_ref, given_ref):
+    rows = values_ref.shape[0]
+    stride = rows // SUBLANES
+    total = stride // halves - 1 + len(y_rolls())
+    nothing = jnp.zeros((SUBLANES, LANES), jnp.float32)
+    for half in range(halves):
+        places = [pl.ds(index, SUBLANES, stride=stride) for index in range(half, stride, halves)]
+        sides = [(None, block_ref[place, :] * values_ref[place, :]) for place in places]
+        nodes = state_parts(state_ref, half * total, total, 3)
+        _, givens = tree_sides(sides, y_rolls(), nodes)
+        for place, value in zip(places, tree_values(nothing, nothing, y_rolls(), len(places), nodes, givens)):
+            given_ref[place, :] = value
 
 
 def read_message(ref):
@@ -349,9 +375,8 @@
 
 def y_back_kernel(halves, axis, rounds, own_ref, other_ref, *refs):
     path_refs = refs[: rounds - 1]
-    state_ref, given_ref, out_ref = refs[rounds - 1 :]
+    given_ref, spread_ref, out_ref = refs[rounds - 1 :]
     rows = out_ref.shape[0]
-    stride = rows // SUBLANES
     joined, path = join_by_bit(read_message(own_ref), read_message(other_ref), own_bit(axis, rounds - 1))
     _, head, tail, side_head, side_tail = joined
     before = after = (side_head + side_tail) * inverse(head + tail)
@@ -362,14 +387,17 @@
         upper = own_bit(axis, bit)
         before = jnp.where(upper, middle, before)
         after = jnp.where(upper, after, middle)
-    total = stride // halves - 1 + len(y_rolls())
-    for half in range(halves):
-        bounds = [jnp.broadcast_to(end[half : half + 1, :], (SUBLANES, LANES)) for end in (before, after)]
-        nodes = state_parts(state_ref, half * total, total, 2)
-        givens = [part[0] for part in state_parts(given_ref, half * total, total, 1, 1)]
-        values = tree_values(*bounds, y_rolls(), stride // halves, nodes, givens)
-        for index, value in enumerate(values):
-            out_ref[pl.ds(index * halves + half, SUBLANES, stride=stride), :] = value
+    sublane = lax.broadcasted_iota(jnp.int32, (SUBLANES, LANES), 0) % halves
+    ends = []
+    for end in (before, after):
+        value = jnp.broadcast_to(end[0:1, :], (SUBLANES, LANES))
+        for half in range(1, halves):
+            value = jnp.where(sublane == half, jnp.broadcast_to(end[half : half + 1, :], value.shape), value)
+        ends.append(value)
+    for start in range(0, rows, SUBLANES):
+        part = slice(start, start + SUBLANES)
+        late = slice(rows + start, rows + start + SUBLANES)
+        out_ref[part, :] = given_ref[part, :] + spread_ref[part, :] * ends[0] + spread_ref[late, :] * ends[1]
 
 
 def trade(value, x_step, y_step):
@@ -473,36 +501,44 @@
         [square] * 3
         + [VMEM((zones * rows, LANES), jnp.float32)]
         + [VMEM((1, zones), jnp.float32)] * 2
-        + [pltpu.SemaphoreType.DMA((6 + zones,))]
+        + [pltpu.SemaphoreType.DMA((7,))]
         + [square] * 3,
         pltpu.HBM,
     )
-    def y_coefs(part):
+    def prepare(part):
         return kernel_call(
-            functools.partial(y_coefs_kernel, halves),
+            functools.partial(prepare_kernel, halves),
             (part,),
-            [held_f32(SUBLANES, LANES), held_f32(3 * y_nodes * SUBLANES, LANES)],
+            [
+                held_f32(SUBLANES, LANES),
+                held_f32(3 * LANES, rows),
+                held_f32(2 * rows, LANES),
+                held_f32(3 * y_nodes * SUBLANES, LANES),
+                held_f32(2 * rows, LANES),
+            ],
             [],
         )
 
     pieces, order = x_exchange(message)
-    y_rows, y_state = y_coefs(block)
-    other_block = trade(block, 1, 0)
-    other_rows, other_state = y_coefs(other_block)
-    kept, sent, givens = kernel_call(
+    y_rows, lines_x, sums, y_state, spread = prepare(block)
+    other_rows, other_lines, other_sums, _, _ = prepare(trade(block, 1, 0))
+    kept, sent, values = kernel_call(
         functools.partial(x_back_kernel, halves, "xg", order, len(pieces)),
-        (*pieces, block, other_block, y_rows, other_rows, y_state, other_state),
+        (*pieces, lines_x, other_lines, sums, other_sums, y_rows, other_rows),
         [
             held_f32(2 * halves, QUANTITIES * LANES),
             f32(2 * halves, QUANTITIES * LANES),
-            held_f32(y_nodes * SUBLANES, LANES),
+            held_f32(rows, LANES),
         ],
-        [square] * 4,
+        [],
+    )
+    (given,) = kernel_call(
+        functools.partial(y_given_kernel, halves), (block, values, y_state), [held_f32(rows, LANES)], []
     )
     pieces, rounds = y_exchange(kept, sent)
     (updated,) = kernel_call(
         functools.partial(y_back_kernel, halves, "yd", rounds),
-        (*pieces, y_state, givens),
+        (*pieces, given, spread),
         [f32(rows, LANES)],
         [],
     )

time: 18.9 us -> 19 us (level)
  Pallas kernels: 3.08 us -> 3.9 us
  waiting for transfers between devices: 5.44 us -> 4.72 us
    pallas_call x8 -> x9, Pallas kernels: 3.08 us -> 3.9 us  [kernel_call(): pl.pallas_call(body, out_shape=outputs, in_specs=[pl.BlockSpec(memory_spa...]
    ppermute x6, waiting for transfers between devices: 5.44 us -> 4.72 us  [trade(): return lax.ppermute(value, ('xg', 'yd'), pairs)]
  transfers between devices with their start and end apart: 6 -> 6, of which waited for: 5 -> 4; matrix products, arithmetic and copies ran while one was open for 0% -> 0% of each run, Pallas kernels for 1% -> 7%
where the time goes in v11:
time: 19 us; the launch traced here: 18.9 us
  starting transfers between devices  10.2 us (54%)
  waiting for transfers between devices  4.72 us (25%)
  Pallas kernels  3.9 us (21%)
    ppermute x6, starting transfers between devices, trade(): return lax.ppermute(value, ('xg', 'yd'), pairs)  10.2 us
    ppermute x6, waiting for transfers between devices, trade(): return lax.ppermute(value, ('xg', 'yd'), pairs)  4.72 us
    pallas_call x9, Pallas kernels, kernel_call(): pl.pallas_call(body, out_shape=outputs, in_specs=[pl.BlockSpec(memory_spa...  3.9 us
  transfers between devices with their start and end apart: 6, of which 4 were waited for; matrix products, arithmetic and copies ran while one was open for 0% of the time, Pallas kernels for 7%

profile of v11, /device:TPU:0, one launch (start us, length us, event | category | flops | bytes accessed | tf_op | source)
XLA Modules:
  0.0 18.9 jit_solution(3429915189005542655)
XLA Ops:
  0.0 1.7 %shard_map.73 = (f32[8,128]{1,0:T(8,128)S(1)}, f32[712,128]{1,0:T(8,128)S(1)}) custom-call(f32[128,128]{1,0:T(8,128)} %bitcast.9, f32[128,128]{1,0:T(8,128)} %bitcast.10, f32[128,128]{1,0:T(8,128)} %bitcast.11, f32[128,128]{1,0:T(8,128)} %bitcast.12, f32[512,128]{1,0:T(8,128)} %bitcast.8, f32[1,4]{1,0:T(1,128)} %bitcast.13, f32[1,4]{1,0:T(1,128)} %bitcast.14), custom_call_target="tpu_custom_call" | custom-call | flops 500000 | bytes 500000 | tf_op jit(solution)/shard_map/pallas_call | solution.py:465
  1.7 2.4 %collective-permute-start = (f32[8,128]{1,0:T(8,128)S(1)}, f32[8,128]{1,0:T(8,128)S(1)}, u32[]{:S(2)}, u32[]{:S(2)}) collective-permute-start(f32[8,128]{1,0:T(8,128)S(1)} %get-tuple-element.24.first_ref.refs_0_), channel_id=1, source_target_pairs={{0,24},{1,25},{2,26},{3,27},{4,28},{5,29},{6,30},{7,31},{8,16},{9,... | collective-permute-start | bytes 12296 | tf_op jit(solution)/shard_map/ppermute | solution.py:409
  4.1 0.7 %collective-permute-start.2 = (f32[712,128]{1,0:T(8,128)S(1)}, f32[712,128]{1,0:T(8,128)S(1)}, u32[]{:S(2)}, u32[]{:S(2)}) collective-permute-start(f32[712,128]{1,0:T(8,128)S(1)} %get-tuple-element.25.block_ref), channel_id=1, source_target_pairs={{0,8},{1,9},{2,10},{3,11},{4,12},{5,13},{6,14},{7,15},{8,0},{9,1},... | collective-permute-start | bytes 1093640 | tf_op jit(solution)/shard_map/ppermute | solution.py:409
  4.8 0.7 %collective-permute-done.second_ref.refs_1_ = f32[8,128]{1,0:T(8,128)S(1)} collective-permute-done((f32[8,128]{1,0:T(8,128)S(1)}, f32[8,128]{1,0:T(8,128)S(1)}, u32[]{:S(2)}, u32[]{:S(2)}) %collective-permute-start) | collective-permute-done | bytes 4128 | tf_op jit(solution)/shard_map/ppermute | solution.py:409
  5.5 0.6 %collective-permute-start.1 = (f32[16,128]{1,0:T(8,128)S(1)}, f32[16,128]{1,0:T(8,128)S(1)}, u32[]{:S(2)}, u32[]{:S(2)}) collective-permute-start(f32[16,128]{1,0:T(8,128)S(1)} %shard_map.74), channel_id=1, source_target_pairs={{0,8},{1,9},{2,10},{3,11},{4,12},{5,13},{6,14},{7,15},{8,0},{9,1},... | collective-permute-start | bytes 24584 | tf_op jit(solution)/shard_map/ppermute | solution.py:409
  6.1 0.2 %shard_map.75 = (f32[8,128]{1,0:T(8,128)S(1)}, f32[384,128]{1,0:T(8,128)S(1)}, f32[256,128]{1,0:T(8,128)S(1)}, f32[480,128]{1,0:T(8,128)S(1)}, f32[256,128]{1,0:T(8,128)S(1)}) custom-call(f32[712,128]{1,0:T(8,128)S(1)} %get-tuple-element.25.block_ref), custom_call_target="tpu_custom_call" | custom-call | flops 500000 | bytes 500000 | tf_op jit(solution)/shard_map/pallas_call | solution.py:465
  6.4 0.0 collective-permute-done.2.block_ref
  6.4 0.9 %shard_map.76 = (f32[8,128]{1,0:T(8,128)S(1)}, f32[384,128]{1,0:T(8,128)S(1)}, f32[256,128]{1,0:T(8,128)S(1)}, f32[480,128]{1,0:T(8,128)}, f32[256,128]{1,0:T(8,128)}) custom-call(f32[712,128]{1,0:T(8,128)S(1)} %collective-permute-done.2.block_ref), custom_call_target="tpu_custom_call" | custom-call | flops 500000 | bytes 500000 | tf_op jit(solution)/shard_map/pallas_call | solution.py:465
  7.3 0.0 collective-permute-done.1.refs_2_
  7.3 0.2 %shard_map.77 = (f32[4,640]{1,0:T(4,128)S(1)}, f32[4,640]{1,0:T(4,128)S(1)}, f32[128,128]{1,0:T(8,128)S(1)}) custom-call(f32[8,128]{1,0:T(8,128)S(1)} %get-tuple-element.24.first_ref.refs_0_, f32[8,128]{1,0:T(8,128)S(1)} %collective-permute-done.second_ref.refs_1_, f32[16,128]{1,0:T(8,128)S(1)} %collective-permute-done.1.refs_2_, ...), custom_call_target="tpu_custom_call" | custom-call | flops 500000 | bytes 500000 | tf_op jit(solution)/shard_map/pallas_call | solution.py:465
  7.6 1.8 %collective-permute-start.3 = (f32[4,640]{1,0:T(4,128)S(1)}, f32[4,640]{1,0:T(4,128)S(1)}, u32[]{:S(2)}, u32[]{:S(2)}) collective-permute-start(f32[4,640]{1,0:T(4,128)S(1)} %get-tuple-element.33), channel_id=1, source_target_pairs={{0,9},{1,8},{2,11},{3,10},{4,13},{5,12},{6,15},{7,14},{8,1},{9,0},... | collective-permute-start | bytes 30728 | tf_op jit(solution)/shard_map/ppermute | solution.py:409
  9.4 1.4 %collective-permute-done.3.other_ref = f32[4,640]{1,0:T(4,128)S(1)} collective-permute-done((f32[4,640]{1,0:T(4,128)S(1)}, f32[4,640]{1,0:T(4,128)S(1)}, u32[]{:S(2)}, u32[]{:S(2)}) %collective-permute-start.3) | collective-permute-done | bytes 10272 | tf_op jit(solution)/shard_map/ppermute | solution.py:409
  10.8 1.8 %collective-permute-start.4 = (f32[4,640]{1,0:T(4,128)S(1)}, f32[4,640]{1,0:T(4,128)S(1)}, u32[]{:S(2)}, u32[]{:S(2)}) collective-permute-start(f32[4,640]{1,0:T(4,128)S(1)} %get-tuple-element.35), channel_id=1, source_target_pairs={{0,10},{1,11},{2,8},{3,9},{4,14},{5,15},{6,12},{7,13},{8,2},{9,3},... | collective-permute-start | bytes 30728 | tf_op jit(solution)/shard_map/ppermute | solution.py:409
  12.6 1.4 %collective-permute-done.4.other_ref = f32[4,640]{1,0:T(4,128)S(1)} collective-permute-done((f32[4,640]{1,0:T(4,128)S(1)}, f32[4,640]{1,0:T(4,128)S(1)}, u32[]{:S(2)}, u32[]{:S(2)}) %collective-permute-start.4) | collective-permute-done | bytes 10272 | tf_op jit(solution)/shard_map/ppermute | solution.py:409
  14.0 2.8 %collective-permute-start.5 = (f32[4,640]{1,0:T(4,128)S(1)}, f32[4,640]{1,0:T(4,128)S(1)}, u32[]{:S(2)}, u32[]{:S(2)}) collective-permute-start(f32[4,640]{1,0:T(4,128)S(1)} %get-tuple-element.37), channel_id=1, source_target_pairs={{0,12},{1,13},{2,14},{3,15},{4,8},{5,9},{6,10},{7,11},{8,4},{9,5},... | collective-permute-start | bytes 30728 | tf_op jit(solution)/shard_map/ppermute | solution.py:409
  16.8 0.1 shard_map.80.refs_2_
  16.9 1.3 %collective-permute-done.5.other_ref = f32[4,640]{1,0:T(4,128)S(1)} collective-permute-done((f32[4,640]{1,0:T(4,128)S(1)}, f32[4,640]{1,0:T(4,128)S(1)}, u32[]{:S(2)}, u32[]{:S(2)}) %collective-permute-start.5) | collective-permute-done | bytes 10272 | tf_op jit(solution)/shard_map/ppermute | solution.py:409
  18.2 0.7 %shard_map.81 = f32[128,128]{1,0:T(8,128)} custom-call(f32[4,640]{1,0:T(4,128)S(1)} %get-tuple-element.36.own_ref, f32[4,640]{1,0:T(4,128)S(1)} %collective-permute-done.5.other_ref, f32[4,384]{1,0:T(4,128)S(1)} %get-tuple-element.38.refs_0_, f32[4,384]{1,0:T(4,128)S(1)} %get-tuple-element.39.refs_1_, f32[128,128]{1,0:T(8,128)S(1)} %shard_map.80.refs_2_, ...), custom_call_target="tpu_custom_call" | custom-call | flops 500000 | bytes 500000 | tf_op jit(solution)/shard_map/pallas_call | solution.py:465
  (3 shorter events, 0.0 us)
Async XLA Ops:
  1.7 3.8 %collective-permute-start = (f32[8,128]{1,0:T(8,128)S(1)}, f32[8,128]{1,0:T(8,128)S(1)}, u32[]{:S(2)}, u32[]{:S(2)}) collective-permute-start(f32[8,128]{1,0:T(8,128)S(1)} %get-tuple-element.24.first_ref.refs_0_), channel_id=1, source_target_pairs={{0,24},{1,25},{2,26},{3,27},{4,28},{5,29},{6,30},{7,31},{8,16},{9,... | collective-permute-start | bytes 12296 | tf_op jit(solution)/shard_map/ppermute | solution.py:409
  4.1 2.2 %collective-permute-start.2 = (f32[712,128]{1,0:T(8,128)S(1)}, f32[712,128]{1,0:T(8,128)S(1)}, u32[]{:S(2)}, u32[]{:S(2)}) collective-permute-start(f32[712,128]{1,0:T(8,128)S(1)} %get-tuple-element.25.block_ref), channel_id=1, source_target_pairs={{0,8},{1,9},{2,10},{3,11},{4,12},{5,13},{6,14},{7,15},{8,0},{9,1},... | collective-permute-start | bytes 1093640 | tf_op jit(solution)/shard_map/ppermute | solution.py:409
  5.5 1.8 %collective-permute-start.1 = (f32[16,128]{1,0:T(8,128)S(1)}, f32[16,128]{1,0:T(8,128)S(1)}, u32[]{:S(2)}, u32[]{:S(2)}) collective-permute-start(f32[16,128]{1,0:T(8,128)S(1)} %shard_map.74), channel_id=1, source_target_pairs={{0,8},{1,9},{2,10},{3,11},{4,12},{5,13},{6,14},{7,15},{8,0},{9,1},... | collective-permute-start | bytes 24584 | tf_op jit(solution)/shard_map/ppermute | solution.py:409
  7.6 3.2 %collective-permute-start.3 = (f32[4,640]{1,0:T(4,128)S(1)}, f32[4,640]{1,0:T(4,128)S(1)}, u32[]{:S(2)}, u32[]{:S(2)}) collective-permute-start(f32[4,640]{1,0:T(4,128)S(1)} %get-tuple-element.33), channel_id=1, source_target_pairs={{0,9},{1,8},{2,11},{3,10},{4,13},{5,12},{6,15},{7,14},{8,1},{9,0},... | collective-permute-start | bytes 30728 | tf_op jit(solution)/shard_map/ppermute | solution.py:409
  10.8 3.2 %collective-permute-start.4 = (f32[4,640]{1,0:T(4,128)S(1)}, f32[4,640]{1,0:T(4,128)S(1)}, u32[]{:S(2)}, u32[]{:S(2)}) collective-permute-start(f32[4,640]{1,0:T(4,128)S(1)} %get-tuple-element.35), channel_id=1, source_target_pairs={{0,10},{1,11},{2,8},{3,9},{4,14},{5,15},{6,12},{7,13},{8,2},{9,3},... | collective-permute-start | bytes 30728 | tf_op jit(solution)/shard_map/ppermute | solution.py:409
  14.0 4.2 %collective-permute-start.5 = (f32[4,640]{1,0:T(4,128)S(1)}, f32[4,640]{1,0:T(4,128)S(1)}, u32[]{:S(2)}, u32[]{:S(2)}) collective-permute-start(f32[4,640]{1,0:T(4,128)S(1)} %get-tuple-element.37), channel_id=1, source_target_pairs={{0,12},{1,13},{2,14},{3,15},{4,8},{5,9},{6,10},{7,11},{8,4},{9,5},... | collective-permute-start | bytes 30728 | tf_op jit(solution)/shard_map/ppermute | solution.py:409

commit v12 on v11

--- a/solution.py
+++ b/solution.py
@@ -185,29 +185,27 @@
 ):
     rows = mobile_ref.shape[0]
     pairs = (
-        (immobile_hbm, immobile_ref), (capacity_hbm, capacity_ref), (mobile_hbm, mobile_ref), (faces_hbm, faces_ref),
-        (rates_hbm, rates_ref), (shares_hbm, shares_ref), (across_hbm, block_ref.at[rows : 2 * rows, :]),
+        (rates_hbm, rates_ref), (shares_hbm, shares_ref), (capacity_hbm, capacity_ref), (faces_hbm, faces_ref),
+        (immobile_hbm, immobile_ref), (mobile_hbm, mobile_ref), (across_hbm, block_ref.at[rows : 2 * rows, :]),
     )
     copies = [pltpu.make_async_copy(pair[0], pair[1], arrived.at[place]) for place, pair in enumerate(pairs)]
     for copy in copies:
         copy.start()
-    immobile_copy, capacity_copy, mobile_copy, faces_copy, rates_copy, shares_copy, across_copy = copies
     stride = LANES // SUBLANES
-    faces_copy.wait()
-    faces_t[...] = faces_ref[...].T
-    rates_copy.wait()
-    shares_copy.wait()
-    capacity_copy.wait()
+    for copy in copies[:3]:
+        copy.wait()
     weights = capacity_weights(rates_ref[...], shares_ref[...])
     capacity = capacity_ref[...]
     storage = 1.0 + capacity * sum(weights[1:], weights[0])
     block_ref[0:rows, :] = storage
     storage_t[...] = storage.T
-    immobile_copy.wait()
+    copies[3].wait()
+    faces_t[...] = faces_ref[...].T
+    copies[4].wait()
     total = None
     for zone, weight in enumerate(weights):
         total = plus(total, weight * immobile_ref[zone * rows : (zone + 1) * rows, :])
-    mobile_copy.wait()
+    copies[5].wait()
     source_t[...] = (mobile_ref[...] + capacity * total).T
     coefs, sides = [], []
     for index in range(stride):
@@ -223,7 +221,7 @@
             start += SUBLANES
     for row, value in enumerate(piece + side):
         message_ref[row : row + 1, :] = value[0:1, :]
-    across_copy.wait()
+    copies[6].wait()
 
 
 def ends_responses(shape):
@@ -231,7 +229,7 @@
     return ((one, nothing), (nothing, one))
 
 
-def prepare_kernel(halves, block_ref, rows_ref, lines_ref, sums_ref, state_ref, spread_ref):
+def prepare_kernel(halves, block_ref, rows_ref, lines_ref, sums_ref, *own_refs):
     rows = rows_ref.shape[1]
     stride = LANES // SUBLANES
     rolls = x_rolls(halves)
@@ -249,10 +247,9 @@
         storage = [strided(block_ref, index, SUBLANES, stride) for index in range(half, stride, halves)]
         faces = [strided(block_ref, rows + index, SUBLANES, stride) for index in range(half, stride, halves)]
         piece, nodes = tree_coefs([(face, None, held) for face, held in zip(faces, storage)], y_rolls())
-        for node in nodes:
-            for part in node:
-                state_ref[start : start + SUBLANES, :] = part
-                start += SUBLANES
+        for part in [part for node in nodes for part in node] if own_refs else []:
+            own_refs[0][start : start + SUBLANES, :] = part
+            start += SUBLANES
         for number, value in enumerate(piece):
             row = number * halves + half
             rows_ref[row : row + 1, :] = value[0:1, :]
@@ -260,8 +257,9 @@
             values = tree_values(*ends, y_rolls(), len(storage), nodes, [0.0] * len(nodes))
             for index, (value, held) in enumerate(zip(values, storage)):
                 place = pl.ds(case * rows + index * halves + half, SUBLANES, stride=stride)
-                spread_ref[place, :] = value
                 sums_ref[place, :] = value * held
+                if own_refs:
+                    own_refs[1][place, :] = value
 
 
 def state_parts(ref, first, total, parts, pitch=3):
@@ -505,23 +503,15 @@
         + [square] * 3,
         pltpu.HBM,
     )
-    def prepare(part):
-        return kernel_call(
-            functools.partial(prepare_kernel, halves),
-            (part,),
-            [
-                held_f32(SUBLANES, LANES),
-                held_f32(3 * LANES, rows),
-                held_f32(2 * rows, LANES),
-                held_f32(3 * y_nodes * SUBLANES, LANES),
-                held_f32(2 * rows, LANES),
-            ],
-            [],
-        )
+    def prepare(part, own):
+        outputs = [held_f32(SUBLANES, LANES), held_f32(3 * LANES, rows), held_f32(2 * rows, LANES)]
+        if own:
+            outputs += [held_f32(3 * y_nodes * SUBLANES, LANES), held_f32(2 * rows, LANES)]
+        return kernel_call(functools.partial(prepare_kernel, halves), (part,), outputs, [])
 
     pieces, order = x_exchange(message)
-    y_rows, lines_x, sums, y_state, spread = prepare(block)
-    other_rows, other_lines, other_sums, _, _ = prepare(trade(block, 1, 0))
+    y_rows, lines_x, sums, y_state, spread = prepare(block, True)
+    other_rows, other_lines, other_sums = prepare(trade(block, 1, 0), False)
     kept, sent, values = kernel_call(
         functools.partial(x_back_kernel, halves, "xg", order, len(pieces)),
         (*pieces, lines_x, other_lines, sums, other_sums, y_rows, other_rows),

time: 19 us -> 18.6 us (0.979)
  Pallas kernels: 3.9 us -> 3.05 us
  waiting for transfers between devices: 4.72 us -> 5.09 us
    pallas_call x9, Pallas kernels: 3.9 us -> 3.05 us  [kernel_call(): pl.pallas_call(body, out_shape=outputs, in_specs=[pl.BlockSpec(memory_spa...]
    ppermute x6, waiting for transfers between devices: 4.72 us -> 5.09 us  [trade(): return lax.ppermute(value, ('xg', 'yd'), pairs)]
  transfers between devices with their start and end apart: 6 -> 6, of which waited for: 4 -> 5; matrix products, arithmetic and copies ran while one was open for 0% -> 0% of each run, Pallas kernels for 7% -> 3%
where the time goes in v12:
time: 18.6 us; the launch traced here: 18.4 us
  starting transfers between devices  10.2 us (55%)
  waiting for transfers between devices  5.09 us (27%)
  Pallas kernels  3.05 us (16%)
    ppermute x6, starting transfers between devices, trade(): return lax.ppermute(value, ('xg', 'yd'), pairs)  10.2 us
    ppermute x6, waiting for transfers between devices, trade(): return lax.ppermute(value, ('xg', 'yd'), pairs)  5.09 us
    pallas_call x9, Pallas kernels, kernel_call(): pl.pallas_call(body, out_shape=outputs, in_specs=[pl.BlockSpec(memory_spa...  3.05 us
  transfers between devices with their start and end apart: 6, of which 5 were waited for; matrix products, arithmetic and copies ran while one was open for 0% of the time, Pallas kernels for 3%

profile of v12, /device:TPU:0, one launch (start us, length us, event | category | flops | bytes accessed | tf_op | source)
XLA Modules:
  0.0 18.4 jit_solution(6964725689110185051)
XLA Ops:
  0.0 1.6 %shard_map.73 = (f32[8,128]{1,0:T(8,128)S(1)}, f32[712,128]{1,0:T(8,128)S(1)}) custom-call(f32[128,128]{1,0:T(8,128)} %bitcast.9, f32[128,128]{1,0:T(8,128)} %bitcast.10, f32[128,128]{1,0:T(8,128)} %bitcast.11, f32[128,128]{1,0:T(8,128)} %bitcast.12, f32[512,128]{1,0:T(8,128)} %bitcast.8, f32[1,4]{1,0:T(1,128)} %bitcast.13, f32[1,4]{1,0:T(1,128)} %bitcast.14), custom_call_target="tpu_custom_call" | custom-call | flops 500000 | bytes 500000 | tf_op jit(solution)/shard_map/pallas_call | solution.py:463
  1.6 2.4 %collective-permute-start = (f32[8,128]{1,0:T(8,128)S(1)}, f32[8,128]{1,0:T(8,128)S(1)}, u32[]{:S(2)}, u32[]{:S(2)}) collective-permute-start(f32[8,128]{1,0:T(8,128)S(1)} %get-tuple-element.24.first_ref.refs_0_), channel_id=1, source_target_pairs={{0,24},{1,25},{2,26},{3,27},{4,28},{5,29},{6,30},{7,31},{8,16},{9,... | collective-permute-start | bytes 12296 | tf_op jit(solution)/shard_map/ppermute | solution.py:407
  4.0 0.7 %collective-permute-start.2 = (f32[712,128]{1,0:T(8,128)S(1)}, f32[712,128]{1,0:T(8,128)S(1)}, u32[]{:S(2)}, u32[]{:S(2)}) collective-permute-start(f32[712,128]{1,0:T(8,128)S(1)} %get-tuple-element.25.block_ref), channel_id=1, source_target_pairs={{0,8},{1,9},{2,10},{3,11},{4,12},{5,13},{6,14},{7,15},{8,0},{9,1},... | collective-permute-start | bytes 1093640 | tf_op jit(solution)/shard_map/ppermute | solution.py:407
  4.7 0.7 %collective-permute-done.second_ref.refs_1_ = f32[8,128]{1,0:T(8,128)S(1)} collective-permute-done((f32[8,128]{1,0:T(8,128)S(1)}, f32[8,128]{1,0:T(8,128)S(1)}, u32[]{:S(2)}, u32[]{:S(2)}) %collective-permute-start) | collective-permute-done | bytes 4128 | tf_op jit(solution)/shard_map/ppermute | solution.py:407
  5.4 0.6 %collective-permute-start.1 = (f32[16,128]{1,0:T(8,128)S(1)}, f32[16,128]{1,0:T(8,128)S(1)}, u32[]{:S(2)}, u32[]{:S(2)}) collective-permute-start(f32[16,128]{1,0:T(8,128)S(1)} %shard_map.74), channel_id=1, source_target_pairs={{0,8},{1,9},{2,10},{3,11},{4,12},{5,13},{6,14},{7,15},{8,0},{9,1},... | collective-permute-start | bytes 24584 | tf_op jit(solution)/shard_map/ppermute | solution.py:407
  6.0 0.2 %shard_map.75 = (f32[8,128]{1,0:T(8,128)S(1)}, f32[384,128]{1,0:T(8,128)S(1)}, f32[256,128]{1,0:T(8,128)S(1)}, f32[480,128]{1,0:T(8,128)S(1)}, f32[256,128]{1,0:T(8,128)S(1)}) custom-call(f32[712,128]{1,0:T(8,128)S(1)} %get-tuple-element.25.block_ref), custom_call_target="tpu_custom_call" | custom-call | flops 500000 | bytes 500000 | tf_op jit(solution)/shard_map/pallas_call | solution.py:463
  6.2 0.0 collective-permute-done.2.block_ref
  6.3 0.2 %shard_map.76 = (f32[8,128]{1,0:T(8,128)S(1)}, f32[384,128]{1,0:T(8,128)S(1)}, f32[256,128]{1,0:T(8,128)S(1)}) custom-call(f32[712,128]{1,0:T(8,128)S(1)} %collective-permute-done.2.block_ref), custom_call_target="tpu_custom_call" | custom-call | flops 500000 | bytes 500000 | tf_op jit(solution)/shard_map/pallas_call | solution.py:463
  6.5 0.4 %collective-permute-done.1.refs_2_ = f32[16,128]{1,0:T(8,128)S(1)} collective-permute-done((f32[16,128]{1,0:T(8,128)S(1)}, f32[16,128]{1,0:T(8,128)S(1)}, u32[]{:S(2)}, u32[]{:S(2)}) %collective-permute-start.1) | collective-permute-done | bytes 8224 | tf_op jit(solution)/shard_map/ppermute | solution.py:407
  6.8 0.2 %shard_map.77 = (f32[4,640]{1,0:T(4,128)S(1)}, f32[4,640]{1,0:T(4,128)S(1)}, f32[128,128]{1,0:T(8,128)S(1)}) custom-call(f32[8,128]{1,0:T(8,128)S(1)} %get-tuple-element.24.first_ref.refs_0_, f32[8,128]{1,0:T(8,128)S(1)} %collective-permute-done.second_ref.refs_1_, f32[16,128]{1,0:T(8,128)S(1)} %collective-permute-done.1.refs_2_, ...), custom_call_target="tpu_custom_call" | custom-call | flops 500000 | bytes 500000 | tf_op jit(solution)/shard_map/pallas_call | solution.py:463
  7.1 1.8 %collective-permute-start.3 = (f32[4,640]{1,0:T(4,128)S(1)}, f32[4,640]{1,0:T(4,128)S(1)}, u32[]{:S(2)}, u32[]{:S(2)}) collective-permute-start(f32[4,640]{1,0:T(4,128)S(1)} %get-tuple-element.33), channel_id=1, source_target_pairs={{0,9},{1,8},{2,11},{3,10},{4,13},{5,12},{6,15},{7,14},{8,1},{9,0},... | collective-permute-start | bytes 30728 | tf_op jit(solution)/shard_map/ppermute | solution.py:407
  8.9 1.4 %collective-permute-done.3.other_ref = f32[4,640]{1,0:T(4,128)S(1)} collective-permute-done((f32[4,640]{1,0:T(4,128)S(1)}, f32[4,640]{1,0:T(4,128)S(1)}, u32[]{:S(2)}, u32[]{:S(2)}) %collective-permute-start.3) | collective-permute-done | bytes 10272 | tf_op jit(solution)/shard_map/ppermute | solution.py:407
  10.3 1.8 %collective-permute-start.4 = (f32[4,640]{1,0:T(4,128)S(1)}, f32[4,640]{1,0:T(4,128)S(1)}, u32[]{:S(2)}, u32[]{:S(2)}) collective-permute-start(f32[4,640]{1,0:T(4,128)S(1)} %get-tuple-element.35), channel_id=1, source_target_pairs={{0,10},{1,11},{2,8},{3,9},{4,14},{5,15},{6,12},{7,13},{8,2},{9,3},... | collective-permute-start | bytes 30728 | tf_op jit(solution)/shard_map/ppermute | solution.py:407
  12.1 1.4 %collective-permute-done.4.other_ref = f32[4,640]{1,0:T(4,128)S(1)} collective-permute-done((f32[4,640]{1,0:T(4,128)S(1)}, f32[4,640]{1,0:T(4,128)S(1)}, u32[]{:S(2)}, u32[]{:S(2)}) %collective-permute-start.4) | collective-permute-done | bytes 10272 | tf_op jit(solution)/shard_map/ppermute | solution.py:407
  13.5 2.8 %collective-permute-start.5 = (f32[4,640]{1,0:T(4,128)S(1)}, f32[4,640]{1,0:T(4,128)S(1)}, u32[]{:S(2)}, u32[]{:S(2)}) collective-permute-start(f32[4,640]{1,0:T(4,128)S(1)} %get-tuple-element.37), channel_id=1, source_target_pairs={{0,12},{1,13},{2,14},{3,15},{4,8},{5,9},{6,10},{7,11},{8,4},{9,5},... | collective-permute-start | bytes 30728 | tf_op jit(solution)/shard_map/ppermute | solution.py:407
  16.3 0.1 shard_map.80.refs_2_
  16.4 1.3 %collective-permute-done.5.other_ref = f32[4,640]{1,0:T(4,128)S(1)} collective-permute-done((f32[4,640]{1,0:T(4,128)S(1)}, f32[4,640]{1,0:T(4,128)S(1)}, u32[]{:S(2)}, u32[]{:S(2)}) %collective-permute-start.5) | collective-permute-done | bytes 10272 | tf_op jit(solution)/shard_map/ppermute | solution.py:407
  17.7 0.7 %shard_map.81 = f32[128,128]{1,0:T(8,128)} custom-call(f32[4,640]{1,0:T(4,128)S(1)} %get-tuple-element.36.own_ref, f32[4,640]{1,0:T(4,128)S(1)} %collective-permute-done.5.other_ref, f32[4,384]{1,0:T(4,128)S(1)} %get-tuple-element.38.refs_0_, f32[4,384]{1,0:T(4,128)S(1)} %get-tuple-element.39.refs_1_, f32[128,128]{1,0:T(8,128)S(1)} %shard_map.80.refs_2_, ...), custom_call_target="tpu_custom_call" | custom-call | flops 500000 | bytes 500000 | tf_op jit(solution)/shard_map/pallas_call | solution.py:463
  (3 shorter events, 0.0 us)
Async XLA Ops:
  1.6 3.8 %collective-permute-start = (f32[8,128]{1,0:T(8,128)S(1)}, f32[8,128]{1,0:T(8,128)S(1)}, u32[]{:S(2)}, u32[]{:S(2)}) collective-permute-start(f32[8,128]{1,0:T(8,128)S(1)} %get-tuple-element.24.first_ref.refs_0_), channel_id=1, source_target_pairs={{0,24},{1,25},{2,26},{3,27},{4,28},{5,29},{6,30},{7,31},{8,16},{9,... | collective-permute-start | bytes 12296 | tf_op jit(solution)/shard_map/ppermute | solution.py:407
  4.0 2.2 %collective-permute-start.2 = (f32[712,128]{1,0:T(8,128)S(1)}, f32[712,128]{1,0:T(8,128)S(1)}, u32[]{:S(2)}, u32[]{:S(2)}) collective-permute-start(f32[712,128]{1,0:T(8,128)S(1)} %get-tuple-element.25.block_ref), channel_id=1, source_target_pairs={{0,8},{1,9},{2,10},{3,11},{4,12},{5,13},{6,14},{7,15},{8,0},{9,1},... | collective-permute-start | bytes 1093640 | tf_op jit(solution)/shard_map/ppermute | solution.py:407
  5.4 1.5 %collective-permute-start.1 = (f32[16,128]{1,0:T(8,128)S(1)}, f32[16,128]{1,0:T(8,128)S(1)}, u32[]{:S(2)}, u32[]{:S(2)}) collective-permute-start(f32[16,128]{1,0:T(8,128)S(1)} %shard_map.74), channel_id=1, source_target_pairs={{0,8},{1,9},{2,10},{3,11},{4,12},{5,13},{6,14},{7,15},{8,0},{9,1},... | collective-permute-start | bytes 24584 | tf_op jit(solution)/shard_map/ppermute | solution.py:407
  7.1 3.2 %collective-permute-start.3 = (f32[4,640]{1,0:T(4,128)S(1)}, f32[4,640]{1,0:T(4,128)S(1)}, u32[]{:S(2)}, u32[]{:S(2)}) collective-permute-start(f32[4,640]{1,0:T(4,128)S(1)} %get-tuple-element.33), channel_id=1, source_target_pairs={{0,9},{1,8},{2,11},{3,10},{4,13},{5,12},{6,15},{7,14},{8,1},{9,0},... | collective-permute-start | bytes 30728 | tf_op jit(solution)/shard_map/ppermute | solution.py:407
  10.3 3.2 %collective-permute-start.4 = (f32[4,640]{1,0:T(4,128)S(1)}, f32[4,640]{1,0:T(4,128)S(1)}, u32[]{:S(2)}, u32[]{:S(2)}) collective-permute-start(f32[4,640]{1,0:T(4,128)S(1)} %get-tuple-element.35), channel_id=1, source_target_pairs={{0,10},{1,11},{2,8},{3,9},{4,14},{5,15},{6,12},{7,13},{8,2},{9,3},... | collective-permute-start | bytes 30728 | tf_op jit(solution)/shard_map/ppermute | solution.py:407
  13.5 4.2 %collective-permute-start.5 = (f32[4,640]{1,0:T(4,128)S(1)}, f32[4,640]{1,0:T(4,128)S(1)}, u32[]{:S(2)}, u32[]{:S(2)}) collective-permute-start(f32[4,640]{1,0:T(4,128)S(1)} %get-tuple-element.37), channel_id=1, source_target_pairs={{0,12},{1,13},{2,14},{3,15},{4,8},{5,9},{6,10},{7,11},{8,4},{9,5},... | collective-permute-start | bytes 30728 | tf_op jit(solution)/shard_map/ppermute | solution.py:407

commit v13 on v12

--- a/solution.py
+++ b/solution.py
@@ -192,21 +192,18 @@
     for copy in copies:
         copy.start()
     stride = LANES // SUBLANES
-    for copy in copies[:3]:
+    for copy in copies[:6]:
         copy.wait()
+    faces_t[...] = faces_ref[...].T
     weights = capacity_weights(rates_ref[...], shares_ref[...])
     capacity = capacity_ref[...]
     storage = 1.0 + capacity * sum(weights[1:], weights[0])
-    block_ref[0:rows, :] = storage
     storage_t[...] = storage.T
-    copies[3].wait()
-    faces_t[...] = faces_ref[...].T
-    copies[4].wait()
     total = None
     for zone, weight in enumerate(weights):
         total = plus(total, weight * immobile_ref[zone * rows : (zone + 1) * rows, :])
-    copies[5].wait()
     source_t[...] = (mobile_ref[...] + capacity * total).T
+    block_ref[0:rows, :] = storage
     coefs, sides = [], []
     for index in range(stride):
         coefs.append((strided(faces_t, index, SUBLANES, stride), None, strided(storage_t, index, SUBLANES, stride)))

time: 18.6 us -> 18.6 us (level)
  no operation moved by 1% of the time
where the time goes in v13:
time: 18.6 us; the launch traced here: 18.4 us
  starting transfers between devices  10.2 us (55%)
  waiting for transfers between devices  5.09 us (27%)
  Pallas kernels  3.07 us (17%)
    ppermute x6, starting transfers between devices, trade(): return lax.ppermute(value, ('xg', 'yd'), pairs)  10.2 us
    ppermute x6, waiting for transfers between devices, trade(): return lax.ppermute(value, ('xg', 'yd'), pairs)  5.09 us
    pallas_call x9, Pallas kernels, kernel_call(): pl.pallas_call(body, out_shape=outputs, in_specs=[pl.BlockSpec(memory_spa...  3.07 us
  transfers between devices with their start and end apart: 6, of which 5 were waited for; matrix products, arithmetic and copies ran while one was open for 0% of the time, Pallas kernels for 3%

profile of v13, /device:TPU:0, one launch (start us, length us, event | category | flops | bytes accessed | tf_op | source)
XLA Modules:
  0.0 18.4 jit_solution(12465086516484684069)
XLA Ops:
  0.0 1.6 %shard_map.73 = (f32[8,128]{1,0:T(8,128)S(1)}, f32[712,128]{1,0:T(8,128)S(1)}) custom-call(f32[128,128]{1,0:T(8,128)} %bitcast.9, f32[128,128]{1,0:T(8,128)} %bitcast.10, f32[128,128]{1,0:T(8,128)} %bitcast.11, f32[128,128]{1,0:T(8,128)} %bitcast.12, f32[512,128]{1,0:T(8,128)} %bitcast.8, f32[1,4]{1,0:T(1,128)} %bitcast.13, f32[1,4]{1,0:T(1,128)} %bitcast.14), custom_call_target="tpu_custom_call" | custom-call | flops 500000 | bytes 500000 | tf_op jit(solution)/shard_map/pallas_call | solution.py:460
  1.6 2.4 %collective-permute-start = (f32[8,128]{1,0:T(8,128)S(1)}, f32[8,128]{1,0:T(8,128)S(1)}, u32[]{:S(2)}, u32[]{:S(2)}) collective-permute-start(f32[8,128]{1,0:T(8,128)S(1)} %get-tuple-element.24.first_ref.refs_0_), channel_id=1, source_target_pairs={{0,24},{1,25},{2,26},{3,27},{4,28},{5,29},{6,30},{7,31},{8,16},{9,... | collective-permute-start | bytes 12296 | tf_op jit(solution)/shard_map/ppermute | solution.py:404
  4.1 0.7 %collective-permute-start.2 = (f32[712,128]{1,0:T(8,128)S(1)}, f32[712,128]{1,0:T(8,128)S(1)}, u32[]{:S(2)}, u32[]{:S(2)}) collective-permute-start(f32[712,128]{1,0:T(8,128)S(1)} %get-tuple-element.25.block_ref), channel_id=1, source_target_pairs={{0,8},{1,9},{2,10},{3,11},{4,12},{5,13},{6,14},{7,15},{8,0},{9,1},... | collective-permute-start | bytes 1093640 | tf_op jit(solution)/shard_map/ppermute | solution.py:404
  4.7 0.7 %collective-permute-done.second_ref.refs_1_ = f32[8,128]{1,0:T(8,128)S(1)} collective-permute-done((f32[8,128]{1,0:T(8,128)S(1)}, f32[8,128]{1,0:T(8,128)S(1)}, u32[]{:S(2)}, u32[]{:S(2)}) %collective-permute-start) | collective-permute-done | bytes 4128 | tf_op jit(solution)/shard_map/ppermute | solution.py:404
  5.4 0.6 %collective-permute-start.1 = (f32[16,128]{1,0:T(8,128)S(1)}, f32[16,128]{1,0:T(8,128)S(1)}, u32[]{:S(2)}, u32[]{:S(2)}) collective-permute-start(f32[16,128]{1,0:T(8,128)S(1)} %shard_map.74), channel_id=1, source_target_pairs={{0,8},{1,9},{2,10},{3,11},{4,12},{5,13},{6,14},{7,15},{8,0},{9,1},... | collective-permute-start | bytes 24584 | tf_op jit(solution)/shard_map/ppermute | solution.py:404
  6.0 0.2 %shard_map.75 = (f32[8,128]{1,0:T(8,128)S(1)}, f32[384,128]{1,0:T(8,128)S(1)}, f32[256,128]{1,0:T(8,128)S(1)}, f32[480,128]{1,0:T(8,128)S(1)}, f32[256,128]{1,0:T(8,128)S(1)}) custom-call(f32[712,128]{1,0:T(8,128)S(1)} %get-tuple-element.25.block_ref), custom_call_target="tpu_custom_call" | custom-call | flops 500000 | bytes 500000 | tf_op jit(solution)/shard_map/pallas_call | solution.py:460
  6.3 0.0 collective-permute-done.2.block_ref
  6.3 0.2 %shard_map.76 = (f32[8,128]{1,0:T(8,128)S(1)}, f32[384,128]{1,0:T(8,128)S(1)}, f32[256,128]{1,0:T(8,128)S(1)}) custom-call(f32[712,128]{1,0:T(8,128)S(1)} %collective-permute-done.2.block_ref), custom_call_target="tpu_custom_call" | custom-call | flops 500000 | bytes 500000 | tf_op jit(solution)/shard_map/pallas_call | solution.py:460
  6.5 0.4 %collective-permute-done.1.refs_2_ = f32[16,128]{1,0:T(8,128)S(1)} collective-permute-done((f32[16,128]{1,0:T(8,128)S(1)}, f32[16,128]{1,0:T(8,128)S(1)}, u32[]{:S(2)}, u32[]{:S(2)}) %collective-permute-start.1) | collective-permute-done | bytes 8224 | tf_op jit(solution)/shard_map/ppermute | solution.py:404
  6.9 0.2 %shard_map.77 = (f32[4,640]{1,0:T(4,128)S(1)}, f32[4,640]{1,0:T(4,128)S(1)}, f32[128,128]{1,0:T(8,128)S(1)}) custom-call(f32[8,128]{1,0:T(8,128)S(1)} %get-tuple-element.24.first_ref.refs_0_, f32[8,128]{1,0:T(8,128)S(1)} %collective-permute-done.second_ref.refs_1_, f32[16,128]{1,0:T(8,128)S(1)} %collective-permute-done.1.refs_2_, ...), custom_call_target="tpu_custom_call" | custom-call | flops 500000 | bytes 500000 | tf_op jit(solution)/shard_map/pallas_call | solution.py:460
  7.1 1.8 %collective-permute-start.3 = (f32[4,640]{1,0:T(4,128)S(1)}, f32[4,640]{1,0:T(4,128)S(1)}, u32[]{:S(2)}, u32[]{:S(2)}) collective-permute-start(f32[4,640]{1,0:T(4,128)S(1)} %get-tuple-element.33), channel_id=1, source_target_pairs={{0,9},{1,8},{2,11},{3,10},{4,13},{5,12},{6,15},{7,14},{8,1},{9,0},... | collective-permute-start | bytes 30728 | tf_op jit(solution)/shard_map/ppermute | solution.py:404
  8.9 1.4 %collective-permute-done.3.other_ref = f32[4,640]{1,0:T(4,128)S(1)} collective-permute-done((f32[4,640]{1,0:T(4,128)S(1)}, f32[4,640]{1,0:T(4,128)S(1)}, u32[]{:S(2)}, u32[]{:S(2)}) %collective-permute-start.3) | collective-permute-done | bytes 10272 | tf_op jit(solution)/shard_map/ppermute | solution.py:404
  10.3 1.8 %collective-permute-start.4 = (f32[4,640]{1,0:T(4,128)S(1)}, f32[4,640]{1,0:T(4,128)S(1)}, u32[]{:S(2)}, u32[]{:S(2)}) collective-permute-start(f32[4,640]{1,0:T(4,128)S(1)} %get-tuple-element.35), channel_id=1, source_target_pairs={{0,10},{1,11},{2,8},{3,9},{4,14},{5,15},{6,12},{7,13},{8,2},{9,3},... | collective-permute-start | bytes 30728 | tf_op jit(solution)/shard_map/ppermute | solution.py:404
  12.2 1.4 %collective-permute-done.4.other_ref = f32[4,640]{1,0:T(4,128)S(1)} collective-permute-done((f32[4,640]{1,0:T(4,128)S(1)}, f32[4,640]{1,0:T(4,128)S(1)}, u32[]{:S(2)}, u32[]{:S(2)}) %collective-permute-start.4) | collective-permute-done | bytes 10272 | tf_op jit(solution)/shard_map/ppermute | solution.py:404
  13.6 2.8 %collective-permute-start.5 = (f32[4,640]{1,0:T(4,128)S(1)}, f32[4,640]{1,0:T(4,128)S(1)}, u32[]{:S(2)}, u32[]{:S(2)}) collective-permute-start(f32[4,640]{1,0:T(4,128)S(1)} %get-tuple-element.37), channel_id=1, source_target_pairs={{0,12},{1,13},{2,14},{3,15},{4,8},{5,9},{6,10},{7,11},{8,4},{9,5},... | collective-permute-start | bytes 30728 | tf_op jit(solution)/shard_map/ppermute | solution.py:404
  16.4 0.1 shard_map.80.refs_2_
  16.5 1.3 %collective-permute-done.5.other_ref = f32[4,640]{1,0:T(4,128)S(1)} collective-permute-done((f32[4,640]{1,0:T(4,128)S(1)}, f32[4,640]{1,0:T(4,128)S(1)}, u32[]{:S(2)}, u32[]{:S(2)}) %collective-permute-start.5) | collective-permute-done | bytes 10272 | tf_op jit(solution)/shard_map/ppermute | solution.py:404
  17.8 0.7 %shard_map.81 = f32[128,128]{1,0:T(8,128)} custom-call(f32[4,640]{1,0:T(4,128)S(1)} %get-tuple-element.36.own_ref, f32[4,640]{1,0:T(4,128)S(1)} %collective-permute-done.5.other_ref, f32[4,384]{1,0:T(4,128)S(1)} %get-tuple-element.38.refs_0_, f32[4,384]{1,0:T(4,128)S(1)} %get-tuple-element.39.refs_1_, f32[128,128]{1,0:T(8,128)S(1)} %shard_map.80.refs_2_, ...), custom_call_target="tpu_custom_call" | custom-call | flops 500000 | bytes 500000 | tf_op jit(solution)/shard_map/pallas_call | solution.py:460
  (3 shorter events, 0.0 us)
Async XLA Ops:
  1.6 3.8 %collective-permute-start = (f32[8,128]{1,0:T(8,128)S(1)}, f32[8,128]{1,0:T(8,128)S(1)}, u32[]{:S(2)}, u32[]{:S(2)}) collective-permute-start(f32[8,128]{1,0:T(8,128)S(1)} %get-tuple-element.24.first_ref.refs_0_), channel_id=1, source_target_pairs={{0,24},{1,25},{2,26},{3,27},{4,28},{5,29},{6,30},{7,31},{8,16},{9,... | collective-permute-start | bytes 12296 | tf_op jit(solution)/shard_map/ppermute | solution.py:404
  4.1 2.2 %collective-permute-start.2 = (f32[712,128]{1,0:T(8,128)S(1)}, f32[712,128]{1,0:T(8,128)S(1)}, u32[]{:S(2)}, u32[]{:S(2)}) collective-permute-start(f32[712,128]{1,0:T(8,128)S(1)} %get-tuple-element.25.block_ref), channel_id=1, source_target_pairs={{0,8},{1,9},{2,10},{3,11},{4,12},{5,13},{6,14},{7,15},{8,0},{9,1},... | collective-permute-start | bytes 1093640 | tf_op jit(solution)/shard_map/ppermute | solution.py:404
  5.4 1.5 %collective-permute-start.1 = (f32[16,128]{1,0:T(8,128)S(1)}, f32[16,128]{1,0:T(8,128)S(1)}, u32[]{:S(2)}, u32[]{:S(2)}) collective-permute-start(f32[16,128]{1,0:T(8,128)S(1)} %shard_map.74), channel_id=1, source_target_pairs={{0,8},{1,9},{2,10},{3,11},{4,12},{5,13},{6,14},{7,15},{8,0},{9,1},... | collective-permute-start | bytes 24584 | tf_op jit(solution)/shard_map/ppermute | solution.py:404
  7.1 3.2 %collective-permute-start.3 = (f32[4,640]{1,0:T(4,128)S(1)}, f32[4,640]{1,0:T(4,128)S(1)}, u32[]{:S(2)}, u32[]{:S(2)}) collective-permute-start(f32[4,640]{1,0:T(4,128)S(1)} %get-tuple-element.33), channel_id=1, source_target_pairs={{0,9},{1,8},{2,11},{3,10},{4,13},{5,12},{6,15},{7,14},{8,1},{9,0},... | collective-permute-start | bytes 30728 | tf_op jit(solution)/shard_map/ppermute | solution.py:404
  10.3 3.2 %collective-permute-start.4 = (f32[4,640]{1,0:T(4,128)S(1)}, f32[4,640]{1,0:T(4,128)S(1)}, u32[]{:S(2)}, u32[]{:S(2)}) collective-permute-start(f32[4,640]{1,0:T(4,128)S(1)} %get-tuple-element.35), channel_id=1, source_target_pairs={{0,10},{1,11},{2,8},{3,9},{4,14},{5,15},{6,12},{7,13},{8,2},{9,3},... | collective-permute-start | bytes 30728 | tf_op jit(solution)/shard_map/ppermute | solution.py:404
  13.6 4.2 %collective-permute-start.5 = (f32[4,640]{1,0:T(4,128)S(1)}, f32[4,640]{1,0:T(4,128)S(1)}, u32[]{:S(2)}, u32[]{:S(2)}) collective-permute-start(f32[4,640]{1,0:T(4,128)S(1)} %get-tuple-element.37), channel_id=1, source_target_pairs={{0,12},{1,13},{2,14},{3,15},{4,8},{5,9},{6,10},{7,11},{8,4},{9,5},... | collective-permute-start | bytes 30728 | tf_op jit(solution)/shard_map/ppermute | solution.py:404

commit v14 on v12

--- a/solution.py
+++ b/solution.py
@@ -189,8 +189,8 @@
         (immobile_hbm, immobile_ref), (mobile_hbm, mobile_ref), (across_hbm, block_ref.at[rows : 2 * rows, :]),
     )
     copies = [pltpu.make_async_copy(pair[0], pair[1], arrived.at[place]) for place, pair in enumerate(pairs)]
-    for copy in copies:
-        copy.start()
+    for place, copy in enumerate(copies):
+        copy.start(priority=int(place in (4, 6)))
     stride = LANES // SUBLANES
     for copy in copies[:3]:
         copy.wait()

time: 18.6 us -> 18.6 us (level)
  no operation moved by 1% of the time
where the time goes in v14:
time: 18.6 us; the launch traced here: 18.4 us
  starting transfers between devices  10.2 us (55%)
  waiting for transfers between devices  5.09 us (27%)
  Pallas kernels  3.05 us (16%)
    ppermute x6, starting transfers between devices, trade(): return lax.ppermute(value, ('xg', 'yd'), pairs)  10.2 us
    ppermute x6, waiting for transfers between devices, trade(): return lax.ppermute(value, ('xg', 'yd'), pairs)  5.09 us
    pallas_call x9, Pallas kernels, kernel_call(): pl.pallas_call(body, out_shape=outputs, in_specs=[pl.BlockSpec(memory_spa...  3.05 us
  transfers between devices with their start and end apart: 6, of which 5 were waited for; matrix products, arithmetic and copies ran while one was open for 0% of the time, Pallas kernels for 3%

profile of v14, /device:TPU:0, one launch (start us, length us, event | category | flops | bytes accessed | tf_op | source)
XLA Modules:
  0.0 18.4 jit_solution(4331598146915569589)
XLA Ops:
  0.0 1.6 %shard_map.73 = (f32[8,128]{1,0:T(8,128)S(1)}, f32[712,128]{1,0:T(8,128)S(1)}) custom-call(f32[128,128]{1,0:T(8,128)} %bitcast.9, f32[128,128]{1,0:T(8,128)} %bitcast.10, f32[128,128]{1,0:T(8,128)} %bitcast.11, f32[128,128]{1,0:T(8,128)} %bitcast.12, f32[512,128]{1,0:T(8,128)} %bitcast.8, f32[1,4]{1,0:T(1,128)} %bitcast.13, f32[1,4]{1,0:T(1,128)} %bitcast.14), custom_call_target="tpu_custom_call" | custom-call | flops 500000 | bytes 500000 | tf_op jit(solution)/shard_map/pallas_call | solution.py:463
  1.6 2.4 %collective-permute-start = (f32[8,128]{1,0:T(8,128)S(1)}, f32[8,128]{1,0:T(8,128)S(1)}, u32[]{:S(2)}, u32[]{:S(2)}) collective-permute-start(f32[8,128]{1,0:T(8,128)S(1)} %get-tuple-element.24.first_ref.refs_0_), channel_id=1, source_target_pairs={{0,24},{1,25},{2,26},{3,27},{4,28},{5,29},{6,30},{7,31},{8,16},{9,... | collective-permute-start | bytes 12296 | tf_op jit(solution)/shard_map/ppermute | solution.py:407
  4.0 0.7 %collective-permute-start.2 = (f32[712,128]{1,0:T(8,128)S(1)}, f32[712,128]{1,0:T(8,128)S(1)}, u32[]{:S(2)}, u32[]{:S(2)}) collective-permute-start(f32[712,128]{1,0:T(8,128)S(1)} %get-tuple-element.25.block_ref), channel_id=1, source_target_pairs={{0,8},{1,9},{2,10},{3,11},{4,12},{5,13},{6,14},{7,15},{8,0},{9,1},... | collective-permute-start | bytes 1093640 | tf_op jit(solution)/shard_map/ppermute | solution.py:407
  4.7 0.7 %collective-permute-done.second_ref.refs_1_ = f32[8,128]{1,0:T(8,128)S(1)} collective-permute-done((f32[8,128]{1,0:T(8,128)S(1)}, f32[8,128]{1,0:T(8,128)S(1)}, u32[]{:S(2)}, u32[]{:S(2)}) %collective-permute-start) | collective-permute-done | bytes 4128 | tf_op jit(solution)/shard_map/ppermute | solution.py:407
  5.4 0.6 %collective-permute-start.1 = (f32[16,128]{1,0:T(8,128)S(1)}, f32[16,128]{1,0:T(8,128)S(1)}, u32[]{:S(2)}, u32[]{:S(2)}) collective-permute-start(f32[16,128]{1,0:T(8,128)S(1)} %shard_map.74), channel_id=1, source_target_pairs={{0,8},{1,9},{2,10},{3,11},{4,12},{5,13},{6,14},{7,15},{8,0},{9,1},... | collective-permute-start | bytes 24584 | tf_op jit(solution)/shard_map/ppermute | solution.py:407
  6.0 0.2 %shard_map.75 = (f32[8,128]{1,0:T(8,128)S(1)}, f32[384,128]{1,0:T(8,128)S(1)}, f32[256,128]{1,0:T(8,128)S(1)}, f32[480,128]{1,0:T(8,128)S(1)}, f32[256,128]{1,0:T(8,128)S(1)}) custom-call(f32[712,128]{1,0:T(8,128)S(1)} %get-tuple-element.25.block_ref), custom_call_target="tpu_custom_call" | custom-call | flops 500000 | bytes 500000 | tf_op jit(solution)/shard_map/pallas_call | solution.py:463
  6.2 0.0 collective-permute-done.2.block_ref
  6.3 0.2 %shard_map.76 = (f32[8,128]{1,0:T(8,128)S(1)}, f32[384,128]{1,0:T(8,128)S(1)}, f32[256,128]{1,0:T(8,128)S(1)}) custom-call(f32[712,128]{1,0:T(8,128)S(1)} %collective-permute-done.2.block_ref), custom_call_target="tpu_custom_call" | custom-call | flops 500000 | bytes 500000 | tf_op jit(solution)/shard_map/pallas_call | solution.py:463
  6.5 0.4 %collective-permute-done.1.refs_2_ = f32[16,128]{1,0:T(8,128)S(1)} collective-permute-done((f32[16,128]{1,0:T(8,128)S(1)}, f32[16,128]{1,0:T(8,128)S(1)}, u32[]{:S(2)}, u32[]{:S(2)}) %collective-permute-start.1) | collective-permute-done | bytes 8224 | tf_op jit(solution)/shard_map/ppermute | solution.py:407
  6.8 0.2 %shard_map.77 = (f32[4,640]{1,0:T(4,128)S(1)}, f32[4,640]{1,0:T(4,128)S(1)}, f32[128,128]{1,0:T(8,128)S(1)}) custom-call(f32[8,128]{1,0:T(8,128)S(1)} %get-tuple-element.24.first_ref.refs_0_, f32[8,128]{1,0:T(8,128)S(1)} %collective-permute-done.second_ref.refs_1_, f32[16,128]{1,0:T(8,128)S(1)} %collective-permute-done.1.refs_2_, ...), custom_call_target="tpu_custom_call" | custom-call | flops 500000 | bytes 500000 | tf_op jit(solution)/shard_map/pallas_call | solution.py:463
  7.1 1.8 %collective-permute-start.3 = (f32[4,640]{1,0:T(4,128)S(1)}, f32[4,640]{1,0:T(4,128)S(1)}, u32[]{:S(2)}, u32[]{:S(2)}) collective-permute-start(f32[4,640]{1,0:T(4,128)S(1)} %get-tuple-element.33), channel_id=1, source_target_pairs={{0,9},{1,8},{2,11},{3,10},{4,13},{5,12},{6,15},{7,14},{8,1},{9,0},... | collective-permute-start | bytes 30728 | tf_op jit(solution)/shard_map/ppermute | solution.py:407
  8.9 1.4 %collective-permute-done.3.other_ref = f32[4,640]{1,0:T(4,128)S(1)} collective-permute-done((f32[4,640]{1,0:T(4,128)S(1)}, f32[4,640]{1,0:T(4,128)S(1)}, u32[]{:S(2)}, u32[]{:S(2)}) %collective-permute-start.3) | collective-permute-done | bytes 10272 | tf_op jit(solution)/shard_map/ppermute | solution.py:407
  10.3 1.8 %collective-permute-start.4 = (f32[4,640]{1,0:T(4,128)S(1)}, f32[4,640]{1,0:T(4,128)S(1)}, u32[]{:S(2)}, u32[]{:S(2)}) collective-permute-start(f32[4,640]{1,0:T(4,128)S(1)} %get-tuple-element.35), channel_id=1, source_target_pairs={{0,10},{1,11},{2,8},{3,9},{4,14},{5,15},{6,12},{7,13},{8,2},{9,3},... | collective-permute-start | bytes 30728 | tf_op jit(solution)/shard_map/ppermute | solution.py:407
  12.1 1.4 %collective-permute-done.4.other_ref = f32[4,640]{1,0:T(4,128)S(1)} collective-permute-done((f32[4,640]{1,0:T(4,128)S(1)}, f32[4,640]{1,0:T(4,128)S(1)}, u32[]{:S(2)}, u32[]{:S(2)}) %collective-permute-start.4) | collective-permute-done | bytes 10272 | tf_op jit(solution)/shard_map/ppermute | solution.py:407
  13.5 2.8 %collective-permute-start.5 = (f32[4,640]{1,0:T(4,128)S(1)}, f32[4,640]{1,0:T(4,128)S(1)}, u32[]{:S(2)}, u32[]{:S(2)}) collective-permute-start(f32[4,640]{1,0:T(4,128)S(1)} %get-tuple-element.37), channel_id=1, source_target_pairs={{0,12},{1,13},{2,14},{3,15},{4,8},{5,9},{6,10},{7,11},{8,4},{9,5},... | collective-permute-start | bytes 30728 | tf_op jit(solution)/shard_map/ppermute | solution.py:407
  16.3 0.1 shard_map.80.refs_2_
  16.4 1.3 %collective-permute-done.5.other_ref = f32[4,640]{1,0:T(4,128)S(1)} collective-permute-done((f32[4,640]{1,0:T(4,128)S(1)}, f32[4,640]{1,0:T(4,128)S(1)}, u32[]{:S(2)}, u32[]{:S(2)}) %collective-permute-start.5) | collective-permute-done | bytes 10272 | tf_op jit(solution)/shard_map/ppermute | solution.py:407
  17.7 0.7 %shard_map.81 = f32[128,128]{1,0:T(8,128)} custom-call(f32[4,640]{1,0:T(4,128)S(1)} %get-tuple-element.36.own_ref, f32[4,640]{1,0:T(4,128)S(1)} %collective-permute-done.5.other_ref, f32[4,384]{1,0:T(4,128)S(1)} %get-tuple-element.38.refs_0_, f32[4,384]{1,0:T(4,128)S(1)} %get-tuple-element.39.refs_1_, f32[128,128]{1,0:T(8,128)S(1)} %shard_map.80.refs_2_, ...), custom_call_target="tpu_custom_call" | custom-call | flops 500000 | bytes 500000 | tf_op jit(solution)/shard_map/pallas_call | solution.py:463
  (3 shorter events, 0.0 us)
Async XLA Ops:
  1.6 3.8 %collective-permute-start = (f32[8,128]{1,0:T(8,128)S(1)}, f32[8,128]{1,0:T(8,128)S(1)}, u32[]{:S(2)}, u32[]{:S(2)}) collective-permute-start(f32[8,128]{1,0:T(8,128)S(1)} %get-tuple-element.24.first_ref.refs_0_), channel_id=1, source_target_pairs={{0,24},{1,25},{2,26},{3,27},{4,28},{5,29},{6,30},{7,31},{8,16},{9,... | collective-permute-start | bytes 12296 | tf_op jit(solution)/shard_map/ppermute | solution.py:407
  4.0 2.2 %collective-permute-start.2 = (f32[712,128]{1,0:T(8,128)S(1)}, f32[712,128]{1,0:T(8,128)S(1)}, u32[]{:S(2)}, u32[]{:S(2)}) collective-permute-start(f32[712,128]{1,0:T(8,128)S(1)} %get-tuple-element.25.block_ref), channel_id=1, source_target_pairs={{0,8},{1,9},{2,10},{3,11},{4,12},{5,13},{6,14},{7,15},{8,0},{9,1},... | collective-permute-start | bytes 1093640 | tf_op jit(solution)/shard_map/ppermute | solution.py:407
  5.4 1.5 %collective-permute-start.1 = (f32[16,128]{1,0:T(8,128)S(1)}, f32[16,128]{1,0:T(8,128)S(1)}, u32[]{:S(2)}, u32[]{:S(2)}) collective-permute-start(f32[16,128]{1,0:T(8,128)S(1)} %shard_map.74), channel_id=1, source_target_pairs={{0,8},{1,9},{2,10},{3,11},{4,12},{5,13},{6,14},{7,15},{8,0},{9,1},... | collective-permute-start | bytes 24584 | tf_op jit(solution)/shard_map/ppermute | solution.py:407
  7.1 3.2 %collective-permute-start.3 = (f32[4,640]{1,0:T(4,128)S(1)}, f32[4,640]{1,0:T(4,128)S(1)}, u32[]{:S(2)}, u32[]{:S(2)}) collective-permute-start(f32[4,640]{1,0:T(4,128)S(1)} %get-tuple-element.33), channel_id=1, source_target_pairs={{0,9},{1,8},{2,11},{3,10},{4,13},{5,12},{6,15},{7,14},{8,1},{9,0},... | collective-permute-start | bytes 30728 | tf_op jit(solution)/shard_map/ppermute | solution.py:407
  10.3 3.2 %collective-permute-start.4 = (f32[4,640]{1,0:T(4,128)S(1)}, f32[4,640]{1,0:T(4,128)S(1)}, u32[]{:S(2)}, u32[]{:S(2)}) collective-permute-start(f32[4,640]{1,0:T(4,128)S(1)} %get-tuple-element.35), channel_id=1, source_target_pairs={{0,10},{1,11},{2,8},{3,9},{4,14},{5,15},{6,12},{7,13},{8,2},{9,3},... | collective-permute-start | bytes 30728 | tf_op jit(solution)/shard_map/ppermute | solution.py:407
  13.5 4.2 %collective-permute-start.5 = (f32[4,640]{1,0:T(4,128)S(1)}, f32[4,640]{1,0:T(4,128)S(1)}, u32[]{:S(2)}, u32[]{:S(2)}) collective-permute-start(f32[4,640]{1,0:T(4,128)S(1)} %get-tuple-element.37), channel_id=1, source_target_pairs={{0,12},{1,13},{2,14},{3,15},{4,8},{5,9},{6,10},{7,11},{8,4},{9,5},... | collective-permute-start | bytes 30728 | tf_op jit(solution)/shard_map/ppermute | solution.py:407

commit v15 on v14

--- a/solution.py
+++ b/solution.py
@@ -407,31 +407,9 @@
     return lax.ppermute(value, ("xg", "yd"), pairs)
 
 
-def pack_kernel(first_ref, second_ref, out_ref):
-    height = first_ref.shape[0]
-    out_ref[0:height, :] = first_ref[...]
-    out_ref[height:, :] = second_ref[...]
-
-
-def pack(first, second):
-    (packed,) = kernel_call(
-        pack_kernel, (first, second), [f32(first.shape[0] + second.shape[0], first.shape[1])], [], cost=10000000000
-    )
-    return packed
-
-
 def x_exchange(message):
-    held = message
-    pieces = [message]
-    order = [0]
-    for step in doubling(lax.axis_size("xg") // 2):
-        received = trade(held, 2 * step + 1, 0)
-        pieces.append(received)
-        order += [place ^ (2 * step + 1) for place in order]
-        held = pack(held, received)
-    pieces.append(trade(held, 1, 0))
-    order += [place ^ 1 for place in order]
-    return pieces, order
+    order = [0] + list(range(1, lax.axis_size("xg")))
+    return [message] + [trade(message, step, 0) for step in order[1:]], order
 
 
 def y_exchange(kept, sent):
@@ -507,7 +485,7 @@
         outputs = [held_f32(SUBLANES, LANES), held_f32(3 * LANES, rows), held_f32(2 * rows, LANES)]
         if own:
             outputs += [held_f32(3 * y_nodes * SUBLANES, LANES), held_f32(2 * rows, LANES)]
-        return kernel_call(functools.partial(prepare_kernel, halves), (part,), outputs, [])
+        return kernel_call(functools.partial(prepare_kernel, halves), (part,), outputs, [], cost=10000000000 if own else 500000)
 
     pieces, order = x_exchange(message)
     y_rows, lines_x, sums, y_state, spread = prepare(block, True)

time: 18.6 us -> 19.2 us (1.032)
  waiting for transfers between devices: 5.09 us -> 7.88 us
  starting transfers between devices: 10.2 us -> 8.04 us
    ppermute x6 -> x7, waiting for transfers between devices: 5.09 us -> 7.88 us  [trade(): return lax.ppermute(value, ('xg', 'yd'), pairs)]
    ppermute x6 -> x7, starting transfers between devices: 10.2 us -> 8.04 us  [trade(): return lax.ppermute(value, ('xg', 'yd'), pairs)]
    pallas_call x9 -> x8, Pallas kernels: 3.05 us -> 3.05 us  [kernel_call(): pl.pallas_call(body, out_shape=outputs, in_specs=[pl.BlockSpec(memory_spa...]
  transfers between devices with their start and end apart: 6 -> 7, of which waited for: 5 -> 5; matrix products, arithmetic and copies ran while one was open for 0% -> 0% of each run, Pallas kernels for 3% -> 3%
where the time goes in v15:
time: 19.2 us; the launch traced here: 19 us
  starting transfers between devices  8.04 us (42%)
  waiting for transfers between devices  7.88 us (41%)
  Pallas kernels  3.05 us (16%)
    ppermute x7, starting transfers between devices, trade(): return lax.ppermute(value, ('xg', 'yd'), pairs)  8.04 us
    ppermute x7, waiting for transfers between devices, trade(): return lax.ppermute(value, ('xg', 'yd'), pairs)  7.88 us
    pallas_call x8, Pallas kernels, kernel_call(): pl.pallas_call(body, out_shape=outputs, in_specs=[pl.BlockSpec(memory_spa...  3.05 us
  transfers between devices with their start and end apart: 7, of which 5 were waited for; matrix products, arithmetic and copies ran while one was open for 0% of the time, Pallas kernels for 3%

profile of v15, /device:TPU:0, one launch (start us, length us, event | category | flops | bytes accessed | tf_op | source)
XLA Modules:
  0.0 19.0 jit_solution(8394573556443948929)
XLA Ops:
  0.0 1.6 %shard_map.73 = (f32[8,128]{1,0:T(8,128)S(1)}, f32[712,128]{1,0:T(8,128)S(1)}) custom-call(f32[128,128]{1,0:T(8,128)} %bitcast.9, f32[128,128]{1,0:T(8,128)} %bitcast.10, f32[128,128]{1,0:T(8,128)} %bitcast.11, f32[128,128]{1,0:T(8,128)} %bitcast.12, f32[512,128]{1,0:T(8,128)} %bitcast.8, f32[1,4]{1,0:T(1,128)} %bitcast.13, f32[1,4]{1,0:T(1,128)} %bitcast.14), custom_call_target="tpu_custom_call" | custom-call | flops 500000 | bytes 500000 | tf_op jit(solution)/shard_map/pallas_call | solution.py:441
  1.6 2.4 %collective-permute-start.2 = (f32[8,128]{1,0:T(8,128)S(1)}, f32[8,128]{1,0:T(8,128)S(1)}, u32[]{:S(2)}, u32[]{:S(2)}) collective-permute-start(f32[8,128]{1,0:T(8,128)S(1)} %get-tuple-element.24.refs_0_), channel_id=1, source_target_pairs={{0,24},{1,25},{2,26},{3,27},{4,28},{5,29},{6,30},{7,31},{8,16},{9,... | collective-permute-start | bytes 12296 | tf_op jit(solution)/shard_map/ppermute | solution.py:407
  4.0 0.6 %collective-permute-start.1 = (f32[8,128]{1,0:T(8,128)S(1)}, f32[8,128]{1,0:T(8,128)S(1)}, u32[]{:S(2)}, u32[]{:S(2)}) collective-permute-start(f32[8,128]{1,0:T(8,128)S(1)} %get-tuple-element.24.refs_0_), channel_id=1, source_target_pairs={{0,16},{1,17},{2,18},{3,19},{4,20},{5,21},{6,22},{7,23},{8,24},{9,... | collective-permute-start | bytes 12296 | tf_op jit(solution)/shard_map/ppermute | solution.py:407
  4.7 0.0 collective-permute-start
  4.7 0.5 %collective-permute-start.3 = (f32[712,128]{1,0:T(8,128)S(1)}, f32[712,128]{1,0:T(8,128)S(1)}, u32[]{:S(2)}, u32[]{:S(2)}) collective-permute-start(f32[712,128]{1,0:T(8,128)S(1)} %get-tuple-element.25.block_ref), channel_id=1, source_target_pairs={{0,8},{1,9},{2,10},{3,11},{4,12},{5,13},{6,14},{7,15},{8,0},{9,1},... | collective-permute-start | bytes 1093640 | tf_op jit(solution)/shard_map/ppermute | solution.py:407
  5.2 0.2 %shard_map.74 = (f32[8,128]{1,0:T(8,128)S(1)}, f32[384,128]{1,0:T(8,128)S(1)}, f32[256,128]{1,0:T(8,128)S(1)}, f32[480,128]{1,0:T(8,128)S(1)}, f32[256,128]{1,0:T(8,128)S(1)}) custom-call(f32[712,128]{1,0:T(8,128)S(1)} %get-tuple-element.25.block_ref), custom_call_target="tpu_custom_call" | custom-call | flops 10000000000 | bytes 10000000000 | tf_op jit(solution)/shard_map/pallas_call | solution.py:441
  5.4 1.1 %collective-permute-done.3.block_ref = f32[712,128]{1,0:T(8,128)S(1)} collective-permute-done((f32[712,128]{1,0:T(8,128)S(1)}, f32[712,128]{1,0:T(8,128)S(1)}, u32[]{:S(2)}, u32[]{:S(2)}) %collective-permute-start.3) | collective-permute-done | bytes 364576 | tf_op jit(solution)/shard_map/ppermute | solution.py:407
  6.5 0.2 %shard_map.75 = (f32[8,128]{1,0:T(8,128)S(1)}, f32[384,128]{1,0:T(8,128)S(1)}, f32[256,128]{1,0:T(8,128)S(1)}) custom-call(f32[712,128]{1,0:T(8,128)S(1)} %collective-permute-done.3.block_ref), custom_call_target="tpu_custom_call" | custom-call | flops 500000 | bytes 500000 | tf_op jit(solution)/shard_map/pallas_call | solution.py:441
  6.7 0.0 collective-permute-done.2.refs_3_
  6.7 0.9 %collective-permute-done.1.refs_2_ = f32[8,128]{1,0:T(8,128)S(1)} collective-permute-done((f32[8,128]{1,0:T(8,128)S(1)}, f32[8,128]{1,0:T(8,128)S(1)}, u32[]{:S(2)}, u32[]{:S(2)}) %collective-permute-start.1) | collective-permute-done | bytes 4128 | tf_op jit(solution)/shard_map/ppermute | solution.py:407
  7.6 0.0 collective-permute-done.refs_1_
  7.6 0.2 %shard_map.76 = (f32[4,640]{1,0:T(4,128)S(1)}, f32[4,640]{1,0:T(4,128)S(1)}, f32[128,128]{1,0:T(8,128)S(1)}) custom-call(f32[8,128]{1,0:T(8,128)S(1)} %get-tuple-element.24.refs_0_, f32[8,128]{1,0:T(8,128)S(1)} %collective-permute-done.refs_1_, f32[8,128]{1,0:T(8,128)S(1)} %collective-permute-done.1.refs_2_, f32[8,128]{1,0:T(8,128)S(1)} %collective-permute-done.2.refs_3_, ...), custom_call_target="tpu_custom_call" | custom-call | flops 500000 | bytes 500000 | tf_op jit(solution)/shard_map/pallas_call | solution.py:441
  7.9 0.7 %collective-permute-start.4 = (f32[4,640]{1,0:T(4,128)S(1)}, f32[4,640]{1,0:T(4,128)S(1)}, u32[]{:S(2)}, u32[]{:S(2)}) collective-permute-start(f32[4,640]{1,0:T(4,128)S(1)} %get-tuple-element.33), channel_id=1, source_target_pairs={{0,9},{1,8},{2,11},{3,10},{4,13},{5,12},{6,15},{7,14},{8,1},{9,0},... | collective-permute-start | bytes 30728 | tf_op jit(solution)/shard_map/ppermute | solution.py:407
  8.6 2.5 %collective-permute-done.4.other_ref = f32[4,640]{1,0:T(4,128)S(1)} collective-permute-done((f32[4,640]{1,0:T(4,128)S(1)}, f32[4,640]{1,0:T(4,128)S(1)}, u32[]{:S(2)}, u32[]{:S(2)}) %collective-permute-start.4) | collective-permute-done | bytes 10272 | tf_op jit(solution)/shard_map/ppermute | solution.py:407
  11.1 1.4 %collective-permute-start.5 = (f32[4,640]{1,0:T(4,128)S(1)}, f32[4,640]{1,0:T(4,128)S(1)}, u32[]{:S(2)}, u32[]{:S(2)}) collective-permute-start(f32[4,640]{1,0:T(4,128)S(1)} %get-tuple-element.35), channel_id=1, source_target_pairs={{0,10},{1,11},{2,8},{3,9},{4,14},{5,15},{6,12},{7,13},{8,2},{9,3},... | collective-permute-start | bytes 30728 | tf_op jit(solution)/shard_map/ppermute | solution.py:407
  12.5 1.8 %collective-permute-done.5.other_ref = f32[4,640]{1,0:T(4,128)S(1)} collective-permute-done((f32[4,640]{1,0:T(4,128)S(1)}, f32[4,640]{1,0:T(4,128)S(1)}, u32[]{:S(2)}, u32[]{:S(2)}) %collective-permute-start.5) | collective-permute-done | bytes 10272 | tf_op jit(solution)/shard_map/ppermute | solution.py:407
  14.3 2.4 %collective-permute-start.6 = (f32[4,640]{1,0:T(4,128)S(1)}, f32[4,640]{1,0:T(4,128)S(1)}, u32[]{:S(2)}, u32[]{:S(2)}) collective-permute-start(f32[4,640]{1,0:T(4,128)S(1)} %get-tuple-element.37), channel_id=1, source_target_pairs={{0,12},{1,13},{2,14},{3,15},{4,8},{5,9},{6,10},{7,11},{8,4},{9,5},... | collective-permute-start | bytes 30728 | tf_op jit(solution)/shard_map/ppermute | solution.py:407
  16.7 0.1 shard_map.79.refs_2_
  16.7 1.6 %collective-permute-done.6.other_ref = f32[4,640]{1,0:T(4,128)S(1)} collective-permute-done((f32[4,640]{1,0:T(4,128)S(1)}, f32[4,640]{1,0:T(4,128)S(1)}, u32[]{:S(2)}, u32[]{:S(2)}) %collective-permute-start.6) | collective-permute-done | bytes 10272 | tf_op jit(solution)/shard_map/ppermute | solution.py:407
  18.3 0.7 %shard_map.80 = f32[128,128]{1,0:T(8,128)} custom-call(f32[4,640]{1,0:T(4,128)S(1)} %get-tuple-element.36.own_ref, f32[4,640]{1,0:T(4,128)S(1)} %collective-permute-done.6.other_ref, f32[4,384]{1,0:T(4,128)S(1)} %get-tuple-element.38.refs_0_, f32[4,384]{1,0:T(4,128)S(1)} %get-tuple-element.39.refs_1_, f32[128,128]{1,0:T(8,128)S(1)} %shard_map.79.refs_2_, ...), custom_call_target="tpu_custom_call" | custom-call | flops 500000 | bytes 500000 | tf_op jit(solution)/shard_map/pallas_call | solution.py:441
  (2 shorter events, 0.0 us)
Async XLA Ops:
  1.6 5.1 %collective-permute-start.2 = (f32[8,128]{1,0:T(8,128)S(1)}, f32[8,128]{1,0:T(8,128)S(1)}, u32[]{:S(2)}, u32[]{:S(2)}) collective-permute-start(f32[8,128]{1,0:T(8,128)S(1)} %get-tuple-element.24.refs_0_), channel_id=1, source_target_pairs={{0,24},{1,25},{2,26},{3,27},{4,28},{5,29},{6,30},{7,31},{8,16},{9,... | collective-permute-start | bytes 12296 | tf_op jit(solution)/shard_map/ppermute | solution.py:407
  4.0 3.6 %collective-permute-start.1 = (f32[8,128]{1,0:T(8,128)S(1)}, f32[8,128]{1,0:T(8,128)S(1)}, u32[]{:S(2)}, u32[]{:S(2)}) collective-permute-start(f32[8,128]{1,0:T(8,128)S(1)} %get-tuple-element.24.refs_0_), channel_id=1, source_target_pairs={{0,16},{1,17},{2,18},{3,19},{4,20},{5,21},{6,22},{7,23},{8,24},{9,... | collective-permute-start | bytes 12296 | tf_op jit(solution)/shard_map/ppermute | solution.py:407
  4.7 3.0 %collective-permute-start = (f32[8,128]{1,0:T(8,128)S(1)}, f32[8,128]{1,0:T(8,128)S(1)}, u32[]{:S(2)}, u32[]{:S(2)}) collective-permute-start(f32[8,128]{1,0:T(8,128)S(1)} %get-tuple-element.24.refs_0_), channel_id=1, source_target_pairs={{0,8},{1,9},{2,10},{3,11},{4,12},{5,13},{6,14},{7,15},{8,0},{9,1},... | collective-permute-start | bytes 12296 | tf_op jit(solution)/shard_map/ppermute | solution.py:407
  4.7 1.8 %collective-permute-start.3 = (f32[712,128]{1,0:T(8,128)S(1)}, f32[712,128]{1,0:T(8,128)S(1)}, u32[]{:S(2)}, u32[]{:S(2)}) collective-permute-start(f32[712,128]{1,0:T(8,128)S(1)} %get-tuple-element.25.block_ref), channel_id=1, source_target_pairs={{0,8},{1,9},{2,10},{3,11},{4,12},{5,13},{6,14},{7,15},{8,0},{9,1},... | collective-permute-start | bytes 1093640 | tf_op jit(solution)/shard_map/ppermute | solution.py:407
  7.9 3.2 %collective-permute-start.4 = (f32[4,640]{1,0:T(4,128)S(1)}, f32[4,640]{1,0:T(4,128)S(1)}, u32[]{:S(2)}, u32[]{:S(2)}) collective-permute-start(f32[4,640]{1,0:T(4,128)S(1)} %get-tuple-element.33), channel_id=1, source_target_pairs={{0,9},{1,8},{2,11},{3,10},{4,13},{5,12},{6,15},{7,14},{8,1},{9,0},... | collective-permute-start | bytes 30728 | tf_op jit(solution)/shard_map/ppermute | solution.py:407
  11.1 3.2 %collective-permute-start.5 = (f32[4,640]{1,0:T(4,128)S(1)}, f32[4,640]{1,0:T(4,128)S(1)}, u32[]{:S(2)}, u32[]{:S(2)}) collective-permute-start(f32[4,640]{1,0:T(4,128)S(1)} %get-tuple-element.35), channel_id=1, source_target_pairs={{0,10},{1,11},{2,8},{3,9},{4,14},{5,15},{6,12},{7,13},{8,2},{9,3},... | collective-permute-start | bytes 30728 | tf_op jit(solution)/shard_map/ppermute | solution.py:407
  14.3 4.1 %collective-permute-start.6 = (f32[4,640]{1,0:T(4,128)S(1)}, f32[4,640]{1,0:T(4,128)S(1)}, u32[]{:S(2)}, u32[]{:S(2)}) collective-permute-start(f32[4,640]{1,0:T(4,128)S(1)} %get-tuple-element.37), channel_id=1, source_target_pairs={{0,12},{1,13},{2,14},{3,15},{4,8},{5,9},{6,10},{7,11},{8,4},{9,5},... | collective-permute-start | bytes 30728 | tf_op jit(solution)/shard_map/ppermute | solution.py:407

commit v16 on v15

--- a/solution.py
+++ b/solution.py
@@ -221,6 +221,7 @@
             start += SUBLANES
     for row, value in enumerate(piece + side):
         message_ref[row : row + 1, :] = value[0:1, :]
+        block_ref[start + row : start + row + 1, :] = value[0:1, :]
     copies[6].wait()
 
 
@@ -229,12 +230,15 @@
     return ((one, nothing), (nothing, one))
 
 
-def prepare_kernel(halves, block_ref, rows_ref, lines_ref, sums_ref, *own_refs):
+def prepare_kernel(halves, own, block_ref, rows_ref, lines_ref, sums_ref, *extra_refs):
     rows = rows_ref.shape[1]
     stride = LANES // SUBLANES
     rolls = x_rolls(halves)
     total = stride - 1 + len(rolls)
     nodes = state_parts(block_ref.at[2 * rows :, :], 0, total, 3)
+    own_refs = extra_refs if own else ()
+    if not own:
+        extra_refs[0][...] = block_ref[-SUBLANES:, :]
     nothing = jnp.zeros((SUBLANES, rows), jnp.float32)
     cases = [((nothing, nothing), [node[2] for node in nodes])]
     cases += [(ends, [0.0] * total) for ends in ends_responses((SUBLANES, rows))]
@@ -298,10 +302,10 @@
 
 
 def x_back_kernel(halves, axis, order, pieces, *refs):
-    slots = message_slots(refs[:pieces], SUBLANES, 1, 1, [0] * len(order))
+    lines_refs, sums_refs, rows_refs = (refs[pieces + 2 * pair : pieces + 2 * pair + 2] for pair in range(3))
+    last_ref, kept_ref, sent_ref, values_ref = refs[pieces + 6 :]
+    slots = message_slots([*refs[:pieces], last_ref], SUBLANES, 1, 1, [0] * len(order))
     slots = [slots[order.index(place)] for place in range(len(order))]
-    lines_refs, sums_refs, rows_refs = (refs[pieces + 2 * pair : pieces + 2 * pair + 2] for pair in range(3))
-    kept_ref, sent_ref, values_ref = refs[pieces + 6 :]
     bounds = ring_bounds(slots, lax.axis_index(axis))
     rows = values_ref.shape[0]
 
@@ -407,9 +411,22 @@
     return lax.ppermute(value, ("xg", "yd"), pairs)
 
 
-def x_exchange(message):
-    order = [0] + list(range(1, lax.axis_size("xg")))
-    return [message] + [trade(message, step, 0) for step in order[1:]], order
+def x_exchange(message, block):
+    count = lax.axis_size("xg")
+    held = message
+    pieces = [message]
+    order = [0]
+    other_block = trade(block, 1, 0)
+    for step in doubling(count // 2):
+        received = trade(held, 2 * step + 1, 0)
+        pieces.append(received)
+        order += [place ^ (2 * step + 1) for place in order]
+        if 4 * step < count:
+            held = jnp.concatenate([held, received], axis=0)
+    received = pieces[1] if len(pieces) == 2 else jnp.concatenate(pieces[1:], axis=0)
+    pieces.append(trade(received, 1, 0))
+    order += [place ^ 1 for place in order[1:]] + [1]
+    return pieces, order, other_block
 
 
 def y_exchange(kept, sent):
@@ -473,7 +490,7 @@
                 mobile, dispersion_x, dispersion_y, capacity, immobile, exchange_rates[None], rate_shares[None],
             )
         ),
-        [f32(SUBLANES, rows), held_f32(2 * rows + 3 * x_nodes * SUBLANES, LANES)],
+        [f32(SUBLANES, rows), held_f32(2 * rows + (3 * x_nodes + 1) * SUBLANES, LANES)],
         [square] * 3
         + [VMEM((zones * rows, LANES), jnp.float32)]
         + [VMEM((1, zones), jnp.float32)] * 2
@@ -485,14 +502,16 @@
         outputs = [held_f32(SUBLANES, LANES), held_f32(3 * LANES, rows), held_f32(2 * rows, LANES)]
         if own:
             outputs += [held_f32(3 * y_nodes * SUBLANES, LANES), held_f32(2 * rows, LANES)]
-        return kernel_call(functools.partial(prepare_kernel, halves), (part,), outputs, [], cost=10000000000 if own else 500000)
-
-    pieces, order = x_exchange(message)
+        else:
+            outputs += [held_f32(SUBLANES, rows)]
+        return kernel_call(functools.partial(prepare_kernel, halves, own), (part,), outputs, [], cost=10000000000)
+
+    pieces, order, other_block = x_exchange(message, block)
     y_rows, lines_x, sums, y_state, spread = prepare(block, True)
-    other_rows, other_lines, other_sums = prepare(trade(block, 1, 0), False)
+    other_rows, other_lines, other_sums, other_message = prepare(other_block, False)
     kept, sent, values = kernel_call(
         functools.partial(x_back_kernel, halves, "xg", order, len(pieces)),
-        (*pieces, lines_x, other_lines, sums, other_sums, y_rows, other_rows),
+        (*pieces, lines_x, other_lines, sums, other_sums, y_rows, other_rows, other_message),
         [
             held_f32(2 * halves, QUANTITIES * LANES),
             f32(2 * halves, QUANTITIES * LANES),

time: 19.2 us -> 18.5 us (0.964)
  waiting for transfers between devices: 7.88 us -> 5.08 us
  starting transfers between devices: 8.04 us -> 10.2 us
    ppermute x7 -> x6, waiting for transfers between devices: 7.88 us -> 5.08 us  [trade(): return lax.ppermute(value, ('xg', 'yd'), pairs)]
    ppermute x7 -> x6, starting transfers between devices: 8.04 us -> 10.2 us  [trade(): return lax.ppermute(value, ('xg', 'yd'), pairs)]
  transfers between devices with their start and end apart: 7 -> 6, of which waited for: 5 -> 5; matrix products, arithmetic and copies ran while one was open for 0% -> 0% of each run, Pallas kernels for 3% -> 3%
where the time goes in v16:
time: 18.5 us; the launch traced here: 18.4 us
  starting transfers between devices  10.2 us (55%)
  waiting for transfers between devices  5.08 us (27%)
  Pallas kernels  3.05 us (16%)
    ppermute x6, starting transfers between devices, trade(): return lax.ppermute(value, ('xg', 'yd'), pairs)  10.2 us
    ppermute x6, waiting for transfers between devices, trade(): return lax.ppermute(value, ('xg', 'yd'), pairs)  5.08 us
    pallas_call x8, Pallas kernels, kernel_call(): pl.pallas_call(body, out_shape=outputs, in_specs=[pl.BlockSpec(memory_spa...  3.05 us
  transfers between devices with their start and end apart: 6, of which 5 were waited for; matrix products, arithmetic and copies ran while one was open for 0% of the time, Pallas kernels for 3%

profile of v16, /device:TPU:0, one launch (start us, length us, event | category | flops | bytes accessed | tf_op | source)
XLA Modules:
  0.0 18.4 jit_solution(1580291021105103831)
XLA Ops:
  0.0 1.6 %shard_map.73 = (f32[8,128]{1,0:T(8,128)S(1)}, f32[720,128]{1,0:T(8,128)S(1)}) custom-call(f32[128,128]{1,0:T(8,128)} %bitcast.9, f32[128,128]{1,0:T(8,128)} %bitcast.10, f32[128,128]{1,0:T(8,128)} %bitcast.11, f32[128,128]{1,0:T(8,128)} %bitcast.12, f32[512,128]{1,0:T(8,128)} %bitcast.8, f32[1,4]{1,0:T(1,128)} %bitcast.13, f32[1,4]{1,0:T(1,128)} %bitcast.14), custom_call_target="tpu_custom_call" | custom-call | flops 500000 | bytes 500000 | tf_op jit(solution)/shard_map/pallas_call | solution.py:458
  1.6 2.4 %collective-permute-start = (f32[8,128]{1,0:T(8,128)S(1)}, f32[8,128]{1,0:T(8,128)S(1)}, u32[]{:S(2)}, u32[]{:S(2)}) collective-permute-start(f32[8,128]{1,0:T(8,128)S(1)} %get-tuple-element.25.refs_0_), channel_id=1, source_target_pairs={{0,24},{1,25},{2,26},{3,27},{4,28},{5,29},{6,30},{7,31},{8,16},{9,... | collective-permute-start | bytes 12296 | tf_op jit(solution)/shard_map/ppermute | solution.py:411
  4.0 0.7 %collective-permute-start.2 = (f32[720,128]{1,0:T(8,128)S(1)}, f32[720,128]{1,0:T(8,128)S(1)}, u32[]{:S(2)}, u32[]{:S(2)}) collective-permute-start(f32[720,128]{1,0:T(8,128)S(1)} %get-tuple-element.26.block_ref), channel_id=1, source_target_pairs={{0,8},{1,9},{2,10},{3,11},{4,12},{5,13},{6,14},{7,15},{8,0},{9,1},... | collective-permute-start | bytes 1105928 | tf_op jit(solution)/shard_map/ppermute | solution.py:411
  4.7 0.2 %shard_map.74 = (f32[8,128]{1,0:T(8,128)S(1)}, f32[384,128]{1,0:T(8,128)S(1)}, f32[256,128]{1,0:T(8,128)S(1)}, f32[480,128]{1,0:T(8,128)S(1)}, f32[256,128]{1,0:T(8,128)S(1)}) custom-call(f32[720,128]{1,0:T(8,128)S(1)} %get-tuple-element.26.block_ref), custom_call_target="tpu_custom_call" | custom-call | flops 10000000000 | bytes 10000000000 | tf_op jit(solution)/shard_map/pallas_call | solution.py:458
  5.0 0.4 %collective-permute-done.refs_1_ = f32[8,128]{1,0:T(8,128)S(1)} collective-permute-done((f32[8,128]{1,0:T(8,128)S(1)}, f32[8,128]{1,0:T(8,128)S(1)}, u32[]{:S(2)}, u32[]{:S(2)}) %collective-permute-start) | collective-permute-done | bytes 4128 | tf_op jit(solution)/shard_map/ppermute | solution.py:411
  5.4 0.6 %collective-permute-start.1 = (f32[8,128]{1,0:T(8,128)S(1)}, f32[8,128]{1,0:T(8,128)S(1)}, u32[]{:S(2)}, u32[]{:S(2)}) collective-permute-start(f32[8,128]{1,0:T(8,128)S(1)} %collective-permute-done.refs_1_), channel_id=1, source_target_pairs={{0,8},{1,9},{2,10},{3,11},{4,12},{5,13},{6,14},{7,15},{8,0},{9,1},... | collective-permute-start | bytes 12296 | tf_op jit(solution)/shard_map/ppermute | solution.py:411
  6.0 0.0 collective-permute-done.2.block_ref
  6.0 0.2 %shard_map.75 = (f32[8,128]{1,0:T(8,128)S(1)}, f32[384,128]{1,0:T(8,128)S(1)}, f32[256,128]{1,0:T(8,128)S(1)}, f32[8,128]{1,0:T(8,128)S(1)}) custom-call(f32[720,128]{1,0:T(8,128)S(1)} %collective-permute-done.2.block_ref), custom_call_target="tpu_custom_call" | custom-call | flops 10000000000 | bytes 10000000000 | tf_op jit(solution)/shard_map/pallas_call | solution.py:458
  6.2 0.6 %collective-permute-done.1.refs_2_ = f32[8,128]{1,0:T(8,128)S(1)} collective-permute-done((f32[8,128]{1,0:T(8,128)S(1)}, f32[8,128]{1,0:T(8,128)S(1)}, u32[]{:S(2)}, u32[]{:S(2)}) %collective-permute-start.1) | collective-permute-done | bytes 4128 | tf_op jit(solution)/shard_map/ppermute | solution.py:411
  6.8 0.2 %shard_map.76 = (f32[4,640]{1,0:T(4,128)S(1)}, f32[4,640]{1,0:T(4,128)S(1)}, f32[128,128]{1,0:T(8,128)S(1)}) custom-call(f32[8,128]{1,0:T(8,128)S(1)} %get-tuple-element.25.refs_0_, f32[8,128]{1,0:T(8,128)S(1)} %collective-permute-done.refs_1_, f32[8,128]{1,0:T(8,128)S(1)} %collective-permute-done.1.refs_2_, f32[384,128]{1,0:T(8,128)S(1)} %get-tuple-element.27.refs_3_, ...), custom_call_target="tpu_custom_call" | custom-call | flops 500000 | bytes 500000 | tf_op jit(solution)/shard_map/pallas_call | solution.py:458
  7.1 1.8 %collective-permute-start.3 = (f32[4,640]{1,0:T(4,128)S(1)}, f32[4,640]{1,0:T(4,128)S(1)}, u32[]{:S(2)}, u32[]{:S(2)}) collective-permute-start(f32[4,640]{1,0:T(4,128)S(1)} %get-tuple-element.35), channel_id=1, source_target_pairs={{0,9},{1,8},{2,11},{3,10},{4,13},{5,12},{6,15},{7,14},{8,1},{9,0},... | collective-permute-start | bytes 30728 | tf_op jit(solution)/shard_map/ppermute | solution.py:411
  8.9 1.4 %collective-permute-done.3.other_ref = f32[4,640]{1,0:T(4,128)S(1)} collective-permute-done((f32[4,640]{1,0:T(4,128)S(1)}, f32[4,640]{1,0:T(4,128)S(1)}, u32[]{:S(2)}, u32[]{:S(2)}) %collective-permute-start.3) | collective-permute-done | bytes 10272 | tf_op jit(solution)/shard_map/ppermute | solution.py:411
  10.3 1.8 %collective-permute-start.4 = (f32[4,640]{1,0:T(4,128)S(1)}, f32[4,640]{1,0:T(4,128)S(1)}, u32[]{:S(2)}, u32[]{:S(2)}) collective-permute-start(f32[4,640]{1,0:T(4,128)S(1)} %get-tuple-element.37), channel_id=1, source_target_pairs={{0,10},{1,11},{2,8},{3,9},{4,14},{5,15},{6,12},{7,13},{8,2},{9,3},... | collective-permute-start | bytes 30728 | tf_op jit(solution)/shard_map/ppermute | solution.py:411
  12.1 1.4 %collective-permute-done.4.other_ref = f32[4,640]{1,0:T(4,128)S(1)} collective-permute-done((f32[4,640]{1,0:T(4,128)S(1)}, f32[4,640]{1,0:T(4,128)S(1)}, u32[]{:S(2)}, u32[]{:S(2)}) %collective-permute-start.4) | collective-permute-done | bytes 10272 | tf_op jit(solution)/shard_map/ppermute | solution.py:411
  13.5 2.8 %collective-permute-start.5 = (f32[4,640]{1,0:T(4,128)S(1)}, f32[4,640]{1,0:T(4,128)S(1)}, u32[]{:S(2)}, u32[]{:S(2)}) collective-permute-start(f32[4,640]{1,0:T(4,128)S(1)} %get-tuple-element.39), channel_id=1, source_target_pairs={{0,12},{1,13},{2,14},{3,15},{4,8},{5,9},{6,10},{7,11},{8,4},{9,5},... | collective-permute-start | bytes 30728 | tf_op jit(solution)/shard_map/ppermute | solution.py:411
  16.3 0.1 shard_map.79.refs_2_
  16.4 1.3 %collective-permute-done.5.other_ref = f32[4,640]{1,0:T(4,128)S(1)} collective-permute-done((f32[4,640]{1,0:T(4,128)S(1)}, f32[4,640]{1,0:T(4,128)S(1)}, u32[]{:S(2)}, u32[]{:S(2)}) %collective-permute-start.5) | collective-permute-done | bytes 10272 | tf_op jit(solution)/shard_map/ppermute | solution.py:411
  17.7 0.7 %shard_map.80 = f32[128,128]{1,0:T(8,128)} custom-call(f32[4,640]{1,0:T(4,128)S(1)} %get-tuple-element.38.own_ref, f32[4,640]{1,0:T(4,128)S(1)} %collective-permute-done.5.other_ref, f32[4,384]{1,0:T(4,128)S(1)} %get-tuple-element.40.refs_0_, f32[4,384]{1,0:T(4,128)S(1)} %get-tuple-element.41.refs_1_, f32[128,128]{1,0:T(8,128)S(1)} %shard_map.79.refs_2_, ...), custom_call_target="tpu_custom_call" | custom-call | flops 500000 | bytes 500000 | tf_op jit(solution)/shard_map/pallas_call | solution.py:458
  (2 shorter events, 0.0 us)
Async XLA Ops:
  1.6 3.8 %collective-permute-start = (f32[8,128]{1,0:T(8,128)S(1)}, f32[8,128]{1,0:T(8,128)S(1)}, u32[]{:S(2)}, u32[]{:S(2)}) collective-permute-start(f32[8,128]{1,0:T(8,128)S(1)} %get-tuple-element.25.refs_0_), channel_id=1, source_target_pairs={{0,24},{1,25},{2,26},{3,27},{4,28},{5,29},{6,30},{7,31},{8,16},{9,... | collective-permute-start | bytes 12296 | tf_op jit(solution)/shard_map/ppermute | solution.py:411
  4.0 2.0 %collective-permute-start.2 = (f32[720,128]{1,0:T(8,128)S(1)}, f32[720,128]{1,0:T(8,128)S(1)}, u32[]{:S(2)}, u32[]{:S(2)}) collective-permute-start(f32[720,128]{1,0:T(8,128)S(1)} %get-tuple-element.26.block_ref), channel_id=1, source_target_pairs={{0,8},{1,9},{2,10},{3,11},{4,12},{5,13},{6,14},{7,15},{8,0},{9,1},... | collective-permute-start | bytes 1105928 | tf_op jit(solution)/shard_map/ppermute | solution.py:411
  5.4 1.5 %collective-permute-start.1 = (f32[8,128]{1,0:T(8,128)S(1)}, f32[8,128]{1,0:T(8,128)S(1)}, u32[]{:S(2)}, u32[]{:S(2)}) collective-permute-start(f32[8,128]{1,0:T(8,128)S(1)} %collective-permute-done.refs_1_), channel_id=1, source_target_pairs={{0,8},{1,9},{2,10},{3,11},{4,12},{5,13},{6,14},{7,15},{8,0},{9,1},... | collective-permute-start | bytes 12296 | tf_op jit(solution)/shard_map/ppermute | solution.py:411
  7.1 3.2 %collective-permute-start.3 = (f32[4,640]{1,0:T(4,128)S(1)}, f32[4,640]{1,0:T(4,128)S(1)}, u32[]{:S(2)}, u32[]{:S(2)}) collective-permute-start(f32[4,640]{1,0:T(4,128)S(1)} %get-tuple-element.35), channel_id=1, source_target_pairs={{0,9},{1,8},{2,11},{3,10},{4,13},{5,12},{6,15},{7,14},{8,1},{9,0},... | collective-permute-start | bytes 30728 | tf_op jit(solution)/shard_map/ppermute | solution.py:411
  10.3 3.2 %collective-permute-start.4 = (f32[4,640]{1,0:T(4,128)S(1)}, f32[4,640]{1,0:T(4,128)S(1)}, u32[]{:S(2)}, u32[]{:S(2)}) collective-permute-start(f32[4,640]{1,0:T(4,128)S(1)} %get-tuple-element.37), channel_id=1, source_target_pairs={{0,10},{1,11},{2,8},{3,9},{4,14},{5,15},{6,12},{7,13},{8,2},{9,3},... | collective-permute-start | bytes 30728 | tf_op jit(solution)/shard_map/ppermute | solution.py:411
  13.5 4.2 %collective-permute-start.5 = (f32[4,640]{1,0:T(4,128)S(1)}, f32[4,640]{1,0:T(4,128)S(1)}, u32[]{:S(2)}, u32[]{:S(2)}) collective-permute-start(f32[4,640]{1,0:T(4,128)S(1)} %get-tuple-element.39), channel_id=1, source_target_pairs={{0,12},{1,13},{2,14},{3,15},{4,8},{5,9},{6,10},{7,11},{8,4},{9,5},... | collective-permute-start | bytes 30728 | tf_op jit(solution)/shard_map/ppermute | solution.py:411

commit v17 on v16

--- a/solution.py
+++ b/solution.py
@@ -160,9 +160,13 @@
     return bounds
 
 
-def capacity_weights(rates, shares):
-    weights = shares * rates / (1.0 + rates)
-    return [weights[:, zone : zone + 1] for zone in range(weights.shape[1])]
+def capacity_weights(rates_ref, shares_ref):
+    weights = []
+    for zone in range(rates_ref.shape[1]):
+        rate = jnp.full((SUBLANES, LANES), rates_ref[0, zone], jnp.float32)
+        share = jnp.full((SUBLANES, LANES), shares_ref[0, zone], jnp.float32)
+        weights.append((share * rate / (1.0 + rate))[0:1, :])
+    return weights
 
 
 def strided(ref, start, size, stride):
@@ -194,7 +198,7 @@
     stride = LANES // SUBLANES
     for copy in copies[:3]:
         copy.wait()
-    weights = capacity_weights(rates_ref[...], shares_ref[...])
+    weights = capacity_weights(rates_ref, shares_ref)
     capacity = capacity_ref[...]
     storage = 1.0 + capacity * sum(weights[1:], weights[0])
     block_ref[0:rows, :] = storage
@@ -231,7 +235,7 @@
 
 
 def prepare_kernel(halves, own, block_ref, rows_ref, lines_ref, sums_ref, *extra_refs):
-    rows = rows_ref.shape[1]
+    rows = lines_ref.shape[1]
     stride = LANES // SUBLANES
     rolls = x_rolls(halves)
     total = stride - 1 + len(rolls)
@@ -247,6 +251,8 @@
             lines_ref[pl.ds(case * LANES + index, SUBLANES, stride=stride), :] = value
     stride = rows // SUBLANES
     start = 0
+    sublane = lax.broadcasted_iota(jnp.int32, (SUBLANES, LANES), 0) % halves
+    tiles = None
     for half in range(halves):
         storage = [strided(block_ref, index, SUBLANES, stride) for index in range(half, stride, halves)]
         faces = [strided(block_ref, rows + index, SUBLANES, stride) for index in range(half, stride, halves)]
@@ -254,9 +260,8 @@
         for part in [part for node in nodes for part in node] if own_refs else []:
             own_refs[0][start : start + SUBLANES, :] = part
             start += SUBLANES
-        for number, value in enumerate(piece):
-            row = number * halves + half
-            rows_ref[row : row + 1, :] = value[0:1, :]
+        values = [jnp.broadcast_to(value[0:1, :], value.shape) for value in piece]
+        tiles = [jnp.where(sublane == half, new, old) for new, old in zip(values, tiles or values)]
         for case, ends in enumerate(ends_responses((SUBLANES, LANES))):
             values = tree_values(*ends, y_rolls(), len(storage), nodes, [0.0] * len(nodes))
             for index, (value, held) in enumerate(zip(values, storage)):
@@ -264,6 +269,8 @@
                 sums_ref[place, :] = value * held
                 if own_refs:
                     own_refs[1][place, :] = value
+    for number, tile in enumerate(tiles):
+        rows_ref[:, quantity(number)] = tile
 
 
 def state_parts(ref, first, total, parts, pitch=3):
@@ -309,15 +316,16 @@
     bounds = ring_bounds(slots, lax.axis_index(axis))
     rows = values_ref.shape[0]
 
-    def put(row, number, value):
-        kept_ref[row : row + 1, quantity(number)] = value
-        put_traded(sent_ref, row, 2 * halves, number, value)
-
-    for block in range(2):
-        for half in range(halves):
-            for number in range(3):
-                row = number * halves + half
-                put(block * halves + half, number, rows_refs[block][row : row + 1, :])
+    height = 2 * halves
+    first = lax.broadcasted_iota(jnp.int32, (SUBLANES, LANES), 0) < halves
+
+    def put(number, own, other):
+        kept_ref[:, quantity(number)] = jnp.where(first, own, other)[0:height, :]
+        sent_ref[:, quantity(number)] = jnp.where(first, other, own)[0:height, :]
+
+    for number in range(3):
+        put(number, *(ref[:, quantity(number)] for ref in rows_refs))
+    sides = []
     for block in range(2):
         lines_ref, sums_ref = lines_refs[block], sums_refs[block]
         before, after = (along_line(bound, halves, rows) for bound in bounds[block])
@@ -330,8 +338,9 @@
             side = jnp.sum(parts, axis=0)
             for step in doubling(SUBLANES // halves):
                 side = side + behind(side, step * halves, 0)
-            for half in range(halves):
-                put(block * halves + half, 3 + end, side[half : half + 1, :])
+            sides.append(side)
+    for end in range(2):
+        put(3 + end, sides[end], sides[2 + end])
 
 
 def y_given_kernel(halves, block_ref, values_ref, state_ref, given_ref):
@@ -493,13 +502,13 @@
         [f32(SUBLANES, rows), held_f32(2 * rows + (3 * x_nodes + 1) * SUBLANES, LANES)],
         [square] * 3
         + [VMEM((zones * rows, LANES), jnp.float32)]
-        + [VMEM((1, zones), jnp.float32)] * 2
+        + [pltpu.SMEM((1, zones), jnp.float32)] * 2
         + [pltpu.SemaphoreType.DMA((7,))]
         + [square] * 3,
         pltpu.HBM,
     )
     def prepare(part, own):
-        outputs = [held_f32(SUBLANES, LANES), held_f32(3 * LANES, rows), held_f32(2 * rows, LANES)]
+        outputs = [held_f32(SUBLANES, 3 * LANES), held_f32(3 * LANES, rows), held_f32(2 * rows, LANES)]
         if own:
             outputs += [held_f32(3 * y_nodes * SUBLANES, LANES), held_f32(2 * rows, LANES)]
         else:

time: 18.5 us -> 18.3 us (0.989)
  Pallas kernels: 3.05 us -> 2.82 us
    pallas_call x8, Pallas kernels: 3.05 us -> 2.82 us  [kernel_call(): pl.pallas_call(body, out_shape=outputs, in_specs=[pl.BlockSpec(memory_spa...]
where the time goes in v17:
time: 18.3 us; the launch traced here: 18.2 us
  starting transfers between devices  10.2 us (56%)
  waiting for transfers between devices  5.08 us (28%)
  Pallas kernels  2.82 us (15%)
    ppermute x6, starting transfers between devices, trade(): return lax.ppermute(value, ('xg', 'yd'), pairs)  10.2 us
    ppermute x6, waiting for transfers between devices, trade(): return lax.ppermute(value, ('xg', 'yd'), pairs)  5.08 us
    pallas_call x8, Pallas kernels, kernel_call(): pl.pallas_call(body, out_shape=outputs, in_specs=[pl.BlockSpec(memory_spa...  2.82 us
  transfers between devices with their start and end apart: 6, of which 5 were waited for; matrix products, arithmetic and copies ran while one was open for 0% of the time, Pallas kernels for 3%

profile of v17, /device:TPU:0, one launch (start us, length us, event | category | flops | bytes accessed | tf_op | source)
XLA Modules:
  0.0 18.2 jit_solution(17449503010351300376)
XLA Ops:
  0.0 1.4 %shard_map.73 = (f32[8,128]{1,0:T(8,128)S(1)}, f32[720,128]{1,0:T(8,128)S(1)}) custom-call(f32[128,128]{1,0:T(8,128)} %bitcast.9, f32[128,128]{1,0:T(8,128)} %bitcast.10, f32[128,128]{1,0:T(8,128)} %bitcast.11, f32[128,128]{1,0:T(8,128)} %bitcast.12, f32[512,128]{1,0:T(8,128)} %bitcast.8, f32[1,4]{1,0:T(1,128)} %bitcast.13, f32[1,4]{1,0:T(1,128)} %bitcast.14), custom_call_target="tpu_custom_call" | custom-call | flops 500000 | bytes 500000 | tf_op jit(solution)/shard_map/pallas_call | solution.py:467
  1.4 2.4 %collective-permute-start = (f32[8,128]{1,0:T(8,128)S(1)}, f32[8,128]{1,0:T(8,128)S(1)}, u32[]{:S(2)}, u32[]{:S(2)}) collective-permute-start(f32[8,128]{1,0:T(8,128)S(1)} %get-tuple-element.25.refs_0_), channel_id=1, source_target_pairs={{0,24},{1,25},{2,26},{3,27},{4,28},{5,29},{6,30},{7,31},{8,16},{9,... | collective-permute-start | bytes 12296 | tf_op jit(solution)/shard_map/ppermute | solution.py:420
  3.8 0.7 %collective-permute-start.2 = (f32[720,128]{1,0:T(8,128)S(1)}, f32[720,128]{1,0:T(8,128)S(1)}, u32[]{:S(2)}, u32[]{:S(2)}) collective-permute-start(f32[720,128]{1,0:T(8,128)S(1)} %get-tuple-element.26.block_ref), channel_id=1, source_target_pairs={{0,8},{1,9},{2,10},{3,11},{4,12},{5,13},{6,14},{7,15},{8,0},{9,1},... | collective-permute-start | bytes 1105928 | tf_op jit(solution)/shard_map/ppermute | solution.py:420
  4.5 0.2 %shard_map.74 = (f32[8,384]{1,0:T(8,128)S(1)}, f32[384,128]{1,0:T(8,128)S(1)}, f32[256,128]{1,0:T(8,128)S(1)}, f32[480,128]{1,0:T(8,128)S(1)}, f32[256,128]{1,0:T(8,128)S(1)}) custom-call(f32[720,128]{1,0:T(8,128)S(1)} %get-tuple-element.26.block_ref), custom_call_target="tpu_custom_call" | custom-call | flops 10000000000 | bytes 10000000000 | tf_op jit(solution)/shard_map/pallas_call | solution.py:467
  4.7 0.4 %collective-permute-done.refs_1_ = f32[8,128]{1,0:T(8,128)S(1)} collective-permute-done((f32[8,128]{1,0:T(8,128)S(1)}, f32[8,128]{1,0:T(8,128)S(1)}, u32[]{:S(2)}, u32[]{:S(2)}) %collective-permute-start) | collective-permute-done | bytes 4128 | tf_op jit(solution)/shard_map/ppermute | solution.py:420
  5.1 0.6 %collective-permute-start.1 = (f32[8,128]{1,0:T(8,128)S(1)}, f32[8,128]{1,0:T(8,128)S(1)}, u32[]{:S(2)}, u32[]{:S(2)}) collective-permute-start(f32[8,128]{1,0:T(8,128)S(1)} %collective-permute-done.refs_1_), channel_id=1, source_target_pairs={{0,8},{1,9},{2,10},{3,11},{4,12},{5,13},{6,14},{7,15},{8,0},{9,1},... | collective-permute-start | bytes 12296 | tf_op jit(solution)/shard_map/ppermute | solution.py:420
  5.8 0.0 collective-permute-done.2.block_ref
  5.8 0.2 %shard_map.75 = (f32[8,384]{1,0:T(8,128)S(1)}, f32[384,128]{1,0:T(8,128)S(1)}, f32[256,128]{1,0:T(8,128)S(1)}, f32[8,128]{1,0:T(8,128)S(1)}) custom-call(f32[720,128]{1,0:T(8,128)S(1)} %collective-permute-done.2.block_ref), custom_call_target="tpu_custom_call" | custom-call | flops 10000000000 | bytes 10000000000 | tf_op jit(solution)/shard_map/pallas_call | solution.py:467
  6.0 0.6 %collective-permute-done.1.refs_2_ = f32[8,128]{1,0:T(8,128)S(1)} collective-permute-done((f32[8,128]{1,0:T(8,128)S(1)}, f32[8,128]{1,0:T(8,128)S(1)}, u32[]{:S(2)}, u32[]{:S(2)}) %collective-permute-start.1) | collective-permute-done | bytes 4128 | tf_op jit(solution)/shard_map/ppermute | solution.py:420
  6.6 0.2 %shard_map.76 = (f32[4,640]{1,0:T(4,128)S(1)}, f32[4,640]{1,0:T(4,128)S(1)}, f32[128,128]{1,0:T(8,128)S(1)}) custom-call(f32[8,128]{1,0:T(8,128)S(1)} %get-tuple-element.25.refs_0_, f32[8,128]{1,0:T(8,128)S(1)} %collective-permute-done.refs_1_, f32[8,128]{1,0:T(8,128)S(1)} %collective-permute-done.1.refs_2_, f32[384,128]{1,0:T(8,128)S(1)} %get-tuple-element.27.refs_3_, ...), custom_call_target="tpu_custom_call" | custom-call | flops 500000 | bytes 500000 | tf_op jit(solution)/shard_map/pallas_call | solution.py:467
  6.8 1.8 %collective-permute-start.3 = (f32[4,640]{1,0:T(4,128)S(1)}, f32[4,640]{1,0:T(4,128)S(1)}, u32[]{:S(2)}, u32[]{:S(2)}) collective-permute-start(f32[4,640]{1,0:T(4,128)S(1)} %get-tuple-element.35), channel_id=1, source_target_pairs={{0,9},{1,8},{2,11},{3,10},{4,13},{5,12},{6,15},{7,14},{8,1},{9,0},... | collective-permute-start | bytes 30728 | tf_op jit(solution)/shard_map/ppermute | solution.py:420
  8.7 1.4 %collective-permute-done.3.other_ref = f32[4,640]{1,0:T(4,128)S(1)} collective-permute-done((f32[4,640]{1,0:T(4,128)S(1)}, f32[4,640]{1,0:T(4,128)S(1)}, u32[]{:S(2)}, u32[]{:S(2)}) %collective-permute-start.3) | collective-permute-done | bytes 10272 | tf_op jit(solution)/shard_map/ppermute | solution.py:420
  10.1 1.8 %collective-permute-start.4 = (f32[4,640]{1,0:T(4,128)S(1)}, f32[4,640]{1,0:T(4,128)S(1)}, u32[]{:S(2)}, u32[]{:S(2)}) collective-permute-start(f32[4,640]{1,0:T(4,128)S(1)} %get-tuple-element.37), channel_id=1, source_target_pairs={{0,10},{1,11},{2,8},{3,9},{4,14},{5,15},{6,12},{7,13},{8,2},{9,3},... | collective-permute-start | bytes 30728 | tf_op jit(solution)/shard_map/ppermute | solution.py:420
  11.9 1.4 %collective-permute-done.4.other_ref = f32[4,640]{1,0:T(4,128)S(1)} collective-permute-done((f32[4,640]{1,0:T(4,128)S(1)}, f32[4,640]{1,0:T(4,128)S(1)}, u32[]{:S(2)}, u32[]{:S(2)}) %collective-permute-start.4) | collective-permute-done | bytes 10272 | tf_op jit(solution)/shard_map/ppermute | solution.py:420
  13.3 2.8 %collective-permute-start.5 = (f32[4,640]{1,0:T(4,128)S(1)}, f32[4,640]{1,0:T(4,128)S(1)}, u32[]{:S(2)}, u32[]{:S(2)}) collective-permute-start(f32[4,640]{1,0:T(4,128)S(1)} %get-tuple-element.39), channel_id=1, source_target_pairs={{0,12},{1,13},{2,14},{3,15},{4,8},{5,9},{6,10},{7,11},{8,4},{9,5},... | collective-permute-start | bytes 30728 | tf_op jit(solution)/shard_map/ppermute | solution.py:420
  16.1 0.1 shard_map.79.refs_2_
  16.2 1.3 %collective-permute-done.5.other_ref = f32[4,640]{1,0:T(4,128)S(1)} collective-permute-done((f32[4,640]{1,0:T(4,128)S(1)}, f32[4,640]{1,0:T(4,128)S(1)}, u32[]{:S(2)}, u32[]{:S(2)}) %collective-permute-start.5) | collective-permute-done | bytes 10272 | tf_op jit(solution)/shard_map/ppermute | solution.py:420
  17.5 0.7 %shard_map.80 = f32[128,128]{1,0:T(8,128)} custom-call(f32[4,640]{1,0:T(4,128)S(1)} %get-tuple-element.38.own_ref, f32[4,640]{1,0:T(4,128)S(1)} %collective-permute-done.5.other_ref, f32[4,384]{1,0:T(4,128)S(1)} %get-tuple-element.40.refs_0_, f32[4,384]{1,0:T(4,128)S(1)} %get-tuple-element.41.refs_1_, f32[128,128]{1,0:T(8,128)S(1)} %shard_map.79.refs_2_, ...), custom_call_target="tpu_custom_call" | custom-call | flops 500000 | bytes 500000 | tf_op jit(solution)/shard_map/pallas_call | solution.py:467
  (2 shorter events, 0.0 us)
Async XLA Ops:
  1.4 3.8 %collective-permute-start = (f32[8,128]{1,0:T(8,128)S(1)}, f32[8,128]{1,0:T(8,128)S(1)}, u32[]{:S(2)}, u32[]{:S(2)}) collective-permute-start(f32[8,128]{1,0:T(8,128)S(1)} %get-tuple-element.25.refs_0_), channel_id=1, source_target_pairs={{0,24},{1,25},{2,26},{3,27},{4,28},{5,29},{6,30},{7,31},{8,16},{9,... | collective-permute-start | bytes 12296 | tf_op jit(solution)/shard_map/ppermute | solution.py:420
  3.8 2.0 %collective-permute-start.2 = (f32[720,128]{1,0:T(8,128)S(1)}, f32[720,128]{1,0:T(8,128)S(1)}, u32[]{:S(2)}, u32[]{:S(2)}) collective-permute-start(f32[720,128]{1,0:T(8,128)S(1)} %get-tuple-element.26.block_ref), channel_id=1, source_target_pairs={{0,8},{1,9},{2,10},{3,11},{4,12},{5,13},{6,14},{7,15},{8,0},{9,1},... | collective-permute-start | bytes 1105928 | tf_op jit(solution)/shard_map/ppermute | solution.py:420
  5.1 1.5 %collective-permute-start.1 = (f32[8,128]{1,0:T(8,128)S(1)}, f32[8,128]{1,0:T(8,128)S(1)}, u32[]{:S(2)}, u32[]{:S(2)}) collective-permute-start(f32[8,128]{1,0:T(8,128)S(1)} %collective-permute-done.refs_1_), channel_id=1, source_target_pairs={{0,8},{1,9},{2,10},{3,11},{4,12},{5,13},{6,14},{7,15},{8,0},{9,1},... | collective-permute-start | bytes 12296 | tf_op jit(solution)/shard_map/ppermute | solution.py:420
  6.8 3.2 %collective-permute-start.3 = (f32[4,640]{1,0:T(4,128)S(1)}, f32[4,640]{1,0:T(4,128)S(1)}, u32[]{:S(2)}, u32[]{:S(2)}) collective-permute-start(f32[4,640]{1,0:T(4,128)S(1)} %get-tuple-element.35), channel_id=1, source_target_pairs={{0,9},{1,8},{2,11},{3,10},{4,13},{5,12},{6,15},{7,14},{8,1},{9,0},... | collective-permute-start | bytes 30728 | tf_op jit(solution)/shard_map/ppermute | solution.py:420
  10.1 3.2 %collective-permute-start.4 = (f32[4,640]{1,0:T(4,128)S(1)}, f32[4,640]{1,0:T(4,128)S(1)}, u32[]{:S(2)}, u32[]{:S(2)}) collective-permute-start(f32[4,640]{1,0:T(4,128)S(1)} %get-tuple-element.37), channel_id=1, source_target_pairs={{0,10},{1,11},{2,8},{3,9},{4,14},{5,15},{6,12},{7,13},{8,2},{9,3},... | collective-permute-start | bytes 30728 | tf_op jit(solution)/shard_map/ppermute | solution.py:420
  13.3 4.2 %collective-permute-start.5 = (f32[4,640]{1,0:T(4,128)S(1)}, f32[4,640]{1,0:T(4,128)S(1)}, u32[]{:S(2)}, u32[]{:S(2)}) collective-permute-start(f32[4,640]{1,0:T(4,128)S(1)} %get-tuple-element.39), channel_id=1, source_target_pairs={{0,12},{1,13},{2,14},{3,15},{4,8},{5,9},{6,10},{7,11},{8,4},{9,5},... | collective-permute-start | bytes 30728 | tf_op jit(solution)/shard_map/ppermute | solution.py:420

commit v18 on v17

--- a/solution.py
+++ b/solution.py
@@ -165,7 +165,7 @@
     for zone in range(rates_ref.shape[1]):
         rate = jnp.full((SUBLANES, LANES), rates_ref[0, zone], jnp.float32)
         share = jnp.full((SUBLANES, LANES), shares_ref[0, zone], jnp.float32)
-        weights.append((share * rate / (1.0 + rate))[0:1, :])
+        weights.append(share * rate / (1.0 + rate))
     return weights
 
 
@@ -199,33 +199,40 @@
     for copy in copies[:3]:
         copy.wait()
     weights = capacity_weights(rates_ref, shares_ref)
-    capacity = capacity_ref[...]
-    storage = 1.0 + capacity * sum(weights[1:], weights[0])
+
+    def tiles(ref, start=0):
+        return ref[start : start + rows, :].reshape(-1, SUBLANES, LANES)
+
+    capacity = tiles(capacity_ref)
+    storage = (1.0 + capacity * sum(weights[1:], weights[0])).reshape(rows, LANES)
     block_ref[0:rows, :] = storage
     storage_t[...] = storage.T
     copies[3].wait()
     faces_t[...] = faces_ref[...].T
+    coefs = []
+    for index in range(stride):
+        coefs.append((strided(faces_t, index, SUBLANES, stride), None, strided(storage_t, index, SUBLANES, stride)))
+    rolls = x_rolls(halves)
+    piece, nodes = tree_coefs(coefs, rolls)
+    start = 2 * rows
+    for part in [part for node in nodes for part in node]:
+        block_ref[start : start + SUBLANES, :] = part
+        start += SUBLANES
     copies[4].wait()
     total = None
     for zone, weight in enumerate(weights):
-        total = plus(total, weight * immobile_ref[zone * rows : (zone + 1) * rows, :])
+        total = plus(total, weight * tiles(immobile_ref, zone * rows))
     copies[5].wait()
-    source_t[...] = (mobile_ref[...] + capacity * total).T
-    coefs, sides = [], []
-    for index in range(stride):
-        coefs.append((strided(faces_t, index, SUBLANES, stride), None, strided(storage_t, index, SUBLANES, stride)))
-        sides.append((None, strided(source_t, index, SUBLANES, stride)))
-    rolls = x_rolls(halves)
-    piece, nodes = tree_coefs(coefs, rolls)
+    source_t[...] = (tiles(mobile_ref) + capacity * total).reshape(rows, LANES).T
+    sides = [(None, strided(source_t, index, SUBLANES, stride)) for index in range(stride)]
+    nodes = state_parts(block_ref.at[2 * rows :, :], 0, len(nodes), 3)
     side, givens = tree_sides(sides, rolls, nodes)
-    start = 2 * rows
-    for node, given in zip(nodes, givens):
-        for part in (node[0], node[1], given):
-            block_ref[start : start + SUBLANES, :] = part
-            start += SUBLANES
     for row, value in enumerate(piece + side):
         message_ref[row : row + 1, :] = value[0:1, :]
         block_ref[start + row : start + row + 1, :] = value[0:1, :]
+    for place, given in enumerate(givens):
+        last = 2 * rows + (3 * place + 2) * SUBLANES
+        block_ref[last : last + SUBLANES, :] = given
     copies[6].wait()
 
 

time: 18.3 us -> 18.5 us (1.011)
  no operation moved by 1% of the time
where the time goes in v18:
time: 18.5 us; the launch traced here: 18.3 us
  starting transfers between devices  10.2 us (55%)
  waiting for transfers between devices  5.08 us (27%)
  Pallas kernels  3 us (16%)
    ppermute x6, starting transfers between devices, trade(): return lax.ppermute(value, ('xg', 'yd'), pairs)  10.2 us
    ppermute x6, waiting for transfers between devices, trade(): return lax.ppermute(value, ('xg', 'yd'), pairs)  5.08 us
    pallas_call x8, Pallas kernels, kernel_call(): pl.pallas_call(body, out_shape=outputs, in_specs=[pl.BlockSpec(memory_spa...  3 us
  transfers between devices with their start and end apart: 6, of which 5 were waited for; matrix products, arithmetic and copies ran while one was open for 0% of the time, Pallas kernels for 3%

profile of v18, /device:TPU:0, one launch (start us, length us, event | category | flops | bytes accessed | tf_op | source)
XLA Modules:
  0.0 18.3 jit_solution(5409051853455849092)
XLA Ops:
  0.0 1.5 %shard_map.73 = (f32[8,128]{1,0:T(8,128)S(1)}, f32[720,128]{1,0:T(8,128)S(1)}) custom-call(f32[128,128]{1,0:T(8,128)} %bitcast.9, f32[128,128]{1,0:T(8,128)} %bitcast.10, f32[128,128]{1,0:T(8,128)} %bitcast.11, f32[128,128]{1,0:T(8,128)} %bitcast.12, f32[512,128]{1,0:T(8,128)} %bitcast.8, f32[1,4]{1,0:T(1,128)} %bitcast.13, f32[1,4]{1,0:T(1,128)} %bitcast.14), custom_call_target="tpu_custom_call" | custom-call | flops 500000 | bytes 500000 | tf_op jit(solution)/shard_map/pallas_call | solution.py:474
  1.5 2.4 %collective-permute-start = (f32[8,128]{1,0:T(8,128)S(1)}, f32[8,128]{1,0:T(8,128)S(1)}, u32[]{:S(2)}, u32[]{:S(2)}) collective-permute-start(f32[8,128]{1,0:T(8,128)S(1)} %get-tuple-element.25.refs_0_), channel_id=1, source_target_pairs={{0,24},{1,25},{2,26},{3,27},{4,28},{5,29},{6,30},{7,31},{8,16},{9,... | collective-permute-start | bytes 12296 | tf_op jit(solution)/shard_map/ppermute | solution.py:427
  4.0 0.7 %collective-permute-start.2 = (f32[720,128]{1,0:T(8,128)S(1)}, f32[720,128]{1,0:T(8,128)S(1)}, u32[]{:S(2)}, u32[]{:S(2)}) collective-permute-start(f32[720,128]{1,0:T(8,128)S(1)} %get-tuple-element.26.block_ref), channel_id=1, source_target_pairs={{0,8},{1,9},{2,10},{3,11},{4,12},{5,13},{6,14},{7,15},{8,0},{9,1},... | collective-permute-start | bytes 1105928 | tf_op jit(solution)/shard_map/ppermute | solution.py:427
  4.7 0.2 %shard_map.74 = (f32[8,384]{1,0:T(8,128)S(1)}, f32[384,128]{1,0:T(8,128)S(1)}, f32[256,128]{1,0:T(8,128)S(1)}, f32[480,128]{1,0:T(8,128)S(1)}, f32[256,128]{1,0:T(8,128)S(1)}) custom-call(f32[720,128]{1,0:T(8,128)S(1)} %get-tuple-element.26.block_ref), custom_call_target="tpu_custom_call" | custom-call | flops 10000000000 | bytes 10000000000 | tf_op jit(solution)/shard_map/pallas_call | solution.py:474
  4.9 0.4 %collective-permute-done.refs_1_ = f32[8,128]{1,0:T(8,128)S(1)} collective-permute-done((f32[8,128]{1,0:T(8,128)S(1)}, f32[8,128]{1,0:T(8,128)S(1)}, u32[]{:S(2)}, u32[]{:S(2)}) %collective-permute-start) | collective-permute-done | bytes 4128 | tf_op jit(solution)/shard_map/ppermute | solution.py:427
  5.3 0.6 %collective-permute-start.1 = (f32[8,128]{1,0:T(8,128)S(1)}, f32[8,128]{1,0:T(8,128)S(1)}, u32[]{:S(2)}, u32[]{:S(2)}) collective-permute-start(f32[8,128]{1,0:T(8,128)S(1)} %collective-permute-done.refs_1_), channel_id=1, source_target_pairs={{0,8},{1,9},{2,10},{3,11},{4,12},{5,13},{6,14},{7,15},{8,0},{9,1},... | collective-permute-start | bytes 12296 | tf_op jit(solution)/shard_map/ppermute | solution.py:427
  6.0 0.0 collective-permute-done.2.block_ref
  6.0 0.2 %shard_map.75 = (f32[8,384]{1,0:T(8,128)S(1)}, f32[384,128]{1,0:T(8,128)S(1)}, f32[256,128]{1,0:T(8,128)S(1)}, f32[8,128]{1,0:T(8,128)S(1)}) custom-call(f32[720,128]{1,0:T(8,128)S(1)} %collective-permute-done.2.block_ref), custom_call_target="tpu_custom_call" | custom-call | flops 10000000000 | bytes 10000000000 | tf_op jit(solution)/shard_map/pallas_call | solution.py:474
  6.2 0.6 %collective-permute-done.1.refs_2_ = f32[8,128]{1,0:T(8,128)S(1)} collective-permute-done((f32[8,128]{1,0:T(8,128)S(1)}, f32[8,128]{1,0:T(8,128)S(1)}, u32[]{:S(2)}, u32[]{:S(2)}) %collective-permute-start.1) | collective-permute-done | bytes 4128 | tf_op jit(solution)/shard_map/ppermute | solution.py:427
  6.8 0.2 %shard_map.76 = (f32[4,640]{1,0:T(4,128)S(1)}, f32[4,640]{1,0:T(4,128)S(1)}, f32[128,128]{1,0:T(8,128)S(1)}) custom-call(f32[8,128]{1,0:T(8,128)S(1)} %get-tuple-element.25.refs_0_, f32[8,128]{1,0:T(8,128)S(1)} %collective-permute-done.refs_1_, f32[8,128]{1,0:T(8,128)S(1)} %collective-permute-done.1.refs_2_, f32[384,128]{1,0:T(8,128)S(1)} %get-tuple-element.27.refs_3_, ...), custom_call_target="tpu_custom_call" | custom-call | flops 500000 | bytes 500000 | tf_op jit(solution)/shard_map/pallas_call | solution.py:474
  7.0 1.8 %collective-permute-start.3 = (f32[4,640]{1,0:T(4,128)S(1)}, f32[4,640]{1,0:T(4,128)S(1)}, u32[]{:S(2)}, u32[]{:S(2)}) collective-permute-start(f32[4,640]{1,0:T(4,128)S(1)} %get-tuple-element.35), channel_id=1, source_target_pairs={{0,9},{1,8},{2,11},{3,10},{4,13},{5,12},{6,15},{7,14},{8,1},{9,0},... | collective-permute-start | bytes 30728 | tf_op jit(solution)/shard_map/ppermute | solution.py:427
  8.8 1.4 %collective-permute-done.3.other_ref = f32[4,640]{1,0:T(4,128)S(1)} collective-permute-done((f32[4,640]{1,0:T(4,128)S(1)}, f32[4,640]{1,0:T(4,128)S(1)}, u32[]{:S(2)}, u32[]{:S(2)}) %collective-permute-start.3) | collective-permute-done | bytes 10272 | tf_op jit(solution)/shard_map/ppermute | solution.py:427
  10.2 1.8 %collective-permute-start.4 = (f32[4,640]{1,0:T(4,128)S(1)}, f32[4,640]{1,0:T(4,128)S(1)}, u32[]{:S(2)}, u32[]{:S(2)}) collective-permute-start(f32[4,640]{1,0:T(4,128)S(1)} %get-tuple-element.37), channel_id=1, source_target_pairs={{0,10},{1,11},{2,8},{3,9},{4,14},{5,15},{6,12},{7,13},{8,2},{9,3},... | collective-permute-start | bytes 30728 | tf_op jit(solution)/shard_map/ppermute | solution.py:427
  12.1 1.4 %collective-permute-done.4.other_ref = f32[4,640]{1,0:T(4,128)S(1)} collective-permute-done((f32[4,640]{1,0:T(4,128)S(1)}, f32[4,640]{1,0:T(4,128)S(1)}, u32[]{:S(2)}, u32[]{:S(2)}) %collective-permute-start.4) | collective-permute-done | bytes 10272 | tf_op jit(solution)/shard_map/ppermute | solution.py:427
  13.5 2.8 %collective-permute-start.5 = (f32[4,640]{1,0:T(4,128)S(1)}, f32[4,640]{1,0:T(4,128)S(1)}, u32[]{:S(2)}, u32[]{:S(2)}) collective-permute-start(f32[4,640]{1,0:T(4,128)S(1)} %get-tuple-element.39), channel_id=1, source_target_pairs={{0,12},{1,13},{2,14},{3,15},{4,8},{5,9},{6,10},{7,11},{8,4},{9,5},... | collective-permute-start | bytes 30728 | tf_op jit(solution)/shard_map/ppermute | solution.py:427
  16.3 0.1 shard_map.79.refs_2_
  16.4 1.3 %collective-permute-done.5.other_ref = f32[4,640]{1,0:T(4,128)S(1)} collective-permute-done((f32[4,640]{1,0:T(4,128)S(1)}, f32[4,640]{1,0:T(4,128)S(1)}, u32[]{:S(2)}, u32[]{:S(2)}) %collective-permute-start.5) | collective-permute-done | bytes 10272 | tf_op jit(solution)/shard_map/ppermute | solution.py:427
  17.7 0.7 %shard_map.80 = f32[128,128]{1,0:T(8,128)} custom-call(f32[4,640]{1,0:T(4,128)S(1)} %get-tuple-element.38.own_ref, f32[4,640]{1,0:T(4,128)S(1)} %collective-permute-done.5.other_ref, f32[4,384]{1,0:T(4,128)S(1)} %get-tuple-element.40.refs_0_, f32[4,384]{1,0:T(4,128)S(1)} %get-tuple-element.41.refs_1_, f32[128,128]{1,0:T(8,128)S(1)} %shard_map.79.refs_2_, ...), custom_call_target="tpu_custom_call" | custom-call | flops 500000 | bytes 500000 | tf_op jit(solution)/shard_map/pallas_call | solution.py:474
  (2 shorter events, 0.0 us)
Async XLA Ops:
  1.5 3.8 %collective-permute-start = (f32[8,128]{1,0:T(8,128)S(1)}, f32[8,128]{1,0:T(8,128)S(1)}, u32[]{:S(2)}, u32[]{:S(2)}) collective-permute-start(f32[8,128]{1,0:T(8,128)S(1)} %get-tuple-element.25.refs_0_), channel_id=1, source_target_pairs={{0,24},{1,25},{2,26},{3,27},{4,28},{5,29},{6,30},{7,31},{8,16},{9,... | collective-permute-start | bytes 12296 | tf_op jit(solution)/shard_map/ppermute | solution.py:427
  4.0 2.0 %collective-permute-start.2 = (f32[720,128]{1,0:T(8,128)S(1)}, f32[720,128]{1,0:T(8,128)S(1)}, u32[]{:S(2)}, u32[]{:S(2)}) collective-permute-start(f32[720,128]{1,0:T(8,128)S(1)} %get-tuple-element.26.block_ref), channel_id=1, source_target_pairs={{0,8},{1,9},{2,10},{3,11},{4,12},{5,13},{6,14},{7,15},{8,0},{9,1},... | collective-permute-start | bytes 1105928 | tf_op jit(solution)/shard_map/ppermute | solution.py:427
  5.3 1.5 %collective-permute-start.1 = (f32[8,128]{1,0:T(8,128)S(1)}, f32[8,128]{1,0:T(8,128)S(1)}, u32[]{:S(2)}, u32[]{:S(2)}) collective-permute-start(f32[8,128]{1,0:T(8,128)S(1)} %collective-permute-done.refs_1_), channel_id=1, source_target_pairs={{0,8},{1,9},{2,10},{3,11},{4,12},{5,13},{6,14},{7,15},{8,0},{9,1},... | collective-permute-start | bytes 12296 | tf_op jit(solution)/shard_map/ppermute | solution.py:427
  7.0 3.2 %collective-permute-start.3 = (f32[4,640]{1,0:T(4,128)S(1)}, f32[4,640]{1,0:T(4,128)S(1)}, u32[]{:S(2)}, u32[]{:S(2)}) collective-permute-start(f32[4,640]{1,0:T(4,128)S(1)} %get-tuple-element.35), channel_id=1, source_target_pairs={{0,9},{1,8},{2,11},{3,10},{4,13},{5,12},{6,15},{7,14},{8,1},{9,0},... | collective-permute-start | bytes 30728 | tf_op jit(solution)/shard_map/ppermute | solution.py:427
  10.2 3.2 %collective-permute-start.4 = (f32[4,640]{1,0:T(4,128)S(1)}, f32[4,640]{1,0:T(4,128)S(1)}, u32[]{:S(2)}, u32[]{:S(2)}) collective-permute-start(f32[4,640]{1,0:T(4,128)S(1)} %get-tuple-element.37), channel_id=1, source_target_pairs={{0,10},{1,11},{2,8},{3,9},{4,14},{5,15},{6,12},{7,13},{8,2},{9,3},... | collective-permute-start | bytes 30728 | tf_op jit(solution)/shard_map/ppermute | solution.py:427
  13.5 4.2 %collective-permute-start.5 = (f32[4,640]{1,0:T(4,128)S(1)}, f32[4,640]{1,0:T(4,128)S(1)}, u32[]{:S(2)}, u32[]{:S(2)}) collective-permute-start(f32[4,640]{1,0:T(4,128)S(1)} %get-tuple-element.39), channel_id=1, source_target_pairs={{0,12},{1,13},{2,14},{3,15},{4,8},{5,9},{6,10},{7,11},{8,4},{9,5},... | collective-permute-start | bytes 30728 | tf_op jit(solution)/shard_map/ppermute | solution.py:427

commit v19 on v17

--- a/solution.py
+++ b/solution.py
@@ -169,6 +169,19 @@
     return weights
 
 
+def flipped(value):
+    rows = value.shape[1]
+    row, column = (lax.broadcasted_iota(jnp.int32, (rows, rows), axis) for axis in range(2))
+    unit = (row == column).astype(jnp.bfloat16)
+    total = None
+    for _ in range(3):
+        part = value.astype(jnp.bfloat16)
+        value = value - part.astype(jnp.float32)
+        moved = lax.dot_general(unit, part, (((1,), (1,)), ((), ())), preferred_element_type=jnp.float32)
+        total = plus(total, moved)
+    return total
+
+
 def strided(ref, start, size, stride):
     return ref[pl.ds(start, size, stride=stride), :]
 
@@ -210,7 +223,7 @@
     for zone, weight in enumerate(weights):
         total = plus(total, weight * immobile_ref[zone * rows : (zone + 1) * rows, :])
     copies[5].wait()
-    source_t[...] = (mobile_ref[...] + capacity * total).T
+    source_t[...] = flipped(mobile_ref[...] + capacity * total)
     coefs, sides = [], []
     for index in range(stride):
         coefs.append((strided(faces_t, index, SUBLANES, stride), None, strided(storage_t, index, SUBLANES, stride)))
@@ -330,7 +343,7 @@
         lines_ref, sums_ref = lines_refs[block], sums_refs[block]
         before, after = (along_line(bound, halves, rows) for bound in bounds[block])
         values = lines_ref[0:LANES, :] + lines_ref[LANES : 2 * LANES, :] * before + lines_ref[2 * LANES :, :] * after
-        values = values.T
+        values = flipped(values)
         if block == 0:
             values_ref[...] = values
         for end in range(2):

time: 18.3 us -> 18.6 us (1.016)
  Pallas kernels: 2.82 us -> 3.1 us
    pallas_call x8, Pallas kernels: 2.82 us -> 3.1 us  [kernel_call(): pl.pallas_call(body, out_shape=outputs, in_specs=[pl.BlockSpec(memory_spa...]
where the time goes in v19:
time: 18.6 us; the launch traced here: 18.4 us
  starting transfers between devices  10.2 us (55%)
  waiting for transfers between devices  5.08 us (27%)
  Pallas kernels  3.1 us (17%)
    ppermute x6, starting transfers between devices, trade(): return lax.ppermute(value, ('xg', 'yd'), pairs)  10.2 us
    ppermute x6, waiting for transfers between devices, trade(): return lax.ppermute(value, ('xg', 'yd'), pairs)  5.08 us
    pallas_call x8, Pallas kernels, kernel_call(): pl.pallas_call(body, out_shape=outputs, in_specs=[pl.BlockSpec(memory_spa...  3.1 us
  transfers between devices with their start and end apart: 6, of which 5 were waited for; matrix products, arithmetic and copies ran while one was open for 0% of the time, Pallas kernels for 3%

profile of v19, /device:TPU:0, one launch (start us, length us, event | category | flops | bytes accessed | tf_op | source)
XLA Modules:
  0.0 18.4 jit_solution(17235837069150965373)
XLA Ops:
  0.0 1.5 %shard_map.73 = (f32[8,128]{1,0:T(8,128)S(1)}, f32[720,128]{1,0:T(8,128)S(1)}) custom-call(f32[128,128]{1,0:T(8,128)} %bitcast.9, f32[128,128]{1,0:T(8,128)} %bitcast.10, f32[128,128]{1,0:T(8,128)} %bitcast.11, f32[128,128]{1,0:T(8,128)} %bitcast.12, f32[512,128]{1,0:T(8,128)} %bitcast.8, f32[1,4]{1,0:T(1,128)} %bitcast.13, f32[1,4]{1,0:T(1,128)} %bitcast.14), custom_call_target="tpu_custom_call" | custom-call | flops 500000 | bytes 500000 | tf_op jit(solution)/shard_map/pallas_call | solution.py:480
  1.5 2.4 %collective-permute-start = (f32[8,128]{1,0:T(8,128)S(1)}, f32[8,128]{1,0:T(8,128)S(1)}, u32[]{:S(2)}, u32[]{:S(2)}) collective-permute-start(f32[8,128]{1,0:T(8,128)S(1)} %get-tuple-element.25.refs_0_), channel_id=1, source_target_pairs={{0,24},{1,25},{2,26},{3,27},{4,28},{5,29},{6,30},{7,31},{8,16},{9,... | collective-permute-start | bytes 12296 | tf_op jit(solution)/shard_map/ppermute | solution.py:433
  3.9 0.7 %collective-permute-start.2 = (f32[720,128]{1,0:T(8,128)S(1)}, f32[720,128]{1,0:T(8,128)S(1)}, u32[]{:S(2)}, u32[]{:S(2)}) collective-permute-start(f32[720,128]{1,0:T(8,128)S(1)} %get-tuple-element.26.block_ref), channel_id=1, source_target_pairs={{0,8},{1,9},{2,10},{3,11},{4,12},{5,13},{6,14},{7,15},{8,0},{9,1},... | collective-permute-start | bytes 1105928 | tf_op jit(solution)/shard_map/ppermute | solution.py:433
  4.6 0.2 %shard_map.74 = (f32[8,384]{1,0:T(8,128)S(1)}, f32[384,128]{1,0:T(8,128)S(1)}, f32[256,128]{1,0:T(8,128)S(1)}, f32[480,128]{1,0:T(8,128)S(1)}, f32[256,128]{1,0:T(8,128)S(1)}) custom-call(f32[720,128]{1,0:T(8,128)S(1)} %get-tuple-element.26.block_ref), custom_call_target="tpu_custom_call" | custom-call | flops 10000000000 | bytes 10000000000 | tf_op jit(solution)/shard_map/pallas_call | solution.py:480
  4.8 0.4 %collective-permute-done.refs_1_ = f32[8,128]{1,0:T(8,128)S(1)} collective-permute-done((f32[8,128]{1,0:T(8,128)S(1)}, f32[8,128]{1,0:T(8,128)S(1)}, u32[]{:S(2)}, u32[]{:S(2)}) %collective-permute-start) | collective-permute-done | bytes 4128 | tf_op jit(solution)/shard_map/ppermute | solution.py:433
  5.2 0.6 %collective-permute-start.1 = (f32[8,128]{1,0:T(8,128)S(1)}, f32[8,128]{1,0:T(8,128)S(1)}, u32[]{:S(2)}, u32[]{:S(2)}) collective-permute-start(f32[8,128]{1,0:T(8,128)S(1)} %collective-permute-done.refs_1_), channel_id=1, source_target_pairs={{0,8},{1,9},{2,10},{3,11},{4,12},{5,13},{6,14},{7,15},{8,0},{9,1},... | collective-permute-start | bytes 12296 | tf_op jit(solution)/shard_map/ppermute | solution.py:433
  5.9 0.0 collective-permute-done.2.block_ref
  5.9 0.2 %shard_map.75 = (f32[8,384]{1,0:T(8,128)S(1)}, f32[384,128]{1,0:T(8,128)S(1)}, f32[256,128]{1,0:T(8,128)S(1)}, f32[8,128]{1,0:T(8,128)S(1)}) custom-call(f32[720,128]{1,0:T(8,128)S(1)} %collective-permute-done.2.block_ref), custom_call_target="tpu_custom_call" | custom-call | flops 10000000000 | bytes 10000000000 | tf_op jit(solution)/shard_map/pallas_call | solution.py:480
  6.1 0.6 %collective-permute-done.1.refs_2_ = f32[8,128]{1,0:T(8,128)S(1)} collective-permute-done((f32[8,128]{1,0:T(8,128)S(1)}, f32[8,128]{1,0:T(8,128)S(1)}, u32[]{:S(2)}, u32[]{:S(2)}) %collective-permute-start.1) | collective-permute-done | bytes 4128 | tf_op jit(solution)/shard_map/ppermute | solution.py:433
  6.7 0.4 %shard_map.76 = (f32[4,640]{1,0:T(4,128)S(1)}, f32[4,640]{1,0:T(4,128)S(1)}, f32[128,128]{1,0:T(8,128)S(1)}) custom-call(f32[8,128]{1,0:T(8,128)S(1)} %get-tuple-element.25.refs_0_, f32[8,128]{1,0:T(8,128)S(1)} %collective-permute-done.refs_1_, f32[8,128]{1,0:T(8,128)S(1)} %collective-permute-done.1.refs_2_, f32[384,128]{1,0:T(8,128)S(1)} %get-tuple-element.27.refs_3_, ...), custom_call_target="tpu_custom_call" | custom-call | flops 500000 | bytes 500000 | tf_op jit(solution)/shard_map/pallas_call | solution.py:480
  7.1 1.8 %collective-permute-start.3 = (f32[4,640]{1,0:T(4,128)S(1)}, f32[4,640]{1,0:T(4,128)S(1)}, u32[]{:S(2)}, u32[]{:S(2)}) collective-permute-start(f32[4,640]{1,0:T(4,128)S(1)} %get-tuple-element.35), channel_id=1, source_target_pairs={{0,9},{1,8},{2,11},{3,10},{4,13},{5,12},{6,15},{7,14},{8,1},{9,0},... | collective-permute-start | bytes 30728 | tf_op jit(solution)/shard_map/ppermute | solution.py:433
  8.9 1.4 %collective-permute-done.3.other_ref = f32[4,640]{1,0:T(4,128)S(1)} collective-permute-done((f32[4,640]{1,0:T(4,128)S(1)}, f32[4,640]{1,0:T(4,128)S(1)}, u32[]{:S(2)}, u32[]{:S(2)}) %collective-permute-start.3) | collective-permute-done | bytes 10272 | tf_op jit(solution)/shard_map/ppermute | solution.py:433
  10.3 1.8 %collective-permute-start.4 = (f32[4,640]{1,0:T(4,128)S(1)}, f32[4,640]{1,0:T(4,128)S(1)}, u32[]{:S(2)}, u32[]{:S(2)}) collective-permute-start(f32[4,640]{1,0:T(4,128)S(1)} %get-tuple-element.37), channel_id=1, source_target_pairs={{0,10},{1,11},{2,8},{3,9},{4,14},{5,15},{6,12},{7,13},{8,2},{9,3},... | collective-permute-start | bytes 30728 | tf_op jit(solution)/shard_map/ppermute | solution.py:433
  12.2 1.4 %collective-permute-done.4.other_ref = f32[4,640]{1,0:T(4,128)S(1)} collective-permute-done((f32[4,640]{1,0:T(4,128)S(1)}, f32[4,640]{1,0:T(4,128)S(1)}, u32[]{:S(2)}, u32[]{:S(2)}) %collective-permute-start.4) | collective-permute-done | bytes 10272 | tf_op jit(solution)/shard_map/ppermute | solution.py:433
  13.6 2.8 %collective-permute-start.5 = (f32[4,640]{1,0:T(4,128)S(1)}, f32[4,640]{1,0:T(4,128)S(1)}, u32[]{:S(2)}, u32[]{:S(2)}) collective-permute-start(f32[4,640]{1,0:T(4,128)S(1)} %get-tuple-element.39), channel_id=1, source_target_pairs={{0,12},{1,13},{2,14},{3,15},{4,8},{5,9},{6,10},{7,11},{8,4},{9,5},... | collective-permute-start | bytes 30728 | tf_op jit(solution)/shard_map/ppermute | solution.py:433
  16.4 0.1 shard_map.79.refs_2_
  16.5 1.3 %collective-permute-done.5.other_ref = f32[4,640]{1,0:T(4,128)S(1)} collective-permute-done((f32[4,640]{1,0:T(4,128)S(1)}, f32[4,640]{1,0:T(4,128)S(1)}, u32[]{:S(2)}, u32[]{:S(2)}) %collective-permute-start.5) | collective-permute-done | bytes 10272 | tf_op jit(solution)/shard_map/ppermute | solution.py:433
  17.8 0.7 %shard_map.80 = f32[128,128]{1,0:T(8,128)} custom-call(f32[4,640]{1,0:T(4,128)S(1)} %get-tuple-element.38.own_ref, f32[4,640]{1,0:T(4,128)S(1)} %collective-permute-done.5.other_ref, f32[4,384]{1,0:T(4,128)S(1)} %get-tuple-element.40.refs_0_, f32[4,384]{1,0:T(4,128)S(1)} %get-tuple-element.41.refs_1_, f32[128,128]{1,0:T(8,128)S(1)} %shard_map.79.refs_2_, ...), custom_call_target="tpu_custom_call" | custom-call | flops 500000 | bytes 500000 | tf_op jit(solution)/shard_map/pallas_call | solution.py:480
  (2 shorter events, 0.0 us)
Async XLA Ops:
  1.5 3.8 %collective-permute-start = (f32[8,128]{1,0:T(8,128)S(1)}, f32[8,128]{1,0:T(8,128)S(1)}, u32[]{:S(2)}, u32[]{:S(2)}) collective-permute-start(f32[8,128]{1,0:T(8,128)S(1)} %get-tuple-element.25.refs_0_), channel_id=1, source_target_pairs={{0,24},{1,25},{2,26},{3,27},{4,28},{5,29},{6,30},{7,31},{8,16},{9,... | collective-permute-start | bytes 12296 | tf_op jit(solution)/shard_map/ppermute | solution.py:433
  3.9 2.0 %collective-permute-start.2 = (f32[720,128]{1,0:T(8,128)S(1)}, f32[720,128]{1,0:T(8,128)S(1)}, u32[]{:S(2)}, u32[]{:S(2)}) collective-permute-start(f32[720,128]{1,0:T(8,128)S(1)} %get-tuple-element.26.block_ref), channel_id=1, source_target_pairs={{0,8},{1,9},{2,10},{3,11},{4,12},{5,13},{6,14},{7,15},{8,0},{9,1},... | collective-permute-start | bytes 1105928 | tf_op jit(solution)/shard_map/ppermute | solution.py:433
  5.2 1.5 %collective-permute-start.1 = (f32[8,128]{1,0:T(8,128)S(1)}, f32[8,128]{1,0:T(8,128)S(1)}, u32[]{:S(2)}, u32[]{:S(2)}) collective-permute-start(f32[8,128]{1,0:T(8,128)S(1)} %collective-permute-done.refs_1_), channel_id=1, source_target_pairs={{0,8},{1,9},{2,10},{3,11},{4,12},{5,13},{6,14},{7,15},{8,0},{9,1},... | collective-permute-start | bytes 12296 | tf_op jit(solution)/shard_map/ppermute | solution.py:433
  7.1 3.2 %collective-permute-start.3 = (f32[4,640]{1,0:T(4,128)S(1)}, f32[4,640]{1,0:T(4,128)S(1)}, u32[]{:S(2)}, u32[]{:S(2)}) collective-permute-start(f32[4,640]{1,0:T(4,128)S(1)} %get-tuple-element.35), channel_id=1, source_target_pairs={{0,9},{1,8},{2,11},{3,10},{4,13},{5,12},{6,15},{7,14},{8,1},{9,0},... | collective-permute-start | bytes 30728 | tf_op jit(solution)/shard_map/ppermute | solution.py:433
  10.3 3.2 %collective-permute-start.4 = (f32[4,640]{1,0:T(4,128)S(1)}, f32[4,640]{1,0:T(4,128)S(1)}, u32[]{:S(2)}, u32[]{:S(2)}) collective-permute-start(f32[4,640]{1,0:T(4,128)S(1)} %get-tuple-element.37), channel_id=1, source_target_pairs={{0,10},{1,11},{2,8},{3,9},{4,14},{5,15},{6,12},{7,13},{8,2},{9,3},... | collective-permute-start | bytes 30728 | tf_op jit(solution)/shard_map/ppermute | solution.py:433
  13.6 4.2 %collective-permute-start.5 = (f32[4,640]{1,0:T(4,128)S(1)}, f32[4,640]{1,0:T(4,128)S(1)}, u32[]{:S(2)}, u32[]{:S(2)}) collective-permute-start(f32[4,640]{1,0:T(4,128)S(1)} %get-tuple-element.39), channel_id=1, source_target_pairs={{0,12},{1,13},{2,14},{3,15},{4,8},{5,9},{6,10},{7,11},{8,4},{9,5},... | collective-permute-start | bytes 30728 | tf_op jit(solution)/shard_map/ppermute | solution.py:433

commit v20 on v17

--- a/solution.py
+++ b/solution.py
@@ -196,21 +196,18 @@
     for place, copy in enumerate(copies):
         copy.start(priority=int(place in (4, 6)))
     stride = LANES // SUBLANES
-    for copy in copies[:3]:
+    for copy in copies[:6]:
         copy.wait()
     weights = capacity_weights(rates_ref, shares_ref)
     capacity = capacity_ref[...]
     storage = 1.0 + capacity * sum(weights[1:], weights[0])
-    block_ref[0:rows, :] = storage
     storage_t[...] = storage.T
-    copies[3].wait()
     faces_t[...] = faces_ref[...].T
-    copies[4].wait()
     total = None
     for zone, weight in enumerate(weights):
         total = plus(total, weight * immobile_ref[zone * rows : (zone + 1) * rows, :])
-    copies[5].wait()
     source_t[...] = (mobile_ref[...] + capacity * total).T
+    block_ref[0:rows, :] = storage
     coefs, sides = [], []
     for index in range(stride):
         coefs.append((strided(faces_t, index, SUBLANES, stride), None, strided(storage_t, index, SUBLANES, stride)))

time: 18.3 us -> 18.4 us (level)
  no operation moved by 1% of the time
where the time goes in v20:
time: 18.4 us; the launch traced here: 18.2 us
  starting transfers between devices  10.2 us (55%)
  waiting for transfers between devices  5.08 us (28%)
  Pallas kernels  2.88 us (16%)
    ppermute x6, starting transfers between devices, trade(): return lax.ppermute(value, ('xg', 'yd'), pairs)  10.2 us
    ppermute x6, waiting for transfers between devices, trade(): return lax.ppermute(value, ('xg', 'yd'), pairs)  5.08 us
    pallas_call x8, Pallas kernels, kernel_call(): pl.pallas_call(body, out_shape=outputs, in_specs=[pl.BlockSpec(memory_spa...  2.88 us
  transfers between devices with their start and end apart: 6, of which 5 were waited for; matrix products, arithmetic and copies ran while one was open for 0% of the time, Pallas kernels for 3%

profile of v20, /device:TPU:0, one launch (start us, length us, event | category | flops | bytes accessed | tf_op | source)
XLA Modules:
  0.0 18.2 jit_solution(325125728259889243)
XLA Ops:
  0.0 1.4 %shard_map.73 = (f32[8,128]{1,0:T(8,128)S(1)}, f32[720,128]{1,0:T(8,128)S(1)}) custom-call(f32[128,128]{1,0:T(8,128)} %bitcast.9, f32[128,128]{1,0:T(8,128)} %bitcast.10, f32[128,128]{1,0:T(8,128)} %bitcast.11, f32[128,128]{1,0:T(8,128)} %bitcast.12, f32[512,128]{1,0:T(8,128)} %bitcast.8, f32[1,4]{1,0:T(1,128)} %bitcast.13, f32[1,4]{1,0:T(1,128)} %bitcast.14), custom_call_target="tpu_custom_call" | custom-call | flops 500000 | bytes 500000 | tf_op jit(solution)/shard_map/pallas_call | solution.py:464
  1.4 2.4 %collective-permute-start = (f32[8,128]{1,0:T(8,128)S(1)}, f32[8,128]{1,0:T(8,128)S(1)}, u32[]{:S(2)}, u32[]{:S(2)}) collective-permute-start(f32[8,128]{1,0:T(8,128)S(1)} %get-tuple-element.25.refs_0_), channel_id=1, source_target_pairs={{0,24},{1,25},{2,26},{3,27},{4,28},{5,29},{6,30},{7,31},{8,16},{9,... | collective-permute-start | bytes 12296 | tf_op jit(solution)/shard_map/ppermute | solution.py:417
  3.9 0.7 %collective-permute-start.2 = (f32[720,128]{1,0:T(8,128)S(1)}, f32[720,128]{1,0:T(8,128)S(1)}, u32[]{:S(2)}, u32[]{:S(2)}) collective-permute-start(f32[720,128]{1,0:T(8,128)S(1)} %get-tuple-element.26.block_ref), channel_id=1, source_target_pairs={{0,8},{1,9},{2,10},{3,11},{4,12},{5,13},{6,14},{7,15},{8,0},{9,1},... | collective-permute-start | bytes 1105928 | tf_op jit(solution)/shard_map/ppermute | solution.py:417
  4.5 0.2 %shard_map.74 = (f32[8,384]{1,0:T(8,128)S(1)}, f32[384,128]{1,0:T(8,128)S(1)}, f32[256,128]{1,0:T(8,128)S(1)}, f32[480,128]{1,0:T(8,128)S(1)}, f32[256,128]{1,0:T(8,128)S(1)}) custom-call(f32[720,128]{1,0:T(8,128)S(1)} %get-tuple-element.26.block_ref), custom_call_target="tpu_custom_call" | custom-call | flops 10000000000 | bytes 10000000000 | tf_op jit(solution)/shard_map/pallas_call | solution.py:464
  4.8 0.4 %collective-permute-done.refs_1_ = f32[8,128]{1,0:T(8,128)S(1)} collective-permute-done((f32[8,128]{1,0:T(8,128)S(1)}, f32[8,128]{1,0:T(8,128)S(1)}, u32[]{:S(2)}, u32[]{:S(2)}) %collective-permute-start) | collective-permute-done | bytes 4128 | tf_op jit(solution)/shard_map/ppermute | solution.py:417
  5.2 0.6 %collective-permute-start.1 = (f32[8,128]{1,0:T(8,128)S(1)}, f32[8,128]{1,0:T(8,128)S(1)}, u32[]{:S(2)}, u32[]{:S(2)}) collective-permute-start(f32[8,128]{1,0:T(8,128)S(1)} %collective-permute-done.refs_1_), channel_id=1, source_target_pairs={{0,8},{1,9},{2,10},{3,11},{4,12},{5,13},{6,14},{7,15},{8,0},{9,1},... | collective-permute-start | bytes 12296 | tf_op jit(solution)/shard_map/ppermute | solution.py:417
  5.8 0.0 collective-permute-done.2.block_ref
  5.9 0.2 %shard_map.75 = (f32[8,384]{1,0:T(8,128)S(1)}, f32[384,128]{1,0:T(8,128)S(1)}, f32[256,128]{1,0:T(8,128)S(1)}, f32[8,128]{1,0:T(8,128)S(1)}) custom-call(f32[720,128]{1,0:T(8,128)S(1)} %collective-permute-done.2.block_ref), custom_call_target="tpu_custom_call" | custom-call | flops 10000000000 | bytes 10000000000 | tf_op jit(solution)/shard_map/pallas_call | solution.py:464
  6.1 0.6 %collective-permute-done.1.refs_2_ = f32[8,128]{1,0:T(8,128)S(1)} collective-permute-done((f32[8,128]{1,0:T(8,128)S(1)}, f32[8,128]{1,0:T(8,128)S(1)}, u32[]{:S(2)}, u32[]{:S(2)}) %collective-permute-start.1) | collective-permute-done | bytes 4128 | tf_op jit(solution)/shard_map/ppermute | solution.py:417
  6.7 0.2 %shard_map.76 = (f32[4,640]{1,0:T(4,128)S(1)}, f32[4,640]{1,0:T(4,128)S(1)}, f32[128,128]{1,0:T(8,128)S(1)}) custom-call(f32[8,128]{1,0:T(8,128)S(1)} %get-tuple-element.25.refs_0_, f32[8,128]{1,0:T(8,128)S(1)} %collective-permute-done.refs_1_, f32[8,128]{1,0:T(8,128)S(1)} %collective-permute-done.1.refs_2_, f32[384,128]{1,0:T(8,128)S(1)} %get-tuple-element.27.refs_3_, ...), custom_call_target="tpu_custom_call" | custom-call | flops 500000 | bytes 500000 | tf_op jit(solution)/shard_map/pallas_call | solution.py:464
  6.9 1.8 %collective-permute-start.3 = (f32[4,640]{1,0:T(4,128)S(1)}, f32[4,640]{1,0:T(4,128)S(1)}, u32[]{:S(2)}, u32[]{:S(2)}) collective-permute-start(f32[4,640]{1,0:T(4,128)S(1)} %get-tuple-element.35), channel_id=1, source_target_pairs={{0,9},{1,8},{2,11},{3,10},{4,13},{5,12},{6,15},{7,14},{8,1},{9,0},... | collective-permute-start | bytes 30728 | tf_op jit(solution)/shard_map/ppermute | solution.py:417
  8.7 1.4 %collective-permute-done.3.other_ref = f32[4,640]{1,0:T(4,128)S(1)} collective-permute-done((f32[4,640]{1,0:T(4,128)S(1)}, f32[4,640]{1,0:T(4,128)S(1)}, u32[]{:S(2)}, u32[]{:S(2)}) %collective-permute-start.3) | collective-permute-done | bytes 10272 | tf_op jit(solution)/shard_map/ppermute | solution.py:417
  10.1 1.8 %collective-permute-start.4 = (f32[4,640]{1,0:T(4,128)S(1)}, f32[4,640]{1,0:T(4,128)S(1)}, u32[]{:S(2)}, u32[]{:S(2)}) collective-permute-start(f32[4,640]{1,0:T(4,128)S(1)} %get-tuple-element.37), channel_id=1, source_target_pairs={{0,10},{1,11},{2,8},{3,9},{4,14},{5,15},{6,12},{7,13},{8,2},{9,3},... | collective-permute-start | bytes 30728 | tf_op jit(solution)/shard_map/ppermute | solution.py:417
  12.0 1.4 %collective-permute-done.4.other_ref = f32[4,640]{1,0:T(4,128)S(1)} collective-permute-done((f32[4,640]{1,0:T(4,128)S(1)}, f32[4,640]{1,0:T(4,128)S(1)}, u32[]{:S(2)}, u32[]{:S(2)}) %collective-permute-start.4) | collective-permute-done | bytes 10272 | tf_op jit(solution)/shard_map/ppermute | solution.py:417
  13.4 2.8 %collective-permute-start.5 = (f32[4,640]{1,0:T(4,128)S(1)}, f32[4,640]{1,0:T(4,128)S(1)}, u32[]{:S(2)}, u32[]{:S(2)}) collective-permute-start(f32[4,640]{1,0:T(4,128)S(1)} %get-tuple-element.39), channel_id=1, source_target_pairs={{0,12},{1,13},{2,14},{3,15},{4,8},{5,9},{6,10},{7,11},{8,4},{9,5},... | collective-permute-start | bytes 30728 | tf_op jit(solution)/shard_map/ppermute | solution.py:417
  16.2 0.1 shard_map.79.refs_2_
  16.2 1.3 %collective-permute-done.5.other_ref = f32[4,640]{1,0:T(4,128)S(1)} collective-permute-done((f32[4,640]{1,0:T(4,128)S(1)}, f32[4,640]{1,0:T(4,128)S(1)}, u32[]{:S(2)}, u32[]{:S(2)}) %collective-permute-start.5) | collective-permute-done | bytes 10272 | tf_op jit(solution)/shard_map/ppermute | solution.py:417
  17.5 0.7 %shard_map.80 = f32[128,128]{1,0:T(8,128)} custom-call(f32[4,640]{1,0:T(4,128)S(1)} %get-tuple-element.38.own_ref, f32[4,640]{1,0:T(4,128)S(1)} %collective-permute-done.5.other_ref, f32[4,384]{1,0:T(4,128)S(1)} %get-tuple-element.40.refs_0_, f32[4,384]{1,0:T(4,128)S(1)} %get-tuple-element.41.refs_1_, f32[128,128]{1,0:T(8,128)S(1)} %shard_map.79.refs_2_, ...), custom_call_target="tpu_custom_call" | custom-call | flops 500000 | bytes 500000 | tf_op jit(solution)/shard_map/pallas_call | solution.py:464
  (2 shorter events, 0.0 us)
Async XLA Ops:
  1.4 3.8 %collective-permute-start = (f32[8,128]{1,0:T(8,128)S(1)}, f32[8,128]{1,0:T(8,128)S(1)}, u32[]{:S(2)}, u32[]{:S(2)}) collective-permute-start(f32[8,128]{1,0:T(8,128)S(1)} %get-tuple-element.25.refs_0_), channel_id=1, source_target_pairs={{0,24},{1,25},{2,26},{3,27},{4,28},{5,29},{6,30},{7,31},{8,16},{9,... | collective-permute-start | bytes 12296 | tf_op jit(solution)/shard_map/ppermute | solution.py:417
  3.9 2.0 %collective-permute-start.2 = (f32[720,128]{1,0:T(8,128)S(1)}, f32[720,128]{1,0:T(8,128)S(1)}, u32[]{:S(2)}, u32[]{:S(2)}) collective-permute-start(f32[720,128]{1,0:T(8,128)S(1)} %get-tuple-element.26.block_ref), channel_id=1, source_target_pairs={{0,8},{1,9},{2,10},{3,11},{4,12},{5,13},{6,14},{7,15},{8,0},{9,1},... | collective-permute-start | bytes 1105928 | tf_op jit(solution)/shard_map/ppermute | solution.py:417
  5.2 1.5 %collective-permute-start.1 = (f32[8,128]{1,0:T(8,128)S(1)}, f32[8,128]{1,0:T(8,128)S(1)}, u32[]{:S(2)}, u32[]{:S(2)}) collective-permute-start(f32[8,128]{1,0:T(8,128)S(1)} %collective-permute-done.refs_1_), channel_id=1, source_target_pairs={{0,8},{1,9},{2,10},{3,11},{4,12},{5,13},{6,14},{7,15},{8,0},{9,1},... | collective-permute-start | bytes 12296 | tf_op jit(solution)/shard_map/ppermute | solution.py:417
  6.9 3.2 %collective-permute-start.3 = (f32[4,640]{1,0:T(4,128)S(1)}, f32[4,640]{1,0:T(4,128)S(1)}, u32[]{:S(2)}, u32[]{:S(2)}) collective-permute-start(f32[4,640]{1,0:T(4,128)S(1)} %get-tuple-element.35), channel_id=1, source_target_pairs={{0,9},{1,8},{2,11},{3,10},{4,13},{5,12},{6,15},{7,14},{8,1},{9,0},... | collective-permute-start | bytes 30728 | tf_op jit(solution)/shard_map/ppermute | solution.py:417
  10.1 3.2 %collective-permute-start.4 = (f32[4,640]{1,0:T(4,128)S(1)}, f32[4,640]{1,0:T(4,128)S(1)}, u32[]{:S(2)}, u32[]{:S(2)}) collective-permute-start(f32[4,640]{1,0:T(4,128)S(1)} %get-tuple-element.37), channel_id=1, source_target_pairs={{0,10},{1,11},{2,8},{3,9},{4,14},{5,15},{6,12},{7,13},{8,2},{9,3},... | collective-permute-start | bytes 30728 | tf_op jit(solution)/shard_map/ppermute | solution.py:417
  13.4 4.2 %collective-permute-start.5 = (f32[4,640]{1,0:T(4,128)S(1)}, f32[4,640]{1,0:T(4,128)S(1)}, u32[]{:S(2)}, u32[]{:S(2)}) collective-permute-start(f32[4,640]{1,0:T(4,128)S(1)} %get-tuple-element.39), channel_id=1, source_target_pairs={{0,12},{1,13},{2,14},{3,15},{4,8},{5,9},{6,10},{7,11},{8,4},{9,5},... | collective-permute-start | bytes 30728 | tf_op jit(solution)/shard_map/ppermute | solution.py:417

commit v21 on v17

--- a/solution.py
+++ b/solution.py
@@ -205,19 +205,16 @@
     storage_t[...] = storage.T
     copies[3].wait()
     faces_t[...] = faces_ref[...].T
+    rolls = x_rolls(halves)
+    places = [pl.ds(index, SUBLANES, stride=stride) for index in range(stride)]
+    piece, nodes = tree_coefs([(faces_t[place, :], None, storage_t[place, :]) for place in places], rolls)
     copies[4].wait()
     total = None
     for zone, weight in enumerate(weights):
         total = plus(total, weight * immobile_ref[zone * rows : (zone + 1) * rows, :])
     copies[5].wait()
     source_t[...] = (mobile_ref[...] + capacity * total).T
-    coefs, sides = [], []
-    for index in range(stride):
-        coefs.append((strided(faces_t, index, SUBLANES, stride), None, strided(storage_t, index, SUBLANES, stride)))
-        sides.append((None, strided(source_t, index, SUBLANES, stride)))
-    rolls = x_rolls(halves)
-    piece, nodes = tree_coefs(coefs, rolls)
-    side, givens = tree_sides(sides, rolls, nodes)
+    side, givens = tree_sides([(None, source_t[place, :]) for place in places], rolls, nodes)
     start = 2 * rows
     for node, given in zip(nodes, givens):
         for part in (node[0], node[1], given):

time: 18.3 us -> 18.5 us (1.011)
  no operation moved by 1% of the time
where the time goes in v21:
time: 18.5 us; the launch traced here: 18.3 us
  starting transfers between devices  10.2 us (55%)
  waiting for transfers between devices  5.08 us (27%)
  Pallas kernels  3 us (16%)
    ppermute x6, starting transfers between devices, trade(): return lax.ppermute(value, ('xg', 'yd'), pairs)  10.2 us
    ppermute x6, waiting for transfers between devices, trade(): return lax.ppermute(value, ('xg', 'yd'), pairs)  5.08 us
    pallas_call x8, Pallas kernels, kernel_call(): pl.pallas_call(body, out_shape=outputs, in_specs=[pl.BlockSpec(memory_spa...  3 us
  transfers between devices with their start and end apart: 6, of which 5 were waited for; matrix products, arithmetic and copies ran while one was open for 0% of the time, Pallas kernels for 3%

profile of v21, /device:TPU:0, one launch (start us, length us, event | category | flops | bytes accessed | tf_op | source)
XLA Modules:
  0.0 18.3 jit_solution(14907005613705532828)
XLA Ops:
  0.0 1.5 %shard_map.73 = (f32[8,128]{1,0:T(8,128)S(1)}, f32[720,128]{1,0:T(8,128)S(1)}) custom-call(f32[128,128]{1,0:T(8,128)} %bitcast.9, f32[128,128]{1,0:T(8,128)} %bitcast.10, f32[128,128]{1,0:T(8,128)} %bitcast.11, f32[128,128]{1,0:T(8,128)} %bitcast.12, f32[512,128]{1,0:T(8,128)} %bitcast.8, f32[1,4]{1,0:T(1,128)} %bitcast.13, f32[1,4]{1,0:T(1,128)} %bitcast.14), custom_call_target="tpu_custom_call" | custom-call | flops 500000 | bytes 500000 | tf_op jit(solution)/shard_map/pallas_call | solution.py:464
  1.5 2.4 %collective-permute-start = (f32[8,128]{1,0:T(8,128)S(1)}, f32[8,128]{1,0:T(8,128)S(1)}, u32[]{:S(2)}, u32[]{:S(2)}) collective-permute-start(f32[8,128]{1,0:T(8,128)S(1)} %get-tuple-element.25.refs_0_), channel_id=1, source_target_pairs={{0,24},{1,25},{2,26},{3,27},{4,28},{5,29},{6,30},{7,31},{8,16},{9,... | collective-permute-start | bytes 12296 | tf_op jit(solution)/shard_map/ppermute | solution.py:417
  4.0 0.7 %collective-permute-start.2 = (f32[720,128]{1,0:T(8,128)S(1)}, f32[720,128]{1,0:T(8,128)S(1)}, u32[]{:S(2)}, u32[]{:S(2)}) collective-permute-start(f32[720,128]{1,0:T(8,128)S(1)} %get-tuple-element.26.block_ref), channel_id=1, source_target_pairs={{0,8},{1,9},{2,10},{3,11},{4,12},{5,13},{6,14},{7,15},{8,0},{9,1},... | collective-permute-start | bytes 1105928 | tf_op jit(solution)/shard_map/ppermute | solution.py:417
  4.7 0.2 %shard_map.74 = (f32[8,384]{1,0:T(8,128)S(1)}, f32[384,128]{1,0:T(8,128)S(1)}, f32[256,128]{1,0:T(8,128)S(1)}, f32[480,128]{1,0:T(8,128)S(1)}, f32[256,128]{1,0:T(8,128)S(1)}) custom-call(f32[720,128]{1,0:T(8,128)S(1)} %get-tuple-element.26.block_ref), custom_call_target="tpu_custom_call" | custom-call | flops 10000000000 | bytes 10000000000 | tf_op jit(solution)/shard_map/pallas_call | solution.py:464
  4.9 0.4 %collective-permute-done.refs_1_ = f32[8,128]{1,0:T(8,128)S(1)} collective-permute-done((f32[8,128]{1,0:T(8,128)S(1)}, f32[8,128]{1,0:T(8,128)S(1)}, u32[]{:S(2)}, u32[]{:S(2)}) %collective-permute-start) | collective-permute-done | bytes 4128 | tf_op jit(solution)/shard_map/ppermute | solution.py:417
  5.3 0.6 %collective-permute-start.1 = (f32[8,128]{1,0:T(8,128)S(1)}, f32[8,128]{1,0:T(8,128)S(1)}, u32[]{:S(2)}, u32[]{:S(2)}) collective-permute-start(f32[8,128]{1,0:T(8,128)S(1)} %collective-permute-done.refs_1_), channel_id=1, source_target_pairs={{0,8},{1,9},{2,10},{3,11},{4,12},{5,13},{6,14},{7,15},{8,0},{9,1},... | collective-permute-start | bytes 12296 | tf_op jit(solution)/shard_map/ppermute | solution.py:417
  6.0 0.0 collective-permute-done.2.block_ref
  6.0 0.2 %shard_map.75 = (f32[8,384]{1,0:T(8,128)S(1)}, f32[384,128]{1,0:T(8,128)S(1)}, f32[256,128]{1,0:T(8,128)S(1)}, f32[8,128]{1,0:T(8,128)S(1)}) custom-call(f32[720,128]{1,0:T(8,128)S(1)} %collective-permute-done.2.block_ref), custom_call_target="tpu_custom_call" | custom-call | flops 10000000000 | bytes 10000000000 | tf_op jit(solution)/shard_map/pallas_call | solution.py:464
  6.2 0.6 %collective-permute-done.1.refs_2_ = f32[8,128]{1,0:T(8,128)S(1)} collective-permute-done((f32[8,128]{1,0:T(8,128)S(1)}, f32[8,128]{1,0:T(8,128)S(1)}, u32[]{:S(2)}, u32[]{:S(2)}) %collective-permute-start.1) | collective-permute-done | bytes 4128 | tf_op jit(solution)/shard_map/ppermute | solution.py:417
  6.8 0.2 %shard_map.76 = (f32[4,640]{1,0:T(4,128)S(1)}, f32[4,640]{1,0:T(4,128)S(1)}, f32[128,128]{1,0:T(8,128)S(1)}) custom-call(f32[8,128]{1,0:T(8,128)S(1)} %get-tuple-element.25.refs_0_, f32[8,128]{1,0:T(8,128)S(1)} %collective-permute-done.refs_1_, f32[8,128]{1,0:T(8,128)S(1)} %collective-permute-done.1.refs_2_, f32[384,128]{1,0:T(8,128)S(1)} %get-tuple-element.27.refs_3_, ...), custom_call_target="tpu_custom_call" | custom-call | flops 500000 | bytes 500000 | tf_op jit(solution)/shard_map/pallas_call | solution.py:464
  7.0 1.8 %collective-permute-start.3 = (f32[4,640]{1,0:T(4,128)S(1)}, f32[4,640]{1,0:T(4,128)S(1)}, u32[]{:S(2)}, u32[]{:S(2)}) collective-permute-start(f32[4,640]{1,0:T(4,128)S(1)} %get-tuple-element.35), channel_id=1, source_target_pairs={{0,9},{1,8},{2,11},{3,10},{4,13},{5,12},{6,15},{7,14},{8,1},{9,0},... | collective-permute-start | bytes 30728 | tf_op jit(solution)/shard_map/ppermute | solution.py:417
  8.8 1.4 %collective-permute-done.3.other_ref = f32[4,640]{1,0:T(4,128)S(1)} collective-permute-done((f32[4,640]{1,0:T(4,128)S(1)}, f32[4,640]{1,0:T(4,128)S(1)}, u32[]{:S(2)}, u32[]{:S(2)}) %collective-permute-start.3) | collective-permute-done | bytes 10272 | tf_op jit(solution)/shard_map/ppermute | solution.py:417
  10.2 1.8 %collective-permute-start.4 = (f32[4,640]{1,0:T(4,128)S(1)}, f32[4,640]{1,0:T(4,128)S(1)}, u32[]{:S(2)}, u32[]{:S(2)}) collective-permute-start(f32[4,640]{1,0:T(4,128)S(1)} %get-tuple-element.37), channel_id=1, source_target_pairs={{0,10},{1,11},{2,8},{3,9},{4,14},{5,15},{6,12},{7,13},{8,2},{9,3},... | collective-permute-start | bytes 30728 | tf_op jit(solution)/shard_map/ppermute | solution.py:417
  12.1 1.4 %collective-permute-done.4.other_ref = f32[4,640]{1,0:T(4,128)S(1)} collective-permute-done((f32[4,640]{1,0:T(4,128)S(1)}, f32[4,640]{1,0:T(4,128)S(1)}, u32[]{:S(2)}, u32[]{:S(2)}) %collective-permute-start.4) | collective-permute-done | bytes 10272 | tf_op jit(solution)/shard_map/ppermute | solution.py:417
  13.5 2.8 %collective-permute-start.5 = (f32[4,640]{1,0:T(4,128)S(1)}, f32[4,640]{1,0:T(4,128)S(1)}, u32[]{:S(2)}, u32[]{:S(2)}) collective-permute-start(f32[4,640]{1,0:T(4,128)S(1)} %get-tuple-element.39), channel_id=1, source_target_pairs={{0,12},{1,13},{2,14},{3,15},{4,8},{5,9},{6,10},{7,11},{8,4},{9,5},... | collective-permute-start | bytes 30728 | tf_op jit(solution)/shard_map/ppermute | solution.py:417
  16.3 0.1 shard_map.79.refs_2_
  16.4 1.3 %collective-permute-done.5.other_ref = f32[4,640]{1,0:T(4,128)S(1)} collective-permute-done((f32[4,640]{1,0:T(4,128)S(1)}, f32[4,640]{1,0:T(4,128)S(1)}, u32[]{:S(2)}, u32[]{:S(2)}) %collective-permute-start.5) | collective-permute-done | bytes 10272 | tf_op jit(solution)/shard_map/ppermute | solution.py:417
  17.7 0.7 %shard_map.80 = f32[128,128]{1,0:T(8,128)} custom-call(f32[4,640]{1,0:T(4,128)S(1)} %get-tuple-element.38.own_ref, f32[4,640]{1,0:T(4,128)S(1)} %collective-permute-done.5.other_ref, f32[4,384]{1,0:T(4,128)S(1)} %get-tuple-element.40.refs_0_, f32[4,384]{1,0:T(4,128)S(1)} %get-tuple-element.41.refs_1_, f32[128,128]{1,0:T(8,128)S(1)} %shard_map.79.refs_2_, ...), custom_call_target="tpu_custom_call" | custom-call | flops 500000 | bytes 500000 | tf_op jit(solution)/shard_map/pallas_call | solution.py:464
  (2 shorter events, 0.0 us)
Async XLA Ops:
  1.5 3.8 %collective-permute-start = (f32[8,128]{1,0:T(8,128)S(1)}, f32[8,128]{1,0:T(8,128)S(1)}, u32[]{:S(2)}, u32[]{:S(2)}) collective-permute-start(f32[8,128]{1,0:T(8,128)S(1)} %get-tuple-element.25.refs_0_), channel_id=1, source_target_pairs={{0,24},{1,25},{2,26},{3,27},{4,28},{5,29},{6,30},{7,31},{8,16},{9,... | collective-permute-start | bytes 12296 | tf_op jit(solution)/shard_map/ppermute | solution.py:417
  4.0 2.0 %collective-permute-start.2 = (f32[720,128]{1,0:T(8,128)S(1)}, f32[720,128]{1,0:T(8,128)S(1)}, u32[]{:S(2)}, u32[]{:S(2)}) collective-permute-start(f32[720,128]{1,0:T(8,128)S(1)} %get-tuple-element.26.block_ref), channel_id=1, source_target_pairs={{0,8},{1,9},{2,10},{3,11},{4,12},{5,13},{6,14},{7,15},{8,0},{9,1},... | collective-permute-start | bytes 1105928 | tf_op jit(solution)/shard_map/ppermute | solution.py:417
  5.3 1.5 %collective-permute-start.1 = (f32[8,128]{1,0:T(8,128)S(1)}, f32[8,128]{1,0:T(8,128)S(1)}, u32[]{:S(2)}, u32[]{:S(2)}) collective-permute-start(f32[8,128]{1,0:T(8,128)S(1)} %collective-permute-done.refs_1_), channel_id=1, source_target_pairs={{0,8},{1,9},{2,10},{3,11},{4,12},{5,13},{6,14},{7,15},{8,0},{9,1},... | collective-permute-start | bytes 12296 | tf_op jit(solution)/shard_map/ppermute | solution.py:417
  7.0 3.2 %collective-permute-start.3 = (f32[4,640]{1,0:T(4,128)S(1)}, f32[4,640]{1,0:T(4,128)S(1)}, u32[]{:S(2)}, u32[]{:S(2)}) collective-permute-start(f32[4,640]{1,0:T(4,128)S(1)} %get-tuple-element.35), channel_id=1, source_target_pairs={{0,9},{1,8},{2,11},{3,10},{4,13},{5,12},{6,15},{7,14},{8,1},{9,0},... | collective-permute-start | bytes 30728 | tf_op jit(solution)/shard_map/ppermute | solution.py:417
  10.2 3.2 %collective-permute-start.4 = (f32[4,640]{1,0:T(4,128)S(1)}, f32[4,640]{1,0:T(4,128)S(1)}, u32[]{:S(2)}, u32[]{:S(2)}) collective-permute-start(f32[4,640]{1,0:T(4,128)S(1)} %get-tuple-element.37), channel_id=1, source_target_pairs={{0,10},{1,11},{2,8},{3,9},{4,14},{5,15},{6,12},{7,13},{8,2},{9,3},... | collective-permute-start | bytes 30728 | tf_op jit(solution)/shard_map/ppermute | solution.py:417
  13.5 4.2 %collective-permute-start.5 = (f32[4,640]{1,0:T(4,128)S(1)}, f32[4,640]{1,0:T(4,128)S(1)}, u32[]{:S(2)}, u32[]{:S(2)}) collective-permute-start(f32[4,640]{1,0:T(4,128)S(1)} %get-tuple-element.39), channel_id=1, source_target_pairs={{0,12},{1,13},{2,14},{3,15},{4,8},{5,9},{6,10},{7,11},{8,4},{9,5},... | collective-permute-start | bytes 30728 | tf_op jit(solution)/shard_map/ppermute | solution.py:417

commit v22 on v21

--- a/solution.py
+++ b/solution.py
@@ -97,6 +97,33 @@
         piece, given = join_sides(piece, other, nodes[len(givens)])
         givens.append(given)
     return piece, givens
+
+
+def join_all(left, right):
+    coefs, node = join_coefs(left[:3], right[:3])
+    sides, given = join_sides(left[3:], right[3:], node)
+    return coefs + sides, (node[0], node[1], given)
+
+
+def tree_all(leaves, rolls):
+    nodes = []
+    level = leaves
+    while len(level) > 1:
+        pairs = [join_all(level[index], level[index + 1]) for index in range(0, len(level), 2)]
+        nodes += [node for _, node in pairs]
+        level = [joined for joined, _ in pairs]
+    piece = level[0]
+    count = SUBLANES
+    level = [piece] + [tuple(ahead(part, step, 0) for part in piece) for step in range(1, count)]
+    while len(level) > 1:
+        pairs = [join_all(level[index], level[index + 1]) for index in range(0, len(level), 2)]
+        nodes.append(pairs[0][1])
+        level = [joined for joined, _ in pairs]
+    piece = level[0]
+    for step, axis in rolls[len(doubling(count)) :]:
+        piece, node = join_all(piece, tuple(ahead(part, step, axis) for part in piece))
+        nodes.append(node)
+    return piece, nodes
 
 
 def tree_values(before, after, rolls, count, nodes, givens):
@@ -205,22 +232,22 @@
     storage_t[...] = storage.T
     copies[3].wait()
     faces_t[...] = faces_ref[...].T
-    rolls = x_rolls(halves)
-    places = [pl.ds(index, SUBLANES, stride=stride) for index in range(stride)]
-    piece, nodes = tree_coefs([(faces_t[place, :], None, storage_t[place, :]) for place in places], rolls)
     copies[4].wait()
     total = None
     for zone, weight in enumerate(weights):
         total = plus(total, weight * immobile_ref[zone * rows : (zone + 1) * rows, :])
     copies[5].wait()
     source_t[...] = (mobile_ref[...] + capacity * total).T
-    side, givens = tree_sides([(None, source_t[place, :]) for place in places], rolls, nodes)
+    leaves = []
+    for index in range(stride):
+        face, held, source = (strided(ref, index, SUBLANES, stride) for ref in (faces_t, storage_t, source_t))
+        leaves.append((face, None, held, None, source))
+    piece, nodes = tree_all(leaves, x_rolls(halves))
     start = 2 * rows
-    for node, given in zip(nodes, givens):
-        for part in (node[0], node[1], given):
-            block_ref[start : start + SUBLANES, :] = part
-            start += SUBLANES
-    for row, value in enumerate(piece + side):
+    for part in [part for node in nodes for part in node]:
+        block_ref[start : start + SUBLANES, :] = part
+        start += SUBLANES
+    for row, value in enumerate(piece):
         message_ref[row : row + 1, :] = value[0:1, :]
         block_ref[start + row : start + row + 1, :] = value[0:1, :]
     copies[6].wait()
@@ -333,9 +360,7 @@
         for end in range(2):
             parts = (values * sums_ref[end * rows : (end + 1) * rows, :]).reshape(-1, SUBLANES, LANES)
             side = jnp.sum(parts, axis=0)
-            for step in doubling(SUBLANES // halves):
-                side = side + behind(side, step * halves, 0)
-            sides.append(side)
+            sides.append(sum([behind(side, step, 0) for step in range(halves, SUBLANES, halves)], side))
     for end in range(2):
         put(3 + end, sides[end], sides[2 + end])
 

time: 18.5 us -> 18.3 us (0.989)
  no operation moved by 1% of the time
where the time goes in v22:
time: 18.3 us; the launch traced here: 18.2 us
  starting transfers between devices  10.2 us (56%)
  waiting for transfers between devices  5.08 us (28%)
  Pallas kernels  2.82 us (15%)
    ppermute x6, starting transfers between devices, trade(): return lax.ppermute(value, ('xg', 'yd'), pairs)  10.2 us
    ppermute x6, waiting for transfers between devices, trade(): return lax.ppermute(value, ('xg', 'yd'), pairs)  5.08 us
    pallas_call x8, Pallas kernels, kernel_call(): pl.pallas_call(body, out_shape=outputs, in_specs=[pl.BlockSpec(memory_spa...  2.82 us
  transfers between devices with their start and end apart: 6, of which 5 were waited for; matrix products, arithmetic and copies ran while one was open for 0% of the time, Pallas kernels for 3%

profile of v22, /device:TPU:0, one launch (start us, length us, event | category | flops | bytes accessed | tf_op | source)
XLA Modules:
  0.0 18.2 jit_solution(16453156520720081635)
XLA Ops:
  0.0 1.4 %shard_map.73 = (f32[8,128]{1,0:T(8,128)S(1)}, f32[720,128]{1,0:T(8,128)S(1)}) custom-call(f32[128,128]{1,0:T(8,128)} %bitcast.9, f32[128,128]{1,0:T(8,128)} %bitcast.10, f32[128,128]{1,0:T(8,128)} %bitcast.11, f32[128,128]{1,0:T(8,128)} %bitcast.12, f32[512,128]{1,0:T(8,128)} %bitcast.8, f32[1,4]{1,0:T(1,128)} %bitcast.13, f32[1,4]{1,0:T(1,128)} %bitcast.14), custom_call_target="tpu_custom_call" | custom-call | flops 500000 | bytes 500000 | tf_op jit(solution)/shard_map/pallas_call | solution.py:489
  1.4 2.4 %collective-permute-start = (f32[8,128]{1,0:T(8,128)S(1)}, f32[8,128]{1,0:T(8,128)S(1)}, u32[]{:S(2)}, u32[]{:S(2)}) collective-permute-start(f32[8,128]{1,0:T(8,128)S(1)} %get-tuple-element.25.refs_0_), channel_id=1, source_target_pairs={{0,24},{1,25},{2,26},{3,27},{4,28},{5,29},{6,30},{7,31},{8,16},{9,... | collective-permute-start | bytes 12296 | tf_op jit(solution)/shard_map/ppermute | solution.py:442
  3.8 0.7 %collective-permute-start.2 = (f32[720,128]{1,0:T(8,128)S(1)}, f32[720,128]{1,0:T(8,128)S(1)}, u32[]{:S(2)}, u32[]{:S(2)}) collective-permute-start(f32[720,128]{1,0:T(8,128)S(1)} %get-tuple-element.26.block_ref), channel_id=1, source_target_pairs={{0,8},{1,9},{2,10},{3,11},{4,12},{5,13},{6,14},{7,15},{8,0},{9,1},... | collective-permute-start | bytes 1105928 | tf_op jit(solution)/shard_map/ppermute | solution.py:442
  4.5 0.2 %shard_map.74 = (f32[8,384]{1,0:T(8,128)S(1)}, f32[384,128]{1,0:T(8,128)S(1)}, f32[256,128]{1,0:T(8,128)S(1)}, f32[480,128]{1,0:T(8,128)S(1)}, f32[256,128]{1,0:T(8,128)S(1)}) custom-call(f32[720,128]{1,0:T(8,128)S(1)} %get-tuple-element.26.block_ref), custom_call_target="tpu_custom_call" | custom-call | flops 10000000000 | bytes 10000000000 | tf_op jit(solution)/shard_map/pallas_call | solution.py:489
  4.7 0.4 %collective-permute-done.refs_1_ = f32[8,128]{1,0:T(8,128)S(1)} collective-permute-done((f32[8,128]{1,0:T(8,128)S(1)}, f32[8,128]{1,0:T(8,128)S(1)}, u32[]{:S(2)}, u32[]{:S(2)}) %collective-permute-start) | collective-permute-done | bytes 4128 | tf_op jit(solution)/shard_map/ppermute | solution.py:442
  5.1 0.6 %collective-permute-start.1 = (f32[8,128]{1,0:T(8,128)S(1)}, f32[8,128]{1,0:T(8,128)S(1)}, u32[]{:S(2)}, u32[]{:S(2)}) collective-permute-start(f32[8,128]{1,0:T(8,128)S(1)} %collective-permute-done.refs_1_), channel_id=1, source_target_pairs={{0,8},{1,9},{2,10},{3,11},{4,12},{5,13},{6,14},{7,15},{8,0},{9,1},... | collective-permute-start | bytes 12296 | tf_op jit(solution)/shard_map/ppermute | solution.py:442
  5.8 0.0 collective-permute-done.2.block_ref
  5.8 0.2 %shard_map.75 = (f32[8,384]{1,0:T(8,128)S(1)}, f32[384,128]{1,0:T(8,128)S(1)}, f32[256,128]{1,0:T(8,128)S(1)}, f32[8,128]{1,0:T(8,128)S(1)}) custom-call(f32[720,128]{1,0:T(8,128)S(1)} %collective-permute-done.2.block_ref), custom_call_target="tpu_custom_call" | custom-call | flops 10000000000 | bytes 10000000000 | tf_op jit(solution)/shard_map/pallas_call | solution.py:489
  6.0 0.6 %collective-permute-done.1.refs_2_ = f32[8,128]{1,0:T(8,128)S(1)} collective-permute-done((f32[8,128]{1,0:T(8,128)S(1)}, f32[8,128]{1,0:T(8,128)S(1)}, u32[]{:S(2)}, u32[]{:S(2)}) %collective-permute-start.1) | collective-permute-done | bytes 4128 | tf_op jit(solution)/shard_map/ppermute | solution.py:442
  6.6 0.2 %shard_map.76 = (f32[4,640]{1,0:T(4,128)S(1)}, f32[4,640]{1,0:T(4,128)S(1)}, f32[128,128]{1,0:T(8,128)S(1)}) custom-call(f32[8,128]{1,0:T(8,128)S(1)} %get-tuple-element.25.refs_0_, f32[8,128]{1,0:T(8,128)S(1)} %collective-permute-done.refs_1_, f32[8,128]{1,0:T(8,128)S(1)} %collective-permute-done.1.refs_2_, f32[384,128]{1,0:T(8,128)S(1)} %get-tuple-element.27.refs_3_, ...), custom_call_target="tpu_custom_call" | custom-call | flops 500000 | bytes 500000 | tf_op jit(solution)/shard_map/pallas_call | solution.py:489
  6.8 1.8 %collective-permute-start.3 = (f32[4,640]{1,0:T(4,128)S(1)}, f32[4,640]{1,0:T(4,128)S(1)}, u32[]{:S(2)}, u32[]{:S(2)}) collective-permute-start(f32[4,640]{1,0:T(4,128)S(1)} %get-tuple-element.35), channel_id=1, source_target_pairs={{0,9},{1,8},{2,11},{3,10},{4,13},{5,12},{6,15},{7,14},{8,1},{9,0},... | collective-permute-start | bytes 30728 | tf_op jit(solution)/shard_map/ppermute | solution.py:442
  8.7 1.4 %collective-permute-done.3.other_ref = f32[4,640]{1,0:T(4,128)S(1)} collective-permute-done((f32[4,640]{1,0:T(4,128)S(1)}, f32[4,640]{1,0:T(4,128)S(1)}, u32[]{:S(2)}, u32[]{:S(2)}) %collective-permute-start.3) | collective-permute-done | bytes 10272 | tf_op jit(solution)/shard_map/ppermute | solution.py:442
  10.1 1.8 %collective-permute-start.4 = (f32[4,640]{1,0:T(4,128)S(1)}, f32[4,640]{1,0:T(4,128)S(1)}, u32[]{:S(2)}, u32[]{:S(2)}) collective-permute-start(f32[4,640]{1,0:T(4,128)S(1)} %get-tuple-element.37), channel_id=1, source_target_pairs={{0,10},{1,11},{2,8},{3,9},{4,14},{5,15},{6,12},{7,13},{8,2},{9,3},... | collective-permute-start | bytes 30728 | tf_op jit(solution)/shard_map/ppermute | solution.py:442
  11.9 1.4 %collective-permute-done.4.other_ref = f32[4,640]{1,0:T(4,128)S(1)} collective-permute-done((f32[4,640]{1,0:T(4,128)S(1)}, f32[4,640]{1,0:T(4,128)S(1)}, u32[]{:S(2)}, u32[]{:S(2)}) %collective-permute-start.4) | collective-permute-done | bytes 10272 | tf_op jit(solution)/shard_map/ppermute | solution.py:442
  13.3 2.8 %collective-permute-start.5 = (f32[4,640]{1,0:T(4,128)S(1)}, f32[4,640]{1,0:T(4,128)S(1)}, u32[]{:S(2)}, u32[]{:S(2)}) collective-permute-start(f32[4,640]{1,0:T(4,128)S(1)} %get-tuple-element.39), channel_id=1, source_target_pairs={{0,12},{1,13},{2,14},{3,15},{4,8},{5,9},{6,10},{7,11},{8,4},{9,5},... | collective-permute-start | bytes 30728 | tf_op jit(solution)/shard_map/ppermute | solution.py:442
  16.1 0.1 shard_map.79.refs_2_
  16.2 1.3 %collective-permute-done.5.other_ref = f32[4,640]{1,0:T(4,128)S(1)} collective-permute-done((f32[4,640]{1,0:T(4,128)S(1)}, f32[4,640]{1,0:T(4,128)S(1)}, u32[]{:S(2)}, u32[]{:S(2)}) %collective-permute-start.5) | collective-permute-done | bytes 10272 | tf_op jit(solution)/shard_map/ppermute | solution.py:442
  17.5 0.7 %shard_map.80 = f32[128,128]{1,0:T(8,128)} custom-call(f32[4,640]{1,0:T(4,128)S(1)} %get-tuple-element.38.own_ref, f32[4,640]{1,0:T(4,128)S(1)} %collective-permute-done.5.other_ref, f32[4,384]{1,0:T(4,128)S(1)} %get-tuple-element.40.refs_0_, f32[4,384]{1,0:T(4,128)S(1)} %get-tuple-element.41.refs_1_, f32[128,128]{1,0:T(8,128)S(1)} %shard_map.79.refs_2_, ...), custom_call_target="tpu_custom_call" | custom-call | flops 500000 | bytes 500000 | tf_op jit(solution)/shard_map/pallas_call | solution.py:489
  (2 shorter events, 0.0 us)
Async XLA Ops:
  1.4 3.8 %collective-permute-start = (f32[8,128]{1,0:T(8,128)S(1)}, f32[8,128]{1,0:T(8,128)S(1)}, u32[]{:S(2)}, u32[]{:S(2)}) collective-permute-start(f32[8,128]{1,0:T(8,128)S(1)} %get-tuple-element.25.refs_0_), channel_id=1, source_target_pairs={{0,24},{1,25},{2,26},{3,27},{4,28},{5,29},{6,30},{7,31},{8,16},{9,... | collective-permute-start | bytes 12296 | tf_op jit(solution)/shard_map/ppermute | solution.py:442
  3.8 2.0 %collective-permute-start.2 = (f32[720,128]{1,0:T(8,128)S(1)}, f32[720,128]{1,0:T(8,128)S(1)}, u32[]{:S(2)}, u32[]{:S(2)}) collective-permute-start(f32[720,128]{1,0:T(8,128)S(1)} %get-tuple-element.26.block_ref), channel_id=1, source_target_pairs={{0,8},{1,9},{2,10},{3,11},{4,12},{5,13},{6,14},{7,15},{8,0},{9,1},... | collective-permute-start | bytes 1105928 | tf_op jit(solution)/shard_map/ppermute | solution.py:442
  5.1 1.5 %collective-permute-start.1 = (f32[8,128]{1,0:T(8,128)S(1)}, f32[8,128]{1,0:T(8,128)S(1)}, u32[]{:S(2)}, u32[]{:S(2)}) collective-permute-start(f32[8,128]{1,0:T(8,128)S(1)} %collective-permute-done.refs_1_), channel_id=1, source_target_pairs={{0,8},{1,9},{2,10},{3,11},{4,12},{5,13},{6,14},{7,15},{8,0},{9,1},... | collective-permute-start | bytes 12296 | tf_op jit(solution)/shard_map/ppermute | solution.py:442
  6.8 3.2 %collective-permute-start.3 = (f32[4,640]{1,0:T(4,128)S(1)}, f32[4,640]{1,0:T(4,128)S(1)}, u32[]{:S(2)}, u32[]{:S(2)}) collective-permute-start(f32[4,640]{1,0:T(4,128)S(1)} %get-tuple-element.35), channel_id=1, source_target_pairs={{0,9},{1,8},{2,11},{3,10},{4,13},{5,12},{6,15},{7,14},{8,1},{9,0},... | collective-permute-start | bytes 30728 | tf_op jit(solution)/shard_map/ppermute | solution.py:442
  10.1 3.2 %collective-permute-start.4 = (f32[4,640]{1,0:T(4,128)S(1)}, f32[4,640]{1,0:T(4,128)S(1)}, u32[]{:S(2)}, u32[]{:S(2)}) collective-permute-start(f32[4,640]{1,0:T(4,128)S(1)} %get-tuple-element.37), channel_id=1, source_target_pairs={{0,10},{1,11},{2,8},{3,9},{4,14},{5,15},{6,12},{7,13},{8,2},{9,3},... | collective-permute-start | bytes 30728 | tf_op jit(solution)/shard_map/ppermute | solution.py:442
  13.3 4.2 %collective-permute-start.5 = (f32[4,640]{1,0:T(4,128)S(1)}, f32[4,640]{1,0:T(4,128)S(1)}, u32[]{:S(2)}, u32[]{:S(2)}) collective-permute-start(f32[4,640]{1,0:T(4,128)S(1)} %get-tuple-element.39), channel_id=1, source_target_pairs={{0,12},{1,13},{2,14},{3,15},{4,8},{5,9},{6,10},{7,11},{8,4},{9,5},... | collective-permute-start | bytes 30728 | tf_op jit(solution)/shard_map/ppermute | solution.py:442

commit v23 on v22

--- a/solution.py
+++ b/solution.py
@@ -408,7 +408,7 @@
 
 def y_back_kernel(halves, axis, rounds, own_ref, other_ref, *refs):
     path_refs = refs[: rounds - 1]
-    given_ref, spread_ref, out_ref = refs[rounds - 1 :]
+    given_ref, spread_ref, out_hbm, out_ref, gone = refs[rounds - 1 :]
     rows = out_ref.shape[0]
     joined, path = join_by_bit(read_message(own_ref), read_message(other_ref), own_bit(axis, rounds - 1))
     _, head, tail, side_head, side_tail = joined
@@ -431,6 +431,9 @@
         part = slice(start, start + SUBLANES)
         late = slice(rows + start, rows + start + SUBLANES)
         out_ref[part, :] = given_ref[part, :] + spread_ref[part, :] * ends[0] + spread_ref[late, :] * ends[1]
+    copy = pltpu.make_async_copy(out_ref, out_hbm, gone)
+    copy.start()
+    copy.wait()
 
 
 def trade(value, x_step, y_step):
@@ -485,12 +488,12 @@
     return VMEM(shape, jnp.float32)
 
 
-def kernel_call(body, operands, outputs, scratch, space=VMEM, cost=500000):
+def kernel_call(body, operands, outputs, scratch, space=VMEM, cost=500000, out_space=VMEM):
     return pl.pallas_call(
         body,
         out_shape=outputs,
         in_specs=[pl.BlockSpec(memory_space=space)] * len(operands),
-        out_specs=[pl.BlockSpec(memory_space=VMEM)] * len(outputs),
+        out_specs=[pl.BlockSpec(memory_space=out_space)] * len(outputs),
         scratch_shapes=scratch,
         cost_estimate=pl.CostEstimate(flops=cost, bytes_accessed=cost, transcendentals=0),
         compiler_params=pltpu.CompilerParams(vmem_limit_bytes=16 * 1024 * 1024),
@@ -558,7 +561,8 @@
         functools.partial(y_back_kernel, halves, "yd", rounds),
         (*pieces, given, spread),
         [f32(rows, LANES)],
-        [],
+        [square, pltpu.SemaphoreType.DMA],
+        out_space=pltpu.HBM,
     )
     return updated.reshape(shape)
 

time: 18.3 us -> 18.3 us (level)
  no operation moved by 1% of the time
where the time goes in v23:
time: 18.3 us; the launch traced here: 18.2 us
  starting transfers between devices  10.2 us (56%)
  waiting for transfers between devices  5.08 us (28%)
  Pallas kernels  2.83 us (15%)
    ppermute x6, starting transfers between devices, trade(): return lax.ppermute(value, ('xg', 'yd'), pairs)  10.2 us
    ppermute x6, waiting for transfers between devices, trade(): return lax.ppermute(value, ('xg', 'yd'), pairs)  5.08 us
    pallas_call x8, Pallas kernels, kernel_call(): pl.pallas_call(body, out_shape=outputs, in_specs=[pl.BlockSpec(memory_spa...  2.83 us
  transfers between devices with their start and end apart: 6, of which 5 were waited for; matrix products, arithmetic and copies ran while one was open for 0% of the time, Pallas kernels for 3%

profile of v23, /device:TPU:0, one launch (start us, length us, event | category | flops | bytes accessed | tf_op | source)
XLA Modules:
  0.0 18.2 jit_solution(14327519528451750463)
XLA Ops:
  0.0 1.4 %shard_map.73 = (f32[8,128]{1,0:T(8,128)S(1)}, f32[720,128]{1,0:T(8,128)S(1)}) custom-call(f32[128,128]{1,0:T(8,128)} %bitcast.9, f32[128,128]{1,0:T(8,128)} %bitcast.10, f32[128,128]{1,0:T(8,128)} %bitcast.11, f32[128,128]{1,0:T(8,128)} %bitcast.12, f32[512,128]{1,0:T(8,128)} %bitcast.8, f32[1,4]{1,0:T(1,128)} %bitcast.13, f32[1,4]{1,0:T(1,128)} %bitcast.14), custom_call_target="tpu_custom_call" | custom-call | flops 500000 | bytes 500000 | tf_op jit(solution)/shard_map/pallas_call | solution.py:492
  1.4 2.4 %collective-permute-start = (f32[8,128]{1,0:T(8,128)S(1)}, f32[8,128]{1,0:T(8,128)S(1)}, u32[]{:S(2)}, u32[]{:S(2)}) collective-permute-start(f32[8,128]{1,0:T(8,128)S(1)} %get-tuple-element.25.refs_0_), channel_id=1, source_target_pairs={{0,24},{1,25},{2,26},{3,27},{4,28},{5,29},{6,30},{7,31},{8,16},{9,... | collective-permute-start | bytes 12296 | tf_op jit(solution)/shard_map/ppermute | solution.py:445
  3.8 0.7 %collective-permute-start.2 = (f32[720,128]{1,0:T(8,128)S(1)}, f32[720,128]{1,0:T(8,128)S(1)}, u32[]{:S(2)}, u32[]{:S(2)}) collective-permute-start(f32[720,128]{1,0:T(8,128)S(1)} %get-tuple-element.26.block_ref), channel_id=1, source_target_pairs={{0,8},{1,9},{2,10},{3,11},{4,12},{5,13},{6,14},{7,15},{8,0},{9,1},... | collective-permute-start | bytes 1105928 | tf_op jit(solution)/shard_map/ppermute | solution.py:445
  4.5 0.2 %shard_map.74 = (f32[8,384]{1,0:T(8,128)S(1)}, f32[384,128]{1,0:T(8,128)S(1)}, f32[256,128]{1,0:T(8,128)S(1)}, f32[480,128]{1,0:T(8,128)S(1)}, f32[256,128]{1,0:T(8,128)S(1)}) custom-call(f32[720,128]{1,0:T(8,128)S(1)} %get-tuple-element.26.block_ref), custom_call_target="tpu_custom_call" | custom-call | flops 10000000000 | bytes 10000000000 | tf_op jit(solution)/shard_map/pallas_call | solution.py:492
  4.7 0.4 %collective-permute-done.refs_1_ = f32[8,128]{1,0:T(8,128)S(1)} collective-permute-done((f32[8,128]{1,0:T(8,128)S(1)}, f32[8,128]{1,0:T(8,128)S(1)}, u32[]{:S(2)}, u32[]{:S(2)}) %collective-permute-start) | collective-permute-done | bytes 4128 | tf_op jit(solution)/shard_map/ppermute | solution.py:445
  5.1 0.6 %collective-permute-start.1 = (f32[8,128]{1,0:T(8,128)S(1)}, f32[8,128]{1,0:T(8,128)S(1)}, u32[]{:S(2)}, u32[]{:S(2)}) collective-permute-start(f32[8,128]{1,0:T(8,128)S(1)} %collective-permute-done.refs_1_), channel_id=1, source_target_pairs={{0,8},{1,9},{2,10},{3,11},{4,12},{5,13},{6,14},{7,15},{8,0},{9,1},... | collective-permute-start | bytes 12296 | tf_op jit(solution)/shard_map/ppermute | solution.py:445
  5.8 0.0 collective-permute-done.2.block_ref
  5.8 0.2 %shard_map.75 = (f32[8,384]{1,0:T(8,128)S(1)}, f32[384,128]{1,0:T(8,128)S(1)}, f32[256,128]{1,0:T(8,128)S(1)}, f32[8,128]{1,0:T(8,128)S(1)}) custom-call(f32[720,128]{1,0:T(8,128)S(1)} %collective-permute-done.2.block_ref), custom_call_target="tpu_custom_call" | custom-call | flops 10000000000 | bytes 10000000000 | tf_op jit(solution)/shard_map/pallas_call | solution.py:492
  6.0 0.6 %collective-permute-done.1.refs_2_ = f32[8,128]{1,0:T(8,128)S(1)} collective-permute-done((f32[8,128]{1,0:T(8,128)S(1)}, f32[8,128]{1,0:T(8,128)S(1)}, u32[]{:S(2)}, u32[]{:S(2)}) %collective-permute-start.1) | collective-permute-done | bytes 4128 | tf_op jit(solution)/shard_map/ppermute | solution.py:445
  6.6 0.2 %shard_map.76 = (f32[4,640]{1,0:T(4,128)S(1)}, f32[4,640]{1,0:T(4,128)S(1)}, f32[128,128]{1,0:T(8,128)S(1)}) custom-call(f32[8,128]{1,0:T(8,128)S(1)} %get-tuple-element.25.refs_0_, f32[8,128]{1,0:T(8,128)S(1)} %collective-permute-done.refs_1_, f32[8,128]{1,0:T(8,128)S(1)} %collective-permute-done.1.refs_2_, f32[384,128]{1,0:T(8,128)S(1)} %get-tuple-element.27.refs_3_, ...), custom_call_target="tpu_custom_call" | custom-call | flops 500000 | bytes 500000 | tf_op jit(solution)/shard_map/pallas_call | solution.py:492
  6.8 1.8 %collective-permute-start.3 = (f32[4,640]{1,0:T(4,128)S(1)}, f32[4,640]{1,0:T(4,128)S(1)}, u32[]{:S(2)}, u32[]{:S(2)}) collective-permute-start(f32[4,640]{1,0:T(4,128)S(1)} %get-tuple-element.35), channel_id=1, source_target_pairs={{0,9},{1,8},{2,11},{3,10},{4,13},{5,12},{6,15},{7,14},{8,1},{9,0},... | collective-permute-start | bytes 30728 | tf_op jit(solution)/shard_map/ppermute | solution.py:445
  8.7 1.4 %collective-permute-done.3.other_ref = f32[4,640]{1,0:T(4,128)S(1)} collective-permute-done((f32[4,640]{1,0:T(4,128)S(1)}, f32[4,640]{1,0:T(4,128)S(1)}, u32[]{:S(2)}, u32[]{:S(2)}) %collective-permute-start.3) | collective-permute-done | bytes 10272 | tf_op jit(solution)/shard_map/ppermute | solution.py:445
  10.1 1.8 %collective-permute-start.4 = (f32[4,640]{1,0:T(4,128)S(1)}, f32[4,640]{1,0:T(4,128)S(1)}, u32[]{:S(2)}, u32[]{:S(2)}) collective-permute-start(f32[4,640]{1,0:T(4,128)S(1)} %get-tuple-element.37), channel_id=1, source_target_pairs={{0,10},{1,11},{2,8},{3,9},{4,14},{5,15},{6,12},{7,13},{8,2},{9,3},... | collective-permute-start | bytes 30728 | tf_op jit(solution)/shard_map/ppermute | solution.py:445
  11.9 1.4 %collective-permute-done.4.other_ref = f32[4,640]{1,0:T(4,128)S(1)} collective-permute-done((f32[4,640]{1,0:T(4,128)S(1)}, f32[4,640]{1,0:T(4,128)S(1)}, u32[]{:S(2)}, u32[]{:S(2)}) %collective-permute-start.4) | collective-permute-done | bytes 10272 | tf_op jit(solution)/shard_map/ppermute | solution.py:445
  13.3 2.8 %collective-permute-start.5 = (f32[4,640]{1,0:T(4,128)S(1)}, f32[4,640]{1,0:T(4,128)S(1)}, u32[]{:S(2)}, u32[]{:S(2)}) collective-permute-start(f32[4,640]{1,0:T(4,128)S(1)} %get-tuple-element.39), channel_id=1, source_target_pairs={{0,12},{1,13},{2,14},{3,15},{4,8},{5,9},{6,10},{7,11},{8,4},{9,5},... | collective-permute-start | bytes 30728 | tf_op jit(solution)/shard_map/ppermute | solution.py:445
  16.1 0.1 shard_map.79.refs_2_
  16.2 1.3 %collective-permute-done.5.other_ref = f32[4,640]{1,0:T(4,128)S(1)} collective-permute-done((f32[4,640]{1,0:T(4,128)S(1)}, f32[4,640]{1,0:T(4,128)S(1)}, u32[]{:S(2)}, u32[]{:S(2)}) %collective-permute-start.5) | collective-permute-done | bytes 10272 | tf_op jit(solution)/shard_map/ppermute | solution.py:445
  17.5 0.7 %shard_map.80 = f32[128,128]{1,0:T(8,128)} custom-call(f32[4,640]{1,0:T(4,128)S(1)} %get-tuple-element.38.own_ref, f32[4,640]{1,0:T(4,128)S(1)} %collective-permute-done.5.other_ref, f32[4,384]{1,0:T(4,128)S(1)} %get-tuple-element.40.refs_0_, f32[4,384]{1,0:T(4,128)S(1)} %get-tuple-element.41.refs_1_, f32[128,128]{1,0:T(8,128)S(1)} %shard_map.79.refs_2_, ...), custom_call_target="tpu_custom_call" | custom-call | flops 500000 | bytes 500000 | tf_op jit(solution)/shard_map/pallas_call | solution.py:492
  (2 shorter events, 0.0 us)
Async XLA Ops:
  1.4 3.8 %collective-permute-start = (f32[8,128]{1,0:T(8,128)S(1)}, f32[8,128]{1,0:T(8,128)S(1)}, u32[]{:S(2)}, u32[]{:S(2)}) collective-permute-start(f32[8,128]{1,0:T(8,128)S(1)} %get-tuple-element.25.refs_0_), channel_id=1, source_target_pairs={{0,24},{1,25},{2,26},{3,27},{4,28},{5,29},{6,30},{7,31},{8,16},{9,... | collective-permute-start | bytes 12296 | tf_op jit(solution)/shard_map/ppermute | solution.py:445
  3.8 2.0 %collective-permute-start.2 = (f32[720,128]{1,0:T(8,128)S(1)}, f32[720,128]{1,0:T(8,128)S(1)}, u32[]{:S(2)}, u32[]{:S(2)}) collective-permute-start(f32[720,128]{1,0:T(8,128)S(1)} %get-tuple-element.26.block_ref), channel_id=1, source_target_pairs={{0,8},{1,9},{2,10},{3,11},{4,12},{5,13},{6,14},{7,15},{8,0},{9,1},... | collective-permute-start | bytes 1105928 | tf_op jit(solution)/shard_map/ppermute | solution.py:445
  5.1 1.5 %collective-permute-start.1 = (f32[8,128]{1,0:T(8,128)S(1)}, f32[8,128]{1,0:T(8,128)S(1)}, u32[]{:S(2)}, u32[]{:S(2)}) collective-permute-start(f32[8,128]{1,0:T(8,128)S(1)} %collective-permute-done.refs_1_), channel_id=1, source_target_pairs={{0,8},{1,9},{2,10},{3,11},{4,12},{5,13},{6,14},{7,15},{8,0},{9,1},... | collective-permute-start | bytes 12296 | tf_op jit(solution)/shard_map/ppermute | solution.py:445
  6.8 3.2 %collective-permute-start.3 = (f32[4,640]{1,0:T(4,128)S(1)}, f32[4,640]{1,0:T(4,128)S(1)}, u32[]{:S(2)}, u32[]{:S(2)}) collective-permute-start(f32[4,640]{1,0:T(4,128)S(1)} %get-tuple-element.35), channel_id=1, source_target_pairs={{0,9},{1,8},{2,11},{3,10},{4,13},{5,12},{6,15},{7,14},{8,1},{9,0},... | collective-permute-start | bytes 30728 | tf_op jit(solution)/shard_map/ppermute | solution.py:445
  10.1 3.2 %collective-permute-start.4 = (f32[4,640]{1,0:T(4,128)S(1)}, f32[4,640]{1,0:T(4,128)S(1)}, u32[]{:S(2)}, u32[]{:S(2)}) collective-permute-start(f32[4,640]{1,0:T(4,128)S(1)} %get-tuple-element.37), channel_id=1, source_target_pairs={{0,10},{1,11},{2,8},{3,9},{4,14},{5,15},{6,12},{7,13},{8,2},{9,3},... | collective-permute-start | bytes 30728 | tf_op jit(solution)/shard_map/ppermute | solution.py:445
  13.3 4.2 %collective-permute-start.5 = (f32[4,640]{1,0:T(4,128)S(1)}, f32[4,640]{1,0:T(4,128)S(1)}, u32[]{:S(2)}, u32[]{:S(2)}) collective-permute-start(f32[4,640]{1,0:T(4,128)S(1)} %get-tuple-element.39), channel_id=1, source_target_pairs={{0,12},{1,13},{2,14},{3,15},{4,8},{5,9},{6,10},{7,11},{8,4},{9,5},... | collective-permute-start | bytes 30728 | tf_op jit(solution)/shard_map/ppermute | solution.py:445

commit v24 on v22

--- a/solution.py
+++ b/solution.py
@@ -320,10 +320,6 @@
     return slice(number * LANES, (number + 1) * LANES)
 
 
-def put_traded(ref, row, rows, number, value):
-    ref[(row + rows // 2) % rows : (row + rows // 2) % rows + value.shape[0], quantity(number)] = value
-
-
 def along_line(bound, halves, rows):
     value = jnp.broadcast_to(bound, (SUBLANES, rows))
     lane = lax.broadcasted_iota(jnp.int32, value.shape, 1)
@@ -379,8 +375,8 @@
             given_ref[place, :] = value
 
 
-def read_message(ref):
-    return [ref[:, quantity(number)] for number in range(QUANTITIES)]
+def read_message(ref, rows=None):
+    return [ref[0:rows, quantity(number)] for number in range(QUANTITIES)]
 
 
 def join_by_bit(own, other, upper):
@@ -397,11 +393,12 @@
 
 def y_join_kernel(axis, bit, own_ref, other_ref, kept_ref, sent_ref, path_ref):
     joined, path = join_by_bit(read_message(own_ref), read_message(other_ref), own_bit(axis, bit))
-    rows = own_ref.shape[0]
+    half = own_ref.shape[0] // 2
     for number, value in enumerate(joined):
         kept_ref[:, quantity(number)] = value
-        for row in (0, rows // 2):
-            put_traded(sent_ref, row, rows, number, value[row : row + rows // 2, :])
+        sent_ref[0:half, quantity(number)] = value[half:, :]
+        if sent_ref.shape[0] > half:
+            sent_ref[half:, quantity(number)] = value[0:half, :]
     for number, value in enumerate(path):
         path_ref[:, quantity(number)] = value
 
@@ -410,10 +407,11 @@
     path_refs = refs[: rounds - 1]
     given_ref, spread_ref, out_ref = refs[rounds - 1 :]
     rows = out_ref.shape[0]
-    joined, path = join_by_bit(read_message(own_ref), read_message(other_ref), own_bit(axis, rounds - 1))
+    own, other = (read_message(ref, halves) for ref in (own_ref, other_ref))
+    joined, path = join_by_bit(own, other, own_bit(axis, rounds - 1))
     _, head, tail, side_head, side_tail = joined
     before = after = (side_head + side_tail) * inverse(head + tail)
-    paths = [[ref[:, quantity(number)] for number in range(3)] for ref in path_refs] + [path]
+    paths = [[ref[0:halves, quantity(number)] for number in range(3)] for ref in path_refs] + [path]
     for bit in reversed(range(rounds)):
         node = paths[bit]
         middle = middle_value(node, node[2], before, after)
@@ -470,7 +468,7 @@
             kept, sent, path = kernel_call(
                 functools.partial(y_join_kernel, "yd", bit),
                 (kept, received),
-                [held_f32(*kept.shape), f32(*kept.shape), held_f32(rows, 3 * LANES)],
+                [held_f32(*kept.shape), f32(rows // 2 if bit == len(steps) - 2 else rows, kept.shape[1]), held_f32(rows, 3 * LANES)],
                 [],
             )
             paths.append(path)

time: 18.3 us -> 18.3 us (level)
  no operation moved by 1% of the time
where the time goes in v24:
time: 18.3 us; the launch traced here: 18.1 us
  starting transfers between devices  10.2 us (56%)
  waiting for transfers between devices  5.03 us (27%)
  Pallas kernels  2.82 us (15%)
    ppermute x6, starting transfers between devices, trade(): return lax.ppermute(value, ('xg', 'yd'), pairs)  10.2 us
    ppermute x6, waiting for transfers between devices, trade(): return lax.ppermute(value, ('xg', 'yd'), pairs)  5.03 us
    pallas_call x8, Pallas kernels, kernel_call(): pl.pallas_call(body, out_shape=outputs, in_specs=[pl.BlockSpec(memory_spa...  2.82 us
  transfers between devices with their start and end apart: 6, of which 5 were waited for; matrix products, arithmetic and copies ran while one was open for 0% of the time, Pallas kernels for 3%

profile of v24, /device:TPU:0, one launch (start us, length us, event | category | flops | bytes accessed | tf_op | source)
XLA Modules:
  0.0 18.1 jit_solution(10882987299139664401)
XLA Ops:
  0.0 1.4 %shard_map.73 = (f32[8,128]{1,0:T(8,128)S(1)}, f32[720,128]{1,0:T(8,128)S(1)}) custom-call(f32[128,128]{1,0:T(8,128)} %bitcast.9, f32[128,128]{1,0:T(8,128)} %bitcast.10, f32[128,128]{1,0:T(8,128)} %bitcast.11, f32[128,128]{1,0:T(8,128)} %bitcast.12, f32[512,128]{1,0:T(8,128)} %bitcast.8, f32[1,4]{1,0:T(1,128)} %bitcast.13, f32[1,4]{1,0:T(1,128)} %bitcast.14), custom_call_target="tpu_custom_call" | custom-call | flops 500000 | bytes 500000 | tf_op jit(solution)/shard_map/pallas_call | solution.py:487
  1.4 2.4 %collective-permute-start = (f32[8,128]{1,0:T(8,128)S(1)}, f32[8,128]{1,0:T(8,128)S(1)}, u32[]{:S(2)}, u32[]{:S(2)}) collective-permute-start(f32[8,128]{1,0:T(8,128)S(1)} %get-tuple-element.25.refs_0_), channel_id=1, source_target_pairs={{0,24},{1,25},{2,26},{3,27},{4,28},{5,29},{6,30},{7,31},{8,16},{9,... | collective-permute-start | bytes 12296 | tf_op jit(solution)/shard_map/ppermute | solution.py:440
  3.8 0.7 %collective-permute-start.2 = (f32[720,128]{1,0:T(8,128)S(1)}, f32[720,128]{1,0:T(8,128)S(1)}, u32[]{:S(2)}, u32[]{:S(2)}) collective-permute-start(f32[720,128]{1,0:T(8,128)S(1)} %get-tuple-element.26.block_ref), channel_id=1, source_target_pairs={{0,8},{1,9},{2,10},{3,11},{4,12},{5,13},{6,14},{7,15},{8,0},{9,1},... | collective-permute-start | bytes 1105928 | tf_op jit(solution)/shard_map/ppermute | solution.py:440
  4.5 0.2 %shard_map.74 = (f32[8,384]{1,0:T(8,128)S(1)}, f32[384,128]{1,0:T(8,128)S(1)}, f32[256,128]{1,0:T(8,128)S(1)}, f32[480,128]{1,0:T(8,128)S(1)}, f32[256,128]{1,0:T(8,128)S(1)}) custom-call(f32[720,128]{1,0:T(8,128)S(1)} %get-tuple-element.26.block_ref), custom_call_target="tpu_custom_call" | custom-call | flops 10000000000 | bytes 10000000000 | tf_op jit(solution)/shard_map/pallas_call | solution.py:487
  4.7 0.4 %collective-permute-done.refs_1_ = f32[8,128]{1,0:T(8,128)S(1)} collective-permute-done((f32[8,128]{1,0:T(8,128)S(1)}, f32[8,128]{1,0:T(8,128)S(1)}, u32[]{:S(2)}, u32[]{:S(2)}) %collective-permute-start) | collective-permute-done | bytes 4128 | tf_op jit(solution)/shard_map/ppermute | solution.py:440
  5.1 0.6 %collective-permute-start.1 = (f32[8,128]{1,0:T(8,128)S(1)}, f32[8,128]{1,0:T(8,128)S(1)}, u32[]{:S(2)}, u32[]{:S(2)}) collective-permute-start(f32[8,128]{1,0:T(8,128)S(1)} %collective-permute-done.refs_1_), channel_id=1, source_target_pairs={{0,8},{1,9},{2,10},{3,11},{4,12},{5,13},{6,14},{7,15},{8,0},{9,1},... | collective-permute-start | bytes 12296 | tf_op jit(solution)/shard_map/ppermute | solution.py:440
  5.8 0.0 collective-permute-done.2.block_ref
  5.8 0.2 %shard_map.75 = (f32[8,384]{1,0:T(8,128)S(1)}, f32[384,128]{1,0:T(8,128)S(1)}, f32[256,128]{1,0:T(8,128)S(1)}, f32[8,128]{1,0:T(8,128)S(1)}) custom-call(f32[720,128]{1,0:T(8,128)S(1)} %collective-permute-done.2.block_ref), custom_call_target="tpu_custom_call" | custom-call | flops 10000000000 | bytes 10000000000 | tf_op jit(solution)/shard_map/pallas_call | solution.py:487
  6.0 0.6 %collective-permute-done.1.refs_2_ = f32[8,128]{1,0:T(8,128)S(1)} collective-permute-done((f32[8,128]{1,0:T(8,128)S(1)}, f32[8,128]{1,0:T(8,128)S(1)}, u32[]{:S(2)}, u32[]{:S(2)}) %collective-permute-start.1) | collective-permute-done | bytes 4128 | tf_op jit(solution)/shard_map/ppermute | solution.py:440
  6.6 0.2 %shard_map.76 = (f32[4,640]{1,0:T(4,128)S(1)}, f32[4,640]{1,0:T(4,128)S(1)}, f32[128,128]{1,0:T(8,128)S(1)}) custom-call(f32[8,128]{1,0:T(8,128)S(1)} %get-tuple-element.25.refs_0_, f32[8,128]{1,0:T(8,128)S(1)} %collective-permute-done.refs_1_, f32[8,128]{1,0:T(8,128)S(1)} %collective-permute-done.1.refs_2_, f32[384,128]{1,0:T(8,128)S(1)} %get-tuple-element.27.refs_3_, ...), custom_call_target="tpu_custom_call" | custom-call | flops 500000 | bytes 500000 | tf_op jit(solution)/shard_map/pallas_call | solution.py:487
  6.8 1.8 %collective-permute-start.3 = (f32[4,640]{1,0:T(4,128)S(1)}, f32[4,640]{1,0:T(4,128)S(1)}, u32[]{:S(2)}, u32[]{:S(2)}) collective-permute-start(f32[4,640]{1,0:T(4,128)S(1)} %get-tuple-element.35), channel_id=1, source_target_pairs={{0,9},{1,8},{2,11},{3,10},{4,13},{5,12},{6,15},{7,14},{8,1},{9,0},... | collective-permute-start | bytes 30728 | tf_op jit(solution)/shard_map/ppermute | solution.py:440
  8.7 1.4 %collective-permute-done.3.other_ref = f32[4,640]{1,0:T(4,128)S(1)} collective-permute-done((f32[4,640]{1,0:T(4,128)S(1)}, f32[4,640]{1,0:T(4,128)S(1)}, u32[]{:S(2)}, u32[]{:S(2)}) %collective-permute-start.3) | collective-permute-done | bytes 10272 | tf_op jit(solution)/shard_map/ppermute | solution.py:440
  10.1 1.8 %collective-permute-start.4 = (f32[4,640]{1,0:T(4,128)S(1)}, f32[4,640]{1,0:T(4,128)S(1)}, u32[]{:S(2)}, u32[]{:S(2)}) collective-permute-start(f32[4,640]{1,0:T(4,128)S(1)} %get-tuple-element.37), channel_id=1, source_target_pairs={{0,10},{1,11},{2,8},{3,9},{4,14},{5,15},{6,12},{7,13},{8,2},{9,3},... | collective-permute-start | bytes 30728 | tf_op jit(solution)/shard_map/ppermute | solution.py:440
  11.9 1.4 %collective-permute-done.4.other_ref = f32[4,640]{1,0:T(4,128)S(1)} collective-permute-done((f32[4,640]{1,0:T(4,128)S(1)}, f32[4,640]{1,0:T(4,128)S(1)}, u32[]{:S(2)}, u32[]{:S(2)}) %collective-permute-start.4) | collective-permute-done | bytes 10272 | tf_op jit(solution)/shard_map/ppermute | solution.py:440
  13.3 2.8 %collective-permute-start.5 = (f32[2,640]{1,0:T(2,128)S(1)}, f32[2,640]{1,0:T(2,128)S(1)}, u32[]{:S(2)}, u32[]{:S(2)}) collective-permute-start(f32[2,640]{1,0:T(2,128)S(1)} %get-tuple-element.39), channel_id=1, source_target_pairs={{0,12},{1,13},{2,14},{3,15},{4,8},{5,9},{6,10},{7,11},{8,4},{9,5},... | collective-permute-start | bytes 15368 | tf_op jit(solution)/shard_map/ppermute | solution.py:440
  16.1 0.1 shard_map.79.refs_2_
  16.2 1.2 %collective-permute-done.5.other_ref = f32[2,640]{1,0:T(2,128)S(1)} collective-permute-done((f32[2,640]{1,0:T(2,128)S(1)}, f32[2,640]{1,0:T(2,128)S(1)}, u32[]{:S(2)}, u32[]{:S(2)}) %collective-permute-start.5) | collective-permute-done | bytes 5152 | tf_op jit(solution)/shard_map/ppermute | solution.py:440
  17.4 0.7 %shard_map.80 = f32[128,128]{1,0:T(8,128)} custom-call(f32[4,640]{1,0:T(4,128)S(1)} %get-tuple-element.38.own_ref, f32[2,640]{1,0:T(2,128)S(1)} %collective-permute-done.5.other_ref, f32[4,384]{1,0:T(4,128)S(1)} %get-tuple-element.40.refs_0_, f32[4,384]{1,0:T(4,128)S(1)} %get-tuple-element.41.refs_1_, f32[128,128]{1,0:T(8,128)S(1)} %shard_map.79.refs_2_, ...), custom_call_target="tpu_custom_call" | custom-call | flops 500000 | bytes 500000 | tf_op jit(solution)/shard_map/pallas_call | solution.py:487
  (2 shorter events, 0.0 us)
Async XLA Ops:
  1.4 3.8 %collective-permute-start = (f32[8,128]{1,0:T(8,128)S(1)}, f32[8,128]{1,0:T(8,128)S(1)}, u32[]{:S(2)}, u32[]{:S(2)}) collective-permute-start(f32[8,128]{1,0:T(8,128)S(1)} %get-tuple-element.25.refs_0_), channel_id=1, source_target_pairs={{0,24},{1,25},{2,26},{3,27},{4,28},{5,29},{6,30},{7,31},{8,16},{9,... | collective-permute-start | bytes 12296 | tf_op jit(solution)/shard_map/ppermute | solution.py:440
  3.8 2.0 %collective-permute-start.2 = (f32[720,128]{1,0:T(8,128)S(1)}, f32[720,128]{1,0:T(8,128)S(1)}, u32[]{:S(2)}, u32[]{:S(2)}) collective-permute-start(f32[720,128]{1,0:T(8,128)S(1)} %get-tuple-element.26.block_ref), channel_id=1, source_target_pairs={{0,8},{1,9},{2,10},{3,11},{4,12},{5,13},{6,14},{7,15},{8,0},{9,1},... | collective-permute-start | bytes 1105928 | tf_op jit(solution)/shard_map/ppermute | solution.py:440
  5.1 1.5 %collective-permute-start.1 = (f32[8,128]{1,0:T(8,128)S(1)}, f32[8,128]{1,0:T(8,128)S(1)}, u32[]{:S(2)}, u32[]{:S(2)}) collective-permute-start(f32[8,128]{1,0:T(8,128)S(1)} %collective-permute-done.refs_1_), channel_id=1, source_target_pairs={{0,8},{1,9},{2,10},{3,11},{4,12},{5,13},{6,14},{7,15},{8,0},{9,1},... | collective-permute-start | bytes 12296 | tf_op jit(solution)/shard_map/ppermute | solution.py:440
  6.8 3.2 %collective-permute-start.3 = (f32[4,640]{1,0:T(4,128)S(1)}, f32[4,640]{1,0:T(4,128)S(1)}, u32[]{:S(2)}, u32[]{:S(2)}) collective-permute-start(f32[4,640]{1,0:T(4,128)S(1)} %get-tuple-element.35), channel_id=1, source_target_pairs={{0,9},{1,8},{2,11},{3,10},{4,13},{5,12},{6,15},{7,14},{8,1},{9,0},... | collective-permute-start | bytes 30728 | tf_op jit(solution)/shard_map/ppermute | solution.py:440
  10.1 3.2 %collective-permute-start.4 = (f32[4,640]{1,0:T(4,128)S(1)}, f32[4,640]{1,0:T(4,128)S(1)}, u32[]{:S(2)}, u32[]{:S(2)}) collective-permute-start(f32[4,640]{1,0:T(4,128)S(1)} %get-tuple-element.37), channel_id=1, source_target_pairs={{0,10},{1,11},{2,8},{3,9},{4,14},{5,15},{6,12},{7,13},{8,2},{9,3},... | collective-permute-start | bytes 30728 | tf_op jit(solution)/shard_map/ppermute | solution.py:440
  13.3 4.1 %collective-permute-start.5 = (f32[2,640]{1,0:T(2,128)S(1)}, f32[2,640]{1,0:T(2,128)S(1)}, u32[]{:S(2)}, u32[]{:S(2)}) collective-permute-start(f32[2,640]{1,0:T(2,128)S(1)} %get-tuple-element.39), channel_id=1, source_target_pairs={{0,12},{1,13},{2,14},{3,15},{4,8},{5,9},{6,10},{7,11},{8,4},{9,5},... | collective-permute-start | bytes 15368 | tf_op jit(solution)/shard_map/ppermute | solution.py:440

commit v25 on v24

--- a/solution.py
+++ b/solution.py
@@ -229,15 +229,15 @@
     capacity = capacity_ref[...]
     storage = 1.0 + capacity * sum(weights[1:], weights[0])
     block_ref[0:rows, :] = storage
-    storage_t[...] = storage.T
+    storage_t[0:LANES, :] = storage.T
     copies[3].wait()
-    faces_t[...] = faces_ref[...].T
+    faces_t[0:LANES, :] = faces_ref[...].T
     copies[4].wait()
     total = None
     for zone, weight in enumerate(weights):
         total = plus(total, weight * immobile_ref[zone * rows : (zone + 1) * rows, :])
     copies[5].wait()
-    source_t[...] = (mobile_ref[...] + capacity * total).T
+    source_t[0:LANES, :] = (mobile_ref[...] + capacity * total).T
     leaves = []
     for index in range(stride):
         face, held, source = (strided(ref, index, SUBLANES, stride) for ref in (faces_t, storage_t, source_t))
@@ -334,7 +334,7 @@
     slots = message_slots([*refs[:pieces], last_ref], SUBLANES, 1, 1, [0] * len(order))
     slots = [slots[order.index(place)] for place in range(len(order))]
     bounds = ring_bounds(slots, lax.axis_index(axis))
-    rows = values_ref.shape[0]
+    rows = lines_refs[0].shape[1]
 
     height = 2 * halves
     first = lax.broadcasted_iota(jnp.int32, (SUBLANES, LANES), 0) < halves
@@ -349,10 +349,10 @@
     for block in range(2):
         lines_ref, sums_ref = lines_refs[block], sums_refs[block]
         before, after = (along_line(bound, halves, rows) for bound in bounds[block])
-        values = lines_ref[0:LANES, :] + lines_ref[LANES : 2 * LANES, :] * before + lines_ref[2 * LANES :, :] * after
+        values = lines_ref[0:LANES, :] + lines_ref[LANES : 2 * LANES, :] * before + lines_ref[2 * LANES : 3 * LANES, :] * after
         values = values.T
         if block == 0:
-            values_ref[...] = values
+            values_ref[0:rows, :] = values
         for end in range(2):
             parts = (values * sums_ref[end * rows : (end + 1) * rows, :]).reshape(-1, SUBLANES, LANES)
             side = jnp.sum(parts, axis=0)
@@ -361,8 +361,7 @@
         put(3 + end, sides[end], sides[2 + end])
 
 
-def y_given_kernel(halves, block_ref, values_ref, state_ref, given_ref):
-    rows = values_ref.shape[0]
+def y_given_kernel(halves, rows, block_ref, values_ref, state_ref, given_ref):
     stride = rows // SUBLANES
     total = stride // halves - 1 + len(y_rolls())
     nothing = jnp.zeros((SUBLANES, LANES), jnp.float32)
@@ -509,6 +508,7 @@
     mobile, dispersion_x, dispersion_y = flat(mobile), flat(dispersion_x), flat(dispersion_y)
     capacity, immobile = flat(capacity), flat(immobile)
     square = VMEM((rows, LANES), jnp.float32)
+    spare = max(rows, LANES) // SUBLANES
     x_nodes = LANES // SUBLANES - 1 + len(x_rolls(halves))
     y_nodes = halves * (rows // SUBLANES // halves - 1 + len(y_rolls()))
     message, block = kernel_call(
@@ -524,13 +524,13 @@
         + [VMEM((zones * rows, LANES), jnp.float32)]
         + [pltpu.SMEM((1, zones), jnp.float32)] * 2
         + [pltpu.SemaphoreType.DMA((7,))]
-        + [square] * 3,
+        + [VMEM((LANES + LANES // SUBLANES, rows), jnp.float32)] * 3,
         pltpu.HBM,
     )
     def prepare(part, own):
-        outputs = [held_f32(SUBLANES, 3 * LANES), held_f32(3 * LANES, rows), held_f32(2 * rows, LANES)]
+        outputs = [held_f32(SUBLANES, 3 * LANES), held_f32(3 * LANES + spare, rows), held_f32(2 * rows + spare, LANES)]
         if own:
-            outputs += [held_f32(3 * y_nodes * SUBLANES, LANES), held_f32(2 * rows, LANES)]
+            outputs += [held_f32(3 * y_nodes * SUBLANES, LANES), held_f32(2 * rows + spare, LANES)]
         else:
             outputs += [held_f32(SUBLANES, rows)]
         return kernel_call(functools.partial(prepare_kernel, halves, own), (part,), outputs, [], cost=10000000000)
@@ -544,12 +544,12 @@
         [
             held_f32(2 * halves, QUANTITIES * LANES),
             f32(2 * halves, QUANTITIES * LANES),
-            held_f32(rows, LANES),
+            held_f32(rows + spare, LANES),
         ],
         [],
     )
     (given,) = kernel_call(
-        functools.partial(y_given_kernel, halves), (block, values, y_state), [held_f32(rows, LANES)], []
+        functools.partial(y_given_kernel, halves, rows), (block, values, y_state), [held_f32(rows + spare, LANES)], []
     )
     pieces, rounds = y_exchange(kept, sent)
     (updated,) = kernel_call(

time: 18.3 us -> 18.3 us (level)
  no operation moved by 1% of the time
where the time goes in v25:
time: 18.3 us; the launch traced here: 18.1 us
  starting transfers between devices  10.2 us (56%)
  waiting for transfers between devices  5.03 us (27%)
  Pallas kernels  2.83 us (15%)
    ppermute x6, starting transfers between devices, trade(): return lax.ppermute(value, ('xg', 'yd'), pairs)  10.2 us
    ppermute x6, waiting for transfers between devices, trade(): return lax.ppermute(value, ('xg', 'yd'), pairs)  5.03 us
    pallas_call x8, Pallas kernels, kernel_call(): pl.pallas_call(body, out_shape=outputs, in_specs=[pl.BlockSpec(memory_spa...  2.83 us
  transfers between devices with their start and end apart: 6, of which 5 were waited for; matrix products, arithmetic and copies ran while one was open for 0% of the time, Pallas kernels for 3%

profile of v25, /device:TPU:0, one launch (start us, length us, event | category | flops | bytes accessed | tf_op | source)
XLA Modules:
  0.0 18.1 jit_solution(14905715166035640215)
XLA Ops:
  0.0 1.4 %shard_map.73 = (f32[8,128]{1,0:T(8,128)S(1)}, f32[720,128]{1,0:T(8,128)S(1)}) custom-call(f32[128,128]{1,0:T(8,128)} %bitcast.9, f32[128,128]{1,0:T(8,128)} %bitcast.10, f32[128,128]{1,0:T(8,128)} %bitcast.11, f32[128,128]{1,0:T(8,128)} %bitcast.12, f32[512,128]{1,0:T(8,128)} %bitcast.8, f32[1,4]{1,0:T(1,128)} %bitcast.13, f32[1,4]{1,0:T(1,128)} %bitcast.14), custom_call_target="tpu_custom_call" | custom-call | flops 500000 | bytes 500000 | tf_op jit(solution)/shard_map/pallas_call | solution.py:486
  1.4 2.4 %collective-permute-start = (f32[8,128]{1,0:T(8,128)S(1)}, f32[8,128]{1,0:T(8,128)S(1)}, u32[]{:S(2)}, u32[]{:S(2)}) collective-permute-start(f32[8,128]{1,0:T(8,128)S(1)} %get-tuple-element.25.refs_0_), channel_id=1, source_target_pairs={{0,24},{1,25},{2,26},{3,27},{4,28},{5,29},{6,30},{7,31},{8,16},{9,... | collective-permute-start | bytes 12296 | tf_op jit(solution)/shard_map/ppermute | solution.py:439
  3.8 0.7 %collective-permute-start.2 = (f32[720,128]{1,0:T(8,128)S(1)}, f32[720,128]{1,0:T(8,128)S(1)}, u32[]{:S(2)}, u32[]{:S(2)}) collective-permute-start(f32[720,128]{1,0:T(8,128)S(1)} %get-tuple-element.26.block_ref), channel_id=1, source_target_pairs={{0,8},{1,9},{2,10},{3,11},{4,12},{5,13},{6,14},{7,15},{8,0},{9,1},... | collective-permute-start | bytes 1105928 | tf_op jit(solution)/shard_map/ppermute | solution.py:439
  4.5 0.2 %shard_map.74 = (f32[8,384]{1,0:T(8,128)S(1)}, f32[400,128]{1,0:T(8,128)S(1)}, f32[272,128]{1,0:T(8,128)S(1)}, f32[480,128]{1,0:T(8,128)S(1)}, f32[272,128]{1,0:T(8,128)S(1)}) custom-call(f32[720,128]{1,0:T(8,128)S(1)} %get-tuple-element.26.block_ref), custom_call_target="tpu_custom_call" | custom-call | flops 10000000000 | bytes 10000000000 | tf_op jit(solution)/shard_map/pallas_call | solution.py:486
  4.7 0.4 %collective-permute-done.refs_1_ = f32[8,128]{1,0:T(8,128)S(1)} collective-permute-done((f32[8,128]{1,0:T(8,128)S(1)}, f32[8,128]{1,0:T(8,128)S(1)}, u32[]{:S(2)}, u32[]{:S(2)}) %collective-permute-start) | collective-permute-done | bytes 4128 | tf_op jit(solution)/shard_map/ppermute | solution.py:439
  5.1 0.6 %collective-permute-start.1 = (f32[8,128]{1,0:T(8,128)S(1)}, f32[8,128]{1,0:T(8,128)S(1)}, u32[]{:S(2)}, u32[]{:S(2)}) collective-permute-start(f32[8,128]{1,0:T(8,128)S(1)} %collective-permute-done.refs_1_), channel_id=1, source_target_pairs={{0,8},{1,9},{2,10},{3,11},{4,12},{5,13},{6,14},{7,15},{8,0},{9,1},... | collective-permute-start | bytes 12296 | tf_op jit(solution)/shard_map/ppermute | solution.py:439
  5.8 0.0 collective-permute-done.2.block_ref
  5.8 0.2 %shard_map.75 = (f32[8,384]{1,0:T(8,128)S(1)}, f32[400,128]{1,0:T(8,128)S(1)}, f32[272,128]{1,0:T(8,128)S(1)}, f32[8,128]{1,0:T(8,128)S(1)}) custom-call(f32[720,128]{1,0:T(8,128)S(1)} %collective-permute-done.2.block_ref), custom_call_target="tpu_custom_call" | custom-call | flops 10000000000 | bytes 10000000000 | tf_op jit(solution)/shard_map/pallas_call | solution.py:486
  6.0 0.6 %collective-permute-done.1.refs_2_ = f32[8,128]{1,0:T(8,128)S(1)} collective-permute-done((f32[8,128]{1,0:T(8,128)S(1)}, f32[8,128]{1,0:T(8,128)S(1)}, u32[]{:S(2)}, u32[]{:S(2)}) %collective-permute-start.1) | collective-permute-done | bytes 4128 | tf_op jit(solution)/shard_map/ppermute | solution.py:439
  6.6 0.2 %shard_map.76 = (f32[4,640]{1,0:T(4,128)S(1)}, f32[4,640]{1,0:T(4,128)S(1)}, f32[144,128]{1,0:T(8,128)S(1)}) custom-call(f32[8,128]{1,0:T(8,128)S(1)} %get-tuple-element.25.refs_0_, f32[8,128]{1,0:T(8,128)S(1)} %collective-permute-done.refs_1_, f32[8,128]{1,0:T(8,128)S(1)} %collective-permute-done.1.refs_2_, f32[400,128]{1,0:T(8,128)S(1)} %get-tuple-element.27.refs_3_, ...), custom_call_target="tpu_custom_call" | custom-call | flops 500000 | bytes 500000 | tf_op jit(solution)/shard_map/pallas_call | solution.py:486
  6.8 1.8 %collective-permute-start.3 = (f32[4,640]{1,0:T(4,128)S(1)}, f32[4,640]{1,0:T(4,128)S(1)}, u32[]{:S(2)}, u32[]{:S(2)}) collective-permute-start(f32[4,640]{1,0:T(4,128)S(1)} %get-tuple-element.35), channel_id=1, source_target_pairs={{0,9},{1,8},{2,11},{3,10},{4,13},{5,12},{6,15},{7,14},{8,1},{9,0},... | collective-permute-start | bytes 30728 | tf_op jit(solution)/shard_map/ppermute | solution.py:439
  8.7 1.4 %collective-permute-done.3.other_ref = f32[4,640]{1,0:T(4,128)S(1)} collective-permute-done((f32[4,640]{1,0:T(4,128)S(1)}, f32[4,640]{1,0:T(4,128)S(1)}, u32[]{:S(2)}, u32[]{:S(2)}) %collective-permute-start.3) | collective-permute-done | bytes 10272 | tf_op jit(solution)/shard_map/ppermute | solution.py:439
  10.1 1.8 %collective-permute-start.4 = (f32[4,640]{1,0:T(4,128)S(1)}, f32[4,640]{1,0:T(4,128)S(1)}, u32[]{:S(2)}, u32[]{:S(2)}) collective-permute-start(f32[4,640]{1,0:T(4,128)S(1)} %get-tuple-element.37), channel_id=1, source_target_pairs={{0,10},{1,11},{2,8},{3,9},{4,14},{5,15},{6,12},{7,13},{8,2},{9,3},... | collective-permute-start | bytes 30728 | tf_op jit(solution)/shard_map/ppermute | solution.py:439
  11.9 1.4 %collective-permute-done.4.other_ref = f32[4,640]{1,0:T(4,128)S(1)} collective-permute-done((f32[4,640]{1,0:T(4,128)S(1)}, f32[4,640]{1,0:T(4,128)S(1)}, u32[]{:S(2)}, u32[]{:S(2)}) %collective-permute-start.4) | collective-permute-done | bytes 10272 | tf_op jit(solution)/shard_map/ppermute | solution.py:439
  13.3 2.8 %collective-permute-start.5 = (f32[2,640]{1,0:T(2,128)S(1)}, f32[2,640]{1,0:T(2,128)S(1)}, u32[]{:S(2)}, u32[]{:S(2)}) collective-permute-start(f32[2,640]{1,0:T(2,128)S(1)} %get-tuple-element.39), channel_id=1, source_target_pairs={{0,12},{1,13},{2,14},{3,15},{4,8},{5,9},{6,10},{7,11},{8,4},{9,5},... | collective-permute-start | bytes 15368 | tf_op jit(solution)/shard_map/ppermute | solution.py:439
  16.1 0.1 shard_map.79.refs_2_
  16.2 1.2 %collective-permute-done.5.other_ref = f32[2,640]{1,0:T(2,128)S(1)} collective-permute-done((f32[2,640]{1,0:T(2,128)S(1)}, f32[2,640]{1,0:T(2,128)S(1)}, u32[]{:S(2)}, u32[]{:S(2)}) %collective-permute-start.5) | collective-permute-done | bytes 5152 | tf_op jit(solution)/shard_map/ppermute | solution.py:439
  17.4 0.7 %shard_map.80 = f32[128,128]{1,0:T(8,128)} custom-call(f32[4,640]{1,0:T(4,128)S(1)} %get-tuple-element.38.own_ref, f32[2,640]{1,0:T(2,128)S(1)} %collective-permute-done.5.other_ref, f32[4,384]{1,0:T(4,128)S(1)} %get-tuple-element.40.refs_0_, f32[4,384]{1,0:T(4,128)S(1)} %get-tuple-element.41.refs_1_, f32[144,128]{1,0:T(8,128)S(1)} %shard_map.79.refs_2_, ...), custom_call_target="tpu_custom_call" | custom-call | flops 500000 | bytes 500000 | tf_op jit(solution)/shard_map/pallas_call | solution.py:486
  (2 shorter events, 0.0 us)
Async XLA Ops:
  1.4 3.8 %collective-permute-start = (f32[8,128]{1,0:T(8,128)S(1)}, f32[8,128]{1,0:T(8,128)S(1)}, u32[]{:S(2)}, u32[]{:S(2)}) collective-permute-start(f32[8,128]{1,0:T(8,128)S(1)} %get-tuple-element.25.refs_0_), channel_id=1, source_target_pairs={{0,24},{1,25},{2,26},{3,27},{4,28},{5,29},{6,30},{7,31},{8,16},{9,... | collective-permute-start | bytes 12296 | tf_op jit(solution)/shard_map/ppermute | solution.py:439
  3.8 2.0 %collective-permute-start.2 = (f32[720,128]{1,0:T(8,128)S(1)}, f32[720,128]{1,0:T(8,128)S(1)}, u32[]{:S(2)}, u32[]{:S(2)}) collective-permute-start(f32[720,128]{1,0:T(8,128)S(1)} %get-tuple-element.26.block_ref), channel_id=1, source_target_pairs={{0,8},{1,9},{2,10},{3,11},{4,12},{5,13},{6,14},{7,15},{8,0},{9,1},... | collective-permute-start | bytes 1105928 | tf_op jit(solution)/shard_map/ppermute | solution.py:439
  5.1 1.5 %collective-permute-start.1 = (f32[8,128]{1,0:T(8,128)S(1)}, f32[8,128]{1,0:T(8,128)S(1)}, u32[]{:S(2)}, u32[]{:S(2)}) collective-permute-start(f32[8,128]{1,0:T(8,128)S(1)} %collective-permute-done.refs_1_), channel_id=1, source_target_pairs={{0,8},{1,9},{2,10},{3,11},{4,12},{5,13},{6,14},{7,15},{8,0},{9,1},... | collective-permute-start | bytes 12296 | tf_op jit(solution)/shard_map/ppermute | solution.py:439
  6.8 3.2 %collective-permute-start.3 = (f32[4,640]{1,0:T(4,128)S(1)}, f32[4,640]{1,0:T(4,128)S(1)}, u32[]{:S(2)}, u32[]{:S(2)}) collective-permute-start(f32[4,640]{1,0:T(4,128)S(1)} %get-tuple-element.35), channel_id=1, source_target_pairs={{0,9},{1,8},{2,11},{3,10},{4,13},{5,12},{6,15},{7,14},{8,1},{9,0},... | collective-permute-start | bytes 30728 | tf_op jit(solution)/shard_map/ppermute | solution.py:439
  10.1 3.2 %collective-permute-start.4 = (f32[4,640]{1,0:T(4,128)S(1)}, f32[4,640]{1,0:T(4,128)S(1)}, u32[]{:S(2)}, u32[]{:S(2)}) collective-permute-start(f32[4,640]{1,0:T(4,128)S(1)} %get-tuple-element.37), channel_id=1, source_target_pairs={{0,10},{1,11},{2,8},{3,9},{4,14},{5,15},{6,12},{7,13},{8,2},{9,3},... | collective-permute-start | bytes 30728 | tf_op jit(solution)/shard_map/ppermute | solution.py:439
  13.3 4.1 %collective-permute-start.5 = (f32[2,640]{1,0:T(2,128)S(1)}, f32[2,640]{1,0:T(2,128)S(1)}, u32[]{:S(2)}, u32[]{:S(2)}) collective-permute-start(f32[2,640]{1,0:T(2,128)S(1)} %get-tuple-element.39), channel_id=1, source_target_pairs={{0,12},{1,13},{2,14},{3,15},{4,8},{5,9},{6,10},{7,11},{8,4},{9,5},... | collective-permute-start | bytes 15368 | tf_op jit(solution)/shard_map/ppermute | solution.py:439

commit v26 on v25

--- a/solution.py
+++ b/solution.py
@@ -216,22 +216,22 @@
 ):
     rows = mobile_ref.shape[0]
     pairs = (
-        (rates_hbm, rates_ref), (shares_hbm, shares_ref), (capacity_hbm, capacity_ref), (faces_hbm, faces_ref),
+        (faces_hbm, faces_ref), (capacity_hbm, capacity_ref), (rates_hbm, rates_ref), (shares_hbm, shares_ref),
         (immobile_hbm, immobile_ref), (mobile_hbm, mobile_ref), (across_hbm, block_ref.at[rows : 2 * rows, :]),
     )
     copies = [pltpu.make_async_copy(pair[0], pair[1], arrived.at[place]) for place, pair in enumerate(pairs)]
     for place, copy in enumerate(copies):
         copy.start(priority=int(place in (4, 6)))
     stride = LANES // SUBLANES
-    for copy in copies[:3]:
+    copies[0].wait()
+    faces_t[0:LANES, :] = faces_ref[...].T
+    for copy in copies[1:4]:
         copy.wait()
     weights = capacity_weights(rates_ref, shares_ref)
     capacity = capacity_ref[...]
     storage = 1.0 + capacity * sum(weights[1:], weights[0])
     block_ref[0:rows, :] = storage
     storage_t[0:LANES, :] = storage.T
-    copies[3].wait()
-    faces_t[0:LANES, :] = faces_ref[...].T
     copies[4].wait()
     total = None
     for zone, weight in enumerate(weights):

time: 18.3 us -> 18.3 us (level)
  no operation moved by 1% of the time
where the time goes in v26:
time: 18.3 us; the launch traced here: 18.1 us
  starting transfers between devices  10.2 us (56%)
  waiting for transfers between devices  5.03 us (27%)
  Pallas kernels  2.84 us (16%)
    ppermute x6, starting transfers between devices, trade(): return lax.ppermute(value, ('xg', 'yd'), pairs)  10.2 us
    ppermute x6, waiting for transfers between devices, trade(): return lax.ppermute(value, ('xg', 'yd'), pairs)  5.03 us
    pallas_call x8, Pallas kernels, kernel_call(): pl.pallas_call(body, out_shape=outputs, in_specs=[pl.BlockSpec(memory_spa...  2.84 us
  transfers between devices with their start and end apart: 6, of which 5 were waited for; matrix products, arithmetic and copies ran while one was open for 0% of the time, Pallas kernels for 3%

profile of v26, /device:TPU:0, one launch (start us, length us, event | category | flops | bytes accessed | tf_op | source)
XLA Modules:
  0.0 18.1 jit_solution(3142322327686237965)
XLA Ops:
  0.0 1.4 %shard_map.73 = (f32[8,128]{1,0:T(8,128)S(1)}, f32[720,128]{1,0:T(8,128)S(1)}) custom-call(f32[128,128]{1,0:T(8,128)} %bitcast.9, f32[128,128]{1,0:T(8,128)} %bitcast.10, f32[128,128]{1,0:T(8,128)} %bitcast.11, f32[128,128]{1,0:T(8,128)} %bitcast.12, f32[512,128]{1,0:T(8,128)} %bitcast.8, f32[1,4]{1,0:T(1,128)} %bitcast.13, f32[1,4]{1,0:T(1,128)} %bitcast.14), custom_call_target="tpu_custom_call" | custom-call | flops 500000 | bytes 500000 | tf_op jit(solution)/shard_map/pallas_call | solution.py:486
  1.4 2.4 %collective-permute-start = (f32[8,128]{1,0:T(8,128)S(1)}, f32[8,128]{1,0:T(8,128)S(1)}, u32[]{:S(2)}, u32[]{:S(2)}) collective-permute-start(f32[8,128]{1,0:T(8,128)S(1)} %get-tuple-element.25.refs_0_), channel_id=1, source_target_pairs={{0,24},{1,25},{2,26},{3,27},{4,28},{5,29},{6,30},{7,31},{8,16},{9,... | collective-permute-start | bytes 12296 | tf_op jit(solution)/shard_map/ppermute | solution.py:439
  3.8 0.7 %collective-permute-start.2 = (f32[720,128]{1,0:T(8,128)S(1)}, f32[720,128]{1,0:T(8,128)S(1)}, u32[]{:S(2)}, u32[]{:S(2)}) collective-permute-start(f32[720,128]{1,0:T(8,128)S(1)} %get-tuple-element.26.block_ref), channel_id=1, source_target_pairs={{0,8},{1,9},{2,10},{3,11},{4,12},{5,13},{6,14},{7,15},{8,0},{9,1},... | collective-permute-start | bytes 1105928 | tf_op jit(solution)/shard_map/ppermute | solution.py:439
  4.5 0.2 %shard_map.74 = (f32[8,384]{1,0:T(8,128)S(1)}, f32[400,128]{1,0:T(8,128)S(1)}, f32[272,128]{1,0:T(8,128)S(1)}, f32[480,128]{1,0:T(8,128)S(1)}, f32[272,128]{1,0:T(8,128)S(1)}) custom-call(f32[720,128]{1,0:T(8,128)S(1)} %get-tuple-element.26.block_ref), custom_call_target="tpu_custom_call" | custom-call | flops 10000000000 | bytes 10000000000 | tf_op jit(solution)/shard_map/pallas_call | solution.py:486
  4.7 0.4 %collective-permute-done.refs_1_ = f32[8,128]{1,0:T(8,128)S(1)} collective-permute-done((f32[8,128]{1,0:T(8,128)S(1)}, f32[8,128]{1,0:T(8,128)S(1)}, u32[]{:S(2)}, u32[]{:S(2)}) %collective-permute-start) | collective-permute-done | bytes 4128 | tf_op jit(solution)/shard_map/ppermute | solution.py:439
  5.2 0.6 %collective-permute-start.1 = (f32[8,128]{1,0:T(8,128)S(1)}, f32[8,128]{1,0:T(8,128)S(1)}, u32[]{:S(2)}, u32[]{:S(2)}) collective-permute-start(f32[8,128]{1,0:T(8,128)S(1)} %collective-permute-done.refs_1_), channel_id=1, source_target_pairs={{0,8},{1,9},{2,10},{3,11},{4,12},{5,13},{6,14},{7,15},{8,0},{9,1},... | collective-permute-start | bytes 12296 | tf_op jit(solution)/shard_map/ppermute | solution.py:439
  5.8 0.0 collective-permute-done.2.block_ref
  5.8 0.2 %shard_map.75 = (f32[8,384]{1,0:T(8,128)S(1)}, f32[400,128]{1,0:T(8,128)S(1)}, f32[272,128]{1,0:T(8,128)S(1)}, f32[8,128]{1,0:T(8,128)S(1)}) custom-call(f32[720,128]{1,0:T(8,128)S(1)} %collective-permute-done.2.block_ref), custom_call_target="tpu_custom_call" | custom-call | flops 10000000000 | bytes 10000000000 | tf_op jit(solution)/shard_map/pallas_call | solution.py:486
  6.0 0.6 %collective-permute-done.1.refs_2_ = f32[8,128]{1,0:T(8,128)S(1)} collective-permute-done((f32[8,128]{1,0:T(8,128)S(1)}, f32[8,128]{1,0:T(8,128)S(1)}, u32[]{:S(2)}, u32[]{:S(2)}) %collective-permute-start.1) | collective-permute-done | bytes 4128 | tf_op jit(solution)/shard_map/ppermute | solution.py:439
  6.6 0.2 %shard_map.76 = (f32[4,640]{1,0:T(4,128)S(1)}, f32[4,640]{1,0:T(4,128)S(1)}, f32[144,128]{1,0:T(8,128)S(1)}) custom-call(f32[8,128]{1,0:T(8,128)S(1)} %get-tuple-element.25.refs_0_, f32[8,128]{1,0:T(8,128)S(1)} %collective-permute-done.refs_1_, f32[8,128]{1,0:T(8,128)S(1)} %collective-permute-done.1.refs_2_, f32[400,128]{1,0:T(8,128)S(1)} %get-tuple-element.27.refs_3_, ...), custom_call_target="tpu_custom_call" | custom-call | flops 500000 | bytes 500000 | tf_op jit(solution)/shard_map/pallas_call | solution.py:486
  6.9 1.8 %collective-permute-start.3 = (f32[4,640]{1,0:T(4,128)S(1)}, f32[4,640]{1,0:T(4,128)S(1)}, u32[]{:S(2)}, u32[]{:S(2)}) collective-permute-start(f32[4,640]{1,0:T(4,128)S(1)} %get-tuple-element.35), channel_id=1, source_target_pairs={{0,9},{1,8},{2,11},{3,10},{4,13},{5,12},{6,15},{7,14},{8,1},{9,0},... | collective-permute-start | bytes 30728 | tf_op jit(solution)/shard_map/ppermute | solution.py:439
  8.7 1.4 %collective-permute-done.3.other_ref = f32[4,640]{1,0:T(4,128)S(1)} collective-permute-done((f32[4,640]{1,0:T(4,128)S(1)}, f32[4,640]{1,0:T(4,128)S(1)}, u32[]{:S(2)}, u32[]{:S(2)}) %collective-permute-start.3) | collective-permute-done | bytes 10272 | tf_op jit(solution)/shard_map/ppermute | solution.py:439
  10.1 1.8 %collective-permute-start.4 = (f32[4,640]{1,0:T(4,128)S(1)}, f32[4,640]{1,0:T(4,128)S(1)}, u32[]{:S(2)}, u32[]{:S(2)}) collective-permute-start(f32[4,640]{1,0:T(4,128)S(1)} %get-tuple-element.37), channel_id=1, source_target_pairs={{0,10},{1,11},{2,8},{3,9},{4,14},{5,15},{6,12},{7,13},{8,2},{9,3},... | collective-permute-start | bytes 30728 | tf_op jit(solution)/shard_map/ppermute | solution.py:439
  11.9 1.4 %collective-permute-done.4.other_ref = f32[4,640]{1,0:T(4,128)S(1)} collective-permute-done((f32[4,640]{1,0:T(4,128)S(1)}, f32[4,640]{1,0:T(4,128)S(1)}, u32[]{:S(2)}, u32[]{:S(2)}) %collective-permute-start.4) | collective-permute-done | bytes 10272 | tf_op jit(solution)/shard_map/ppermute | solution.py:439
  13.3 2.8 %collective-permute-start.5 = (f32[2,640]{1,0:T(2,128)S(1)}, f32[2,640]{1,0:T(2,128)S(1)}, u32[]{:S(2)}, u32[]{:S(2)}) collective-permute-start(f32[2,640]{1,0:T(2,128)S(1)} %get-tuple-element.39), channel_id=1, source_target_pairs={{0,12},{1,13},{2,14},{3,15},{4,8},{5,9},{6,10},{7,11},{8,4},{9,5},... | collective-permute-start | bytes 15368 | tf_op jit(solution)/shard_map/ppermute | solution.py:439
  16.1 0.1 shard_map.79.refs_2_
  16.2 1.2 %collective-permute-done.5.other_ref = f32[2,640]{1,0:T(2,128)S(1)} collective-permute-done((f32[2,640]{1,0:T(2,128)S(1)}, f32[2,640]{1,0:T(2,128)S(1)}, u32[]{:S(2)}, u32[]{:S(2)}) %collective-permute-start.5) | collective-permute-done | bytes 5152 | tf_op jit(solution)/shard_map/ppermute | solution.py:439
  17.5 0.7 %shard_map.80 = f32[128,128]{1,0:T(8,128)} custom-call(f32[4,640]{1,0:T(4,128)S(1)} %get-tuple-element.38.own_ref, f32[2,640]{1,0:T(2,128)S(1)} %collective-permute-done.5.other_ref, f32[4,384]{1,0:T(4,128)S(1)} %get-tuple-element.40.refs_0_, f32[4,384]{1,0:T(4,128)S(1)} %get-tuple-element.41.refs_1_, f32[144,128]{1,0:T(8,128)S(1)} %shard_map.79.refs_2_, ...), custom_call_target="tpu_custom_call" | custom-call | flops 500000 | bytes 500000 | tf_op jit(solution)/shard_map/pallas_call | solution.py:486
  (2 shorter events, 0.0 us)
Async XLA Ops:
  1.4 3.8 %collective-permute-start = (f32[8,128]{1,0:T(8,128)S(1)}, f32[8,128]{1,0:T(8,128)S(1)}, u32[]{:S(2)}, u32[]{:S(2)}) collective-permute-start(f32[8,128]{1,0:T(8,128)S(1)} %get-tuple-element.25.refs_0_), channel_id=1, source_target_pairs={{0,24},{1,25},{2,26},{3,27},{4,28},{5,29},{6,30},{7,31},{8,16},{9,... | collective-permute-start | bytes 12296 | tf_op jit(solution)/shard_map/ppermute | solution.py:439
  3.8 2.0 %collective-permute-start.2 = (f32[720,128]{1,0:T(8,128)S(1)}, f32[720,128]{1,0:T(8,128)S(1)}, u32[]{:S(2)}, u32[]{:S(2)}) collective-permute-start(f32[720,128]{1,0:T(8,128)S(1)} %get-tuple-element.26.block_ref), channel_id=1, source_target_pairs={{0,8},{1,9},{2,10},{3,11},{4,12},{5,13},{6,14},{7,15},{8,0},{9,1},... | collective-permute-start | bytes 1105928 | tf_op jit(solution)/shard_map/ppermute | solution.py:439
  5.2 1.5 %collective-permute-start.1 = (f32[8,128]{1,0:T(8,128)S(1)}, f32[8,128]{1,0:T(8,128)S(1)}, u32[]{:S(2)}, u32[]{:S(2)}) collective-permute-start(f32[8,128]{1,0:T(8,128)S(1)} %collective-permute-done.refs_1_), channel_id=1, source_target_pairs={{0,8},{1,9},{2,10},{3,11},{4,12},{5,13},{6,14},{7,15},{8,0},{9,1},... | collective-permute-start | bytes 12296 | tf_op jit(solution)/shard_map/ppermute | solution.py:439
  6.9 3.2 %collective-permute-start.3 = (f32[4,640]{1,0:T(4,128)S(1)}, f32[4,640]{1,0:T(4,128)S(1)}, u32[]{:S(2)}, u32[]{:S(2)}) collective-permute-start(f32[4,640]{1,0:T(4,128)S(1)} %get-tuple-element.35), channel_id=1, source_target_pairs={{0,9},{1,8},{2,11},{3,10},{4,13},{5,12},{6,15},{7,14},{8,1},{9,0},... | collective-permute-start | bytes 30728 | tf_op jit(solution)/shard_map/ppermute | solution.py:439
  10.1 3.2 %collective-permute-start.4 = (f32[4,640]{1,0:T(4,128)S(1)}, f32[4,640]{1,0:T(4,128)S(1)}, u32[]{:S(2)}, u32[]{:S(2)}) collective-permute-start(f32[4,640]{1,0:T(4,128)S(1)} %get-tuple-element.37), channel_id=1, source_target_pairs={{0,10},{1,11},{2,8},{3,9},{4,14},{5,15},{6,12},{7,13},{8,2},{9,3},... | collective-permute-start | bytes 30728 | tf_op jit(solution)/shard_map/ppermute | solution.py:439
  13.3 4.1 %collective-permute-start.5 = (f32[2,640]{1,0:T(2,128)S(1)}, f32[2,640]{1,0:T(2,128)S(1)}, u32[]{:S(2)}, u32[]{:S(2)}) collective-permute-start(f32[2,640]{1,0:T(2,128)S(1)} %get-tuple-element.39), channel_id=1, source_target_pairs={{0,12},{1,13},{2,14},{3,15},{4,8},{5,9},{6,10},{7,11},{8,4},{9,5},... | collective-permute-start | bytes 15368 | tf_op jit(solution)/shard_map/ppermute | solution.py:439

commit v27 on v25

--- a/solution.py
+++ b/solution.py
@@ -258,12 +258,18 @@
     return ((one, nothing), (nothing, one))
 
 
-def prepare_kernel(halves, own, block_ref, rows_ref, lines_ref, sums_ref, *extra_refs):
-    rows = lines_ref.shape[1]
+def summed(halves, value):
+    side = jnp.sum(value.reshape(-1, SUBLANES, LANES), axis=0)
+    return sum([behind(side, step, 0) for step in range(halves, SUBLANES, halves)], side)
+
+
+def prepare_kernel(halves, own, block_ref, rows_ref, natural_ref, response_ref, *extra_refs):
+    rows = extra_refs[-2].shape[1]
     stride = LANES // SUBLANES
     rolls = x_rolls(halves)
     total = stride - 1 + len(rolls)
     nodes = state_parts(block_ref.at[2 * rows :, :], 0, total, 3)
+    *extra_refs, lines_ref, sums_ref = extra_refs
     own_refs = extra_refs if own else ()
     if not own:
         extra_refs[0][...] = block_ref[-SUBLANES:, :]
@@ -293,6 +299,14 @@
                 sums_ref[place, :] = value * held
                 if own_refs:
                     own_refs[1][place, :] = value
+    for case in range(3):
+        natural_ref[case * rows : (case + 1) * rows, :] = lines_ref[case * LANES : (case + 1) * LANES, :].T
+    for end in range(2):
+        weight = sums_ref[end * rows : (end + 1) * rows, :]
+        tiles.append(summed(halves, weight * natural_ref[0:rows, :]))
+        for case in range(2):
+            place = (2 * end + case) * rows
+            response_ref[place : place + rows, :] = weight * natural_ref[(case + 1) * rows : (case + 2) * rows, :]
     for number, tile in enumerate(tiles):
         rows_ref[:, quantity(number)] = tile
 
@@ -329,12 +343,12 @@
 
 
 def x_back_kernel(halves, axis, order, pieces, *refs):
-    lines_refs, sums_refs, rows_refs = (refs[pieces + 2 * pair : pieces + 2 * pair + 2] for pair in range(3))
+    natural_refs, response_refs, rows_refs = (refs[pieces + 2 * pair : pieces + 2 * pair + 2] for pair in range(3))
     last_ref, kept_ref, sent_ref, values_ref = refs[pieces + 6 :]
     slots = message_slots([*refs[:pieces], last_ref], SUBLANES, 1, 1, [0] * len(order))
     slots = [slots[order.index(place)] for place in range(len(order))]
     bounds = ring_bounds(slots, lax.axis_index(axis))
-    rows = lines_refs[0].shape[1]
+    rows = natural_refs[0].shape[0] // 3
 
     height = 2 * halves
     first = lax.broadcasted_iota(jnp.int32, (SUBLANES, LANES), 0) < halves
@@ -345,18 +359,25 @@
 
     for number in range(3):
         put(number, *(ref[:, quantity(number)] for ref in rows_refs))
+    row = lax.broadcasted_iota(jnp.int32, (SUBLANES, rows), 0)
+    ends = jnp.zeros((SUBLANES, rows), jnp.float32)
+    for place, bound in enumerate([bound for block in range(2) for bound in bounds[block]]):
+        ends = jnp.where(row == place, along_line(bound, halves, rows), ends)
+    columns = ends.T
     sides = []
     for block in range(2):
-        lines_ref, sums_ref = lines_refs[block], sums_refs[block]
-        before, after = (along_line(bound, halves, rows) for bound in bounds[block])
-        values = lines_ref[0:LANES, :] + lines_ref[LANES : 2 * LANES, :] * before + lines_ref[2 * LANES : 3 * LANES, :] * after
-        values = values.T
+        before, after = (
+            jnp.broadcast_to(columns[:, 2 * block + end : 2 * block + end + 1], (rows, LANES)) for end in range(2)
+        )
         if block == 0:
-            values_ref[0:rows, :] = values
+            natural = [natural_refs[0][case * rows : (case + 1) * rows, :] for case in range(3)]
+            values_ref[0:rows, :] = natural[0] + natural[1] * before + natural[2] * after
         for end in range(2):
-            parts = (values * sums_ref[end * rows : (end + 1) * rows, :]).reshape(-1, SUBLANES, LANES)
-            side = jnp.sum(parts, axis=0)
-            sides.append(sum([behind(side, step, 0) for step in range(halves, SUBLANES, halves)], side))
+            first_part, last_part = (
+                response_refs[block][(2 * end + case) * rows : (2 * end + case + 1) * rows, :] for case in range(2)
+            )
+            side = summed(halves, first_part * before + last_part * after)
+            sides.append(side + rows_refs[block][:, quantity(3 + end)])
     for end in range(2):
         put(3 + end, sides[end], sides[2 + end])
 
@@ -528,12 +549,13 @@
         pltpu.HBM,
     )
     def prepare(part, own):
-        outputs = [held_f32(SUBLANES, 3 * LANES), held_f32(3 * LANES + spare, rows), held_f32(2 * rows + spare, LANES)]
+        outputs = [held_f32(SUBLANES, QUANTITIES * LANES), held_f32(3 * rows, LANES), held_f32(4 * rows, LANES)]
         if own:
             outputs += [held_f32(3 * y_nodes * SUBLANES, LANES), held_f32(2 * rows + spare, LANES)]
         else:
             outputs += [held_f32(SUBLANES, rows)]
-        return kernel_call(functools.partial(prepare_kernel, halves, own), (part,), outputs, [], cost=10000000000)
+        scratch = [VMEM((3 * LANES + spare, rows), jnp.float32), VMEM((2 * rows + spare, LANES), jnp.float32)]
+        return kernel_call(functools.partial(prepare_kernel, halves, own), (part,), outputs, scratch, cost=10000000000)
 
     pieces, order, other_block = x_exchange(message, block)
     y_rows, lines_x, sums, y_state, spread = prepare(block, True)

time: 18.3 us -> 18.4 us (level)
  Pallas kernels: 2.83 us -> 3.22 us
  waiting for transfers between devices: 5.03 us -> 4.81 us
    pallas_call x8, Pallas kernels: 2.83 us -> 3.22 us  [kernel_call(): pl.pallas_call(body, out_shape=outputs, in_specs=[pl.BlockSpec(memory_spa...]
    ppermute x6, waiting for transfers between devices: 5.03 us -> 4.81 us  [trade(): return lax.ppermute(value, ('xg', 'yd'), pairs)]
  transfers between devices with their start and end apart: 6 -> 6, of which waited for: 5 -> 5; matrix products, arithmetic and copies ran while one was open for 0% -> 0% of each run, Pallas kernels for 3% -> 4%
where the time goes in v27:
time: 18.4 us; the launch traced here: 18.3 us
  starting transfers between devices  10.2 us (55%)
  waiting for transfers between devices  4.81 us (26%)
  Pallas kernels  3.22 us (18%)
    ppermute x6, starting transfers between devices, trade(): return lax.ppermute(value, ('xg', 'yd'), pairs)  10.2 us
    ppermute x6, waiting for transfers between devices, trade(): return lax.ppermute(value, ('xg', 'yd'), pairs)  4.81 us
    pallas_call x8, Pallas kernels, kernel_call(): pl.pallas_call(body, out_shape=outputs, in_specs=[pl.BlockSpec(memory_spa...  3.22 us
  transfers between devices with their start and end apart: 6, of which 5 were waited for; matrix products, arithmetic and copies ran while one was open for 0% of the time, Pallas kernels for 4%

profile of v27, /device:TPU:0, one launch (start us, length us, event | category | flops | bytes accessed | tf_op | source)
XLA Modules:
  0.0 18.3 jit_solution(11465505168673365937)
XLA Ops:
  0.0 1.4 %shard_map.73 = (f32[8,128]{1,0:T(8,128)S(1)}, f32[720,128]{1,0:T(8,128)S(1)}) custom-call(f32[128,128]{1,0:T(8,128)} %bitcast.9, f32[128,128]{1,0:T(8,128)} %bitcast.10, f32[128,128]{1,0:T(8,128)} %bitcast.11, f32[128,128]{1,0:T(8,128)} %bitcast.12, f32[512,128]{1,0:T(8,128)} %bitcast.8, f32[1,4]{1,0:T(1,128)} %bitcast.13, f32[1,4]{1,0:T(1,128)} %bitcast.14), custom_call_target="tpu_custom_call" | custom-call | flops 500000 | bytes 500000 | tf_op jit(solution)/shard_map/pallas_call | solution.py:507
  1.4 2.4 %collective-permute-start = (f32[8,128]{1,0:T(8,128)S(1)}, f32[8,128]{1,0:T(8,128)S(1)}, u32[]{:S(2)}, u32[]{:S(2)}) collective-permute-start(f32[8,128]{1,0:T(8,128)S(1)} %get-tuple-element.25.refs_0_), channel_id=1, source_target_pairs={{0,24},{1,25},{2,26},{3,27},{4,28},{5,29},{6,30},{7,31},{8,16},{9,... | collective-permute-start | bytes 12296 | tf_op jit(solution)/shard_map/ppermute | solution.py:460
  3.8 0.7 %collective-permute-start.2 = (f32[720,128]{1,0:T(8,128)S(1)}, f32[720,128]{1,0:T(8,128)S(1)}, u32[]{:S(2)}, u32[]{:S(2)}) collective-permute-start(f32[720,128]{1,0:T(8,128)S(1)} %get-tuple-element.26.block_ref), channel_id=1, source_target_pairs={{0,8},{1,9},{2,10},{3,11},{4,12},{5,13},{6,14},{7,15},{8,0},{9,1},... | collective-permute-start | bytes 1105928 | tf_op jit(solution)/shard_map/ppermute | solution.py:460
  4.5 0.3 %shard_map.74 = (f32[8,640]{1,0:T(8,128)S(1)}, f32[384,128]{1,0:T(8,128)S(1)}, f32[512,128]{1,0:T(8,128)S(1)}, f32[480,128]{1,0:T(8,128)S(1)}, f32[272,128]{1,0:T(8,128)S(1)}) custom-call(f32[720,128]{1,0:T(8,128)S(1)} %get-tuple-element.26.block_ref), custom_call_target="tpu_custom_call" | custom-call | flops 10000000000 | bytes 10000000000 | tf_op jit(solution)/shard_map/pallas_call | solution.py:507
  4.8 0.3 %collective-permute-done.refs_1_ = f32[8,128]{1,0:T(8,128)S(1)} collective-permute-done((f32[8,128]{1,0:T(8,128)S(1)}, f32[8,128]{1,0:T(8,128)S(1)}, u32[]{:S(2)}, u32[]{:S(2)}) %collective-permute-start) | collective-permute-done | bytes 4128 | tf_op jit(solution)/shard_map/ppermute | solution.py:460
  5.1 0.6 %collective-permute-start.1 = (f32[8,128]{1,0:T(8,128)S(1)}, f32[8,128]{1,0:T(8,128)S(1)}, u32[]{:S(2)}, u32[]{:S(2)}) collective-permute-start(f32[8,128]{1,0:T(8,128)S(1)} %collective-permute-done.refs_1_), channel_id=1, source_target_pairs={{0,8},{1,9},{2,10},{3,11},{4,12},{5,13},{6,14},{7,15},{8,0},{9,1},... | collective-permute-start | bytes 12296 | tf_op jit(solution)/shard_map/ppermute | solution.py:460
  5.8 0.0 collective-permute-done.2.block_ref
  5.8 0.3 %shard_map.75 = (f32[8,640]{1,0:T(8,128)S(1)}, f32[384,128]{1,0:T(8,128)S(1)}, f32[512,128]{1,0:T(8,128)S(1)}, f32[8,128]{1,0:T(8,128)S(1)}) custom-call(f32[720,128]{1,0:T(8,128)S(1)} %collective-permute-done.2.block_ref), custom_call_target="tpu_custom_call" | custom-call | flops 10000000000 | bytes 10000000000 | tf_op jit(solution)/shard_map/pallas_call | solution.py:507
  6.1 0.5 %collective-permute-done.1.refs_2_ = f32[8,128]{1,0:T(8,128)S(1)} collective-permute-done((f32[8,128]{1,0:T(8,128)S(1)}, f32[8,128]{1,0:T(8,128)S(1)}, u32[]{:S(2)}, u32[]{:S(2)}) %collective-permute-start.1) | collective-permute-done | bytes 4128 | tf_op jit(solution)/shard_map/ppermute | solution.py:460
  6.6 0.4 %shard_map.76 = (f32[4,640]{1,0:T(4,128)S(1)}, f32[4,640]{1,0:T(4,128)S(1)}, f32[144,128]{1,0:T(8,128)S(1)}) custom-call(f32[8,128]{1,0:T(8,128)S(1)} %get-tuple-element.25.refs_0_, f32[8,128]{1,0:T(8,128)S(1)} %collective-permute-done.refs_1_, f32[8,128]{1,0:T(8,128)S(1)} %collective-permute-done.1.refs_2_, f32[384,128]{1,0:T(8,128)S(1)} %get-tuple-element.27.refs_3_, ...), custom_call_target="tpu_custom_call" | custom-call | flops 500000 | bytes 500000 | tf_op jit(solution)/shard_map/pallas_call | solution.py:507
  7.0 1.8 %collective-permute-start.3 = (f32[4,640]{1,0:T(4,128)S(1)}, f32[4,640]{1,0:T(4,128)S(1)}, u32[]{:S(2)}, u32[]{:S(2)}) collective-permute-start(f32[4,640]{1,0:T(4,128)S(1)} %get-tuple-element.35), channel_id=1, source_target_pairs={{0,9},{1,8},{2,11},{3,10},{4,13},{5,12},{6,15},{7,14},{8,1},{9,0},... | collective-permute-start | bytes 30728 | tf_op jit(solution)/shard_map/ppermute | solution.py:460
  8.8 1.4 %collective-permute-done.3.other_ref = f32[4,640]{1,0:T(4,128)S(1)} collective-permute-done((f32[4,640]{1,0:T(4,128)S(1)}, f32[4,640]{1,0:T(4,128)S(1)}, u32[]{:S(2)}, u32[]{:S(2)}) %collective-permute-start.3) | collective-permute-done | bytes 10272 | tf_op jit(solution)/shard_map/ppermute | solution.py:460
  10.2 1.8 %collective-permute-start.4 = (f32[4,640]{1,0:T(4,128)S(1)}, f32[4,640]{1,0:T(4,128)S(1)}, u32[]{:S(2)}, u32[]{:S(2)}) collective-permute-start(f32[4,640]{1,0:T(4,128)S(1)} %get-tuple-element.37), channel_id=1, source_target_pairs={{0,10},{1,11},{2,8},{3,9},{4,14},{5,15},{6,12},{7,13},{8,2},{9,3},... | collective-permute-start | bytes 30728 | tf_op jit(solution)/shard_map/ppermute | solution.py:460
  12.1 1.4 %collective-permute-done.4.other_ref = f32[4,640]{1,0:T(4,128)S(1)} collective-permute-done((f32[4,640]{1,0:T(4,128)S(1)}, f32[4,640]{1,0:T(4,128)S(1)}, u32[]{:S(2)}, u32[]{:S(2)}) %collective-permute-start.4) | collective-permute-done | bytes 10272 | tf_op jit(solution)/shard_map/ppermute | solution.py:460
  13.5 2.8 %collective-permute-start.5 = (f32[2,640]{1,0:T(2,128)S(1)}, f32[2,640]{1,0:T(2,128)S(1)}, u32[]{:S(2)}, u32[]{:S(2)}) collective-permute-start(f32[2,640]{1,0:T(2,128)S(1)} %get-tuple-element.39), channel_id=1, source_target_pairs={{0,12},{1,13},{2,14},{3,15},{4,8},{5,9},{6,10},{7,11},{8,4},{9,5},... | collective-permute-start | bytes 15368 | tf_op jit(solution)/shard_map/ppermute | solution.py:460
  16.3 0.1 shard_map.79.refs_2_
  16.4 1.2 %collective-permute-done.5.other_ref = f32[2,640]{1,0:T(2,128)S(1)} collective-permute-done((f32[2,640]{1,0:T(2,128)S(1)}, f32[2,640]{1,0:T(2,128)S(1)}, u32[]{:S(2)}, u32[]{:S(2)}) %collective-permute-start.5) | collective-permute-done | bytes 5152 | tf_op jit(solution)/shard_map/ppermute | solution.py:460
  17.6 0.7 %shard_map.80 = f32[128,128]{1,0:T(8,128)} custom-call(f32[4,640]{1,0:T(4,128)S(1)} %get-tuple-element.38.own_ref, f32[2,640]{1,0:T(2,128)S(1)} %collective-permute-done.5.other_ref, f32[4,384]{1,0:T(4,128)S(1)} %get-tuple-element.40.refs_0_, f32[4,384]{1,0:T(4,128)S(1)} %get-tuple-element.41.refs_1_, f32[144,128]{1,0:T(8,128)S(1)} %shard_map.79.refs_2_, ...), custom_call_target="tpu_custom_call" | custom-call | flops 500000 | bytes 500000 | tf_op jit(solution)/shard_map/pallas_call | solution.py:507
  (2 shorter events, 0.0 us)
Async XLA Ops:
  1.4 3.8 %collective-permute-start = (f32[8,128]{1,0:T(8,128)S(1)}, f32[8,128]{1,0:T(8,128)S(1)}, u32[]{:S(2)}, u32[]{:S(2)}) collective-permute-start(f32[8,128]{1,0:T(8,128)S(1)} %get-tuple-element.25.refs_0_), channel_id=1, source_target_pairs={{0,24},{1,25},{2,26},{3,27},{4,28},{5,29},{6,30},{7,31},{8,16},{9,... | collective-permute-start | bytes 12296 | tf_op jit(solution)/shard_map/ppermute | solution.py:460
  3.8 2.0 %collective-permute-start.2 = (f32[720,128]{1,0:T(8,128)S(1)}, f32[720,128]{1,0:T(8,128)S(1)}, u32[]{:S(2)}, u32[]{:S(2)}) collective-permute-start(f32[720,128]{1,0:T(8,128)S(1)} %get-tuple-element.26.block_ref), channel_id=1, source_target_pairs={{0,8},{1,9},{2,10},{3,11},{4,12},{5,13},{6,14},{7,15},{8,0},{9,1},... | collective-permute-start | bytes 1105928 | tf_op jit(solution)/shard_map/ppermute | solution.py:460
  5.1 1.5 %collective-permute-start.1 = (f32[8,128]{1,0:T(8,128)S(1)}, f32[8,128]{1,0:T(8,128)S(1)}, u32[]{:S(2)}, u32[]{:S(2)}) collective-permute-start(f32[8,128]{1,0:T(8,128)S(1)} %collective-permute-done.refs_1_), channel_id=1, source_target_pairs={{0,8},{1,9},{2,10},{3,11},{4,12},{5,13},{6,14},{7,15},{8,0},{9,1},... | collective-permute-start | bytes 12296 | tf_op jit(solution)/shard_map/ppermute | solution.py:460
  7.0 3.2 %collective-permute-start.3 = (f32[4,640]{1,0:T(4,128)S(1)}, f32[4,640]{1,0:T(4,128)S(1)}, u32[]{:S(2)}, u32[]{:S(2)}) collective-permute-start(f32[4,640]{1,0:T(4,128)S(1)} %get-tuple-element.35), channel_id=1, source_target_pairs={{0,9},{1,8},{2,11},{3,10},{4,13},{5,12},{6,15},{7,14},{8,1},{9,0},... | collective-permute-start | bytes 30728 | tf_op jit(solution)/shard_map/ppermute | solution.py:460
  10.2 3.2 %collective-permute-start.4 = (f32[4,640]{1,0:T(4,128)S(1)}, f32[4,640]{1,0:T(4,128)S(1)}, u32[]{:S(2)}, u32[]{:S(2)}) collective-permute-start(f32[4,640]{1,0:T(4,128)S(1)} %get-tuple-element.37), channel_id=1, source_target_pairs={{0,10},{1,11},{2,8},{3,9},{4,14},{5,15},{6,12},{7,13},{8,2},{9,3},... | collective-permute-start | bytes 30728 | tf_op jit(solution)/shard_map/ppermute | solution.py:460
  13.5 4.1 %collective-permute-start.5 = (f32[2,640]{1,0:T(2,128)S(1)}, f32[2,640]{1,0:T(2,128)S(1)}, u32[]{:S(2)}, u32[]{:S(2)}) collective-permute-start(f32[2,640]{1,0:T(2,128)S(1)} %get-tuple-element.39), channel_id=1, source_target_pairs={{0,12},{1,13},{2,14},{3,15},{4,8},{5,9},{6,10},{7,11},{8,4},{9,5},... | collective-permute-start | bytes 15368 | tf_op jit(solution)/shard_map/ppermute | solution.py:460

commit v28 on v25

--- a/solution.py
+++ b/solution.py
@@ -215,13 +215,16 @@
     faces_t, storage_t, source_t,
 ):
     rows = mobile_ref.shape[0]
+    zones = [slice(start, start + rows) for start in range(0, immobile_ref.shape[0], rows)]
     pairs = (
         (rates_hbm, rates_ref), (shares_hbm, shares_ref), (capacity_hbm, capacity_ref), (faces_hbm, faces_ref),
-        (immobile_hbm, immobile_ref), (mobile_hbm, mobile_ref), (across_hbm, block_ref.at[rows : 2 * rows, :]),
+        (mobile_hbm, mobile_ref),
+        *((immobile_hbm.at[zone, :], immobile_ref.at[zone, :]) for zone in zones),
+        (across_hbm, block_ref.at[rows : 2 * rows, :]),
     )
     copies = [pltpu.make_async_copy(pair[0], pair[1], arrived.at[place]) for place, pair in enumerate(pairs)]
-    for place, copy in enumerate(copies):
-        copy.start(priority=int(place in (4, 6)))
+    for copy in copies:
+        copy.start()
     stride = LANES // SUBLANES
     for copy in copies[:3]:
         copy.wait()
@@ -234,9 +237,9 @@
     faces_t[0:LANES, :] = faces_ref[...].T
     copies[4].wait()
     total = None
-    for zone, weight in enumerate(weights):
-        total = plus(total, weight * immobile_ref[zone * rows : (zone + 1) * rows, :])
-    copies[5].wait()
+    for copy, weight, zone in zip(copies[5:], weights, zones):
+        copy.wait()
+        total = plus(total, weight * immobile_ref[zone, :])
     source_t[0:LANES, :] = (mobile_ref[...] + capacity * total).T
     leaves = []
     for index in range(stride):
@@ -250,7 +253,7 @@
     for row, value in enumerate(piece):
         message_ref[row : row + 1, :] = value[0:1, :]
         block_ref[start + row : start + row + 1, :] = value[0:1, :]
-    copies[6].wait()
+    copies[-1].wait()
 
 
 def ends_responses(shape):
@@ -523,7 +526,7 @@
         [square] * 3
         + [VMEM((zones * rows, LANES), jnp.float32)]
         + [pltpu.SMEM((1, zones), jnp.float32)] * 2
-        + [pltpu.SemaphoreType.DMA((7,))]
+        + [pltpu.SemaphoreType.DMA((6 + zones,))]
         + [VMEM((LANES + LANES // SUBLANES, rows), jnp.float32)] * 3,
         pltpu.HBM,
     )

time: 18.3 us -> 18.3 us (level)
  no operation moved by 1% of the time
where the time goes in v28:
time: 18.3 us; the launch traced here: 18.1 us
  starting transfers between devices  10.2 us (56%)
  waiting for transfers between devices  5.03 us (27%)
  Pallas kernels  2.85 us (16%)
    ppermute x6, starting transfers between devices, trade(): return lax.ppermute(value, ('xg', 'yd'), pairs)  10.2 us
    ppermute x6, waiting for transfers between devices, trade(): return lax.ppermute(value, ('xg', 'yd'), pairs)  5.03 us
    pallas_call x8, Pallas kernels, kernel_call(): pl.pallas_call(body, out_shape=outputs, in_specs=[pl.BlockSpec(memory_spa...  2.85 us
  transfers between devices with their start and end apart: 6, of which 5 were waited for; matrix products, arithmetic and copies ran while one was open for 0% of the time, Pallas kernels for 3%

profile of v28, /device:TPU:0, one launch (start us, length us, event | category | flops | bytes accessed | tf_op | source)
XLA Modules:
  0.0 18.1 jit_solution(15331599158043973141)
XLA Ops:
  0.0 1.4 %shard_map.73 = (f32[8,128]{1,0:T(8,128)S(1)}, f32[720,128]{1,0:T(8,128)S(1)}) custom-call(f32[128,128]{1,0:T(8,128)} %bitcast.9, f32[128,128]{1,0:T(8,128)} %bitcast.10, f32[128,128]{1,0:T(8,128)} %bitcast.11, f32[128,128]{1,0:T(8,128)} %bitcast.12, f32[512,128]{1,0:T(8,128)} %bitcast.8, f32[1,4]{1,0:T(1,128)} %bitcast.13, f32[1,4]{1,0:T(1,128)} %bitcast.14), custom_call_target="tpu_custom_call" | custom-call | flops 500000 | bytes 500000 | tf_op jit(solution)/shard_map/pallas_call | solution.py:489
  1.4 2.4 %collective-permute-start = (f32[8,128]{1,0:T(8,128)S(1)}, f32[8,128]{1,0:T(8,128)S(1)}, u32[]{:S(2)}, u32[]{:S(2)}) collective-permute-start(f32[8,128]{1,0:T(8,128)S(1)} %get-tuple-element.25.refs_0_), channel_id=1, source_target_pairs={{0,24},{1,25},{2,26},{3,27},{4,28},{5,29},{6,30},{7,31},{8,16},{9,... | collective-permute-start | bytes 12296 | tf_op jit(solution)/shard_map/ppermute | solution.py:442
  3.8 0.7 %collective-permute-start.2 = (f32[720,128]{1,0:T(8,128)S(1)}, f32[720,128]{1,0:T(8,128)S(1)}, u32[]{:S(2)}, u32[]{:S(2)}) collective-permute-start(f32[720,128]{1,0:T(8,128)S(1)} %get-tuple-element.26.block_ref), channel_id=1, source_target_pairs={{0,8},{1,9},{2,10},{3,11},{4,12},{5,13},{6,14},{7,15},{8,0},{9,1},... | collective-permute-start | bytes 1105928 | tf_op jit(solution)/shard_map/ppermute | solution.py:442
  4.5 0.2 %shard_map.74 = (f32[8,384]{1,0:T(8,128)S(1)}, f32[400,128]{1,0:T(8,128)S(1)}, f32[272,128]{1,0:T(8,128)S(1)}, f32[480,128]{1,0:T(8,128)S(1)}, f32[272,128]{1,0:T(8,128)S(1)}) custom-call(f32[720,128]{1,0:T(8,128)S(1)} %get-tuple-element.26.block_ref), custom_call_target="tpu_custom_call" | custom-call | flops 10000000000 | bytes 10000000000 | tf_op jit(solution)/shard_map/pallas_call | solution.py:489
  4.8 0.4 %collective-permute-done.refs_1_ = f32[8,128]{1,0:T(8,128)S(1)} collective-permute-done((f32[8,128]{1,0:T(8,128)S(1)}, f32[8,128]{1,0:T(8,128)S(1)}, u32[]{:S(2)}, u32[]{:S(2)}) %collective-permute-start) | collective-permute-done | bytes 4128 | tf_op jit(solution)/shard_map/ppermute | solution.py:442
  5.2 0.6 %collective-permute-start.1 = (f32[8,128]{1,0:T(8,128)S(1)}, f32[8,128]{1,0:T(8,128)S(1)}, u32[]{:S(2)}, u32[]{:S(2)}) collective-permute-start(f32[8,128]{1,0:T(8,128)S(1)} %collective-permute-done.refs_1_), channel_id=1, source_target_pairs={{0,8},{1,9},{2,10},{3,11},{4,12},{5,13},{6,14},{7,15},{8,0},{9,1},... | collective-permute-start | bytes 12296 | tf_op jit(solution)/shard_map/ppermute | solution.py:442
  5.8 0.0 collective-permute-done.2.block_ref
  5.8 0.2 %shard_map.75 = (f32[8,384]{1,0:T(8,128)S(1)}, f32[400,128]{1,0:T(8,128)S(1)}, f32[272,128]{1,0:T(8,128)S(1)}, f32[8,128]{1,0:T(8,128)S(1)}) custom-call(f32[720,128]{1,0:T(8,128)S(1)} %collective-permute-done.2.block_ref), custom_call_target="tpu_custom_call" | custom-call | flops 10000000000 | bytes 10000000000 | tf_op jit(solution)/shard_map/pallas_call | solution.py:489
  6.0 0.6 %collective-permute-done.1.refs_2_ = f32[8,128]{1,0:T(8,128)S(1)} collective-permute-done((f32[8,128]{1,0:T(8,128)S(1)}, f32[8,128]{1,0:T(8,128)S(1)}, u32[]{:S(2)}, u32[]{:S(2)}) %collective-permute-start.1) | collective-permute-done | bytes 4128 | tf_op jit(solution)/shard_map/ppermute | solution.py:442
  6.6 0.2 %shard_map.76 = (f32[4,640]{1,0:T(4,128)S(1)}, f32[4,640]{1,0:T(4,128)S(1)}, f32[144,128]{1,0:T(8,128)S(1)}) custom-call(f32[8,128]{1,0:T(8,128)S(1)} %get-tuple-element.25.refs_0_, f32[8,128]{1,0:T(8,128)S(1)} %collective-permute-done.refs_1_, f32[8,128]{1,0:T(8,128)S(1)} %collective-permute-done.1.refs_2_, f32[400,128]{1,0:T(8,128)S(1)} %get-tuple-element.27.refs_3_, ...), custom_call_target="tpu_custom_call" | custom-call | flops 500000 | bytes 500000 | tf_op jit(solution)/shard_map/pallas_call | solution.py:489
  6.9 1.8 %collective-permute-start.3 = (f32[4,640]{1,0:T(4,128)S(1)}, f32[4,640]{1,0:T(4,128)S(1)}, u32[]{:S(2)}, u32[]{:S(2)}) collective-permute-start(f32[4,640]{1,0:T(4,128)S(1)} %get-tuple-element.35), channel_id=1, source_target_pairs={{0,9},{1,8},{2,11},{3,10},{4,13},{5,12},{6,15},{7,14},{8,1},{9,0},... | collective-permute-start | bytes 30728 | tf_op jit(solution)/shard_map/ppermute | solution.py:442
  8.7 1.4 %collective-permute-done.3.other_ref = f32[4,640]{1,0:T(4,128)S(1)} collective-permute-done((f32[4,640]{1,0:T(4,128)S(1)}, f32[4,640]{1,0:T(4,128)S(1)}, u32[]{:S(2)}, u32[]{:S(2)}) %collective-permute-start.3) | collective-permute-done | bytes 10272 | tf_op jit(solution)/shard_map/ppermute | solution.py:442
  10.1 1.8 %collective-permute-start.4 = (f32[4,640]{1,0:T(4,128)S(1)}, f32[4,640]{1,0:T(4,128)S(1)}, u32[]{:S(2)}, u32[]{:S(2)}) collective-permute-start(f32[4,640]{1,0:T(4,128)S(1)} %get-tuple-element.37), channel_id=1, source_target_pairs={{0,10},{1,11},{2,8},{3,9},{4,14},{5,15},{6,12},{7,13},{8,2},{9,3},... | collective-permute-start | bytes 30728 | tf_op jit(solution)/shard_map/ppermute | solution.py:442
  11.9 1.4 %collective-permute-done.4.other_ref = f32[4,640]{1,0:T(4,128)S(1)} collective-permute-done((f32[4,640]{1,0:T(4,128)S(1)}, f32[4,640]{1,0:T(4,128)S(1)}, u32[]{:S(2)}, u32[]{:S(2)}) %collective-permute-start.4) | collective-permute-done | bytes 10272 | tf_op jit(solution)/shard_map/ppermute | solution.py:442
  13.3 2.8 %collective-permute-start.5 = (f32[2,640]{1,0:T(2,128)S(1)}, f32[2,640]{1,0:T(2,128)S(1)}, u32[]{:S(2)}, u32[]{:S(2)}) collective-permute-start(f32[2,640]{1,0:T(2,128)S(1)} %get-tuple-element.39), channel_id=1, source_target_pairs={{0,12},{1,13},{2,14},{3,15},{4,8},{5,9},{6,10},{7,11},{8,4},{9,5},... | collective-permute-start | bytes 15368 | tf_op jit(solution)/shard_map/ppermute | solution.py:442
  16.1 0.1 shard_map.79.refs_2_
  16.2 1.2 %collective-permute-done.5.other_ref = f32[2,640]{1,0:T(2,128)S(1)} collective-permute-done((f32[2,640]{1,0:T(2,128)S(1)}, f32[2,640]{1,0:T(2,128)S(1)}, u32[]{:S(2)}, u32[]{:S(2)}) %collective-permute-start.5) | collective-permute-done | bytes 5152 | tf_op jit(solution)/shard_map/ppermute | solution.py:442
  17.5 0.7 %shard_map.80 = f32[128,128]{1,0:T(8,128)} custom-call(f32[4,640]{1,0:T(4,128)S(1)} %get-tuple-element.38.own_ref, f32[2,640]{1,0:T(2,128)S(1)} %collective-permute-done.5.other_ref, f32[4,384]{1,0:T(4,128)S(1)} %get-tuple-element.40.refs_0_, f32[4,384]{1,0:T(4,128)S(1)} %get-tuple-element.41.refs_1_, f32[144,128]{1,0:T(8,128)S(1)} %shard_map.79.refs_2_, ...), custom_call_target="tpu_custom_call" | custom-call | flops 500000 | bytes 500000 | tf_op jit(solution)/shard_map/pallas_call | solution.py:489
  (2 shorter events, 0.0 us)
Async XLA Ops:
  1.4 3.8 %collective-permute-start = (f32[8,128]{1,0:T(8,128)S(1)}, f32[8,128]{1,0:T(8,128)S(1)}, u32[]{:S(2)}, u32[]{:S(2)}) collective-permute-start(f32[8,128]{1,0:T(8,128)S(1)} %get-tuple-element.25.refs_0_), channel_id=1, source_target_pairs={{0,24},{1,25},{2,26},{3,27},{4,28},{5,29},{6,30},{7,31},{8,16},{9,... | collective-permute-start | bytes 12296 | tf_op jit(solution)/shard_map/ppermute | solution.py:442
  3.8 2.0 %collective-permute-start.2 = (f32[720,128]{1,0:T(8,128)S(1)}, f32[720,128]{1,0:T(8,128)S(1)}, u32[]{:S(2)}, u32[]{:S(2)}) collective-permute-start(f32[720,128]{1,0:T(8,128)S(1)} %get-tuple-element.26.block_ref), channel_id=1, source_target_pairs={{0,8},{1,9},{2,10},{3,11},{4,12},{5,13},{6,14},{7,15},{8,0},{9,1},... | collective-permute-start | bytes 1105928 | tf_op jit(solution)/shard_map/ppermute | solution.py:442
  5.2 1.5 %collective-permute-start.1 = (f32[8,128]{1,0:T(8,128)S(1)}, f32[8,128]{1,0:T(8,128)S(1)}, u32[]{:S(2)}, u32[]{:S(2)}) collective-permute-start(f32[8,128]{1,0:T(8,128)S(1)} %collective-permute-done.refs_1_), channel_id=1, source_target_pairs={{0,8},{1,9},{2,10},{3,11},{4,12},{5,13},{6,14},{7,15},{8,0},{9,1},... | collective-permute-start | bytes 12296 | tf_op jit(solution)/shard_map/ppermute | solution.py:442
  6.9 3.2 %collective-permute-start.3 = (f32[4,640]{1,0:T(4,128)S(1)}, f32[4,640]{1,0:T(4,128)S(1)}, u32[]{:S(2)}, u32[]{:S(2)}) collective-permute-start(f32[4,640]{1,0:T(4,128)S(1)} %get-tuple-element.35), channel_id=1, source_target_pairs={{0,9},{1,8},{2,11},{3,10},{4,13},{5,12},{6,15},{7,14},{8,1},{9,0},... | collective-permute-start | bytes 30728 | tf_op jit(solution)/shard_map/ppermute | solution.py:442
  10.1 3.2 %collective-permute-start.4 = (f32[4,640]{1,0:T(4,128)S(1)}, f32[4,640]{1,0:T(4,128)S(1)}, u32[]{:S(2)}, u32[]{:S(2)}) collective-permute-start(f32[4,640]{1,0:T(4,128)S(1)} %get-tuple-element.37), channel_id=1, source_target_pairs={{0,10},{1,11},{2,8},{3,9},{4,14},{5,15},{6,12},{7,13},{8,2},{9,3},... | collective-permute-start | bytes 30728 | tf_op jit(solution)/shard_map/ppermute | solution.py:442
  13.3 4.1 %collective-permute-start.5 = (f32[2,640]{1,0:T(2,128)S(1)}, f32[2,640]{1,0:T(2,128)S(1)}, u32[]{:S(2)}, u32[]{:S(2)}) collective-permute-start(f32[2,640]{1,0:T(2,128)S(1)} %get-tuple-element.39), channel_id=1, source_target_pairs={{0,12},{1,13},{2,14},{3,15},{4,8},{5,9},{6,10},{7,11},{8,4},{9,5},... | collective-permute-start | bytes 15368 | tf_op jit(solution)/shard_map/ppermute | solution.py:442

commit v29 on v25

--- a/solution.py
+++ b/solution.py
@@ -208,11 +208,25 @@
     return [(step, 0) for step in doubling(SUBLANES)]
 
 
+def put_line(block_ref, rows, number, value):
+    start = 2 * rows + number * LANES
+    block_ref[start : start + LANES, :] = value.T
+
+
+def line_leaves(block_ref, rows):
+    stride = LANES // SUBLANES
+    leaves = []
+    for index in range(stride):
+        starts = [2 * rows + number * LANES + index for number in range(3)]
+        face, held, source = (strided(block_ref, start, SUBLANES, stride) for start in starts)
+        leaves.append((face, None, held, None, source))
+    return leaves
+
+
 def x_forward_kernel(
     halves, mobile_hbm, faces_hbm, across_hbm, capacity_hbm, immobile_hbm, rates_hbm, shares_hbm,
     message_ref, block_ref,
     mobile_ref, faces_ref, capacity_ref, immobile_ref, rates_ref, shares_ref, arrived,
-    faces_t, storage_t, source_t,
 ):
     rows = mobile_ref.shape[0]
     pairs = (
@@ -229,27 +243,20 @@
     capacity = capacity_ref[...]
     storage = 1.0 + capacity * sum(weights[1:], weights[0])
     block_ref[0:rows, :] = storage
-    storage_t[0:LANES, :] = storage.T
+    put_line(block_ref, rows, 1, storage)
     copies[3].wait()
-    faces_t[0:LANES, :] = faces_ref[...].T
+    put_line(block_ref, rows, 0, faces_ref[...])
     copies[4].wait()
     total = None
     for zone, weight in enumerate(weights):
         total = plus(total, weight * immobile_ref[zone * rows : (zone + 1) * rows, :])
     copies[5].wait()
-    source_t[0:LANES, :] = (mobile_ref[...] + capacity * total).T
-    leaves = []
-    for index in range(stride):
-        face, held, source = (strided(ref, index, SUBLANES, stride) for ref in (faces_t, storage_t, source_t))
-        leaves.append((face, None, held, None, source))
-    piece, nodes = tree_all(leaves, x_rolls(halves))
-    start = 2 * rows
-    for part in [part for node in nodes for part in node]:
-        block_ref[start : start + SUBLANES, :] = part
-        start += SUBLANES
+    put_line(block_ref, rows, 2, mobile_ref[...] + capacity * total)
+    piece, _ = tree_all(line_leaves(block_ref, rows), x_rolls(halves))
+    last = block_ref.shape[0] - SUBLANES
     for row, value in enumerate(piece):
         message_ref[row : row + 1, :] = value[0:1, :]
-        block_ref[start + row : start + row + 1, :] = value[0:1, :]
+        block_ref[last + row : last + row + 1, :] = value[0:1, :]
     copies[6].wait()
 
 
@@ -263,7 +270,7 @@
     stride = LANES // SUBLANES
     rolls = x_rolls(halves)
     total = stride - 1 + len(rolls)
-    nodes = state_parts(block_ref.at[2 * rows :, :], 0, total, 3)
+    _, nodes = tree_all(line_leaves(block_ref, rows), rolls)
     own_refs = extra_refs if own else ()
     if not own:
         extra_refs[0][...] = block_ref[-SUBLANES:, :]
@@ -509,7 +516,6 @@
     capacity, immobile = flat(capacity), flat(immobile)
     square = VMEM((rows, LANES), jnp.float32)
     spare = max(rows, LANES) // SUBLANES
-    x_nodes = LANES // SUBLANES - 1 + len(x_rolls(halves))
     y_nodes = halves * (rows // SUBLANES // halves - 1 + len(y_rolls()))
     message, block = kernel_call(
         functools.partial(x_forward_kernel, halves),
@@ -519,12 +525,11 @@
                 mobile, dispersion_x, dispersion_y, capacity, immobile, exchange_rates[None], rate_shares[None],
             )
         ),
-        [f32(SUBLANES, rows), held_f32(2 * rows + (3 * x_nodes + 1) * SUBLANES, LANES)],
+        [f32(SUBLANES, rows), held_f32(2 * rows + 3 * LANES + spare + SUBLANES, LANES)],
         [square] * 3
         + [VMEM((zones * rows, LANES), jnp.float32)]
         + [pltpu.SMEM((1, zones), jnp.float32)] * 2
-        + [pltpu.SemaphoreType.DMA((7,))]
-        + [VMEM((LANES + LANES // SUBLANES, rows), jnp.float32)] * 3,
+        + [pltpu.SemaphoreType.DMA((7,))],
         pltpu.HBM,
     )
     def prepare(part, own):

time: 18.3 us -> 18.3 us (level)
  waiting for transfers between devices: 5.03 us -> 4.74 us
  Pallas kernels: 2.83 us -> 3.11 us
    ppermute x6, waiting for transfers between devices: 5.03 us -> 4.74 us  [trade(): return lax.ppermute(value, ('xg', 'yd'), pairs)]
    pallas_call x8, Pallas kernels: 2.83 us -> 3.11 us  [kernel_call(): pl.pallas_call(body, out_shape=outputs, in_specs=[pl.BlockSpec(memory_spa...]
  transfers between devices with their start and end apart: 6 -> 6, of which waited for: 5 -> 5; matrix products, arithmetic and copies ran while one was open for 0% -> 0% of each run, Pallas kernels for 3% -> 5%
where the time goes in v29:
time: 18.3 us; the launch traced here: 18.1 us
  starting transfers between devices  10.2 us (56%)
  waiting for transfers between devices  4.74 us (26%)
  Pallas kernels  3.11 us (17%)
    ppermute x6, starting transfers between devices, trade(): return lax.ppermute(value, ('xg', 'yd'), pairs)  10.2 us
    ppermute x6, waiting for transfers between devices, trade(): return lax.ppermute(value, ('xg', 'yd'), pairs)  4.74 us
    pallas_call x8, Pallas kernels, kernel_call(): pl.pallas_call(body, out_shape=outputs, in_specs=[pl.BlockSpec(memory_spa...  3.11 us
  transfers between devices with their start and end apart: 6, of which 5 were waited for; matrix products, arithmetic and copies ran while one was open for 0% of the time, Pallas kernels for 5%

profile of v29, /device:TPU:0, one launch (start us, length us, event | category | flops | bytes accessed | tf_op | source)
XLA Modules:
  0.0 18.1 jit_solution(6191662447474418498)
XLA Ops:
  0.0 1.4 %shard_map.73 = (f32[8,128]{1,0:T(8,128)S(1)}, f32[664,128]{1,0:T(8,128)S(1)}) custom-call(f32[128,128]{1,0:T(8,128)} %bitcast.9, f32[128,128]{1,0:T(8,128)} %bitcast.10, f32[128,128]{1,0:T(8,128)} %bitcast.11, f32[128,128]{1,0:T(8,128)} %bitcast.12, f32[512,128]{1,0:T(8,128)} %bitcast.8, f32[1,4]{1,0:T(1,128)} %bitcast.13, f32[1,4]{1,0:T(1,128)} %bitcast.14), custom_call_target="tpu_custom_call" | custom-call | flops 500000 | bytes 500000 | tf_op jit(solution)/shard_map/pallas_call | solution.py:493
  1.4 2.4 %collective-permute-start = (f32[8,128]{1,0:T(8,128)S(1)}, f32[8,128]{1,0:T(8,128)S(1)}, u32[]{:S(2)}, u32[]{:S(2)}) collective-permute-start(f32[8,128]{1,0:T(8,128)S(1)} %get-tuple-element.25.refs_0_), channel_id=1, source_target_pairs={{0,24},{1,25},{2,26},{3,27},{4,28},{5,29},{6,30},{7,31},{8,16},{9,... | collective-permute-start | bytes 12296 | tf_op jit(solution)/shard_map/ppermute | solution.py:446
  3.8 0.7 %collective-permute-start.2 = (f32[664,128]{1,0:T(8,128)S(1)}, f32[664,128]{1,0:T(8,128)S(1)}, u32[]{:S(2)}, u32[]{:S(2)}) collective-permute-start(f32[664,128]{1,0:T(8,128)S(1)} %get-tuple-element.26.block_ref), channel_id=1, source_target_pairs={{0,8},{1,9},{2,10},{3,11},{4,12},{5,13},{6,14},{7,15},{8,0},{9,1},... | collective-permute-start | bytes 1019912 | tf_op jit(solution)/shard_map/ppermute | solution.py:446
  4.5 0.4 %shard_map.74 = (f32[8,384]{1,0:T(8,128)S(1)}, f32[400,128]{1,0:T(8,128)S(1)}, f32[272,128]{1,0:T(8,128)S(1)}, f32[480,128]{1,0:T(8,128)S(1)}, f32[272,128]{1,0:T(8,128)S(1)}) custom-call(f32[664,128]{1,0:T(8,128)S(1)} %get-tuple-element.26.block_ref), custom_call_target="tpu_custom_call" | custom-call | flops 10000000000 | bytes 10000000000 | tf_op jit(solution)/shard_map/pallas_call | solution.py:493
  4.9 0.3 %collective-permute-done.refs_1_ = f32[8,128]{1,0:T(8,128)S(1)} collective-permute-done((f32[8,128]{1,0:T(8,128)S(1)}, f32[8,128]{1,0:T(8,128)S(1)}, u32[]{:S(2)}, u32[]{:S(2)}) %collective-permute-start) | collective-permute-done | bytes 4128 | tf_op jit(solution)/shard_map/ppermute | solution.py:446
  5.1 0.6 %collective-permute-start.1 = (f32[8,128]{1,0:T(8,128)S(1)}, f32[8,128]{1,0:T(8,128)S(1)}, u32[]{:S(2)}, u32[]{:S(2)}) collective-permute-start(f32[8,128]{1,0:T(8,128)S(1)} %collective-permute-done.refs_1_), channel_id=1, source_target_pairs={{0,8},{1,9},{2,10},{3,11},{4,12},{5,13},{6,14},{7,15},{8,0},{9,1},... | collective-permute-start | bytes 12296 | tf_op jit(solution)/shard_map/ppermute | solution.py:446
  5.8 0.0 collective-permute-done.2.block_ref
  5.8 0.3 %shard_map.75 = (f32[8,384]{1,0:T(8,128)S(1)}, f32[400,128]{1,0:T(8,128)S(1)}, f32[272,128]{1,0:T(8,128)S(1)}, f32[8,128]{1,0:T(8,128)S(1)}) custom-call(f32[664,128]{1,0:T(8,128)S(1)} %collective-permute-done.2.block_ref), custom_call_target="tpu_custom_call" | custom-call | flops 10000000000 | bytes 10000000000 | tf_op jit(solution)/shard_map/pallas_call | solution.py:493
  6.1 0.5 %collective-permute-done.1.refs_2_ = f32[8,128]{1,0:T(8,128)S(1)} collective-permute-done((f32[8,128]{1,0:T(8,128)S(1)}, f32[8,128]{1,0:T(8,128)S(1)}, u32[]{:S(2)}, u32[]{:S(2)}) %collective-permute-start.1) | collective-permute-done | bytes 4128 | tf_op jit(solution)/shard_map/ppermute | solution.py:446
  6.6 0.2 %shard_map.76 = (f32[4,640]{1,0:T(4,128)S(1)}, f32[4,640]{1,0:T(4,128)S(1)}, f32[144,128]{1,0:T(8,128)S(1)}) custom-call(f32[8,128]{1,0:T(8,128)S(1)} %get-tuple-element.25.refs_0_, f32[8,128]{1,0:T(8,128)S(1)} %collective-permute-done.refs_1_, f32[8,128]{1,0:T(8,128)S(1)} %collective-permute-done.1.refs_2_, f32[400,128]{1,0:T(8,128)S(1)} %get-tuple-element.27.refs_3_, ...), custom_call_target="tpu_custom_call" | custom-call | flops 500000 | bytes 500000 | tf_op jit(solution)/shard_map/pallas_call | solution.py:493
  6.8 1.8 %collective-permute-start.3 = (f32[4,640]{1,0:T(4,128)S(1)}, f32[4,640]{1,0:T(4,128)S(1)}, u32[]{:S(2)}, u32[]{:S(2)}) collective-permute-start(f32[4,640]{1,0:T(4,128)S(1)} %get-tuple-element.35), channel_id=1, source_target_pairs={{0,9},{1,8},{2,11},{3,10},{4,13},{5,12},{6,15},{7,14},{8,1},{9,0},... | collective-permute-start | bytes 30728 | tf_op jit(solution)/shard_map/ppermute | solution.py:446
  8.7 1.4 %collective-permute-done.3.other_ref = f32[4,640]{1,0:T(4,128)S(1)} collective-permute-done((f32[4,640]{1,0:T(4,128)S(1)}, f32[4,640]{1,0:T(4,128)S(1)}, u32[]{:S(2)}, u32[]{:S(2)}) %collective-permute-start.3) | collective-permute-done | bytes 10272 | tf_op jit(solution)/shard_map/ppermute | solution.py:446
  10.1 1.8 %collective-permute-start.4 = (f32[4,640]{1,0:T(4,128)S(1)}, f32[4,640]{1,0:T(4,128)S(1)}, u32[]{:S(2)}, u32[]{:S(2)}) collective-permute-start(f32[4,640]{1,0:T(4,128)S(1)} %get-tuple-element.37), channel_id=1, source_target_pairs={{0,10},{1,11},{2,8},{3,9},{4,14},{5,15},{6,12},{7,13},{8,2},{9,3},... | collective-permute-start | bytes 30728 | tf_op jit(solution)/shard_map/ppermute | solution.py:446
  11.9 1.4 %collective-permute-done.4.other_ref = f32[4,640]{1,0:T(4,128)S(1)} collective-permute-done((f32[4,640]{1,0:T(4,128)S(1)}, f32[4,640]{1,0:T(4,128)S(1)}, u32[]{:S(2)}, u32[]{:S(2)}) %collective-permute-start.4) | collective-permute-done | bytes 10272 | tf_op jit(solution)/shard_map/ppermute | solution.py:446
  13.3 2.8 %collective-permute-start.5 = (f32[2,640]{1,0:T(2,128)S(1)}, f32[2,640]{1,0:T(2,128)S(1)}, u32[]{:S(2)}, u32[]{:S(2)}) collective-permute-start(f32[2,640]{1,0:T(2,128)S(1)} %get-tuple-element.39), channel_id=1, source_target_pairs={{0,12},{1,13},{2,14},{3,15},{4,8},{5,9},{6,10},{7,11},{8,4},{9,5},... | collective-permute-start | bytes 15368 | tf_op jit(solution)/shard_map/ppermute | solution.py:446
  16.1 0.1 shard_map.79.refs_2_
  16.2 1.2 %collective-permute-done.5.other_ref = f32[2,640]{1,0:T(2,128)S(1)} collective-permute-done((f32[2,640]{1,0:T(2,128)S(1)}, f32[2,640]{1,0:T(2,128)S(1)}, u32[]{:S(2)}, u32[]{:S(2)}) %collective-permute-start.5) | collective-permute-done | bytes 5152 | tf_op jit(solution)/shard_map/ppermute | solution.py:446
  17.4 0.7 %shard_map.80 = f32[128,128]{1,0:T(8,128)} custom-call(f32[4,640]{1,0:T(4,128)S(1)} %get-tuple-element.38.own_ref, f32[2,640]{1,0:T(2,128)S(1)} %collective-permute-done.5.other_ref, f32[4,384]{1,0:T(4,128)S(1)} %get-tuple-element.40.refs_0_, f32[4,384]{1,0:T(4,128)S(1)} %get-tuple-element.41.refs_1_, f32[144,128]{1,0:T(8,128)S(1)} %shard_map.79.refs_2_, ...), custom_call_target="tpu_custom_call" | custom-call | flops 500000 | bytes 500000 | tf_op jit(solution)/shard_map/pallas_call | solution.py:493
  (2 shorter events, 0.0 us)
Async XLA Ops:
  1.4 3.8 %collective-permute-start = (f32[8,128]{1,0:T(8,128)S(1)}, f32[8,128]{1,0:T(8,128)S(1)}, u32[]{:S(2)}, u32[]{:S(2)}) collective-permute-start(f32[8,128]{1,0:T(8,128)S(1)} %get-tuple-element.25.refs_0_), channel_id=1, source_target_pairs={{0,24},{1,25},{2,26},{3,27},{4,28},{5,29},{6,30},{7,31},{8,16},{9,... | collective-permute-start | bytes 12296 | tf_op jit(solution)/shard_map/ppermute | solution.py:446
  3.8 2.0 %collective-permute-start.2 = (f32[664,128]{1,0:T(8,128)S(1)}, f32[664,128]{1,0:T(8,128)S(1)}, u32[]{:S(2)}, u32[]{:S(2)}) collective-permute-start(f32[664,128]{1,0:T(8,128)S(1)} %get-tuple-element.26.block_ref), channel_id=1, source_target_pairs={{0,8},{1,9},{2,10},{3,11},{4,12},{5,13},{6,14},{7,15},{8,0},{9,1},... | collective-permute-start | bytes 1019912 | tf_op jit(solution)/shard_map/ppermute | solution.py:446
  5.1 1.5 %collective-permute-start.1 = (f32[8,128]{1,0:T(8,128)S(1)}, f32[8,128]{1,0:T(8,128)S(1)}, u32[]{:S(2)}, u32[]{:S(2)}) collective-permute-start(f32[8,128]{1,0:T(8,128)S(1)} %collective-permute-done.refs_1_), channel_id=1, source_target_pairs={{0,8},{1,9},{2,10},{3,11},{4,12},{5,13},{6,14},{7,15},{8,0},{9,1},... | collective-permute-start | bytes 12296 | tf_op jit(solution)/shard_map/ppermute | solution.py:446
  6.8 3.2 %collective-permute-start.3 = (f32[4,640]{1,0:T(4,128)S(1)}, f32[4,640]{1,0:T(4,128)S(1)}, u32[]{:S(2)}, u32[]{:S(2)}) collective-permute-start(f32[4,640]{1,0:T(4,128)S(1)} %get-tuple-element.35), channel_id=1, source_target_pairs={{0,9},{1,8},{2,11},{3,10},{4,13},{5,12},{6,15},{7,14},{8,1},{9,0},... | collective-permute-start | bytes 30728 | tf_op jit(solution)/shard_map/ppermute | solution.py:446
  10.1 3.2 %collective-permute-start.4 = (f32[4,640]{1,0:T(4,128)S(1)}, f32[4,640]{1,0:T(4,128)S(1)}, u32[]{:S(2)}, u32[]{:S(2)}) collective-permute-start(f32[4,640]{1,0:T(4,128)S(1)} %get-tuple-element.37), channel_id=1, source_target_pairs={{0,10},{1,11},{2,8},{3,9},{4,14},{5,15},{6,12},{7,13},{8,2},{9,3},... | collective-permute-start | bytes 30728 | tf_op jit(solution)/shard_map/ppermute | solution.py:446
  13.3 4.1 %collective-permute-start.5 = (f32[2,640]{1,0:T(2,128)S(1)}, f32[2,640]{1,0:T(2,128)S(1)}, u32[]{:S(2)}, u32[]{:S(2)}) collective-permute-start(f32[2,640]{1,0:T(2,128)S(1)} %get-tuple-element.39), channel_id=1, source_target_pairs={{0,12},{1,13},{2,14},{3,15},{4,8},{5,9},{6,10},{7,11},{8,4},{9,5},... | collective-permute-start | bytes 15368 | tf_op jit(solution)/shard_map/ppermute | solution.py:446
